TPU v7x, 32 devices: a whole 2x2x4 slice. The times are simulated.
32 devices in a mesh: groups: 2 (over y), adapter: 8 (over z, x), tensor: 2 (over core).
Axes of the slice: x: 2, y: 2, z: 4, core: 2. Of those that a mesh axis runs over, the one named last changes fastest.
Arguments:
- tokens: bfloat16 [2048, 5120], P(('groups', 'adapter'), 'tensor'), parts along dimension 0, may hold values from -6 to 6
- cotangent: bfloat16 [2048, 5120], P(('groups', 'adapter'), 'tensor'), parts along dimension 0, may hold values from -3 to 3
- down_adapter: bfloat16 [8, 64, 5120], P('adapter', None, 'tensor'), may hold values from -0.078125 to 0.078125
- up_adapter: bfloat16 [8, 64, 5120], P('adapter', None, 'tensor'), may hold values from -0.75 to 0.75
- token_lists: int32 [16, 256], P('groups'), parts along dimension 0, may hold values from 0 to 1023, as said below
- gating: float32 [16, 256], P(('groups', 'adapter')), parts along dimension 0, may hold values from 0.25 to 1
Outputs:
- branch_out: bfloat16 [2048, 5120], P(('groups', 'adapter'), 'tensor'), parts along dimension 0
- input_grad: bfloat16 [2048, 5120], P(('groups', 'adapter'), 'tensor'), parts along dimension 0
- down_grad: bfloat16 [16, 64, 5120], P(('groups', 'adapter'), None, 'tensor'), parts along dimension 0
- up_grad: bfloat16 [16, 64, 5120], P(('groups', 'adapter'), None, 'tensor'), parts along dimension 0
There are 2 independent parts, one for each index of `groups`. A program takes and returns all parts, laid end to end along the dimension named above; an argument that names none is the same for every part. Nothing has to cross between parts.
Inputs may be any that keep to these rules, and one draw needn't show every extreme that they name: `token_lists`: row e holds 256 distinct tokens, grouped by the index of adapter that holds them (tokens t with t // 128 equal), in increasing order of that index; every index supplies between 16 and 48 tokens to every expert, and for every expert some index supplies exactly 48.
All inputs are finite; a program needn't handle non-finite values.
Results may differ from a plain program's by a relative error of at most 0.0064.
Values may be sent and summed in bfloat16 or wider, within the bound.
No kernel may reach another device: no remote copies, remote signals or barrier semaphores. Data moves between devices by JAX's collectives and lax.ppermute only.
A program may use at most 64 MiB of HBM per device.

v0:
```python
import jax
import jax.numpy as jnp
from jax import lax
from jax.sharding import PartitionSpec as P

adapter_scale_factor = 2.0


def contract_last(left_op, right_op):
    return lax.dot_general(
        left_op, right_op, (((1,), (1,)), ((), ())), preferred_element_type=jnp.float32
    )


def contract_first(left_op, right_op):
    return lax.dot_general(
        left_op, right_op, (((0,), (0,)), ((), ())), preferred_element_type=jnp.float32
    )


def gather_rows(source_rows, local_index, live_slot):
    taken_rows = jnp.take(source_rows, local_index.reshape(-1), axis=0)
    taken_rows = taken_rows.reshape(local_index.shape + (source_rows.shape[1],))
    return jnp.where(live_slot[:, :, None], taken_rows, jnp.zeros_like(taken_rows))


def combine(onehot, returned):
    flat_rows = returned.reshape(-1, returned.shape[-1])
    return jnp.dot(onehot, flat_rows, preferred_element_type=jnp.float32).astype(jnp.bfloat16)


def local(tokens, cotangent, down_adapter, up_adapter, token_lists, gating):
    owners = lax.axis_size("adapter")
    my_index = lax.axis_index("adapter")
    tok_local = tokens.shape[0]
    half_width = tokens.shape[1]
    capacity = gating.shape[1]
    slot_count = 3 * capacity // (2 * owners)
    slot_ids = jnp.arange(slot_count, dtype=jnp.int32)
    source = token_lists // tok_local
    sent_count = jnp.sum((source == my_index).astype(jnp.int32), axis=1)
    sent_start = jnp.sum((source < my_index).astype(jnp.int32), axis=1)
    live_send = slot_ids[None, :] < sent_count[:, None]
    position = jnp.minimum(sent_start[:, None] + slot_ids[None, :], capacity - 1)
    local_index = jnp.take_along_axis(token_lists, position, axis=1) - my_index * tok_local
    local_index = jnp.where(live_send, local_index, 0)
    outgoing_rows = gather_rows(tokens, local_index, live_send)
    cot_send = gather_rows(cotangent, local_index, live_send)
    token_ids = jnp.arange(tok_local, dtype=jnp.int32)
    onehot = ((token_ids[:, None] == local_index.reshape(1, -1)) & live_send.reshape(1, -1)).astype(
        jnp.bfloat16
    )
    own_list = lax.dynamic_slice_in_dim(token_lists, my_index, 1, 0)[0]
    own_source = own_list // tok_local
    peer_ids = jnp.arange(owners, dtype=jnp.int32)
    recv_count = jnp.sum((own_source[None, :] == peer_ids[:, None]).astype(jnp.int32), axis=1)
    received_offset = jnp.sum((own_source[None, :] < peer_ids[:, None]).astype(jnp.int32), axis=1)
    active_received = slot_ids[None, :] < recv_count[:, None]
    gate_pos = jnp.minimum(received_offset[:, None] + slot_ids[None, :], capacity - 1)
    gate_slot_values = jnp.take(gating[0], gate_pos.reshape(-1)).reshape(gate_pos.shape)
    scale_factors = (
        adapter_scale_factor * jnp.where(active_received, gate_slot_values, 0.0)
    ).reshape(-1, 1)
    down_matrix = down_adapter[0]
    up_matrix = up_adapter[0]
    flat_shape = (owners * slot_count, half_width)
    block_shape = (owners, slot_count, half_width)
    row_recv = lax.all_to_all(outgoing_rows, "adapter", split_axis=0, concat_axis=0, tiled=True)
    rows_in = row_recv.reshape(flat_shape)
    low_rank = lax.psum(contract_last(rows_in, down_matrix), "tensor").astype(jnp.bfloat16)
    out_rows = (
        scale_factors * jnp.dot(low_rank, up_matrix, preferred_element_type=jnp.float32)
    ).astype(jnp.bfloat16)
    out_back = lax.all_to_all(
        out_rows.reshape(block_shape), "adapter", split_axis=0, concat_axis=0, tiled=True
    )
    cot_recv = lax.all_to_all(cot_send, "adapter", split_axis=0, concat_axis=0, tiled=True)
    weighted = (scale_factors * cot_recv.reshape(flat_shape)).astype(jnp.bfloat16)
    low_grad = lax.psum(contract_last(weighted, up_matrix), "tensor").astype(jnp.bfloat16)
    back_rows = jnp.dot(low_grad, down_matrix, preferred_element_type=jnp.float32).astype(
        jnp.bfloat16
    )
    grad_back = lax.all_to_all(
        back_rows.reshape(block_shape), "adapter", split_axis=0, concat_axis=0, tiled=True
    )
    branch_out = combine(onehot, out_back)
    input_grad = combine(onehot, grad_back)
    down_grad = (contract_first(low_grad, rows_in) / capacity).astype(jnp.bfloat16)[None]
    up_grad = (contract_first(low_rank, weighted) / capacity).astype(jnp.bfloat16)[None]
    return (branch_out, input_grad, down_grad, up_grad)


def solution(mesh):
    in_specs = (
        P(("groups", "adapter"), "tensor"),
        P(("groups", "adapter"), "tensor"),
        P("adapter", None, "tensor"),
        P("adapter", None, "tensor"),
        P("groups", None),
        P(("groups", "adapter"), None),
    )
    out_specs = (
        P(("groups", "adapter"), "tensor"),
        P(("groups", "adapter"), "tensor"),
        P(("groups", "adapter"), None, "tensor"),
        P(("groups", "adapter"), None, "tensor"),
    )
    return jax.shard_map(local, mesh=mesh, in_specs=in_specs, out_specs=out_specs, check_vma=False)
```

profile of v0, /device:TPU:0, one launch (start us, length us, event | category | flops | bytes accessed | tf_op | source)
XLA Modules:
  0.0 230.0 jit_solution(3602579825134336823)
XLA Ops:
  0.7 0.9 convert_reduce_fusion.2
  1.9 2.7 %gather_fusion.1 = s32[384]{0:T(512)S(1)} fusion(s32[8,256]{1,0:T(8,128)S(1)} %copy-done.2, s32[384]{0:T(512)S(1)} %reshape.292), kind=kCustom, calls=%fused_computation.3 | custom fusion | bytes 6144 | tf_op jit(solution)/shard_map/jit(take_along_axis)/gather | solution.py:45
  5.0 3.3 %gather_fusion.2 = bf16[384,2560]{1,0:T(8,128)(2,1)} fusion(bf16[128,2560]{1,0:T(8,128)(2,1)S(1)} %copy-done, s32[1024]{0:T(1024)S(1)} %pad_clamp_fusion), kind=kCustom, calls=%fused_computation.clone | custom fusion | bytes 3933696 | tf_op jit(solution)/shard_map/jit(_take)/gather | solution.py:22
  8.3 3.3 %gather_fusion.3 = bf16[384,2560]{1,0:T(8,128)(2,1)} fusion(bf16[128,2560]{1,0:T(8,128)(2,1)S(1)} %copy-done.3, s32[1024]{0:T(1024)S(1)} %pad_clamp_fusion), kind=kCustom, calls=%fused_computation.1.clone | custom fusion | bytes 3933696 | tf_op jit(solution)/shard_map/jit(_take)/gather | solution.py:22
  11.6 2.5 %broadcast_select_fusion = (bf16[384,2560]{1,0:T(8,128)(2,1)S(1)}, bf16[384,2560]{1,0:T(8,128)(2,1)S(1)}) fusion(bf16[384,2560]{1,0:T(8,128)(2,1)} %gather_fusion.3, pred[384]{0:T(512)(128)(4,1)S(1)} %get-tuple-element.11, bf16[384,2560]{1,0:T(8,128)(2,1)} %gather_fusion.2), kind=kLoop, calls=%fused_computation.18 | loop fusion | flops 1966080 | bytes 7864704 | tf_op jit(solution)/shard_map/jit(_take)/select_n | solution.py:22
  14.1 1.6 broadcast_select_fusion.2
  15.7 52.8 %all_to_all.20 = bf16[8,48,2560]{2,1,0:T(8,128)(2,1)S(1)} all-to-all(bf16[8,48,2560]{2,1,0:T(8,128)(2,1)S(1)} %get-tuple-element.13), channel_id=1, replica_groups=mesh['groups'=2,'adapter'=8,'tensor'=2] {'adapter'}, dimensions={0} | all-to-all | bytes 3932160 | tf_op jit(solution)/shard_map/all_to_all | solution.py:77
  68.6 4.5 %all-to-all-start = ((bf16[8,48,2560]{2,1,0:T(8,128)(2,1)}), bf16[8,48,2560]{2,1,0:T(8,128)(2,1)}, u32[]{:S(2)}, u32[]{:S(2)}) async-start(bf16[8,48,2560]{2,1,0:T(8,128)(2,1)} %get-tuple-element.14), calls=%async_computation | async-start | bytes 3932160 | tf_op jit(solution)/shard_map/all_to_all | solution.py:68
  73.4 2.8 %gather_fusion = f32[384]{0:T(512)S(1)} fusion(f32[256]{0:T(256)S(1)} %bitcast.44, s32[1024]{0:T(1024)S(1)} %pad_clamp_fusion.1), kind=kCustom, calls=%fused_computation.2 | custom fusion | bytes 4608 | tf_op jit(solution)/shard_map/jit(_take)/gather | solution.py:60
  76.8 0.6 copy-done.5
  77.4 0.7 fusion.6
  78.1 39.2 %all-to-all-done = bf16[8,48,2560]{2,1,0:T(8,128)(2,1)} async-done(((bf16[8,48,2560]{2,1,0:T(8,128)(2,1)}), bf16[8,48,2560]{2,1,0:T(8,128)(2,1)}, u32[]{:S(2)}, u32[]{:S(2)}) %all-to-all-start) | async-done | bytes 1966112 | tf_op jit(solution)/shard_map/all_to_all | solution.py:68
  117.3 2.3 fusion.10
  119.6 4.6 %all-reduce.2 = (bf16[384,64]{0,1:T(8,128)(2,1)S(1)}, bf16[384,64]{0,1:T(8,128)(2,1)}) all-reduce(f32[384,64]{0,1:T(8,128)S(1)} %fusion.10, f32[384,64]{0,1:T(8,128)S(1)} %fusion.6), channel_id=1, replica_groups=mesh['groups'=2,'adapter'=8,'tensor'=2] {'tensor'}, use_global_device_ids=true, to_apply=%region_4.6 | all-reduce | flops 49152 | bytes 294912 | tf_op jit(solution)/shard_map/psum | solution.py:70
  124.1 2.8 %convolution_convert_fusion = bf16[384,2560]{1,0:T(8,128)(2,1)} fusion(bf16[1,64,2560]{2,1,0:T(8,128)(2,1)S(1)} %copy-done.4, bf16[384,64]{0,1:T(8,128)(2,1)} %get-tuple-element.10), kind=kOutput, calls=%fused_computation.6 | convolution fusion | flops 126812160 | bytes 2342912 | tf_op jit(solution)/shard_map/dot_general | solution.py:80
  126.9 4.3 %all-to-all-start.3 = ((bf16[8,48,2560]{2,1,0:T(8,128)(2,1)}), bf16[8,48,2560]{2,1,0:T(8,128)(2,1)}, u32[]{:S(2)}, u32[]{:S(2)}) async-start(bf16[8,48,2560]{2,1,0:T(8,128)(2,1)} %bitcast.47), calls=%async_computation.3 | async-start | bytes 3932160 | tf_op jit(solution)/shard_map/all_to_all | solution.py:83
  131.5 2.0 fusion
  133.5 43.8 %all-to-all-done.3 = bf16[8,48,2560]{2,1,0:T(8,128)(2,1)} async-done(((bf16[8,48,2560]{2,1,0:T(8,128)(2,1)}), bf16[8,48,2560]{2,1,0:T(8,128)(2,1)}, u32[]{:S(2)}, u32[]{:S(2)}) %all-to-all-start.3) | async-done | bytes 1966112 | tf_op jit(solution)/shard_map/all_to_all | solution.py:83
  177.4 4.5 %all-to-all-start.1 = ((bf16[8,48,2560]{2,1,0:T(8,128)(2,1)}), bf16[8,48,2560]{2,1,0:T(8,128)(2,1)}, u32[]{:S(2)}, u32[]{:S(2)}) async-start(bf16[8,48,2560]{2,1,0:T(8,128)(2,1)} %bitcast.46), calls=%async_computation.1 | async-start | bytes 3932160 | tf_op jit(solution)/shard_map/all_to_all | solution.py:74
  181.8 2.7 %fusion.5 = bf16[1,64,2560]{2,1,0:T(8,128)(2,1)} fusion(bf16[384,2560]{1,0:T(8,128)(2,1)} %bitcast.3, bf16[384,64]{0,1:T(8,128)(2,1)S(1)} %copy-done.6), kind=kOutput, calls=%fused_computation.17 | convolution fusion | flops 126156800 | bytes 2342912 | tf_op jit(solution)/shard_map/dot_general | solution.py:16
  185.0 1.2 fusion.4
  186.2 2.9 %convolution_convert_fusion.1 = bf16[128,2560]{1,0:T(8,128)(2,1)} fusion(bf16[384,2560]{1,0:T(8,128)(2,1)} %bitcast.11, s32[384]{0:T(512)S(1)} %get-tuple-element.12, pred[384]{0:T(512)(128)(4,1)S(1)} %lt.136), kind=kOutput, calls=%fused_computation.10 | convolution fusion | flops 252084224 | bytes 2623360 | tf_op jit(solution)/shard_map/dot_general | solution.py:29
  189.1 38.1 %all-to-all-done.1 = bf16[8,48,2560]{2,1,0:T(8,128)(2,1)} async-done(((bf16[8,48,2560]{2,1,0:T(8,128)(2,1)}), bf16[8,48,2560]{2,1,0:T(8,128)(2,1)}, u32[]{:S(2)}, u32[]{:S(2)}) %all-to-all-start.1) | async-done | bytes 1966112 | tf_op jit(solution)/shard_map/all_to_all | solution.py:74
  227.1 2.9 %convolution_convert_fusion.2 = bf16[128,2560]{1,0:T(8,128)(2,1)} fusion(bf16[384,2560]{1,0:T(8,128)(2,1)} %bitcast.7, s32[384]{0:T(512)S(1)} %get-tuple-element.12, pred[384]{0:T(512)(128)(4,1)S(1)} %lt.136), kind=kOutput, calls=%fused_computation.11 | convolution fusion | flops 252084224 | bytes 2623360 | tf_op jit(solution)/shard_map/dot_general | solution.py:29
  (38 shorter events, 2.1 us)
Async XLA Ops:
  0.6 4.3 %copy-start = (bf16[128,2560]{1,0:T(8,128)(2,1)S(1)}, bf16[128,2560]{1,0:T(8,128)(2,1)}, u32[]{:S(2)}) copy-start(bf16[128,2560]{1,0:T(8,128)(2,1)} %param.8) | copy-start | bytes 1966084
  0.6 1.3 copy-start.2
  5.0 3.3 %copy-start.3 = (bf16[128,2560]{1,0:T(8,128)(2,1)S(1)}, bf16[128,2560]{1,0:T(8,128)(2,1)}, u32[]{:S(2)}) copy-start(bf16[128,2560]{1,0:T(8,128)(2,1)} %param.9) | copy-start | bytes 1966084
  68.6 4.8 %copy-start.1 = (f32[1,256]{1,0:T(1,128)S(1)}, f32[1,256]{1,0:T(1,128)}, u32[]{:S(2)}) copy-start(f32[1,256]{1,0:T(1,128)} %param.13) | copy-start | bytes 3076
  68.6 48.7 %all-to-all-start = ((bf16[8,48,2560]{2,1,0:T(8,128)(2,1)}), bf16[8,48,2560]{2,1,0:T(8,128)(2,1)}, u32[]{:S(2)}, u32[]{:S(2)}) async-start(bf16[8,48,2560]{2,1,0:T(8,128)(2,1)} %get-tuple-element.14), calls=%async_computation | async-start | bytes 3932160 | tf_op jit(solution)/shard_map/all_to_all | solution.py:68
  76.4 1.0 copy-start.5
  76.8 40.5 %copy-start.4 = (bf16[1,64,2560]{2,1,0:T(8,128)(2,1)S(1)}, bf16[1,64,2560]{2,1,0:T(8,128)(2,1)}, u32[]{:S(2)}) copy-start(bf16[1,64,2560]{2,1,0:T(8,128)(2,1)} %param.10) | copy-start | bytes 983044
  126.9 50.5 %all-to-all-start.3 = ((bf16[8,48,2560]{2,1,0:T(8,128)(2,1)}), bf16[8,48,2560]{2,1,0:T(8,128)(2,1)}, u32[]{:S(2)}, u32[]{:S(2)}) async-start(bf16[8,48,2560]{2,1,0:T(8,128)(2,1)} %bitcast.47), calls=%async_computation.3 | async-start | bytes 3932160 | tf_op jit(solution)/shard_map/all_to_all | solution.py:83
  177.4 4.5 %copy-start.6 = (bf16[384,64]{0,1:T(8,128)(2,1)S(1)}, bf16[384,64]{0,1:T(8,128)(2,1)}, u32[]{:S(2)}) copy-start(bf16[384,64]{0,1:T(8,128)(2,1)} %get-tuple-element.10) | copy-start | bytes 147460
  177.4 49.8 %all-to-all-start.1 = ((bf16[8,48,2560]{2,1,0:T(8,128)(2,1)}), bf16[8,48,2560]{2,1,0:T(8,128)(2,1)}, u32[]{:S(2)}, u32[]{:S(2)}) async-start(bf16[8,48,2560]{2,1,0:T(8,128)(2,1)} %bitcast.46), calls=%async_computation.1 | async-start | bytes 3932160 | tf_op jit(solution)/shard_map/all_to_all | solution.py:74
where the time goes:
time: 231 us; the launch traced here: 230 us
  waiting for transfers between devices  121 us (52%)
  blocking collectives  57.4 us (25%)
  matrix products  17.5 us (8%)
  local copies, waits for them, and re-layouts  13.5 us (6%)
  starting transfers between devices  13.3 us (6%)
  other arithmetic  6.43 us (3%)
    all_to_all x1, blocking collectives, local(): lax.all_to_all(cot_send, 'adapter', split_axis=0, concat_axis=0, tiled=True)  52.8 us
    all_to_all x1, waiting for transfers between devices, local(): lax.all_to_all(back_rows.reshape(block_shape), 'adapter', split_axis=0, c...  43.8 us
    all_to_all x1, waiting for transfers between devices, local(): lax.all_to_all(outgoing_rows, 'adapter', split_axis=0, concat_axis=0, til...  39.2 us
    all_to_all x1, waiting for transfers between devices, local(): lax.all_to_all(out_rows.reshape(block_shape), 'adapter', split_axis=0, co...  38.1 us
    gather x2, local copies, waits for them, and re-layouts, gather_rows(): taken_rows = jnp.take(source_rows, local_index.reshape(-1), axis=0)  6.58 us
    dot_general x2, matrix products, combine(): jnp.dot(onehot, flat_rows, preferred_element_type=jnp.float32)  5.8 us
  transfers between devices with their start and end apart: 3, of which 3 were waited for; matrix products, arithmetic and copies ran while one was open for 6% of the time, Pallas kernels for 0%

commit v1 on v0

--- a/solution.py
+++ b/solution.py
@@ -29,7 +29,7 @@
     return jnp.dot(onehot, flat_rows, preferred_element_type=jnp.float32).astype(jnp.bfloat16)
 
 
-def local(tokens, cotangent, down_adapter, up_adapter, token_lists, gating):
+def by_rows(tokens, cotangent, down_adapter, up_adapter, token_lists, gating):
     owners = lax.axis_size("adapter")
     my_index = lax.axis_index("adapter")
     tok_local = tokens.shape[0]
@@ -90,6 +90,126 @@
     return (branch_out, input_grad, down_grad, up_grad)
 
 
+PLACES = 4
+
+
+def on_line(pairs):
+    return [(2 * a + side, 2 * b + side) for a, b in pairs for side in (0, 1)]
+
+
+RISE = on_line([(0, 1), (1, 2), (2, 3)])
+FALL = on_line([(1, 0), (2, 1), (3, 2)])
+RISE_OUT = on_line([(1, 2), (2, 3)])
+FALL_OUT = on_line([(2, 1), (1, 0)])
+TO_ENDS = on_line([(2, 3), (1, 0)])
+FROM_ENDS = on_line([(3, 2), (0, 1)])
+RISE_IN = on_line([(0, 1), (1, 2)])
+FALL_IN = on_line([(3, 2), (2, 1)])
+TWO_APART = on_line([(0, 2), (1, 3), (2, 0), (3, 1)])
+END_TO_END = on_line([(0, 3), (3, 0)])
+PARTNER = [(2 * a + side, 2 * a + 1 - side) for a in range(PLACES) for side in (0, 1)]
+
+
+def move(value, pairs):
+    return lax.ppermute(value, "adapter", pairs)
+
+
+def spread(matrix, high):
+    below = move(matrix, RISE)
+    above = move(matrix, FALL)
+    rising = move(below, RISE_OUT)
+    falling = move(above, FALL_OUT)
+    second = jnp.where(high, rising, falling)
+    third = move(second, TO_ENDS)
+    return matrix, below, above, second, third
+
+
+def collect(parts):
+    own, below, above, second, third = parts
+    half = jnp.bfloat16
+    back = move(third.astype(half), FROM_ENDS)
+    second = (second + back.astype(jnp.float32)).astype(half)
+    falling = move(second, FALL_IN)
+    rising = move(second, RISE_IN)
+    below = move((below + falling.astype(jnp.float32)).astype(half), FALL)
+    above = move((above + rising.astype(jnp.float32)).astype(half), RISE)
+    return own + below.astype(jnp.float32) + above.astype(jnp.float32)
+
+
+def both_cores(partial):
+    return partial + lax.ppermute(partial, "tensor", [(0, 1), (1, 0)])
+
+
+def by_pairs(tokens, cotangent, down_adapter, up_adapter, token_lists, gating):
+    me = lax.axis_index("adapter")
+    place = me // 2
+    high = place >= 2
+    tok_local = tokens.shape[0]
+    capacity = gating.shape[1]
+    down_matrix = down_adapter[0]
+    up_matrix = up_adapter[0]
+    rank = down_matrix.shape[0]
+
+    gates = (
+        gating,
+        move(gating, RISE),
+        move(gating, FALL),
+        move(gating, TWO_APART),
+        move(gating, END_TO_END),
+    )
+    experts = jnp.stack(
+        [
+            me,
+            jnp.maximum(me - 2, 0),
+            jnp.minimum(me + 2, 2 * PLACES - 1),
+            jnp.where(high, me - 4, me + 4),
+            2 * (PLACES - 1) - 2 * place + me % 2,
+        ]
+    )
+    lists = jnp.take(token_lists, experts, axis=0)
+    gate_rows = adapter_scale_factor * jnp.concatenate(gates, axis=0)
+    token_ids = jnp.arange(tok_local, dtype=jnp.int32)
+    ids = jnp.concatenate([me * tok_local + token_ids, (me ^ 1) * tok_local + token_ids])
+    taken = ids[:, None, None] == lists[None, :, :]
+    scale = jnp.sum(jnp.where(taken, gate_rows[None, :, :], 0.0), axis=2)
+    scale = jnp.repeat(scale, rank, axis=1)
+
+    tokens2 = jnp.concatenate([tokens, move(tokens, PARTNER)], axis=0)
+    downs = spread(down_matrix, high)
+    cot2 = jnp.concatenate([cotangent, move(cotangent, PARTNER)], axis=0)
+    ups = spread(up_matrix, high)
+
+    down_all = jnp.concatenate(downs, axis=0)
+    up_all = jnp.concatenate(ups, axis=0)
+    low = (scale * both_cores(contract_last(tokens2, down_all))).astype(jnp.bfloat16)
+    low_back = (scale * both_cores(contract_last(cot2, up_all))).astype(jnp.bfloat16)
+
+    def parts(weights, rows):
+        return tuple(
+            contract_first(weights[:, k * rank : (k + 1) * rank], rows) for k in range(5)
+        )
+
+    up_grad = collect(parts(low, cot2))
+    down_grad = collect(parts(low_back, tokens2))
+
+    def outward(weights, matrix):
+        theirs = jnp.dot(weights[tok_local:], matrix, preferred_element_type=jnp.float32)
+        back = move(theirs.astype(jnp.bfloat16), PARTNER)
+        mine = jnp.dot(weights[:tok_local], matrix, preferred_element_type=jnp.float32)
+        return (mine + back.astype(jnp.float32)).astype(jnp.bfloat16)
+
+    branch_out = outward(low, up_all)
+    input_grad = outward(low_back, down_all)
+    down_grad = (down_grad / capacity).astype(jnp.bfloat16)[None]
+    up_grad = (up_grad / capacity).astype(jnp.bfloat16)[None]
+    return (branch_out, input_grad, down_grad, up_grad)
+
+
+def local(*args):
+    plan = by_pairs if lax.axis_size("adapter") == 2 * PLACES else by_rows
+    return plan(*args)
+
+
 def solution(mesh):
     in_specs = (
         P(("groups", "adapter"), "tensor"),

time: 231 us -> 121 us (0.52)
  waiting for transfers between devices: 121 us -> 30.6 us
  blocking collectives: 57.4 us -> 0 us
  starting transfers between devices: 13.3 us -> 62.7 us
  matrix products: 17.5 us -> 10 us
  other arithmetic: 6.43 us -> 2.14 us
    all_to_all x3 -> x0, waiting for transfers between devices: 121 us -> none  [the longest x1 43.8 us: local(): lax.all_to_all(back_rows.reshape(block_shape), 'adapter', split_axis=0, c...]
    ppermute x0 -> x30, starting transfers between devices: none -> 62.7 us  [the longest x28 62.6 us: move(): return lax.ppermute(value, 'adapter', pairs)]
    all_to_all x1 -> x0, blocking collectives: 52.8 us -> none  [local(): lax.all_to_all(cot_send, 'adapter', split_axis=0, concat_axis=0, tiled=True)]
    ppermute x0 -> x30, waiting for transfers between devices: none -> 30.6 us  [the longest x28 29.4 us: move(): return lax.ppermute(value, 'adapter', pairs)]
    all_to_all x3 -> x0, starting transfers between devices: 13.3 us -> none  [the longest x1 4.46 us: local(): lax.all_to_all(out_rows.reshape(block_shape), 'adapter', split_axis=0, co...]
    gather x6 -> x1, local copies, waits for them, and re-layouts: 12.3 us -> 0.56 us  [by_pairs(): lists = jnp.take(token_lists, experts, axis=0)]
    unnamed x14 -> x20, local copies, waits for them, and re-layouts: 0.61 us -> 11.7 us
    dot_general x4, matrix products: 10.6 us -> 3.8 us  [the longest x2 2.74 us: outward(): jnp.dot(weights[:tok_local], matrix, preferred_element_type=jnp.float32)]
  transfers between devices with their start and end apart: 3 -> 30, of which waited for: 3 -> 8; matrix products, arithmetic and copies ran while one was open for 6% -> 20% of each run, Pallas kernels for 0% -> 0%
where the time goes in v1:
time: 121 us; the launch traced here: 120 us
  starting transfers between devices  62.7 us (52%)
  waiting for transfers between devices  30.6 us (25%)
  local copies, waits for them, and re-layouts  13.7 us (11%)
  matrix products  10 us (8%)
  other arithmetic  2.14 us (2%)
    ppermute x28, starting transfers between devices, move(): return lax.ppermute(value, 'adapter', pairs)  62.6 us
    ppermute x28, waiting for transfers between devices, move(): return lax.ppermute(value, 'adapter', pairs)  29.4 us
    unnamed x20, local copies, waits for them, and re-layouts  11.7 us
    dot_general x10, matrix products, contract_first(): lax.dot_general(left_op, right_op, (((0,), (0,)), ((), ())), preferred_el...  5.01 us
    dot_general x2, matrix products, outward(): jnp.dot(weights[:tok_local], matrix, preferred_element_type=jnp.float32)  2.74 us
  transfers between devices with their start and end apart: 30, of which 8 were waited for; matrix products, arithmetic and copies ran while one was open for 20% of the time, Pallas kernels for 0%

profile of v1, /device:TPU:0, one launch (start us, length us, event | category | flops | bytes accessed | tf_op | source)
XLA Modules:
  0.0 120.3 jit_solution(9199913899078361084)
XLA Ops:
  0.7 5.1 %collective-permute-start = (f32[1,256]{1,0:T(1,128)}, f32[1,256]{1,0:T(1,128)S(1)}, u32[]{:S(2)}, u32[]{:S(2)}) collective-permute-start(f32[1,256]{1,0:T(1,128)} %param.11), channel_id=1, source_target_pairs={{0,4},{2,6},{4,8},{6,10},{8,12},{10,14},{1,5},{3,7},{5,9},{7,11},{... | collective-permute-start | bytes 3080 | tf_op jit(solution)/shard_map/ppermute | solution.py:114
  7.0 3.7 %collective-permute-start.2 = (f32[1,256]{1,0:T(1,128)}, f32[1,256]{1,0:T(1,128)S(1)}, u32[]{:S(2)}, u32[]{:S(2)}) collective-permute-start(f32[1,256]{1,0:T(1,128)} %param.11), channel_id=1, source_target_pairs={{0,8},{2,10},{4,12},{6,14},{8,0},{10,2},{12,4},{14,6},{1,9},{3,11}... | collective-permute-start | bytes 3080 | tf_op jit(solution)/shard_map/ppermute | solution.py:114
  10.8 3.2 %collective-permute-start.3 = (f32[1,256]{1,0:T(1,128)}, f32[1,256]{1,0:T(1,128)S(1)}, u32[]{:S(2)}, u32[]{:S(2)}) collective-permute-start(f32[1,256]{1,0:T(1,128)} %param.11), channel_id=1, source_target_pairs={{0,12},{2,14},{12,0},{14,2},{1,13},{3,15},{13,1},{15,3},{16,28},{1... | collective-permute-start | bytes 3080 | tf_op jit(solution)/shard_map/ppermute | solution.py:114
  14.0 2.0 %collective-permute-start.5 = (bf16[64,2560]{1,0:T(8,128)(2,1)}, bf16[64,2560]{1,0:T(8,128)(2,1)}, u32[]{:S(2)}, u32[]{:S(2)}) collective-permute-start(bf16[64,2560]{1,0:T(8,128)(2,1)} %bitcast.45), channel_id=1, source_target_pairs={{0,4},{2,6},{4,8},{6,10},{8,12},{10,14},{1,5},{3,7},{5,9},{7,11},{... | collective-permute-start | bytes 983048 | tf_op jit(solution)/shard_map/ppermute | solution.py:114
  16.0 1.7 %constant_dynamic-update-slice_fusion.6 = bf16[320,2560]{1,0:T(8,128)(2,1)} fusion(bf16[1,64,2560]{2,1,0:T(8,128)(2,1)} %param.8), kind=kLoop, calls=%fused_computation.58 | loop fusion | bytes 655360
  23.0 1.6 %collective-permute-start.4 = (bf16[128,2560]{1,0:T(8,128)(2,1)S(1)}, bf16[128,2560]{1,0:T(8,128)(2,1)}, u32[]{:S(2)}, u32[]{:S(2)}) collective-permute-start(bf16[128,2560]{1,0:T(8,128)(2,1)S(1)} %copy-done.3), channel_id=1, source_target_pairs={{0,2},{2,0},{4,6},{6,4},{8,10},{10,8},{12,14},{14,12},{1,3},{3,1},... | collective-permute-start | bytes 1966088 | tf_op jit(solution)/shard_map/ppermute | solution.py:114
  24.6 5.3 %collective-permute-start.11 = (bf16[64,2560]{1,0:T(8,128)(2,1)}, bf16[64,2560]{1,0:T(8,128)(2,1)}, u32[]{:S(2)}, u32[]{:S(2)}) collective-permute-start(bf16[64,2560]{1,0:T(8,128)(2,1)} %bitcast.47), channel_id=1, source_target_pairs={{0,4},{2,6},{4,8},{6,10},{8,12},{10,14},{1,5},{3,7},{5,9},{7,11},{... | collective-permute-start | bytes 983048 | tf_op jit(solution)/shard_map/ppermute | solution.py:114
  31.8 1.7 %constant_dynamic-update-slice_fusion.5 = bf16[320,2560]{1,0:T(8,128)(2,1)} fusion(bf16[320,2560]{1,0:T(8,128)(2,1)} %constant_dynamic-update-slice_fusion.6, bf16[64,2560]{1,0:T(8,128)(2,1)} %collective-permute-done.5), kind=kLoop, calls=%fused_computation.57 | loop fusion | bytes 655360
  34.2 1.7 %constant_dynamic-update-slice_fusion.4 = bf16[320,2560]{1,0:T(8,128)(2,1)} fusion(bf16[320,2560]{1,0:T(8,128)(2,1)} %constant_dynamic-update-slice_fusion.5, bf16[64,2560]{1,0:T(8,128)(2,1)} %collective-permute-done.6), kind=kLoop, calls=%fused_computation.56 | loop fusion | bytes 655360
  37.3 1.7 %constant_dynamic-update-slice_fusion.10 = bf16[320,2560]{1,0:T(8,128)(2,1)} fusion(bf16[320,2560]{1,0:T(8,128)(2,1)} %constant_dynamic-update-slice_fusion.11, bf16[64,2560]{1,0:T(8,128)(2,1)} %collective-permute-done.11), kind=kLoop, calls=%fused_computation.62 | loop fusion | bytes 655360
  40.3 1.7 %constant_dynamic-update-slice_fusion.9 = bf16[320,2560]{1,0:T(8,128)(2,1)} fusion(bf16[320,2560]{1,0:T(8,128)(2,1)} %constant_dynamic-update-slice_fusion.10, bf16[64,2560]{1,0:T(8,128)(2,1)} %collective-permute-done.12), kind=kLoop, calls=%fused_computation.61 | loop fusion | bytes 655360
  43.3 5.1 %collective-permute-done.8 = bf16[64,2560]{1,0:T(8,128)(2,1)S(1)} collective-permute-done((bf16[64,2560]{1,0:T(8,128)(2,1)}, bf16[64,2560]{1,0:T(8,128)(2,1)S(1)}, u32[]{:S(2)}, u32[]{:S(2)}) %collective-permute-start.8) | collective-permute-done | bytes 327712 | tf_op jit(solution)/shard_map/ppermute | solution.py:114
  50.5 10.9 %collective-permute-done.14 = bf16[64,2560]{1,0:T(8,128)(2,1)S(1)} collective-permute-done((bf16[64,2560]{1,0:T(8,128)(2,1)}, bf16[64,2560]{1,0:T(8,128)(2,1)S(1)}, u32[]{:S(2)}, u32[]{:S(2)}) %collective-permute-start.14) | collective-permute-done | bytes 327712 | tf_op jit(solution)/shard_map/ppermute | solution.py:114
  62.2 1.4 %collective-permute-start.15 = (bf16[64,2560]{1,0:T(8,128)(2,1)S(1)}, bf16[64,2560]{1,0:T(8,128)(2,1)S(1)}, u32[]{:S(2)}, u32[]{:S(2)}) collective-permute-start(bf16[64,2560]{1,0:T(8,128)(2,1)S(1)} %get-tuple-element.7), channel_id=1, source_target_pairs={{8,12},{10,14},{4,0},{6,2},{9,13},{11,15},{5,1},{7,3},{24,28},{26,... | collective-permute-start | bytes 983048 | tf_op jit(solution)/shard_map/ppermute | solution.py:114
  64.9 2.8 %collective-permute-done.9 = bf16[64,2560]{1,0:T(8,128)(2,1)S(1)} collective-permute-done((bf16[64,2560]{1,0:T(8,128)(2,1)S(1)}, bf16[64,2560]{1,0:T(8,128)(2,1)S(1)}, u32[]{:S(2)}, u32[]{:S(2)}) %collective-permute-start.9) | collective-permute-done | bytes 327712 | tf_op jit(solution)/shard_map/ppermute | solution.py:114
  68.4 2.9 %collective-permute-done.15 = bf16[64,2560]{1,0:T(8,128)(2,1)S(1)} collective-permute-done((bf16[64,2560]{1,0:T(8,128)(2,1)S(1)}, bf16[64,2560]{1,0:T(8,128)(2,1)S(1)}, u32[]{:S(2)}, u32[]{:S(2)}) %collective-permute-start.15) | collective-permute-done | bytes 327712 | tf_op jit(solution)/shard_map/ppermute | solution.py:114
  74.1 1.5 %collective-permute-start.25 = (bf16[64,2560]{1,0:T(8,128)(2,1)S(1)}, bf16[64,2560]{1,0:T(8,128)(2,1)S(1)}, u32[]{:S(2)}, u32[]{:S(2)}) collective-permute-start(bf16[64,2560]{1,0:T(8,128)(2,1)S(1)} %convolution_convert_fusion.2), channel_id=1, source_target_pairs={{12,8},{14,10},{0,4},{2,6},{13,9},{15,11},{1,5},{3,7},{28,24},{30,... | collective-permute-start | bytes 983048 | tf_op jit(solution)/shard_map/ppermute | solution.py:114
  77.8 5.8 %collective-permute-done.25 = bf16[64,2560]{1,0:T(8,128)(2,1)S(1)} collective-permute-done((bf16[64,2560]{1,0:T(8,128)(2,1)S(1)}, bf16[64,2560]{1,0:T(8,128)(2,1)S(1)}, u32[]{:S(2)}, u32[]{:S(2)}) %collective-permute-start.25) | collective-permute-done | bytes 327712 | tf_op jit(solution)/shard_map/ppermute | solution.py:114
  85.2 1.5 %collective-permute-start.19 = (bf16[128,2560]{1,0:T(8,128)(2,1)S(1)}, bf16[128,2560]{1,0:T(8,128)(2,1)S(1)}, u32[]{:S(2)}, u32[]{:S(2)}) collective-permute-start(bf16[128,2560]{1,0:T(8,128)(2,1)S(1)} %convolution_convert_fusion), channel_id=1, source_target_pairs={{0,2},{2,0},{4,6},{6,4},{8,10},{10,8},{12,14},{14,12},{1,3},{3,1},... | collective-permute-start | bytes 1966088 | tf_op jit(solution)/shard_map/ppermute | solution.py:114
  87.3 5.0 %collective-permute-start.28 = (bf16[64,2560]{1,0:T(8,128)(2,1)S(1)}, bf16[64,2560]{1,0:T(8,128)(2,1)S(1)}, u32[]{:S(2)}, u32[]{:S(2)}) collective-permute-start(bf16[64,2560]{1,0:T(8,128)(2,1)S(1)} %fusion.10), channel_id=1, source_target_pairs={{0,4},{2,6},{4,8},{6,10},{1,5},{3,7},{5,9},{7,11},{16,20},{18,22},... | collective-permute-start | bytes 983048 | tf_op jit(solution)/shard_map/ppermute | solution.py:114
  93.4 5.3 %collective-permute-start.23 = (bf16[64,2560]{1,0:T(8,128)(2,1)S(1)}, bf16[64,2560]{1,0:T(8,128)(2,1)S(1)}, u32[]{:S(2)}, u32[]{:S(2)}) collective-permute-start(bf16[64,2560]{1,0:T(8,128)(2,1)S(1)} %fusion.7), channel_id=1, source_target_pairs={{0,4},{2,6},{4,8},{6,10},{1,5},{3,7},{5,9},{7,11},{16,20},{18,22},... | collective-permute-start | bytes 983048 | tf_op jit(solution)/shard_map/ppermute | solution.py:114
  100.7 7.0 %collective-permute-start.29 = (bf16[64,2560]{1,0:T(8,128)(2,1)S(1)}, bf16[64,2560]{1,0:T(8,128)(2,1)S(1)}, u32[]{:S(2)}, u32[]{:S(2)}) collective-permute-start(bf16[64,2560]{1,0:T(8,128)(2,1)S(1)} %fusion.11), channel_id=1, source_target_pairs={{0,4},{2,6},{4,8},{6,10},{8,12},{10,14},{1,5},{3,7},{5,9},{7,11},{... | collective-permute-start | bytes 983048 | tf_op jit(solution)/shard_map/ppermute | solution.py:114
  109.7 4.6 %collective-permute-start.24 = (bf16[64,2560]{1,0:T(8,128)(2,1)S(1)}, bf16[64,2560]{1,0:T(8,128)(2,1)S(1)}, u32[]{:S(2)}, u32[]{:S(2)}) collective-permute-start(bf16[64,2560]{1,0:T(8,128)(2,1)S(1)} %fusion.8), channel_id=1, source_target_pairs={{0,4},{2,6},{4,8},{6,10},{8,12},{10,14},{1,5},{3,7},{5,9},{7,11},{... | collective-permute-start | bytes 983048 | tf_op jit(solution)/shard_map/ppermute | solution.py:114
  114.2 1.4 %fusion.1 = bf16[128,2560]{1,0:T(8,128)(2,1)} fusion(bf16[320,2560]{1,0:T(8,128)(2,1)S(1)} %constant_dynamic-update-slice_fusion.2, bf16[128,2560]{1,0:T(8,128)(2,1)S(1)} %collective-permute-done.19, bf16[256,320]{0,1:T(8,128)(2,1)S(1)} %get-tuple-element.8), kind=kOutput, calls=%fused_computation.4 | convolution fusion | flops 210698240 | bytes 3031040 | tf_op jit(solution)/shard_map/dot_general | solution.py:198
  (91 shorter events, 34.5 us)
Async XLA Ops:
  0.7 21.1 %collective-permute-start = (f32[1,256]{1,0:T(1,128)}, f32[1,256]{1,0:T(1,128)S(1)}, u32[]{:S(2)}, u32[]{:S(2)}) collective-permute-start(f32[1,256]{1,0:T(1,128)} %param.11), channel_id=1, source_target_pairs={{0,4},{2,6},{4,8},{6,10},{8,12},{10,14},{1,5},{3,7},{5,9},{7,11},{... | collective-permute-start | bytes 3080 | tf_op jit(solution)/shard_map/ppermute | solution.py:114
  5.7 17.3 %collective-permute-start.1 = (f32[1,256]{1,0:T(1,128)}, f32[1,256]{1,0:T(1,128)S(1)}, u32[]{:S(2)}, u32[]{:S(2)}) collective-permute-start(f32[1,256]{1,0:T(1,128)} %param.11), channel_id=1, source_target_pairs={{4,0},{6,2},{8,4},{10,6},{12,8},{14,10},{5,1},{7,3},{9,5},{11,7},{... | collective-permute-start | bytes 3080 | tf_op jit(solution)/shard_map/ppermute | solution.py:114
  7.0 17.6 %collective-permute-start.2 = (f32[1,256]{1,0:T(1,128)}, f32[1,256]{1,0:T(1,128)S(1)}, u32[]{:S(2)}, u32[]{:S(2)}) collective-permute-start(f32[1,256]{1,0:T(1,128)} %param.11), channel_id=1, source_target_pairs={{0,8},{2,10},{4,12},{6,14},{8,0},{10,2},{12,4},{14,6},{1,9},{3,11}... | collective-permute-start | bytes 3080 | tf_op jit(solution)/shard_map/ppermute | solution.py:114
  10.8 19.1 %collective-permute-start.3 = (f32[1,256]{1,0:T(1,128)}, f32[1,256]{1,0:T(1,128)S(1)}, u32[]{:S(2)}, u32[]{:S(2)}) collective-permute-start(f32[1,256]{1,0:T(1,128)} %param.11), channel_id=1, source_target_pairs={{0,12},{2,14},{12,0},{14,2},{1,13},{3,15},{13,1},{15,3},{16,28},{1... | collective-permute-start | bytes 3080 | tf_op jit(solution)/shard_map/ppermute | solution.py:114
  14.0 17.2 %collective-permute-start.5 = (bf16[64,2560]{1,0:T(8,128)(2,1)}, bf16[64,2560]{1,0:T(8,128)(2,1)}, u32[]{:S(2)}, u32[]{:S(2)}) collective-permute-start(bf16[64,2560]{1,0:T(8,128)(2,1)} %bitcast.45), channel_id=1, source_target_pairs={{0,4},{2,6},{4,8},{6,10},{8,12},{10,14},{1,5},{3,7},{5,9},{7,11},{... | collective-permute-start | bytes 983048 | tf_op jit(solution)/shard_map/ppermute | solution.py:114
  21.7 11.8 %collective-permute-start.6 = (bf16[64,2560]{1,0:T(8,128)(2,1)}, bf16[64,2560]{1,0:T(8,128)(2,1)}, u32[]{:S(2)}, u32[]{:S(2)}) collective-permute-start(bf16[64,2560]{1,0:T(8,128)(2,1)} %bitcast.46), channel_id=1, source_target_pairs={{4,0},{6,2},{8,4},{10,6},{12,8},{14,10},{5,1},{7,3},{9,5},{11,7},{... | collective-permute-start | bytes 983048 | tf_op jit(solution)/shard_map/ppermute | solution.py:114
  23.0 40.6 %collective-permute-start.4 = (bf16[128,2560]{1,0:T(8,128)(2,1)S(1)}, bf16[128,2560]{1,0:T(8,128)(2,1)}, u32[]{:S(2)}, u32[]{:S(2)}) collective-permute-start(bf16[128,2560]{1,0:T(8,128)(2,1)S(1)} %copy-done.3), channel_id=1, source_target_pairs={{0,2},{2,0},{4,6},{6,4},{8,10},{10,8},{12,14},{14,12},{1,3},{3,1},... | collective-permute-start | bytes 1966088 | tf_op jit(solution)/shard_map/ppermute | solution.py:114
  24.6 11.4 %collective-permute-start.11 = (bf16[64,2560]{1,0:T(8,128)(2,1)}, bf16[64,2560]{1,0:T(8,128)(2,1)}, u32[]{:S(2)}, u32[]{:S(2)}) collective-permute-start(bf16[64,2560]{1,0:T(8,128)(2,1)} %bitcast.47), channel_id=1, source_target_pairs={{0,4},{2,6},{4,8},{6,10},{8,12},{10,14},{1,5},{3,7},{5,9},{7,11},{... | collective-permute-start | bytes 983048 | tf_op jit(solution)/shard_map/ppermute | solution.py:114
  29.9 9.7 %collective-permute-start.12 = (bf16[64,2560]{1,0:T(8,128)(2,1)}, bf16[64,2560]{1,0:T(8,128)(2,1)}, u32[]{:S(2)}, u32[]{:S(2)}) collective-permute-start(bf16[64,2560]{1,0:T(8,128)(2,1)} %bitcast.48), channel_id=1, source_target_pairs={{4,0},{6,2},{8,4},{10,6},{12,8},{14,10},{5,1},{7,3},{9,5},{11,7},{... | collective-permute-start | bytes 983048 | tf_op jit(solution)/shard_map/ppermute | solution.py:114
  31.2 33.6 %collective-permute-start.17 = (bf16[128,2560]{1,0:T(8,128)(2,1)}, bf16[128,2560]{1,0:T(8,128)(2,1)S(1)}, u32[]{:S(2)}, u32[]{:S(2)}) collective-permute-start(bf16[128,2560]{1,0:T(8,128)(2,1)} %param.7), channel_id=1, source_target_pairs={{0,2},{2,0},{4,6},{6,4},{8,10},{10,8},{12,14},{14,12},{1,3},{3,1},... | collective-permute-start | bytes 1966088 | tf_op jit(solution)/shard_map/ppermute | solution.py:114
  36.0 12.5 %collective-permute-start.8 = (bf16[64,2560]{1,0:T(8,128)(2,1)}, bf16[64,2560]{1,0:T(8,128)(2,1)S(1)}, u32[]{:S(2)}, u32[]{:S(2)}) collective-permute-start(bf16[64,2560]{1,0:T(8,128)(2,1)} %collective-permute-done.6), channel_id=1, source_target_pairs={{8,4},{10,6},{4,0},{6,2},{9,5},{11,7},{5,1},{7,3},{24,20},{26,22},... | collective-permute-start | bytes 983048 | tf_op jit(solution)/shard_map/ppermute | solution.py:114
  39.6 10.9 %collective-permute-start.13 = (bf16[64,2560]{1,0:T(8,128)(2,1)}, bf16[64,2560]{1,0:T(8,128)(2,1)S(1)}, u32[]{:S(2)}, u32[]{:S(2)}) collective-permute-start(bf16[64,2560]{1,0:T(8,128)(2,1)} %collective-permute-done.11), channel_id=1, source_target_pairs={{4,8},{6,10},{8,12},{10,14},{5,9},{7,11},{9,13},{11,15},{20,24},{2... | collective-permute-start | bytes 983048 | tf_op jit(solution)/shard_map/ppermute | solution.py:114
  42.0 19.4 %collective-permute-start.14 = (bf16[64,2560]{1,0:T(8,128)(2,1)}, bf16[64,2560]{1,0:T(8,128)(2,1)S(1)}, u32[]{:S(2)}, u32[]{:S(2)}) collective-permute-start(bf16[64,2560]{1,0:T(8,128)(2,1)} %collective-permute-done.12), channel_id=1, source_target_pairs={{8,4},{10,6},{4,0},{6,2},{9,5},{11,7},{5,1},{7,3},{24,20},{26,22},... | collective-permute-start | bytes 983048 | tf_op jit(solution)/shard_map/ppermute | solution.py:114
  49.2 18.4 %collective-permute-start.9 = (bf16[64,2560]{1,0:T(8,128)(2,1)S(1)}, bf16[64,2560]{1,0:T(8,128)(2,1)S(1)}, u32[]{:S(2)}, u32[]{:S(2)}) collective-permute-start(bf16[64,2560]{1,0:T(8,128)(2,1)S(1)} %get-tuple-element.5), channel_id=1, source_target_pairs={{8,12},{10,14},{4,0},{6,2},{9,13},{11,15},{5,1},{7,3},{24,28},{26,... | collective-permute-start | bytes 983048 | tf_op jit(solution)/shard_map/ppermute | solution.py:114
  74.1 9.5 %collective-permute-start.25 = (bf16[64,2560]{1,0:T(8,128)(2,1)S(1)}, bf16[64,2560]{1,0:T(8,128)(2,1)S(1)}, u32[]{:S(2)}, u32[]{:S(2)}) collective-permute-start(bf16[64,2560]{1,0:T(8,128)(2,1)S(1)} %convolution_convert_fusion.2), channel_id=1, source_target_pairs={{12,8},{14,10},{0,4},{2,6},{13,9},{15,11},{1,5},{3,7},{28,24},{30,... | collective-permute-start | bytes 983048 | tf_op jit(solution)/shard_map/ppermute | solution.py:114
  75.9 16.4 %collective-permute-start.20 = (bf16[64,2560]{1,0:T(8,128)(2,1)S(1)}, bf16[64,2560]{1,0:T(8,128)(2,1)S(1)}, u32[]{:S(2)}, u32[]{:S(2)}) collective-permute-start(bf16[64,2560]{1,0:T(8,128)(2,1)S(1)} %convolution_convert_fusion.3), channel_id=1, source_target_pairs={{12,8},{14,10},{0,4},{2,6},{13,9},{15,11},{1,5},{3,7},{28,24},{30,... | collective-permute-start | bytes 983048 | tf_op jit(solution)/shard_map/ppermute | solution.py:114
  85.2 24.5 %collective-permute-start.19 = (bf16[128,2560]{1,0:T(8,128)(2,1)S(1)}, bf16[128,2560]{1,0:T(8,128)(2,1)S(1)}, u32[]{:S(2)}, u32[]{:S(2)}) collective-permute-start(bf16[128,2560]{1,0:T(8,128)(2,1)S(1)} %convolution_convert_fusion), channel_id=1, source_target_pairs={{0,2},{2,0},{4,6},{6,4},{8,10},{10,8},{12,14},{14,12},{1,3},{3,1},... | collective-permute-start | bytes 1966088 | tf_op jit(solution)/shard_map/ppermute | solution.py:114
  86.7 28.9 %collective-permute-start.16 = (bf16[128,2560]{1,0:T(8,128)(2,1)S(1)}, bf16[128,2560]{1,0:T(8,128)(2,1)S(1)}, u32[]{:S(2)}, u32[]{:S(2)}) collective-permute-start(bf16[128,2560]{1,0:T(8,128)(2,1)S(1)} %convolution_convert_fusion.1), channel_id=1, source_target_pairs={{0,2},{2,0},{4,6},{6,4},{8,10},{10,8},{12,14},{14,12},{1,3},{3,1},... | collective-permute-start | bytes 1966088 | tf_op jit(solution)/shard_map/ppermute | solution.py:114
  87.3 11.7 %collective-permute-start.28 = (bf16[64,2560]{1,0:T(8,128)(2,1)S(1)}, bf16[64,2560]{1,0:T(8,128)(2,1)S(1)}, u32[]{:S(2)}, u32[]{:S(2)}) collective-permute-start(bf16[64,2560]{1,0:T(8,128)(2,1)S(1)} %fusion.10), channel_id=1, source_target_pairs={{0,4},{2,6},{4,8},{6,10},{1,5},{3,7},{5,9},{7,11},{16,20},{18,22},... | collective-permute-start | bytes 983048 | tf_op jit(solution)/shard_map/ppermute | solution.py:114
  93.4 14.6 %collective-permute-start.23 = (bf16[64,2560]{1,0:T(8,128)(2,1)S(1)}, bf16[64,2560]{1,0:T(8,128)(2,1)S(1)}, u32[]{:S(2)}, u32[]{:S(2)}) collective-permute-start(bf16[64,2560]{1,0:T(8,128)(2,1)S(1)} %fusion.7), channel_id=1, source_target_pairs={{0,4},{2,6},{4,8},{6,10},{1,5},{3,7},{5,9},{7,11},{16,20},{18,22},... | collective-permute-start | bytes 983048 | tf_op jit(solution)/shard_map/ppermute | solution.py:114
  99.0 18.0 %collective-permute-start.27 = (bf16[64,2560]{1,0:T(8,128)(2,1)S(1)}, bf16[64,2560]{1,0:T(8,128)(2,1)S(1)}, u32[]{:S(2)}, u32[]{:S(2)}) collective-permute-start(bf16[64,2560]{1,0:T(8,128)(2,1)S(1)} %fusion.9), channel_id=1, source_target_pairs={{4,0},{6,2},{8,4},{10,6},{12,8},{14,10},{5,1},{7,3},{9,5},{11,7},{... | collective-permute-start | bytes 983048 | tf_op jit(solution)/shard_map/ppermute | solution.py:114
  100.7 16.3 %collective-permute-start.29 = (bf16[64,2560]{1,0:T(8,128)(2,1)S(1)}, bf16[64,2560]{1,0:T(8,128)(2,1)S(1)}, u32[]{:S(2)}, u32[]{:S(2)}) collective-permute-start(bf16[64,2560]{1,0:T(8,128)(2,1)S(1)} %fusion.11), channel_id=1, source_target_pairs={{0,4},{2,6},{4,8},{6,10},{8,12},{10,14},{1,5},{3,7},{5,9},{7,11},{... | collective-permute-start | bytes 983048 | tf_op jit(solution)/shard_map/ppermute | solution.py:114
  108.0 10.1 %collective-permute-start.22 = (bf16[64,2560]{1,0:T(8,128)(2,1)S(1)}, bf16[64,2560]{1,0:T(8,128)(2,1)S(1)}, u32[]{:S(2)}, u32[]{:S(2)}) collective-permute-start(bf16[64,2560]{1,0:T(8,128)(2,1)S(1)} %fusion.6), channel_id=1, source_target_pairs={{4,0},{6,2},{8,4},{10,6},{12,8},{14,10},{5,1},{7,3},{9,5},{11,7},{... | collective-permute-start | bytes 983048 | tf_op jit(solution)/shard_map/ppermute | solution.py:114
  109.7 9.6 %collective-permute-start.24 = (bf16[64,2560]{1,0:T(8,128)(2,1)S(1)}, bf16[64,2560]{1,0:T(8,128)(2,1)S(1)}, u32[]{:S(2)}, u32[]{:S(2)}) collective-permute-start(bf16[64,2560]{1,0:T(8,128)(2,1)S(1)} %fusion.8), channel_id=1, source_target_pairs={{0,4},{2,6},{4,8},{6,10},{8,12},{10,14},{1,5},{3,7},{5,9},{7,11},{... | collective-permute-start | bytes 983048 | tf_op jit(solution)/shard_map/ppermute | solution.py:114
  (12 other events, 104.8 us)

commit v2 on v0

--- a/solution.py
+++ b/solution.py
@@ -29,7 +29,7 @@
     return jnp.dot(onehot, flat_rows, preferred_element_type=jnp.float32).astype(jnp.bfloat16)
 
 
-def local(tokens, cotangent, down_adapter, up_adapter, token_lists, gating):
+def by_rows(tokens, cotangent, down_adapter, up_adapter, token_lists, gating):
     owners = lax.axis_size("adapter")
     my_index = lax.axis_index("adapter")
     tok_local = tokens.shape[0]
@@ -90,6 +90,125 @@
     return (branch_out, input_grad, down_grad, up_grad)
 
 
+PLACES = 4
+
+
+def on_line(pairs):
+    return [(2 * a + side, 2 * b + side) for a, b in pairs for side in (0, 1)]
+
+
+def xor_line(bit):
+    return on_line([(a, a ^ bit) for a in range(PLACES)])
+
+
+RISE = on_line([(0, 1), (1, 2), (2, 3)])
+FALL = on_line([(1, 0), (2, 1), (3, 2)])
+FROM_ENDS = on_line([(3, 2), (0, 1)])
+RISE_IN = on_line([(0, 1), (1, 2)])
+FALL_IN = on_line([(3, 2), (2, 1)])
+PARTNER = [(2 * a + side, 2 * a + 1 - side) for a in range(PLACES) for side in (0, 1)]
+SWAP = [(0, 1), (1, 0)]
+OWNERS = 2 * PLACES
+FAR = xor_line(2) + [(OWNERS + a, OWNERS + b) for a, b in xor_line(3)]
+
+
+def move(value, pairs):
+    return lax.ppermute(value, "adapter", pairs)
+
+
+def after(value, earlier):
+    return lax.optimization_barrier((value, earlier))[0]
+
+
+def collect(weights, rows):
+    own, third, second, below, above = weights
+    half = jnp.bfloat16
+    back = move(contract_first(third, rows).astype(half), FROM_ENDS)
+    second = (contract_first(second, rows) + back.astype(jnp.float32)).astype(half)
+    falling = move(second, FALL_IN)
+    rising = move(second, RISE_IN)
+    below = move((contract_first(below, rows) + falling.astype(jnp.float32)).astype(half), FALL)
+    above = move((contract_first(above, rows) + rising.astype(jnp.float32)).astype(half), RISE)
+    return contract_first(own, rows) + below.astype(jnp.float32) + above.astype(jnp.float32)
+
+
+def both_cores(partial):
+    return partial + lax.ppermute(partial, "tensor", SWAP)
+
+
+def by_pairs(tokens, cotangent, down_adapter, up_adapter, token_lists, gating):
+    me = lax.axis_index("adapter")
+    first_group = lax.axis_index("groups") == 0
+    place = me // 2
+    odd = place % 2 == 1
+    tok_local = tokens.shape[0]
+    capacity = gating.shape[1]
+    down_matrix = down_adapter[0]
+    up_matrix = up_adapter[0]
+    rank = down_matrix.shape[0]
+
+    far_down = lax.ppermute(down_matrix, ("groups", "adapter"), FAR)
+    near_down = move(down_matrix, xor_line(1))
+    tokens2 = move(tokens, PARTNER)
+    far_up = lax.ppermute(after(up_matrix, far_down), ("groups", "adapter"), FAR)
+    cross_down = lax.ppermute(far_down, "groups", SWAP)
+    near_up = move(after(up_matrix, near_down), xor_line(1))
+    cot2 = move(after(cotangent, tokens2), PARTNER)
+    later = after(gating, far_down)
+    gates = [gating, move(later, xor_line(1)), move(later, xor_line(2)), move(later, xor_line(3))]
+    cross_up = lax.ppermute(far_up, "groups", SWAP)
+
+    far_bit = jnp.where(first_group, 2, 3)
+    experts = jnp.stack([me, me ^ 2, me ^ (2 * far_bit), me ^ (2 * (far_bit ^ 1))])
+    lists = jnp.take(token_lists, experts, axis=0)
+    far_gate = jnp.where(first_group, gates[2], gates[3])
+    cross_gate = jnp.where(first_group, gates[3], gates[2])
+    gate_rows = adapter_scale_factor * jnp.concatenate([gates[0], gates[1], far_gate, cross_gate])
+    token_ids = jnp.arange(tok_local, dtype=jnp.int32)
+    ids = jnp.concatenate([me * tok_local + token_ids, (me ^ 1) * tok_local + token_ids])
+    taken = ids[:, None, None] == lists[None, :, :]
+    scale = jnp.sum(jnp.where(taken, gate_rows[None, :, :], 0.0), axis=2)
+    scale = jnp.repeat(scale, rank, axis=1)
+
+    tokens2 = jnp.concatenate([tokens, tokens2], axis=0)
+    cot2 = jnp.concatenate([cotangent, cot2], axis=0)
+    down_all = jnp.concatenate([down_matrix, near_down, far_down, cross_down], axis=0)
+    up_all = jnp.concatenate([up_matrix, near_up, far_up, cross_up], axis=0)
+
+    def low_rank(rows, matrices):
+        return (scale * both_cores(contract_last(rows, matrices))).astype(jnp.bfloat16)
+
+    def for_line(low):
+        own, near, far, cross = (low[:, k * rank : (k + 1) * rank] for k in range(4))
+        second = jnp.where(first_group, far, cross)
+        third = jnp.where(first_group, cross, far)
+        below = jnp.where(odd, near, third)
+        above = jnp.where(odd, third, near)
+        return own, third, second, below, above
+
+    def outward(weights, matrix):
+        theirs = jnp.dot(weights[tok_local:], matrix, preferred_element_type=jnp.float32)
+        back = move(theirs.astype(jnp.bfloat16), PARTNER)
+        mine = jnp.dot(weights[:tok_local], matrix, preferred_element_type=jnp.float32)
+        return (mine + back.astype(jnp.float32)).astype(jnp.bfloat16)
+
+    low = low_rank(tokens2, down_all)
+    up_grad = collect(for_line(low), cot2)
+    low_back = low_rank(cot2, up_all)
+    down_grad = collect(for_line(low_back), tokens2)
+    branch_out = outward(low, up_all)
+    input_grad = outward(low_back, down_all)
+    down_grad = (down_grad / capacity).astype(jnp.bfloat16)[None]
+    up_grad = (up_grad / capacity).astype(jnp.bfloat16)[None]
+    return (branch_out, input_grad, down_grad, up_grad)
+
+
+def local(*args):
+    fits = lax.axis_size("adapter") == OWNERS and lax.axis_size("groups") == 2
+    plan = by_pairs if fits else by_rows
+    return plan(*args)
+
+
 def solution(mesh):
     in_specs = (
         P(("groups", "adapter"), "tensor"),

time: 231 us -> 105 us (0.45)
  waiting for transfers between devices: 121 us -> 42.9 us
  blocking collectives: 57.4 us -> 0 us
  starting transfers between devices: 13.3 us -> 48.8 us
  local copies, waits for them, and re-layouts: 13.5 us -> 1.9 us
  matrix products: 17.5 us -> 9.2 us
  other arithmetic: 6.43 us -> 0.7 us
    all_to_all x3 -> x0, waiting for transfers between devices: 121 us -> none  [the longest x1 43.8 us: local(): lax.all_to_all(back_rows.reshape(block_shape), 'adapter', split_axis=0, c...]
    all_to_all x1 -> x0, blocking collectives: 52.8 us -> none  [local(): lax.all_to_all(cot_send, 'adapter', split_axis=0, concat_axis=0, tiled=True)]
    ppermute x0 -> x25, starting transfers between devices: none -> 48.8 us  [the longest x19 39 us: move(): return lax.ppermute(value, 'adapter', pairs)]
    ppermute x0 -> x25, waiting for transfers between devices: none -> 42.9 us  [the longest x19 20.6 us: move(): return lax.ppermute(value, 'adapter', pairs)]
    all_to_all x3 -> x0, starting transfers between devices: 13.3 us -> none  [the longest x1 4.46 us: local(): lax.all_to_all(out_rows.reshape(block_shape), 'adapter', split_axis=0, co...]
    gather x6 -> x1, local copies, waits for them, and re-layouts: 12.3 us -> 0.56 us  [by_pairs(): lists = jnp.take(token_lists, experts, axis=0)]
    dot_general x4, matrix products: 10.6 us -> 3.13 us  [the longest x2 2.41 us: outward(): jnp.dot(weights[:tok_local], matrix, preferred_element_type=jnp.float32)]
    psum x1 -> x0, blocking collectives: 4.56 us -> none  [local(): lax.psum(contract_last(rows_in, down_matrix), 'tensor').astype(jnp.bfloat16)]
  transfers between devices with their start and end apart: 3 -> 25, of which waited for: 3 -> 13; matrix products, arithmetic and copies ran while one was open for 6% -> 10% of each run, Pallas kernels for 0% -> 0%
where the time goes in v2:
time: 105 us; the launch traced here: 104 us
  starting transfers between devices  48.8 us (46%)
  waiting for transfers between devices  42.9 us (41%)
  matrix products  9.2 us (9%)
  local copies, waits for them, and re-layouts  1.9 us (2%)
    ppermute x19, starting transfers between devices, move(): return lax.ppermute(value, 'adapter', pairs)  39 us
    ppermute x19, waiting for transfers between devices, move(): return lax.ppermute(value, 'adapter', pairs)  20.6 us
    ppermute x1, waiting for transfers between devices, by_pairs(): far_down = lax.ppermute(down_matrix, ('groups', 'adapter'), FAR)  9.86 us
    ppermute x1, waiting for transfers between devices, by_pairs(): lax.ppermute(after(up_matrix, far_down), ('groups', 'adapter'), FAR)  5.94 us
    ppermute x1, waiting for transfers between devices, by_pairs(): cross_down = lax.ppermute(far_down, 'groups', SWAP)  5.73 us
    dot_general x10, matrix products, contract_first(): lax.dot_general(left_op, right_op, (((0,), (0,)), ((), ())), preferred_el...  5.01 us
    ppermute x1, starting transfers between devices, by_pairs(): far_down = lax.ppermute(down_matrix, ('groups', 'adapter'), FAR)  4.1 us
    dot_general x2, matrix products, outward(): jnp.dot(weights[:tok_local], matrix, preferred_element_type=jnp.float32)  2.41 us
  transfers between devices with their start and end apart: 25, of which 13 were waited for; matrix products, arithmetic and copies ran while one was open for 10% of the time, Pallas kernels for 0%

profile of v2, /device:TPU:0, one launch (start us, length us, event | category | flops | bytes accessed | tf_op | source)
XLA Modules:
  0.0 104.4 jit_solution(14858605173138369380)
XLA Ops:
  0.7 4.1 %collective-permute-start = (bf16[64,2560]{1,0:T(8,128)(2,1)}, bf16[64,2560]{1,0:T(8,128)(2,1)S(1)}, u32[]{:S(2)}, u32[]{:S(2)}) collective-permute-start(bf16[64,2560]{1,0:T(8,128)(2,1)} %bitcast.42), channel_id=1, source_target_pairs={{0,8},{2,10},{4,12},{6,14},{8,0},{10,2},{12,4},{14,6},{16,28},{18,... | collective-permute-start | bytes 983048 | tf_op jit(solution)/shard_map/ppermute | solution.py:150
  4.8 1.6 %collective-permute-start.5 = (bf16[64,2560]{1,0:T(8,128)(2,1)}, bf16[64,2560]{1,0:T(8,128)(2,1)S(1)}, u32[]{:S(2)}, u32[]{:S(2)}) collective-permute-start(bf16[64,2560]{1,0:T(8,128)(2,1)} %bitcast.43), channel_id=1, source_target_pairs={{0,4},{2,6},{4,0},{6,2},{8,12},{10,14},{12,8},{14,10},{1,5},{3,7},... | collective-permute-start | bytes 983048 | tf_op jit(solution)/shard_map/ppermute | solution.py:116
  6.3 1.5 %collective-permute-start.4 = (bf16[128,2560]{1,0:T(8,128)(2,1)}, bf16[128,2560]{1,0:T(8,128)(2,1)S(1)}, u32[]{:S(2)}, u32[]{:S(2)}) collective-permute-start(bf16[128,2560]{1,0:T(8,128)(2,1)} %param.6), channel_id=1, source_target_pairs={{0,2},{2,0},{4,6},{6,4},{8,10},{10,8},{12,14},{14,12},{1,3},{3,1},... | collective-permute-start | bytes 1966088 | tf_op jit(solution)/shard_map/ppermute | solution.py:116
  10.0 9.9 %collective-permute-done = bf16[64,2560]{1,0:T(8,128)(2,1)S(1)} collective-permute-done((bf16[64,2560]{1,0:T(8,128)(2,1)}, bf16[64,2560]{1,0:T(8,128)(2,1)S(1)}, u32[]{:S(2)}, u32[]{:S(2)}) %collective-permute-start) | collective-permute-done | bytes 327712 | tf_op jit(solution)/shard_map/ppermute | solution.py:150
  19.8 3.4 %collective-permute-start.3 = (f32[1,256]{1,0:T(1,128)S(1)}, f32[1,256]{1,0:T(1,128)S(1)}, u32[]{:S(2)}, u32[]{:S(2)}) collective-permute-start(f32[1,256]{1,0:T(1,128)S(1)} %copy-done.2), channel_id=1, source_target_pairs={{0,12},{2,14},{4,8},{6,10},{8,4},{10,6},{12,0},{14,2},{1,13},{3,15... | collective-permute-start | bytes 3080 | tf_op jit(solution)/shard_map/ppermute | solution.py:116
  23.2 2.0 %collective-permute-start.9 = (bf16[64,2560]{1,0:T(8,128)(2,1)S(1)}, bf16[64,2560]{1,0:T(8,128)(2,1)S(1)}, u32[]{:S(2)}, u32[]{:S(2)}) collective-permute-start(bf16[64,2560]{1,0:T(8,128)(2,1)S(1)} %bitcast.37), channel_id=1, source_target_pairs={{0,8},{2,10},{4,12},{6,14},{8,0},{10,2},{12,4},{14,6},{16,28},{18,... | collective-permute-start | bytes 983048 | tf_op jit(solution)/shard_map/ppermute | solution.py:153
  25.3 1.5 %collective-permute-start.6 = (bf16[64,2560]{1,0:T(8,128)(2,1)S(1)}, bf16[64,2560]{1,0:T(8,128)(2,1)S(1)}, u32[]{:S(2)}, u32[]{:S(2)}) collective-permute-start(bf16[64,2560]{1,0:T(8,128)(2,1)S(1)} %collective-permute-done), channel_id=1, source_target_pairs={{0,16},{16,0},{1,17},{17,1},{2,18},{18,2},{3,19},{19,3},{4,20},{20... | collective-permute-start | bytes 983048 | tf_op jit(solution)/shard_map/ppermute | solution.py:154
  26.8 1.5 %collective-permute-start.12 = (bf16[128,2560]{1,0:T(8,128)(2,1)S(1)}, bf16[128,2560]{1,0:T(8,128)(2,1)S(1)}, u32[]{:S(2)}, u32[]{:S(2)}) collective-permute-start(bf16[128,2560]{1,0:T(8,128)(2,1)S(1)} %copy-done.1), channel_id=1, source_target_pairs={{0,2},{2,0},{4,6},{6,4},{8,10},{10,8},{12,14},{14,12},{1,3},{3,1},... | collective-permute-start | bytes 1966088 | tf_op jit(solution)/shard_map/ppermute | solution.py:116
  28.3 5.7 %collective-permute-done.6 = bf16[64,2560]{1,0:T(8,128)(2,1)S(1)} collective-permute-done((bf16[64,2560]{1,0:T(8,128)(2,1)S(1)}, bf16[64,2560]{1,0:T(8,128)(2,1)S(1)}, u32[]{:S(2)}, u32[]{:S(2)}) %collective-permute-start.6) | collective-permute-done | bytes 327712 | tf_op jit(solution)/shard_map/ppermute | solution.py:154
  34.6 5.9 %collective-permute-done.9 = bf16[64,2560]{1,0:T(8,128)(2,1)S(1)} collective-permute-done((bf16[64,2560]{1,0:T(8,128)(2,1)S(1)}, bf16[64,2560]{1,0:T(8,128)(2,1)S(1)}, u32[]{:S(2)}, u32[]{:S(2)}) %collective-permute-start.9) | collective-permute-done | bytes 327712 | tf_op jit(solution)/shard_map/ppermute | solution.py:153
  41.3 1.6 %collective-permute-start.10 = (bf16[64,2560]{1,0:T(8,128)(2,1)S(1)}, bf16[64,2560]{1,0:T(8,128)(2,1)S(1)}, u32[]{:S(2)}, u32[]{:S(2)}) collective-permute-start(bf16[64,2560]{1,0:T(8,128)(2,1)S(1)} %collective-permute-done.9), channel_id=1, source_target_pairs={{0,16},{16,0},{1,17},{17,1},{2,18},{18,2},{3,19},{19,3},{4,20},{20... | collective-permute-start | bytes 983048 | tf_op jit(solution)/shard_map/ppermute | solution.py:159
  42.9 7.3 %collective-permute-done.8 = bf16[64,2560]{1,0:T(8,128)(2,1)S(1)} collective-permute-done((bf16[64,2560]{1,0:T(8,128)(2,1)S(1)}, bf16[64,2560]{1,0:T(8,128)(2,1)S(1)}, u32[]{:S(2)}, u32[]{:S(2)}) %collective-permute-start.8) | collective-permute-done | bytes 327712 | tf_op jit(solution)/shard_map/ppermute | solution.py:116
  52.9 3.5 %collective-permute-start.15 = (bf16[64,2560]{1,0:T(8,128)(2,1)S(1)}, bf16[64,2560]{1,0:T(8,128)(2,1)S(1)}, u32[]{:S(2)}, u32[]{:S(2)}) collective-permute-start(bf16[64,2560]{1,0:T(8,128)(2,1)S(1)} %convolution_convert_fusion.3), channel_id=1, source_target_pairs={{12,8},{14,10},{0,4},{2,6},{13,9},{15,11},{1,5},{3,7},{28,24},{30,... | collective-permute-start | bytes 983048 | tf_op jit(solution)/shard_map/ppermute | solution.py:116
  56.9 1.6 %collective-permute-start.11 = (bf16[128,2560]{1,0:T(8,128)(2,1)S(1)}, bf16[128,2560]{1,0:T(8,128)(2,1)S(1)}, u32[]{:S(2)}, u32[]{:S(2)}) collective-permute-start(bf16[128,2560]{1,0:T(8,128)(2,1)S(1)} %convolution_convert_fusion.1), channel_id=1, source_target_pairs={{0,2},{2,0},{4,6},{6,4},{8,10},{10,8},{12,14},{14,12},{1,3},{3,1},... | collective-permute-start | bytes 1966088 | tf_op jit(solution)/shard_map/ppermute | solution.py:116
  58.8 1.3 %collective-permute-start.20 = (bf16[64,2560]{1,0:T(8,128)(2,1)S(1)}, bf16[64,2560]{1,0:T(8,128)(2,1)S(1)}, u32[]{:S(2)}, u32[]{:S(2)}) collective-permute-start(bf16[64,2560]{1,0:T(8,128)(2,1)S(1)} %convolution_convert_fusion.2), channel_id=1, source_target_pairs={{12,8},{14,10},{0,4},{2,6},{13,9},{15,11},{1,5},{3,7},{28,24},{30,... | collective-permute-start | bytes 983048 | tf_op jit(solution)/shard_map/ppermute | solution.py:116
  60.1 4.4 %collective-permute-done.15 = bf16[64,2560]{1,0:T(8,128)(2,1)S(1)} collective-permute-done((bf16[64,2560]{1,0:T(8,128)(2,1)S(1)}, bf16[64,2560]{1,0:T(8,128)(2,1)S(1)}, u32[]{:S(2)}, u32[]{:S(2)}) %collective-permute-start.15) | collective-permute-done | bytes 327712 | tf_op jit(solution)/shard_map/ppermute | solution.py:116
  64.9 4.4 %collective-permute-start.18 = (bf16[64,2560]{1,0:T(8,128)(2,1)S(1)}, bf16[64,2560]{1,0:T(8,128)(2,1)S(1)}, u32[]{:S(2)}, u32[]{:S(2)}) collective-permute-start(bf16[64,2560]{1,0:T(8,128)(2,1)S(1)} %fusion.7), channel_id=1, source_target_pairs={{0,4},{2,6},{4,8},{6,10},{1,5},{3,7},{5,9},{7,11},{16,20},{18,22},... | collective-permute-start | bytes 983048 | tf_op jit(solution)/shard_map/ppermute | solution.py:116
  69.6 1.6 %collective-permute-start.14 = (bf16[128,2560]{1,0:T(8,128)(2,1)S(1)}, bf16[128,2560]{1,0:T(8,128)(2,1)S(1)}, u32[]{:S(2)}, u32[]{:S(2)}) collective-permute-start(bf16[128,2560]{1,0:T(8,128)(2,1)S(1)} %convolution_convert_fusion), channel_id=1, source_target_pairs={{0,2},{2,0},{4,6},{6,4},{8,10},{10,8},{12,14},{14,12},{1,3},{3,1},... | collective-permute-start | bytes 1966088 | tf_op jit(solution)/shard_map/ppermute | solution.py:116
  72.2 4.0 %collective-permute-start.23 = (bf16[64,2560]{1,0:T(8,128)(2,1)S(1)}, bf16[64,2560]{1,0:T(8,128)(2,1)S(1)}, u32[]{:S(2)}, u32[]{:S(2)}) collective-permute-start(bf16[64,2560]{1,0:T(8,128)(2,1)S(1)} %fusion.10), channel_id=1, source_target_pairs={{0,4},{2,6},{4,8},{6,10},{1,5},{3,7},{5,9},{7,11},{16,20},{18,22},... | collective-permute-start | bytes 983048 | tf_op jit(solution)/shard_map/ppermute | solution.py:116
  76.3 2.3 %collective-permute-done.18 = bf16[64,2560]{1,0:T(8,128)(2,1)S(1)} collective-permute-done((bf16[64,2560]{1,0:T(8,128)(2,1)S(1)}, bf16[64,2560]{1,0:T(8,128)(2,1)S(1)}, u32[]{:S(2)}, u32[]{:S(2)}) %collective-permute-start.18) | collective-permute-done | bytes 327712 | tf_op jit(solution)/shard_map/ppermute | solution.py:116
  79.6 5.0 %collective-permute-start.19 = (bf16[64,2560]{1,0:T(8,128)(2,1)S(1)}, bf16[64,2560]{1,0:T(8,128)(2,1)S(1)}, u32[]{:S(2)}, u32[]{:S(2)}) collective-permute-start(bf16[64,2560]{1,0:T(8,128)(2,1)S(1)} %fusion.8), channel_id=1, source_target_pairs={{0,4},{2,6},{4,8},{6,10},{8,12},{10,14},{1,5},{3,7},{5,9},{7,11},{... | collective-permute-start | bytes 983048 | tf_op jit(solution)/shard_map/ppermute | solution.py:116
  87.2 5.7 %collective-permute-start.24 = (bf16[64,2560]{1,0:T(8,128)(2,1)S(1)}, bf16[64,2560]{1,0:T(8,128)(2,1)S(1)}, u32[]{:S(2)}, u32[]{:S(2)}) collective-permute-start(bf16[64,2560]{1,0:T(8,128)(2,1)S(1)} %fusion.11), channel_id=1, source_target_pairs={{0,4},{2,6},{4,8},{6,10},{8,12},{10,14},{1,5},{3,7},{5,9},{7,11},{... | collective-permute-start | bytes 983048 | tf_op jit(solution)/shard_map/ppermute | solution.py:116
  93.3 1.3 %collective-permute-start.22 = (bf16[64,2560]{1,0:T(8,128)(2,1)S(1)}, bf16[64,2560]{1,0:T(8,128)(2,1)S(1)}, u32[]{:S(2)}, u32[]{:S(2)}) collective-permute-start(bf16[64,2560]{1,0:T(8,128)(2,1)S(1)} %fusion.9), channel_id=1, source_target_pairs={{4,0},{6,2},{8,4},{10,6},{12,8},{14,10},{5,1},{7,3},{9,5},{11,7},{... | collective-permute-start | bytes 983048 | tf_op jit(solution)/shard_map/ppermute | solution.py:116
  98.8 4.5 %collective-permute-done.22 = bf16[64,2560]{1,0:T(8,128)(2,1)S(1)} collective-permute-done((bf16[64,2560]{1,0:T(8,128)(2,1)S(1)}, bf16[64,2560]{1,0:T(8,128)(2,1)S(1)}, u32[]{:S(2)}, u32[]{:S(2)}) %collective-permute-start.22) | collective-permute-done | bytes 327712 | tf_op jit(solution)/shard_map/ppermute | solution.py:116
  (69 shorter events, 17.9 us)
Async XLA Ops:
  0.7 19.2 %collective-permute-start = (bf16[64,2560]{1,0:T(8,128)(2,1)}, bf16[64,2560]{1,0:T(8,128)(2,1)S(1)}, u32[]{:S(2)}, u32[]{:S(2)}) collective-permute-start(bf16[64,2560]{1,0:T(8,128)(2,1)} %bitcast.42), channel_id=1, source_target_pairs={{0,8},{2,10},{4,12},{6,14},{8,0},{10,2},{12,4},{14,6},{16,28},{18,... | collective-permute-start | bytes 983048 | tf_op jit(solution)/shard_map/ppermute | solution.py:150
  4.8 20.5 %collective-permute-start.5 = (bf16[64,2560]{1,0:T(8,128)(2,1)}, bf16[64,2560]{1,0:T(8,128)(2,1)S(1)}, u32[]{:S(2)}, u32[]{:S(2)}) collective-permute-start(bf16[64,2560]{1,0:T(8,128)(2,1)} %bitcast.43), channel_id=1, source_target_pairs={{0,4},{2,6},{4,0},{6,2},{8,12},{10,14},{12,8},{14,10},{1,5},{3,7},... | collective-permute-start | bytes 983048 | tf_op jit(solution)/shard_map/ppermute | solution.py:116
  6.3 20.5 %collective-permute-start.4 = (bf16[128,2560]{1,0:T(8,128)(2,1)}, bf16[128,2560]{1,0:T(8,128)(2,1)S(1)}, u32[]{:S(2)}, u32[]{:S(2)}) collective-permute-start(bf16[128,2560]{1,0:T(8,128)(2,1)} %param.6), channel_id=1, source_target_pairs={{0,2},{2,0},{4,6},{6,4},{8,10},{10,8},{12,14},{14,12},{1,3},{3,1},... | collective-permute-start | bytes 1966088 | tf_op jit(solution)/shard_map/ppermute | solution.py:116
  19.8 31.5 %collective-permute-start.2 = (f32[1,256]{1,0:T(1,128)S(1)}, f32[1,256]{1,0:T(1,128)S(1)}, u32[]{:S(2)}, u32[]{:S(2)}) collective-permute-start(f32[1,256]{1,0:T(1,128)S(1)} %copy-done.2), channel_id=1, source_target_pairs={{0,8},{2,10},{4,12},{6,14},{8,0},{10,2},{12,4},{14,6},{1,9},{3,11}... | collective-permute-start | bytes 3080 | tf_op jit(solution)/shard_map/ppermute | solution.py:116
  19.8 31.5 %collective-permute-start.3 = (f32[1,256]{1,0:T(1,128)S(1)}, f32[1,256]{1,0:T(1,128)S(1)}, u32[]{:S(2)}, u32[]{:S(2)}) collective-permute-start(f32[1,256]{1,0:T(1,128)S(1)} %copy-done.2), channel_id=1, source_target_pairs={{0,12},{2,14},{4,8},{6,10},{8,4},{10,6},{12,0},{14,2},{1,13},{3,15... | collective-permute-start | bytes 3080 | tf_op jit(solution)/shard_map/ppermute | solution.py:116
  23.2 17.3 %collective-permute-start.9 = (bf16[64,2560]{1,0:T(8,128)(2,1)S(1)}, bf16[64,2560]{1,0:T(8,128)(2,1)S(1)}, u32[]{:S(2)}, u32[]{:S(2)}) collective-permute-start(bf16[64,2560]{1,0:T(8,128)(2,1)S(1)} %bitcast.37), channel_id=1, source_target_pairs={{0,8},{2,10},{4,12},{6,14},{8,0},{10,2},{12,4},{14,6},{16,28},{18,... | collective-permute-start | bytes 983048 | tf_op jit(solution)/shard_map/ppermute | solution.py:153
  25.3 8.8 %collective-permute-start.6 = (bf16[64,2560]{1,0:T(8,128)(2,1)S(1)}, bf16[64,2560]{1,0:T(8,128)(2,1)S(1)}, u32[]{:S(2)}, u32[]{:S(2)}) collective-permute-start(bf16[64,2560]{1,0:T(8,128)(2,1)S(1)} %collective-permute-done), channel_id=1, source_target_pairs={{0,16},{16,0},{1,17},{17,1},{2,18},{18,2},{3,19},{19,3},{4,20},{20... | collective-permute-start | bytes 983048 | tf_op jit(solution)/shard_map/ppermute | solution.py:154
  26.8 14.5 %collective-permute-start.12 = (bf16[128,2560]{1,0:T(8,128)(2,1)S(1)}, bf16[128,2560]{1,0:T(8,128)(2,1)S(1)}, u32[]{:S(2)}, u32[]{:S(2)}) collective-permute-start(bf16[128,2560]{1,0:T(8,128)(2,1)S(1)} %copy-done.1), channel_id=1, source_target_pairs={{0,2},{2,0},{4,6},{6,4},{8,10},{10,8},{12,14},{14,12},{1,3},{3,1},... | collective-permute-start | bytes 1966088 | tf_op jit(solution)/shard_map/ppermute | solution.py:116
  34.1 17.2 %collective-permute-start.1 = (f32[1,256]{1,0:T(1,128)S(1)}, f32[1,256]{1,0:T(1,128)S(1)}, u32[]{:S(2)}, u32[]{:S(2)}) collective-permute-start(f32[1,256]{1,0:T(1,128)S(1)} %copy-done.2), channel_id=1, source_target_pairs={{0,4},{2,6},{4,0},{6,2},{8,12},{10,14},{12,8},{14,10},{1,5},{3,7},... | collective-permute-start | bytes 3080 | tf_op jit(solution)/shard_map/ppermute | solution.py:116
  40.6 9.6 %collective-permute-start.8 = (bf16[64,2560]{1,0:T(8,128)(2,1)S(1)}, bf16[64,2560]{1,0:T(8,128)(2,1)S(1)}, u32[]{:S(2)}, u32[]{:S(2)}) collective-permute-start(bf16[64,2560]{1,0:T(8,128)(2,1)S(1)} %bitcast.38), channel_id=1, source_target_pairs={{0,4},{2,6},{4,0},{6,2},{8,12},{10,14},{12,8},{14,10},{1,5},{3,7},... | collective-permute-start | bytes 983048 | tf_op jit(solution)/shard_map/ppermute | solution.py:116
  41.3 8.9 %collective-permute-start.10 = (bf16[64,2560]{1,0:T(8,128)(2,1)S(1)}, bf16[64,2560]{1,0:T(8,128)(2,1)S(1)}, u32[]{:S(2)}, u32[]{:S(2)}) collective-permute-start(bf16[64,2560]{1,0:T(8,128)(2,1)S(1)} %collective-permute-done.9), channel_id=1, source_target_pairs={{0,16},{16,0},{1,17},{17,1},{2,18},{18,2},{3,19},{19,3},{4,20},{20... | collective-permute-start | bytes 983048 | tf_op jit(solution)/shard_map/ppermute | solution.py:159
  50.7 1.7 %collective-permute-start.13 = (f32[256,256]{0,1:T(8,128)S(1)}, f32[256,256]{0,1:T(8,128)S(1)}, u32[]{:S(2)}, u32[]{:S(2)}) collective-permute-start(f32[256,256]{0,1:T(8,128)S(1)} %fusion.45), channel_id=1, source_target_pairs={{0,1},{1,0},{2,3},{3,2},{4,5},{5,4},{6,7},{7,6},{8,9},{9,8},{10,11... | collective-permute-start | bytes 786440 | tf_op jit(solution)/shard_map/ppermute | solution.py:136
  52.9 11.6 %collective-permute-start.15 = (bf16[64,2560]{1,0:T(8,128)(2,1)S(1)}, bf16[64,2560]{1,0:T(8,128)(2,1)S(1)}, u32[]{:S(2)}, u32[]{:S(2)}) collective-permute-start(bf16[64,2560]{1,0:T(8,128)(2,1)S(1)} %convolution_convert_fusion.3), channel_id=1, source_target_pairs={{12,8},{14,10},{0,4},{2,6},{13,9},{15,11},{1,5},{3,7},{28,24},{30,... | collective-permute-start | bytes 983048 | tf_op jit(solution)/shard_map/ppermute | solution.py:116
  56.9 36.5 %collective-permute-start.11 = (bf16[128,2560]{1,0:T(8,128)(2,1)S(1)}, bf16[128,2560]{1,0:T(8,128)(2,1)S(1)}, u32[]{:S(2)}, u32[]{:S(2)}) collective-permute-start(bf16[128,2560]{1,0:T(8,128)(2,1)S(1)} %convolution_convert_fusion.1), channel_id=1, source_target_pairs={{0,2},{2,0},{4,6},{6,4},{8,10},{10,8},{12,14},{14,12},{1,3},{3,1},... | collective-permute-start | bytes 1966088 | tf_op jit(solution)/shard_map/ppermute | solution.py:116
  58.8 13.1 %collective-permute-start.20 = (bf16[64,2560]{1,0:T(8,128)(2,1)S(1)}, bf16[64,2560]{1,0:T(8,128)(2,1)S(1)}, u32[]{:S(2)}, u32[]{:S(2)}) collective-permute-start(bf16[64,2560]{1,0:T(8,128)(2,1)S(1)} %convolution_convert_fusion.2), channel_id=1, source_target_pairs={{12,8},{14,10},{0,4},{2,6},{13,9},{15,11},{1,5},{3,7},{28,24},{30,... | collective-permute-start | bytes 983048 | tf_op jit(solution)/shard_map/ppermute | solution.py:116
  64.9 13.7 %collective-permute-start.18 = (bf16[64,2560]{1,0:T(8,128)(2,1)S(1)}, bf16[64,2560]{1,0:T(8,128)(2,1)S(1)}, u32[]{:S(2)}, u32[]{:S(2)}) collective-permute-start(bf16[64,2560]{1,0:T(8,128)(2,1)S(1)} %fusion.7), channel_id=1, source_target_pairs={{0,4},{2,6},{4,8},{6,10},{1,5},{3,7},{5,9},{7,11},{16,20},{18,22},... | collective-permute-start | bytes 983048 | tf_op jit(solution)/shard_map/ppermute | solution.py:116
  69.6 26.2 %collective-permute-start.14 = (bf16[128,2560]{1,0:T(8,128)(2,1)S(1)}, bf16[128,2560]{1,0:T(8,128)(2,1)S(1)}, u32[]{:S(2)}, u32[]{:S(2)}) collective-permute-start(bf16[128,2560]{1,0:T(8,128)(2,1)S(1)} %convolution_convert_fusion), channel_id=1, source_target_pairs={{0,2},{2,0},{4,6},{6,4},{8,10},{10,8},{12,14},{14,12},{1,3},{3,1},... | collective-permute-start | bytes 1966088 | tf_op jit(solution)/shard_map/ppermute | solution.py:116
  71.2 8.4 %collective-permute-start.16 = (bf16[64,2560]{1,0:T(8,128)(2,1)S(1)}, bf16[64,2560]{1,0:T(8,128)(2,1)S(1)}, u32[]{:S(2)}, u32[]{:S(2)}) collective-permute-start(bf16[64,2560]{1,0:T(8,128)(2,1)S(1)} %fusion.7), channel_id=1, source_target_pairs={{12,8},{14,10},{8,4},{10,6},{13,9},{15,11},{9,5},{11,7},{28,24},{3... | collective-permute-start | bytes 983048 | tf_op jit(solution)/shard_map/ppermute | solution.py:116
  72.2 13.3 %collective-permute-start.23 = (bf16[64,2560]{1,0:T(8,128)(2,1)S(1)}, bf16[64,2560]{1,0:T(8,128)(2,1)S(1)}, u32[]{:S(2)}, u32[]{:S(2)}) collective-permute-start(bf16[64,2560]{1,0:T(8,128)(2,1)S(1)} %fusion.10), channel_id=1, source_target_pairs={{0,4},{2,6},{4,8},{6,10},{1,5},{3,7},{5,9},{7,11},{16,20},{18,22},... | collective-permute-start | bytes 983048 | tf_op jit(solution)/shard_map/ppermute | solution.py:116
  78.6 8.7 %collective-permute-start.21 = (bf16[64,2560]{1,0:T(8,128)(2,1)S(1)}, bf16[64,2560]{1,0:T(8,128)(2,1)S(1)}, u32[]{:S(2)}, u32[]{:S(2)}) collective-permute-start(bf16[64,2560]{1,0:T(8,128)(2,1)S(1)} %fusion.10), channel_id=1, source_target_pairs={{12,8},{14,10},{8,4},{10,6},{13,9},{15,11},{9,5},{11,7},{28,24},{3... | collective-permute-start | bytes 983048 | tf_op jit(solution)/shard_map/ppermute | solution.py:116
  79.6 17.4 %collective-permute-start.19 = (bf16[64,2560]{1,0:T(8,128)(2,1)S(1)}, bf16[64,2560]{1,0:T(8,128)(2,1)S(1)}, u32[]{:S(2)}, u32[]{:S(2)}) collective-permute-start(bf16[64,2560]{1,0:T(8,128)(2,1)S(1)} %fusion.8), channel_id=1, source_target_pairs={{0,4},{2,6},{4,8},{6,10},{8,12},{10,14},{1,5},{3,7},{5,9},{7,11},{... | collective-permute-start | bytes 983048 | tf_op jit(solution)/shard_map/ppermute | solution.py:116
  85.6 11.7 %collective-permute-start.17 = (bf16[64,2560]{1,0:T(8,128)(2,1)S(1)}, bf16[64,2560]{1,0:T(8,128)(2,1)S(1)}, u32[]{:S(2)}, u32[]{:S(2)}) collective-permute-start(bf16[64,2560]{1,0:T(8,128)(2,1)S(1)} %fusion.6), channel_id=1, source_target_pairs={{4,0},{6,2},{8,4},{10,6},{12,8},{14,10},{5,1},{7,3},{9,5},{11,7},{... | collective-permute-start | bytes 983048 | tf_op jit(solution)/shard_map/ppermute | solution.py:116
  87.2 11.6 %collective-permute-start.24 = (bf16[64,2560]{1,0:T(8,128)(2,1)S(1)}, bf16[64,2560]{1,0:T(8,128)(2,1)S(1)}, u32[]{:S(2)}, u32[]{:S(2)}) collective-permute-start(bf16[64,2560]{1,0:T(8,128)(2,1)S(1)} %fusion.11), channel_id=1, source_target_pairs={{0,4},{2,6},{4,8},{6,10},{8,12},{10,14},{1,5},{3,7},{5,9},{7,11},{... | collective-permute-start | bytes 983048 | tf_op jit(solution)/shard_map/ppermute | solution.py:116
  93.3 10.0 %collective-permute-start.22 = (bf16[64,2560]{1,0:T(8,128)(2,1)S(1)}, bf16[64,2560]{1,0:T(8,128)(2,1)S(1)}, u32[]{:S(2)}, u32[]{:S(2)}) collective-permute-start(bf16[64,2560]{1,0:T(8,128)(2,1)S(1)} %fusion.9), channel_id=1, source_target_pairs={{4,0},{6,2},{8,4},{10,6},{12,8},{14,10},{5,1},{7,3},{9,5},{11,7},{... | collective-permute-start | bytes 983048 | tf_op jit(solution)/shard_map/ppermute | solution.py:116
  (6 other events, 68.0 us)

commit v3 on v2

--- a/solution.py
+++ b/solution.py
@@ -101,11 +101,9 @@
     return on_line([(a, a ^ bit) for a in range(PLACES)])
 
 
-RISE = on_line([(0, 1), (1, 2), (2, 3)])
-FALL = on_line([(1, 0), (2, 1), (3, 2)])
-FROM_ENDS = on_line([(3, 2), (0, 1)])
-RISE_IN = on_line([(0, 1), (1, 2)])
-FALL_IN = on_line([(3, 2), (2, 1)])
+ENDS_IN = on_line([(0, 1), (3, 2)])
+MIDDLE = on_line([(1, 2), (2, 1)])
+ENDS_OUT = on_line([(1, 0), (2, 3)])
 PARTNER = [(2 * a + side, 2 * a + 1 - side) for a in range(PLACES) for side in (0, 1)]
 SWAP = [(0, 1), (1, 0)]
 OWNERS = 2 * PLACES
@@ -120,16 +118,31 @@
     return lax.optimization_barrier((value, earlier))[0]
 
 
-def collect(weights, rows):
-    own, third, second, below, above = weights
-    half = jnp.bfloat16
-    back = move(contract_first(third, rows).astype(half), FROM_ENDS)
-    second = (contract_first(second, rows) + back.astype(jnp.float32)).astype(half)
-    falling = move(second, FALL_IN)
-    rising = move(second, RISE_IN)
-    below = move((contract_first(below, rows) + falling.astype(jnp.float32)).astype(half), FALL)
-    above = move((contract_first(above, rows) + rising.astype(jnp.float32)).astype(half), RISE)
-    return contract_first(own, rows) + below.astype(jnp.float32) + above.astype(jnp.float32)
+def narrow(value):
+    return value.astype(jnp.bfloat16)
+
+
+def add_up(*values):
+    total = values[0]
+    for value in values[1:]:
+        total = total + value.astype(jnp.float32)
+    return total
+
+
+def collect_start(weights, rows):
+    parts = [contract_first(weight, rows) for weight in weights]
+    for_end = move(narrow(parts[3]), ENDS_IN)
+    rest = move(narrow(jnp.concatenate([parts[2], parts[1]])), ENDS_IN)
+    return parts, for_end, rest
+
+
+def collect_end(started):
+    (own, first, second, third), for_end, rest = started
+    for_middle, for_near = jnp.split(rest, 2)
+    for_end = move(narrow(add_up(second, for_end)), MIDDLE)
+    for_middle = move(narrow(add_up(third, for_middle)), MIDDLE)
+    for_end = move(narrow(add_up(first, for_end)), ENDS_OUT)
+    return add_up(own, for_near, for_middle, for_end)
 
 
 def both_cores(partial):
@@ -139,8 +152,6 @@
 def by_pairs(tokens, cotangent, down_adapter, up_adapter, token_lists, gating):
     me = lax.axis_index("adapter")
     first_group = lax.axis_index("groups") == 0
-    place = me // 2
-    odd = place % 2 == 1
     tok_local = tokens.shape[0]
     capacity = gating.shape[1]
     down_matrix = down_adapter[0]
@@ -148,15 +159,15 @@
     rank = down_matrix.shape[0]
 
     far_down = lax.ppermute(down_matrix, ("groups", "adapter"), FAR)
+    tokens2 = move(tokens, PARTNER)
     near_down = move(down_matrix, xor_line(1))
-    tokens2 = move(tokens, PARTNER)
+    cross_down = lax.ppermute(far_down, "groups", SWAP)
     far_up = lax.ppermute(after(up_matrix, far_down), ("groups", "adapter"), FAR)
-    cross_down = lax.ppermute(far_down, "groups", SWAP)
+    cot2 = move(after(cotangent, (tokens2, far_down)), PARTNER)
     near_up = move(after(up_matrix, near_down), xor_line(1))
-    cot2 = move(after(cotangent, tokens2), PARTNER)
-    later = after(gating, far_down)
+    cross_up = lax.ppermute(far_up, "groups", SWAP)
+    later = after(gating, (far_down, near_down, tokens2))
     gates = [gating, move(later, xor_line(1)), move(later, xor_line(2)), move(later, xor_line(3))]
-    cross_up = lax.ppermute(far_up, "groups", SWAP)
 
     far_bit = jnp.where(first_group, 2, 3)
     experts = jnp.stack([me, me ^ 2, me ^ (2 * far_bit), me ^ (2 * (far_bit ^ 1))])
@@ -173,7 +184,6 @@
     tokens2 = jnp.concatenate([tokens, tokens2], axis=0)
     cot2 = jnp.concatenate([cotangent, cot2], axis=0)
     down_all = jnp.concatenate([down_matrix, near_down, far_down, cross_down], axis=0)
-    up_all = jnp.concatenate([up_matrix, near_up, far_up, cross_up], axis=0)
 
     def low_rank(rows, matrices):
         return (scale * both_cores(contract_last(rows, matrices))).astype(jnp.bfloat16)
@@ -182,22 +192,28 @@
         own, near, far, cross = (low[:, k * rank : (k + 1) * rank] for k in range(4))
         second = jnp.where(first_group, far, cross)
         third = jnp.where(first_group, cross, far)
-        below = jnp.where(odd, near, third)
-        above = jnp.where(odd, third, near)
-        return own, third, second, below, above
-
-    def outward(weights, matrix):
+        return own, near, second, third
+
+    def outward_start(weights, matrix):
         theirs = jnp.dot(weights[tok_local:], matrix, preferred_element_type=jnp.float32)
-        back = move(theirs.astype(jnp.bfloat16), PARTNER)
+        return move(narrow(theirs), PARTNER)
+
+    def outward_end(weights, matrix, back):
         mine = jnp.dot(weights[:tok_local], matrix, preferred_element_type=jnp.float32)
-        return (mine + back.astype(jnp.float32)).astype(jnp.bfloat16)
+        return narrow(mine + back.astype(jnp.float32))
 
     low = low_rank(tokens2, down_all)
-    up_grad = collect(for_line(low), cot2)
+    up_parts = collect_start(for_line(low), cot2)
+    cross_up = after(cross_up, low)
+    up_all = jnp.concatenate([up_matrix, near_up, far_up, cross_up], axis=0)
     low_back = low_rank(cot2, up_all)
-    down_grad = collect(for_line(low_back), tokens2)
-    branch_out = outward(low, up_all)
-    input_grad = outward(low_back, down_all)
+    branch_back = outward_start(low, up_all)
+    down_parts = collect_start(for_line(low_back), tokens2)
+    input_back = outward_start(low_back, down_all)
+    up_grad = collect_end(up_parts)
+    branch_out = outward_end(low, up_all, branch_back)
+    input_grad = outward_end(low_back, down_all, input_back)
+    down_grad = collect_end(down_parts)
     down_grad = (down_grad / capacity).astype(jnp.bfloat16)[None]
     up_grad = (up_grad / capacity).astype(jnp.bfloat16)[None]
     return (branch_out, input_grad, down_grad, up_grad)

time: 105 us -> 127 us (1.21)
  waiting for transfers between devices: 42.9 us -> 75.9 us
  starting transfers between devices: 48.8 us -> 38.6 us
    ppermute x19, waiting for transfers between devices: 20.6 us -> 48.8 us  [move(): return lax.ppermute(value, 'adapter', pairs)]
    ppermute x1, waiting for transfers between devices: 0.01 us -> 9.15 us  [by_pairs(): cross_up = lax.ppermute(far_up, 'groups', SWAP)]
    ppermute x19, starting transfers between devices: 39 us -> 33.1 us  [move(): return lax.ppermute(value, 'adapter', pairs)]
    ppermute x1, waiting for transfers between devices: 5.94 us -> 2.99 us  [by_pairs(): lax.ppermute(after(up_matrix, far_down), ('groups', 'adapter'), FAR)]
    ppermute x1, starting transfers between devices: 2.02 us -> 0.01 us  [by_pairs(): lax.ppermute(after(up_matrix, far_down), ('groups', 'adapter'), FAR)]
    ppermute x1, starting transfers between devices: 1.56 us -> 0.01 us  [by_pairs(): cross_up = lax.ppermute(far_up, 'groups', SWAP)]
    dot_general x10 -> x8, matrix products: 5.01 us -> 4.33 us  [contract_first(): lax.dot_general(left_op, right_op, (((0,), (0,)), ((), ())), preferred_el...]
  transfers between devices with their start and end apart: 25 -> 25, of which waited for: 13 -> 13; matrix products, arithmetic and copies ran while one was open for 10% -> 8% of each run, Pallas kernels for 0% -> 0%
where the time goes in v3:
time: 127 us
  waiting for transfers between devices  75.9 us (60%)
  starting transfers between devices  38.6 us (30%)
  matrix products  8.52 us (7%)
  local copies, waits for them, and re-layouts  1.9 us (1%)
    ppermute x19, waiting for transfers between devices, move(): return lax.ppermute(value, 'adapter', pairs)  48.8 us
    ppermute x19, starting transfers between devices, move(): return lax.ppermute(value, 'adapter', pairs)  33.1 us
    ppermute x1, waiting for transfers between devices, by_pairs(): far_down = lax.ppermute(down_matrix, ('groups', 'adapter'), FAR)  9.87 us
    ppermute x1, waiting for transfers between devices, by_pairs(): cross_up = lax.ppermute(far_up, 'groups', SWAP)  9.15 us
    ppermute x1, waiting for transfers between devices, by_pairs(): cross_down = lax.ppermute(far_down, 'groups', SWAP)  5.07 us
    dot_general x8, matrix products, contract_first(): lax.dot_general(left_op, right_op, (((0,), (0,)), ((), ())), preferred_el...  4.33 us
    ppermute x1, starting transfers between devices, by_pairs(): far_down = lax.ppermute(down_matrix, ('groups', 'adapter'), FAR)  4.1 us
    ppermute x1, waiting for transfers between devices, by_pairs(): lax.ppermute(after(up_matrix, far_down), ('groups', 'adapter'), FAR)  2.99 us
  transfers between devices with their start and end apart: 25, of which 13 were waited for; matrix products, arithmetic and copies ran while one was open for 8% of the time, Pallas kernels for 0%

profile of v3, /device:TPU:0, one launch (start us, length us, event | category | flops | bytes accessed | tf_op | source)
XLA Modules:
  0.0 126.9 jit_solution(10563203656193044286)
XLA Ops:
  0.7 4.1 %collective-permute-start = (bf16[64,2560]{1,0:T(8,128)(2,1)}, bf16[64,2560]{1,0:T(8,128)(2,1)S(1)}, u32[]{:S(2)}, u32[]{:S(2)}) collective-permute-start(bf16[64,2560]{1,0:T(8,128)(2,1)} %bitcast.38), channel_id=1, source_target_pairs={{0,8},{2,10},{4,12},{6,14},{8,0},{10,2},{12,4},{14,6},{16,28},{18,... | collective-permute-start | bytes 983048 | tf_op jit(solution)/shard_map/ppermute | solution.py:161
  4.8 1.6 %collective-permute-start.1 = (bf16[64,2560]{1,0:T(8,128)(2,1)}, bf16[64,2560]{1,0:T(8,128)(2,1)S(1)}, u32[]{:S(2)}, u32[]{:S(2)}) collective-permute-start(bf16[64,2560]{1,0:T(8,128)(2,1)} %bitcast.39), channel_id=1, source_target_pairs={{0,4},{2,6},{4,0},{6,2},{8,12},{10,14},{12,8},{14,10},{1,5},{3,7},... | collective-permute-start | bytes 983048 | tf_op jit(solution)/shard_map/ppermute | solution.py:114
  6.3 1.5 %collective-permute-start.2 = (bf16[128,2560]{1,0:T(8,128)(2,1)}, bf16[128,2560]{1,0:T(8,128)(2,1)S(1)}, u32[]{:S(2)}, u32[]{:S(2)}) collective-permute-start(bf16[128,2560]{1,0:T(8,128)(2,1)} %param.6), channel_id=1, source_target_pairs={{0,2},{2,0},{4,6},{6,4},{8,10},{10,8},{12,14},{14,12},{1,3},{3,1},... | collective-permute-start | bytes 1966088 | tf_op jit(solution)/shard_map/ppermute | solution.py:114
  9.9 9.9 %collective-permute-done = bf16[64,2560]{1,0:T(8,128)(2,1)S(1)} collective-permute-done((bf16[64,2560]{1,0:T(8,128)(2,1)}, bf16[64,2560]{1,0:T(8,128)(2,1)S(1)}, u32[]{:S(2)}, u32[]{:S(2)}) %collective-permute-start) | collective-permute-done | bytes 327712 | tf_op jit(solution)/shard_map/ppermute | solution.py:161
  20.0 3.8 %collective-permute-start.8 = (bf16[64,2560]{1,0:T(8,128)(2,1)S(1)}, bf16[64,2560]{1,0:T(8,128)(2,1)S(1)}, u32[]{:S(2)}, u32[]{:S(2)}) collective-permute-start(bf16[64,2560]{1,0:T(8,128)(2,1)S(1)} %bitcast.34), channel_id=1, source_target_pairs={{0,4},{2,6},{4,0},{6,2},{8,12},{10,14},{12,8},{14,10},{1,5},{3,7},... | collective-permute-start | bytes 983048 | tf_op jit(solution)/shard_map/ppermute | solution.py:114
  23.8 1.3 %collective-permute-start.6 = (bf16[64,2560]{1,0:T(8,128)(2,1)S(1)}, bf16[64,2560]{1,0:T(8,128)(2,1)S(1)}, u32[]{:S(2)}, u32[]{:S(2)}) collective-permute-start(bf16[64,2560]{1,0:T(8,128)(2,1)S(1)} %collective-permute-done), channel_id=1, source_target_pairs={{0,16},{16,0},{1,17},{17,1},{2,18},{18,2},{3,19},{19,3},{4,20},{20... | collective-permute-start | bytes 983048 | tf_op jit(solution)/shard_map/ppermute | solution.py:164
  25.1 2.6 %collective-permute-start.5 = (f32[1,256]{1,0:T(1,128)S(1)}, f32[1,256]{1,0:T(1,128)S(1)}, u32[]{:S(2)}, u32[]{:S(2)}) collective-permute-start(f32[1,256]{1,0:T(1,128)S(1)} %copy-done.2), channel_id=1, source_target_pairs={{0,12},{2,14},{4,8},{6,10},{8,4},{10,6},{12,0},{14,2},{1,13},{3,15... | collective-permute-start | bytes 3080 | tf_op jit(solution)/shard_map/ppermute | solution.py:114
  27.8 5.1 %collective-permute-done.6 = bf16[64,2560]{1,0:T(8,128)(2,1)S(1)} collective-permute-done((bf16[64,2560]{1,0:T(8,128)(2,1)S(1)}, bf16[64,2560]{1,0:T(8,128)(2,1)S(1)}, u32[]{:S(2)}, u32[]{:S(2)}) %collective-permute-start.6) | collective-permute-done | bytes 327712 | tf_op jit(solution)/shard_map/ppermute | solution.py:164
  33.7 3.0 %collective-permute-done.9 = bf16[64,2560]{1,0:T(8,128)(2,1)S(1)} collective-permute-done((bf16[64,2560]{1,0:T(8,128)(2,1)S(1)}, bf16[64,2560]{1,0:T(8,128)(2,1)S(1)}, u32[]{:S(2)}, u32[]{:S(2)}) %collective-permute-start.9) | collective-permute-done | bytes 327712 | tf_op jit(solution)/shard_map/ppermute | solution.py:165
  38.6 9.1 %collective-permute-done.10 = bf16[64,2560]{1,0:T(8,128)(2,1)S(1)} collective-permute-done((bf16[64,2560]{1,0:T(8,128)(2,1)S(1)}, bf16[64,2560]{1,0:T(8,128)(2,1)S(1)}, u32[]{:S(2)}, u32[]{:S(2)}) %collective-permute-start.10) | collective-permute-done | bytes 327712 | tf_op jit(solution)/shard_map/ppermute | solution.py:168
  49.0 5.3 %collective-permute-done.12 = bf16[128,2560]{1,0:T(8,128)(2,1)S(1)} collective-permute-done((bf16[128,2560]{1,0:T(8,128)(2,1)S(1)}, bf16[128,2560]{1,0:T(8,128)(2,1)S(1)}, u32[]{:S(2)}, u32[]{:S(2)}) %collective-permute-start.12) | collective-permute-done | bytes 655392 | tf_op jit(solution)/shard_map/ppermute | solution.py:114
  55.7 4.1 %collective-permute-start.20 = (bf16[128,2560]{1,0:T(8,128)(2,1)S(1)}, bf16[128,2560]{1,0:T(8,128)(2,1)S(1)}, u32[]{:S(2)}, u32[]{:S(2)}) collective-permute-start(bf16[128,2560]{1,0:T(8,128)(2,1)S(1)} %pad_maximum_fusion.3), channel_id=1, source_target_pairs={{0,4},{2,6},{12,8},{14,10},{1,5},{3,7},{13,9},{15,11},{16,20},{18,... | collective-permute-start | bytes 1966088 | tf_op jit(solution)/shard_map/ppermute | solution.py:114
  60.7 1.4 %collective-permute-start.15 = (bf16[128,2560]{1,0:T(8,128)(2,1)S(1)}, bf16[128,2560]{1,0:T(8,128)(2,1)S(1)}, u32[]{:S(2)}, u32[]{:S(2)}) collective-permute-start(bf16[128,2560]{1,0:T(8,128)(2,1)S(1)} %pad_maximum_fusion.2), channel_id=1, source_target_pairs={{0,4},{2,6},{12,8},{14,10},{1,5},{3,7},{13,9},{15,11},{16,20},{18,... | collective-permute-start | bytes 1966088 | tf_op jit(solution)/shard_map/ppermute | solution.py:114
  62.5 1.6 %collective-permute-start.14 = (bf16[128,2560]{1,0:T(8,128)(2,1)S(1)}, bf16[128,2560]{1,0:T(8,128)(2,1)S(1)}, u32[]{:S(2)}, u32[]{:S(2)}) collective-permute-start(bf16[128,2560]{1,0:T(8,128)(2,1)S(1)} %convolution_convert_fusion), channel_id=1, source_target_pairs={{0,2},{2,0},{4,6},{6,4},{8,10},{10,8},{12,14},{14,12},{1,3},{3,1},... | collective-permute-start | bytes 1966088 | tf_op jit(solution)/shard_map/ppermute | solution.py:114
  64.1 10.8 %collective-permute-done.20 = bf16[128,2560]{1,0:T(8,128)(2,1)S(1)} collective-permute-done((bf16[128,2560]{1,0:T(8,128)(2,1)S(1)}, bf16[128,2560]{1,0:T(8,128)(2,1)S(1)}, u32[]{:S(2)}, u32[]{:S(2)}) %collective-permute-start.20) | collective-permute-done | bytes 655392 | tf_op jit(solution)/shard_map/ppermute | solution.py:114
  75.2 4.4 %collective-permute-start.22 = (bf16[64,2560]{1,0:T(8,128)(2,1)S(1)}, bf16[64,2560]{1,0:T(8,128)(2,1)S(1)}, u32[]{:S(2)}, u32[]{:S(2)}) collective-permute-start(bf16[64,2560]{1,0:T(8,128)(2,1)S(1)} %get-tuple-element.15), channel_id=1, source_target_pairs={{0,4},{2,6},{12,8},{14,10},{1,5},{3,7},{13,9},{15,11},{16,20},{18,... | collective-permute-start | bytes 983048 | tf_op jit(solution)/shard_map/ppermute | solution.py:114
  81.5 7.4 %collective-permute-done.15 = bf16[128,2560]{1,0:T(8,128)(2,1)S(1)} collective-permute-done((bf16[128,2560]{1,0:T(8,128)(2,1)S(1)}, bf16[128,2560]{1,0:T(8,128)(2,1)S(1)}, u32[]{:S(2)}, u32[]{:S(2)}) %collective-permute-start.15) | collective-permute-done | bytes 655392 | tf_op jit(solution)/shard_map/ppermute | solution.py:114
  89.2 4.4 %collective-permute-start.17 = (bf16[64,2560]{1,0:T(8,128)(2,1)S(1)}, bf16[64,2560]{1,0:T(8,128)(2,1)S(1)}, u32[]{:S(2)}, u32[]{:S(2)}) collective-permute-start(bf16[64,2560]{1,0:T(8,128)(2,1)S(1)} %get-tuple-element.17), channel_id=1, source_target_pairs={{0,4},{2,6},{12,8},{14,10},{1,5},{3,7},{13,9},{15,11},{16,20},{18,... | collective-permute-start | bytes 983048 | tf_op jit(solution)/shard_map/ppermute | solution.py:114
  94.3 1.6 %collective-permute-done.22 = bf16[64,2560]{1,0:T(8,128)(2,1)S(1)} collective-permute-done((bf16[64,2560]{1,0:T(8,128)(2,1)S(1)}, bf16[64,2560]{1,0:T(8,128)(2,1)S(1)}, u32[]{:S(2)}, u32[]{:S(2)}) %collective-permute-start.22) | collective-permute-done | bytes 327712 | tf_op jit(solution)/shard_map/ppermute | solution.py:114
  96.7 5.9 %collective-permute-done.17 = bf16[64,2560]{1,0:T(8,128)(2,1)S(1)} collective-permute-done((bf16[64,2560]{1,0:T(8,128)(2,1)S(1)}, bf16[64,2560]{1,0:T(8,128)(2,1)S(1)}, u32[]{:S(2)}, u32[]{:S(2)}) %collective-permute-start.17) | collective-permute-done | bytes 327712 | tf_op jit(solution)/shard_map/ppermute | solution.py:114
  103.4 1.3 %collective-permute-start.24 = (bf16[64,2560]{1,0:T(8,128)(2,1)S(1)}, bf16[64,2560]{1,0:T(8,128)(2,1)S(1)}, u32[]{:S(2)}, u32[]{:S(2)}) collective-permute-start(bf16[64,2560]{1,0:T(8,128)(2,1)S(1)} %add_convert_fusion), channel_id=1, source_target_pairs={{4,0},{6,2},{8,12},{10,14},{5,1},{7,3},{9,13},{11,15},{20,16},{22,... | collective-permute-start | bytes 983048 | tf_op jit(solution)/shard_map/ppermute | solution.py:114
  104.7 1.3 %collective-permute-start.19 = (bf16[64,2560]{1,0:T(8,128)(2,1)S(1)}, bf16[64,2560]{1,0:T(8,128)(2,1)S(1)}, u32[]{:S(2)}, u32[]{:S(2)}) collective-permute-start(bf16[64,2560]{1,0:T(8,128)(2,1)S(1)} %add_convert_fusion.3), channel_id=1, source_target_pairs={{4,0},{6,2},{8,12},{10,14},{5,1},{7,3},{9,13},{11,15},{20,16},{22,... | collective-permute-start | bytes 983048 | tf_op jit(solution)/shard_map/ppermute | solution.py:114
  107.3 11.6 %collective-permute-done.24 = bf16[64,2560]{1,0:T(8,128)(2,1)S(1)} collective-permute-done((bf16[64,2560]{1,0:T(8,128)(2,1)S(1)}, bf16[64,2560]{1,0:T(8,128)(2,1)S(1)}, u32[]{:S(2)}, u32[]{:S(2)}) %collective-permute-start.24) | collective-permute-done | bytes 327712 | tf_op jit(solution)/shard_map/ppermute | solution.py:114
  119.9 5.9 %collective-permute-done.19 = bf16[64,2560]{1,0:T(8,128)(2,1)S(1)} collective-permute-done((bf16[64,2560]{1,0:T(8,128)(2,1)S(1)}, bf16[64,2560]{1,0:T(8,128)(2,1)S(1)}, u32[]{:S(2)}, u32[]{:S(2)}) %collective-permute-start.19) | collective-permute-done | bytes 327712 | tf_op jit(solution)/shard_map/ppermute | solution.py:114
  (72 shorter events, 17.1 us)
Async XLA Ops:
  0.7 19.2 %collective-permute-start = (bf16[64,2560]{1,0:T(8,128)(2,1)}, bf16[64,2560]{1,0:T(8,128)(2,1)S(1)}, u32[]{:S(2)}, u32[]{:S(2)}) collective-permute-start(bf16[64,2560]{1,0:T(8,128)(2,1)} %bitcast.38), channel_id=1, source_target_pairs={{0,8},{2,10},{4,12},{6,14},{8,0},{10,2},{12,4},{14,6},{16,28},{18,... | collective-permute-start | bytes 983048 | tf_op jit(solution)/shard_map/ppermute | solution.py:161
  4.8 15.2 %collective-permute-start.1 = (bf16[64,2560]{1,0:T(8,128)(2,1)}, bf16[64,2560]{1,0:T(8,128)(2,1)S(1)}, u32[]{:S(2)}, u32[]{:S(2)}) collective-permute-start(bf16[64,2560]{1,0:T(8,128)(2,1)} %bitcast.39), channel_id=1, source_target_pairs={{0,4},{2,6},{4,0},{6,2},{8,12},{10,14},{12,8},{14,10},{1,5},{3,7},... | collective-permute-start | bytes 983048 | tf_op jit(solution)/shard_map/ppermute | solution.py:114
  6.3 18.8 %collective-permute-start.2 = (bf16[128,2560]{1,0:T(8,128)(2,1)}, bf16[128,2560]{1,0:T(8,128)(2,1)S(1)}, u32[]{:S(2)}, u32[]{:S(2)}) collective-permute-start(bf16[128,2560]{1,0:T(8,128)(2,1)} %param.6), channel_id=1, source_target_pairs={{0,2},{2,0},{4,6},{6,4},{8,10},{10,8},{12,14},{14,12},{1,3},{3,1},... | collective-permute-start | bytes 1966088 | tf_op jit(solution)/shard_map/ppermute | solution.py:114
  19.8 16.9 %collective-permute-start.9 = (bf16[64,2560]{1,0:T(8,128)(2,1)S(1)}, bf16[64,2560]{1,0:T(8,128)(2,1)S(1)}, u32[]{:S(2)}, u32[]{:S(2)}) collective-permute-start(bf16[64,2560]{1,0:T(8,128)(2,1)S(1)} %bitcast.33), channel_id=1, source_target_pairs={{0,8},{2,10},{4,12},{6,14},{8,0},{10,2},{12,4},{14,6},{16,28},{18,... | collective-permute-start | bytes 983048 | tf_op jit(solution)/shard_map/ppermute | solution.py:165
  20.0 27.8 %collective-permute-start.8 = (bf16[64,2560]{1,0:T(8,128)(2,1)S(1)}, bf16[64,2560]{1,0:T(8,128)(2,1)S(1)}, u32[]{:S(2)}, u32[]{:S(2)}) collective-permute-start(bf16[64,2560]{1,0:T(8,128)(2,1)S(1)} %bitcast.34), channel_id=1, source_target_pairs={{0,4},{2,6},{4,0},{6,2},{8,12},{10,14},{12,8},{14,10},{1,5},{3,7},... | collective-permute-start | bytes 983048 | tf_op jit(solution)/shard_map/ppermute | solution.py:114
  23.8 9.1 %collective-permute-start.6 = (bf16[64,2560]{1,0:T(8,128)(2,1)S(1)}, bf16[64,2560]{1,0:T(8,128)(2,1)S(1)}, u32[]{:S(2)}, u32[]{:S(2)}) collective-permute-start(bf16[64,2560]{1,0:T(8,128)(2,1)S(1)} %collective-permute-done), channel_id=1, source_target_pairs={{0,16},{16,0},{1,17},{17,1},{2,18},{18,2},{3,19},{19,3},{4,20},{20... | collective-permute-start | bytes 983048 | tf_op jit(solution)/shard_map/ppermute | solution.py:164
  25.1 11.6 %collective-permute-start.4 = (f32[1,256]{1,0:T(1,128)S(1)}, f32[1,256]{1,0:T(1,128)S(1)}, u32[]{:S(2)}, u32[]{:S(2)}) collective-permute-start(f32[1,256]{1,0:T(1,128)S(1)} %copy-done.2), channel_id=1, source_target_pairs={{0,8},{2,10},{4,12},{6,14},{8,0},{10,2},{12,4},{14,6},{1,9},{3,11}... | collective-permute-start | bytes 3080 | tf_op jit(solution)/shard_map/ppermute | solution.py:114
  25.1 13.1 %collective-permute-start.5 = (f32[1,256]{1,0:T(1,128)S(1)}, f32[1,256]{1,0:T(1,128)S(1)}, u32[]{:S(2)}, u32[]{:S(2)}) collective-permute-start(f32[1,256]{1,0:T(1,128)S(1)} %copy-done.2), channel_id=1, source_target_pairs={{0,12},{2,14},{4,8},{6,10},{8,4},{10,6},{12,0},{14,2},{1,13},{3,15... | collective-permute-start | bytes 3080 | tf_op jit(solution)/shard_map/ppermute | solution.py:114
  32.9 5.4 %collective-permute-start.3 = (f32[1,256]{1,0:T(1,128)S(1)}, f32[1,256]{1,0:T(1,128)S(1)}, u32[]{:S(2)}, u32[]{:S(2)}) collective-permute-start(f32[1,256]{1,0:T(1,128)S(1)} %copy-done.2), channel_id=1, source_target_pairs={{0,4},{2,6},{4,0},{6,2},{8,12},{10,14},{12,8},{14,10},{1,5},{3,7},... | collective-permute-start | bytes 3080 | tf_op jit(solution)/shard_map/ppermute | solution.py:114
  36.7 17.5 %collective-permute-start.12 = (bf16[128,2560]{1,0:T(8,128)(2,1)S(1)}, bf16[128,2560]{1,0:T(8,128)(2,1)S(1)}, u32[]{:S(2)}, u32[]{:S(2)}) collective-permute-start(bf16[128,2560]{1,0:T(8,128)(2,1)S(1)} %copy-done.1), channel_id=1, source_target_pairs={{0,2},{2,0},{4,6},{6,4},{8,10},{10,8},{12,14},{14,12},{1,3},{3,1},... | collective-permute-start | bytes 1966088 | tf_op jit(solution)/shard_map/ppermute | solution.py:114
  38.3 9.5 %collective-permute-start.10 = (bf16[64,2560]{1,0:T(8,128)(2,1)S(1)}, bf16[64,2560]{1,0:T(8,128)(2,1)S(1)}, u32[]{:S(2)}, u32[]{:S(2)}) collective-permute-start(bf16[64,2560]{1,0:T(8,128)(2,1)S(1)} %collective-permute-done.9), channel_id=1, source_target_pairs={{0,16},{16,0},{1,17},{17,1},{2,18},{18,2},{3,19},{19,3},{4,20},{20... | collective-permute-start | bytes 983048 | tf_op jit(solution)/shard_map/ppermute | solution.py:168
  48.2 31.5 %collective-permute-start.11 = (bf16[128,2560]{1,0:T(8,128)(2,1)S(1)}, bf16[128,2560]{1,0:T(8,128)(2,1)S(1)}, u32[]{:S(2)}, u32[]{:S(2)}) collective-permute-start(bf16[128,2560]{1,0:T(8,128)(2,1)S(1)} %convolution_convert_fusion.1), channel_id=1, source_target_pairs={{0,2},{2,0},{4,6},{6,4},{8,10},{10,8},{12,14},{14,12},{1,3},{3,1},... | collective-permute-start | bytes 1966088 | tf_op jit(solution)/shard_map/ppermute | solution.py:114
  55.6 4.3 %collective-permute-start.13 = (f32[256,256]{0,1:T(8,128)S(1)}, f32[256,256]{0,1:T(8,128)S(1)}, u32[]{:S(2)}, u32[]{:S(2)}) collective-permute-start(f32[256,256]{0,1:T(8,128)S(1)} %fusion.45), channel_id=1, source_target_pairs={{0,1},{1,0},{2,3},{3,2},{4,5},{5,4},{6,7},{7,6},{8,9},{9,8},{10,11... | collective-permute-start | bytes 786440 | tf_op jit(solution)/shard_map/ppermute | solution.py:149
  55.7 19.1 %collective-permute-start.20 = (bf16[128,2560]{1,0:T(8,128)(2,1)S(1)}, bf16[128,2560]{1,0:T(8,128)(2,1)S(1)}, u32[]{:S(2)}, u32[]{:S(2)}) collective-permute-start(bf16[128,2560]{1,0:T(8,128)(2,1)S(1)} %pad_maximum_fusion.3), channel_id=1, source_target_pairs={{0,4},{2,6},{12,8},{14,10},{1,5},{3,7},{13,9},{15,11},{16,20},{18,... | collective-permute-start | bytes 1966088 | tf_op jit(solution)/shard_map/ppermute | solution.py:114
  60.7 28.2 %collective-permute-start.15 = (bf16[128,2560]{1,0:T(8,128)(2,1)S(1)}, bf16[128,2560]{1,0:T(8,128)(2,1)S(1)}, u32[]{:S(2)}, u32[]{:S(2)}) collective-permute-start(bf16[128,2560]{1,0:T(8,128)(2,1)S(1)} %pad_maximum_fusion.2), channel_id=1, source_target_pairs={{0,4},{2,6},{12,8},{14,10},{1,5},{3,7},{13,9},{15,11},{16,20},{18,... | collective-permute-start | bytes 1966088 | tf_op jit(solution)/shard_map/ppermute | solution.py:114
  62.5 43.5 %collective-permute-start.14 = (bf16[128,2560]{1,0:T(8,128)(2,1)S(1)}, bf16[128,2560]{1,0:T(8,128)(2,1)S(1)}, u32[]{:S(2)}, u32[]{:S(2)}) collective-permute-start(bf16[128,2560]{1,0:T(8,128)(2,1)S(1)} %convolution_convert_fusion), channel_id=1, source_target_pairs={{0,2},{2,0},{4,6},{6,4},{8,10},{10,8},{12,14},{14,12},{1,3},{3,1},... | collective-permute-start | bytes 1966088 | tf_op jit(solution)/shard_map/ppermute | solution.py:114
  75.2 20.7 %collective-permute-start.22 = (bf16[64,2560]{1,0:T(8,128)(2,1)S(1)}, bf16[64,2560]{1,0:T(8,128)(2,1)S(1)}, u32[]{:S(2)}, u32[]{:S(2)}) collective-permute-start(bf16[64,2560]{1,0:T(8,128)(2,1)S(1)} %get-tuple-element.15), channel_id=1, source_target_pairs={{0,4},{2,6},{12,8},{14,10},{1,5},{3,7},{13,9},{15,11},{16,20},{18,... | collective-permute-start | bytes 983048 | tf_op jit(solution)/shard_map/ppermute | solution.py:114
  80.8 26.4 %collective-permute-start.21 = (bf16[64,2560]{1,0:T(8,128)(2,1)S(1)}, bf16[64,2560]{1,0:T(8,128)(2,1)S(1)}, u32[]{:S(2)}, u32[]{:S(2)}) collective-permute-start(bf16[64,2560]{1,0:T(8,128)(2,1)S(1)} %get-tuple-element.14), channel_id=1, source_target_pairs={{4,8},{6,10},{8,4},{10,6},{5,9},{7,11},{9,5},{11,7},{20,24},{22,26... | collective-permute-start | bytes 983048 | tf_op jit(solution)/shard_map/ppermute | solution.py:114
  89.2 13.3 %collective-permute-start.17 = (bf16[64,2560]{1,0:T(8,128)(2,1)S(1)}, bf16[64,2560]{1,0:T(8,128)(2,1)S(1)}, u32[]{:S(2)}, u32[]{:S(2)}) collective-permute-start(bf16[64,2560]{1,0:T(8,128)(2,1)S(1)} %get-tuple-element.17), channel_id=1, source_target_pairs={{0,4},{2,6},{12,8},{14,10},{1,5},{3,7},{13,9},{15,11},{16,20},{18,... | collective-permute-start | bytes 983048 | tf_op jit(solution)/shard_map/ppermute | solution.py:114
  93.7 26.3 %collective-permute-start.16 = (bf16[64,2560]{1,0:T(8,128)(2,1)S(1)}, bf16[64,2560]{1,0:T(8,128)(2,1)S(1)}, u32[]{:S(2)}, u32[]{:S(2)}) collective-permute-start(bf16[64,2560]{1,0:T(8,128)(2,1)S(1)} %get-tuple-element.16), channel_id=1, source_target_pairs={{4,8},{6,10},{8,4},{10,6},{5,9},{7,11},{9,5},{11,7},{20,24},{22,26... | collective-permute-start | bytes 983048 | tf_op jit(solution)/shard_map/ppermute | solution.py:114
  96.0 7.3 %collective-permute-start.23 = (bf16[64,2560]{1,0:T(8,128)(2,1)S(1)}, bf16[64,2560]{1,0:T(8,128)(2,1)S(1)}, u32[]{:S(2)}, u32[]{:S(2)}) collective-permute-start(bf16[64,2560]{1,0:T(8,128)(2,1)S(1)} %add_convert_fusion.1), channel_id=1, source_target_pairs={{4,8},{6,10},{8,4},{10,6},{5,9},{7,11},{9,5},{11,7},{20,24},{22,26... | collective-permute-start | bytes 983048 | tf_op jit(solution)/shard_map/ppermute | solution.py:114
  102.6 2.1 %collective-permute-start.18 = (bf16[64,2560]{1,0:T(8,128)(2,1)S(1)}, bf16[64,2560]{1,0:T(8,128)(2,1)S(1)}, u32[]{:S(2)}, u32[]{:S(2)}) collective-permute-start(bf16[64,2560]{1,0:T(8,128)(2,1)S(1)} %add_convert_fusion.4), channel_id=1, source_target_pairs={{4,8},{6,10},{8,4},{10,6},{5,9},{7,11},{9,5},{11,7},{20,24},{22,26... | collective-permute-start | bytes 983048 | tf_op jit(solution)/shard_map/ppermute | solution.py:114
  103.4 15.4 %collective-permute-start.24 = (bf16[64,2560]{1,0:T(8,128)(2,1)S(1)}, bf16[64,2560]{1,0:T(8,128)(2,1)S(1)}, u32[]{:S(2)}, u32[]{:S(2)}) collective-permute-start(bf16[64,2560]{1,0:T(8,128)(2,1)S(1)} %add_convert_fusion), channel_id=1, source_target_pairs={{4,0},{6,2},{8,12},{10,14},{5,1},{7,3},{9,13},{11,15},{20,16},{22,... | collective-permute-start | bytes 983048 | tf_op jit(solution)/shard_map/ppermute | solution.py:114
  104.7 21.1 %collective-permute-start.19 = (bf16[64,2560]{1,0:T(8,128)(2,1)S(1)}, bf16[64,2560]{1,0:T(8,128)(2,1)S(1)}, u32[]{:S(2)}, u32[]{:S(2)}) collective-permute-start(bf16[64,2560]{1,0:T(8,128)(2,1)S(1)} %add_convert_fusion.3), channel_id=1, source_target_pairs={{4,0},{6,2},{8,12},{10,14},{5,1},{7,3},{9,13},{11,15},{20,16},{22,... | collective-permute-start | bytes 983048 | tf_op jit(solution)/shard_map/ppermute | solution.py:114
  (6 other events, 69.3 us)

commit v4 on v3

--- a/solution.py
+++ b/solution.py
@@ -129,20 +129,9 @@
     return total
 
 
-def collect_start(weights, rows):
+def partial_sums(weights, rows):
     parts = [contract_first(weight, rows) for weight in weights]
-    for_end = move(narrow(parts[3]), ENDS_IN)
-    rest = move(narrow(jnp.concatenate([parts[2], parts[1]])), ENDS_IN)
-    return parts, for_end, rest
-
-
-def collect_end(started):
-    (own, first, second, third), for_end, rest = started
-    for_middle, for_near = jnp.split(rest, 2)
-    for_end = move(narrow(add_up(second, for_end)), MIDDLE)
-    for_middle = move(narrow(add_up(third, for_middle)), MIDDLE)
-    for_end = move(narrow(add_up(first, for_end)), ENDS_OUT)
-    return add_up(own, for_near, for_middle, for_end)
+    return lax.optimization_barrier((parts, [narrow(part) for part in parts[1:]]))
 
 
 def both_cores(partial):
@@ -161,13 +150,14 @@
     far_down = lax.ppermute(down_matrix, ("groups", "adapter"), FAR)
     tokens2 = move(tokens, PARTNER)
     near_down = move(down_matrix, xor_line(1))
+    cot2 = move(cotangent, PARTNER)
     cross_down = lax.ppermute(far_down, "groups", SWAP)
     far_up = lax.ppermute(after(up_matrix, far_down), ("groups", "adapter"), FAR)
-    cot2 = move(after(cotangent, (tokens2, far_down)), PARTNER)
     near_up = move(after(up_matrix, near_down), xor_line(1))
     cross_up = lax.ppermute(far_up, "groups", SWAP)
-    later = after(gating, (far_down, near_down, tokens2))
+    later = after(gating, (far_down, near_up))
     gates = [gating, move(later, xor_line(1)), move(later, xor_line(2)), move(later, xor_line(3))]
+    tokens2, cot2, near_up = lax.optimization_barrier((tokens2, cot2, near_up))
 
     far_bit = jnp.where(first_group, 2, 3)
     experts = jnp.stack([me, me ^ 2, me ^ (2 * far_bit), me ^ (2 * (far_bit ^ 1))])
@@ -185,8 +175,9 @@
     cot2 = jnp.concatenate([cotangent, cot2], axis=0)
     down_all = jnp.concatenate([down_matrix, near_down, far_down, cross_down], axis=0)
 
-    def low_rank(rows, matrices):
-        return (scale * both_cores(contract_last(rows, matrices))).astype(jnp.bfloat16)
+    def low_rank(rows, matrices, *earlier):
+        product = both_cores(contract_last(rows, matrices))
+        return narrow(scale * after(product, earlier))
 
     def for_line(low):
         own, near, far, cross = (low[:, k * rank : (k + 1) * rank] for k in range(4))
@@ -202,18 +193,32 @@
         mine = jnp.dot(weights[:tok_local], matrix, preferred_element_type=jnp.float32)
         return narrow(mine + back.astype(jnp.float32))
 
-    low = low_rank(tokens2, down_all)
-    up_parts = collect_start(for_line(low), cot2)
-    cross_up = after(cross_up, low)
+    low = low_rank(tokens2, down_all, far_up)
+    (own, first, second, third), up_send = partial_sums(for_line(low), cot2)
+    up_1a = move(up_send[2], ENDS_IN)
+    up_1b = move(up_send[1], ENDS_IN)
+    up_1c = move(up_send[0], ENDS_IN)
+
+    cross_up = after(cross_up, (up_1a, up_1b))
     up_all = jnp.concatenate([up_matrix, near_up, far_up, cross_up], axis=0)
     low_back = low_rank(cot2, up_all)
     branch_back = outward_start(low, up_all)
-    down_parts = collect_start(for_line(low_back), tokens2)
+    up_2a = move(narrow(add_up(second, up_1a)), MIDDLE)
+    up_2b = move(narrow(add_up(third, up_1b)), MIDDLE)
+    low_back = after(low_back, (up_1c, up_2a))
+    (own_b, first_b, second_b, third_b), down_send = partial_sums(for_line(low_back), tokens2)
+    down_1a = move(down_send[2], ENDS_IN)
+    down_1b = move(down_send[1], ENDS_IN)
+    down_1c = move(down_send[0], ENDS_IN)
+    up_3 = move(narrow(add_up(first, up_2a)), ENDS_OUT)
     input_back = outward_start(low_back, down_all)
-    up_grad = collect_end(up_parts)
+    down_2a = move(narrow(add_up(second_b, down_1a)), MIDDLE)
+    down_2b = move(narrow(add_up(third_b, down_1b)), MIDDLE)
+    up_grad = add_up(own, up_1c, up_2b, up_3)
     branch_out = outward_end(low, up_all, branch_back)
+    down_3 = move(narrow(add_up(first_b, down_2a)), ENDS_OUT)
     input_grad = outward_end(low_back, down_all, input_back)
-    down_grad = collect_end(down_parts)
+    down_grad = add_up(own_b, down_1c, down_2b, down_3)
     down_grad = (down_grad / capacity).astype(jnp.bfloat16)[None]
     up_grad = (up_grad / capacity).astype(jnp.bfloat16)[None]
     return (branch_out, input_grad, down_grad, up_grad)

time: 127 us -> 126 us (level)
  waiting for transfers between devices: 75.9 us -> 52 us
  starting transfers between devices: 38.6 us -> 49.9 us
  matrix products: 8.52 us -> 13.8 us
  local copies, waits for them, and re-layouts: 1.9 us -> 4.94 us
  other arithmetic: 0.97 us -> 3.84 us
    ppermute x19 -> x21, starting transfers between devices: 33.1 us -> 42.2 us  [move(): return lax.ppermute(value, 'adapter', pairs)]
    ppermute x1, waiting for transfers between devices: 9.87 us -> 1.87 us  [by_pairs(): far_down = lax.ppermute(down_matrix, ('groups', 'adapter'), FAR)]
    ppermute x1, waiting for transfers between devices: 9.15 us -> 1.37 us  [by_pairs(): cross_up = lax.ppermute(far_up, 'groups', SWAP)]
    ppermute x1, waiting for transfers between devices: 5.07 us -> 0.01 us  [by_pairs(): cross_down = lax.ppermute(far_down, 'groups', SWAP)]
    ppermute x1, waiting for transfers between devices: 2.99 us -> 0.01 us  [by_pairs(): lax.ppermute(after(up_matrix, far_down), ('groups', 'adapter'), FAR)]
    dot_general x2, matrix products: 1.07 us -> 3.23 us  [contract_last(): lax.dot_general(left_op, right_op, (((1,), (1,)), ((), ())), preferred_el...]
    dot_general x2, matrix products: 2.41 us -> 4.43 us  [outward_end(): jnp.dot(weights[:tok_local], matrix, preferred_element_type=jnp.float32)]
    dot_general x2, matrix products: 0.71 us -> 2.73 us  [outward_start(): jnp.dot(weights[tok_local:], matrix, preferred_element_type=jnp.float32)]
  transfers between devices with their start and end apart: 25 -> 27, of which waited for: 13 -> 11; matrix products, arithmetic and copies ran while one was open for 8% -> 15% of each run, Pallas kernels for 0% -> 0%
where the time goes in v4:
time: 126 us
  waiting for transfers between devices  52 us (41%)
  starting transfers between devices  49.9 us (40%)
  matrix products  13.8 us (11%)
  local copies, waits for them, and re-layouts  4.94 us (4%)
  other arithmetic  3.84 us (3%)
    ppermute x21, waiting for transfers between devices, move(): return lax.ppermute(value, 'adapter', pairs)  48.7 us
    ppermute x21, starting transfers between devices, move(): return lax.ppermute(value, 'adapter', pairs)  42.2 us
    dot_general x2, matrix products, outward_end(): jnp.dot(weights[:tok_local], matrix, preferred_element_type=jnp.float32)  4.43 us
    dot_general x8, matrix products, contract_first(): lax.dot_general(left_op, right_op, (((0,), (0,)), ((), ())), preferred_el...  3.44 us
    dot_general x2, matrix products, contract_last(): lax.dot_general(left_op, right_op, (((1,), (1,)), ((), ())), preferred_el...  3.23 us
    dot_general x2, matrix products, outward_start(): jnp.dot(weights[tok_local:], matrix, preferred_element_type=jnp.float32)  2.73 us
    ppermute x1, starting transfers between devices, by_pairs(): far_down = lax.ppermute(down_matrix, ('groups', 'adapter'), FAR)  2.59 us
  transfers between devices with their start and end apart: 27, of which 11 were waited for; matrix products, arithmetic and copies ran while one was open for 15% of the time, Pallas kernels for 0%

profile of v4, /device:TPU:0, one launch (start us, length us, event | category | flops | bytes accessed | tf_op | source)
XLA Modules:
  0.0 125.5 jit_solution(6982903749355387549)
XLA Ops:
  0.7 3.1 %collective-permute-start.1 = (bf16[64,2560]{1,0:T(8,128)(2,1)}, bf16[64,2560]{1,0:T(8,128)(2,1)S(1)}, u32[]{:S(2)}, u32[]{:S(2)}) collective-permute-start(bf16[64,2560]{1,0:T(8,128)(2,1)} %bitcast.28), channel_id=1, source_target_pairs={{0,4},{2,6},{4,0},{6,2},{8,12},{10,14},{12,8},{14,10},{1,5},{3,7},... | collective-permute-start | bytes 983048 | tf_op jit(solution)/shard_map/ppermute | solution.py:114
  3.7 2.6 %collective-permute-start = (bf16[64,2560]{1,0:T(8,128)(2,1)}, bf16[64,2560]{1,0:T(8,128)(2,1)}, u32[]{:S(2)}, u32[]{:S(2)}) collective-permute-start(bf16[64,2560]{1,0:T(8,128)(2,1)} %bitcast.29), channel_id=1, source_target_pairs={{0,8},{2,10},{4,12},{6,14},{8,0},{10,2},{12,4},{14,6},{16,28},{18,... | collective-permute-start | bytes 983048 | tf_op jit(solution)/shard_map/ppermute | solution.py:150
  6.3 1.5 %collective-permute-start.6 = (bf16[128,2560]{1,0:T(8,128)(2,1)}, bf16[128,2560]{1,0:T(8,128)(2,1)}, u32[]{:S(2)}, u32[]{:S(2)}) collective-permute-start(bf16[128,2560]{1,0:T(8,128)(2,1)} %param.6), channel_id=1, source_target_pairs={{0,2},{2,0},{4,6},{6,4},{8,10},{10,8},{12,14},{14,12},{1,3},{3,1},... | collective-permute-start | bytes 1966088 | tf_op jit(solution)/shard_map/ppermute | solution.py:114
  10.4 8.2 %collective-permute-done.1 = bf16[64,2560]{1,0:T(8,128)(2,1)S(1)} collective-permute-done((bf16[64,2560]{1,0:T(8,128)(2,1)}, bf16[64,2560]{1,0:T(8,128)(2,1)S(1)}, u32[]{:S(2)}, u32[]{:S(2)}) %collective-permute-start.1) | collective-permute-done | bytes 327712 | tf_op jit(solution)/shard_map/ppermute | solution.py:114
  19.3 1.9 %collective-permute-done = bf16[64,2560]{1,0:T(8,128)(2,1)} collective-permute-done((bf16[64,2560]{1,0:T(8,128)(2,1)}, bf16[64,2560]{1,0:T(8,128)(2,1)}, u32[]{:S(2)}, u32[]{:S(2)}) %collective-permute-start) | collective-permute-done | bytes 327712 | tf_op jit(solution)/shard_map/ppermute | solution.py:150
  21.2 1.4 %collective-permute-start.10 = (bf16[64,2560]{1,0:T(8,128)(2,1)}, bf16[64,2560]{1,0:T(8,128)(2,1)}, u32[]{:S(2)}, u32[]{:S(2)}) collective-permute-start(bf16[64,2560]{1,0:T(8,128)(2,1)} %bitcast.10), channel_id=1, source_target_pairs={{0,8},{2,10},{4,12},{6,14},{8,0},{10,2},{12,4},{14,6},{16,28},{18,... | collective-permute-start | bytes 983048 | tf_op jit(solution)/shard_map/ppermute | solution.py:155
  22.6 2.4 %collective-permute-start.8 = (bf16[64,2560]{1,0:T(8,128)(2,1)}, bf16[64,2560]{1,0:T(8,128)(2,1)S(1)}, u32[]{:S(2)}, u32[]{:S(2)}) collective-permute-start(bf16[64,2560]{1,0:T(8,128)(2,1)} %collective-permute-done), channel_id=1, source_target_pairs={{0,16},{16,0},{1,17},{17,1},{2,18},{18,2},{3,19},{19,3},{4,20},{20... | collective-permute-start | bytes 983048 | tf_op jit(solution)/shard_map/ppermute | solution.py:154
  25.0 10.1 %collective-permute-done.2 = bf16[64,2560]{1,0:T(8,128)(2,1)S(1)} collective-permute-done((bf16[64,2560]{1,0:T(8,128)(2,1)}, bf16[64,2560]{1,0:T(8,128)(2,1)S(1)}, u32[]{:S(2)}, u32[]{:S(2)}) %collective-permute-start.2) | collective-permute-done | bytes 327712 | tf_op jit(solution)/shard_map/ppermute | solution.py:114
  35.2 2.0 %collective-permute-start.5 = (f32[1,256]{1,0:T(1,128)S(1)}, f32[1,256]{1,0:T(1,128)S(1)}, u32[]{:S(2)}, u32[]{:S(2)}) collective-permute-start(f32[1,256]{1,0:T(1,128)S(1)} %copy-done.2), channel_id=1, source_target_pairs={{0,12},{2,14},{4,8},{6,10},{8,4},{10,6},{12,0},{14,2},{1,13},{3,15... | collective-permute-start | bytes 3080 | tf_op jit(solution)/shard_map/ppermute | solution.py:114
  37.2 1.5 %collective-permute-start.3 = (f32[1,256]{1,0:T(1,128)S(1)}, f32[1,256]{1,0:T(1,128)S(1)}, u32[]{:S(2)}, u32[]{:S(2)}) collective-permute-start(f32[1,256]{1,0:T(1,128)S(1)} %copy-done.2), channel_id=1, source_target_pairs={{0,4},{2,6},{4,0},{6,2},{8,12},{10,14},{12,8},{14,10},{1,5},{3,7},... | collective-permute-start | bytes 3080 | tf_op jit(solution)/shard_map/ppermute | solution.py:114
  39.8 1.6 %fusion.38 = f32[256,256]{1,0:T(8,128)S(1)} fusion(bf16[256,2560]{1,0:T(8,128)(2,1)S(1)} %constant_dynamic-update-slice_fusion, bf16[64,2560]{1,0:T(8,128)(2,1)S(1)} %collective-permute-done.8, bf16[64,2560]{1,0:T(8,128)(2,1)} %collective-permute-done, bf16[64,2560]{1,0:T(8,128)(2,1)S(1)} %copy-done.6, bf16[64,2560]{1,0:T(8,128)(2,1)S(1)} %bitcast.30), kind=kOutput, calls=%fused_computation.71 | convolution fusion | flops 340787200 | bytes 2883584 | tf_op jit(solution)/shard_map/dot_general | solution.py:10
  46.0 2.5 %collective-permute-start.13 = (bf16[64,2560]{1,0:T(8,128)(2,1)S(1)}, bf16[64,2560]{1,0:T(8,128)(2,1)S(1)}, u32[]{:S(2)}, u32[]{:S(2)}) collective-permute-start(bf16[64,2560]{1,0:T(8,128)(2,1)S(1)} %get-tuple-element.35), channel_id=1, source_target_pairs={{0,4},{2,6},{12,8},{14,10},{1,5},{3,7},{13,9},{15,11},{16,20},{18,... | collective-permute-start | bytes 983048 | tf_op jit(solution)/shard_map/ppermute | solution.py:114
  52.2 4.3 %collective-permute-done.13 = bf16[64,2560]{1,0:T(8,128)(2,1)S(1)} collective-permute-done((bf16[64,2560]{1,0:T(8,128)(2,1)S(1)}, bf16[64,2560]{1,0:T(8,128)(2,1)S(1)}, u32[]{:S(2)}, u32[]{:S(2)}) %collective-permute-start.13) | collective-permute-done | bytes 327712 | tf_op jit(solution)/shard_map/ppermute | solution.py:114
  58.6 4.9 %collective-permute-done.12 = bf16[64,2560]{1,0:T(8,128)(2,1)S(1)} collective-permute-done((bf16[64,2560]{1,0:T(8,128)(2,1)S(1)}, bf16[64,2560]{1,0:T(8,128)(2,1)S(1)}, u32[]{:S(2)}, u32[]{:S(2)}) %collective-permute-start.12) | collective-permute-done | bytes 327712 | tf_op jit(solution)/shard_map/ppermute | solution.py:114
  63.5 1.6 %fusion.37 = f32[256,256]{1,0:T(8,128)S(1)} fusion(bf16[256,2560]{1,0:T(8,128)(2,1)S(1)} %constant_dynamic-update-slice_fusion.2, bf16[64,2560]{1,0:T(8,128)(2,1)S(1)} %collective-permute-done.11, bf16[64,2560]{1,0:T(8,128)(2,1)} %collective-permute-done.10, bf16[64,2560]{1,0:T(8,128)(2,1)S(1)} %copy-done.9, bf16[64,2560]{1,0:T(8,128)(2,1)} %bitcast.10), kind=kOutput, calls=%fused_computation.70 | convolution fusion | flops 340787200 | bytes 2883584 | tf_op jit(solution)/shard_map/dot_general | solution.py:10
  66.0 1.4 %convolution_convert_fusion.1 = bf16[128,2560]{1,0:T(8,128)(2,1)S(1)} fusion(bf16[256,256]{1,0:T(8,128)(2,1)S(1)} %multiply_convert_fusion.3, bf16[64,2560]{1,0:T(8,128)(2,1)S(1)} %collective-permute-done.11, bf16[64,2560]{1,0:T(8,128)(2,1)} %collective-permute-done.10, bf16[64,2560]{1,0:T(8,128)(2,1)S(1)} %copy-done.9, bf16[64,2560]{1,0:T(8,128)(2,1)} %bitcast.10), kind=kOutput, calls=%fused_computation.6 | convolution fusion | flops 173342720 | bytes 2031616 | tf_op jit(solution)/shard_map/dot_general | solution.py:189
  71.9 11.5 %collective-permute-start.20 = (bf16[64,2560]{1,0:T(8,128)(2,1)S(1)}, bf16[64,2560]{1,0:T(8,128)(2,1)S(1)}, u32[]{:S(2)}, u32[]{:S(2)}) collective-permute-start(bf16[64,2560]{1,0:T(8,128)(2,1)S(1)} %get-tuple-element.43), channel_id=1, source_target_pairs={{0,4},{2,6},{12,8},{14,10},{1,5},{3,7},{13,9},{15,11},{16,20},{18,... | collective-permute-start | bytes 983048 | tf_op jit(solution)/shard_map/ppermute | solution.py:114
  84.8 4.6 %collective-permute-start.22 = (bf16[64,2560]{1,0:T(8,128)(2,1)S(1)}, bf16[64,2560]{1,0:T(8,128)(2,1)S(1)}, u32[]{:S(2)}, u32[]{:S(2)}) collective-permute-start(bf16[64,2560]{1,0:T(8,128)(2,1)S(1)} %get-tuple-element.46), channel_id=1, source_target_pairs={{0,4},{2,6},{12,8},{14,10},{1,5},{3,7},{13,9},{15,11},{16,20},{18,... | collective-permute-start | bytes 983048 | tf_op jit(solution)/shard_map/ppermute | solution.py:114
  91.5 4.4 %collective-permute-start.19 = (bf16[64,2560]{1,0:T(8,128)(2,1)S(1)}, bf16[64,2560]{1,0:T(8,128)(2,1)S(1)}, u32[]{:S(2)}, u32[]{:S(2)}) collective-permute-start(bf16[64,2560]{1,0:T(8,128)(2,1)S(1)} %get-tuple-element.41), channel_id=1, source_target_pairs={{0,4},{2,6},{12,8},{14,10},{1,5},{3,7},{13,9},{15,11},{16,20},{18,... | collective-permute-start | bytes 983048 | tf_op jit(solution)/shard_map/ppermute | solution.py:114
  96.0 2.6 %collective-permute-done.22 = bf16[64,2560]{1,0:T(8,128)(2,1)S(1)} collective-permute-done((bf16[64,2560]{1,0:T(8,128)(2,1)S(1)}, bf16[64,2560]{1,0:T(8,128)(2,1)S(1)}, u32[]{:S(2)}, u32[]{:S(2)}) %collective-permute-start.22) | collective-permute-done | bytes 327712 | tf_op jit(solution)/shard_map/ppermute | solution.py:114
  103.6 2.3 %fusion = bf16[128,2560]{1,0:T(8,128)(2,1)} fusion(bf16[128,2560]{1,0:T(8,128)(2,1)S(1)} %collective-permute-done.14, bf16[256,256]{1,0:T(8,128)(2,1)S(1)} %multiply_convert_fusion.3, bf16[64,2560]{1,0:T(8,128)(2,1)S(1)} %collective-permute-done.11, bf16[64,2560]{1,0:T(8,128)(2,1)} %collective-permute-done.10, bf16[64,2560]{1,0:T(8,128)(2,1)S(1)} %copy-done.9, ...), kind=kOutput, calls=%fused_computation.3 | convolution fusion | flops 173998080 | bytes 2686976 | tf_op jit(solution)/shard_map/dot_general | solution.py:193
  105.9 6.8 %collective-permute-done.18 = bf16[128,2560]{1,0:T(8,128)(2,1)S(1)} collective-permute-done((bf16[128,2560]{1,0:T(8,128)(2,1)S(1)}, bf16[128,2560]{1,0:T(8,128)(2,1)S(1)}, u32[]{:S(2)}, u32[]{:S(2)}) %collective-permute-start.18) | collective-permute-done | bytes 655392 | tf_op jit(solution)/shard_map/ppermute | solution.py:114
  112.7 2.2 %fusion.1 = bf16[128,2560]{1,0:T(8,128)(2,1)} fusion(bf16[128,2560]{1,0:T(8,128)(2,1)S(1)} %collective-permute-done.18, bf16[256,256]{1,0:T(8,128)(2,1)S(1)} %multiply_convert_fusion.2, bf16[64,2560]{1,0:T(8,128)(2,1)S(1)} %copy-done.11, bf16[64,2560]{1,0:T(8,128)(2,1)} %collective-permute-done, bf16[64,2560]{1,0:T(8,128)(2,1)S(1)} %copy-done.7, ...), kind=kOutput, calls=%fused_computation.4 | convolution fusion | flops 173998080 | bytes 2686976 | tf_op jit(solution)/shard_map/dot_general | solution.py:193
  114.9 9.8 %collective-permute-done.24 = bf16[64,2560]{1,0:T(8,128)(2,1)S(1)} collective-permute-done((bf16[64,2560]{1,0:T(8,128)(2,1)S(1)}, bf16[64,2560]{1,0:T(8,128)(2,1)S(1)}, u32[]{:S(2)}, u32[]{:S(2)}) %collective-permute-start.24) | collective-permute-done | bytes 327712 | tf_op jit(solution)/shard_map/ppermute | solution.py:114
  (96 shorter events, 29.4 us)
Async XLA Ops:
  0.7 17.9 %collective-permute-start.1 = (bf16[64,2560]{1,0:T(8,128)(2,1)}, bf16[64,2560]{1,0:T(8,128)(2,1)S(1)}, u32[]{:S(2)}, u32[]{:S(2)}) collective-permute-start(bf16[64,2560]{1,0:T(8,128)(2,1)} %bitcast.28), channel_id=1, source_target_pairs={{0,4},{2,6},{4,0},{6,2},{8,12},{10,14},{12,8},{14,10},{1,5},{3,7},... | collective-permute-start | bytes 983048 | tf_op jit(solution)/shard_map/ppermute | solution.py:114
  3.7 17.5 %collective-permute-start = (bf16[64,2560]{1,0:T(8,128)(2,1)}, bf16[64,2560]{1,0:T(8,128)(2,1)}, u32[]{:S(2)}, u32[]{:S(2)}) collective-permute-start(bf16[64,2560]{1,0:T(8,128)(2,1)} %bitcast.29), channel_id=1, source_target_pairs={{0,8},{2,10},{4,12},{6,14},{8,0},{10,2},{12,4},{14,6},{16,28},{18,... | collective-permute-start | bytes 983048 | tf_op jit(solution)/shard_map/ppermute | solution.py:150
  6.3 28.8 %collective-permute-start.6 = (bf16[128,2560]{1,0:T(8,128)(2,1)}, bf16[128,2560]{1,0:T(8,128)(2,1)}, u32[]{:S(2)}, u32[]{:S(2)}) collective-permute-start(bf16[128,2560]{1,0:T(8,128)(2,1)} %param.6), channel_id=1, source_target_pairs={{0,2},{2,0},{4,6},{6,4},{8,10},{10,8},{12,14},{14,12},{1,3},{3,1},... | collective-permute-start | bytes 1966088 | tf_op jit(solution)/shard_map/ppermute | solution.py:114
  7.8 29.3 %collective-permute-start.7 = (bf16[128,2560]{1,0:T(8,128)(2,1)}, bf16[128,2560]{1,0:T(8,128)(2,1)}, u32[]{:S(2)}, u32[]{:S(2)}) collective-permute-start(bf16[128,2560]{1,0:T(8,128)(2,1)} %param.7), channel_id=1, source_target_pairs={{0,2},{2,0},{4,6},{6,4},{8,10},{10,8},{12,14},{14,12},{1,3},{3,1},... | collective-permute-start | bytes 1966088 | tf_op jit(solution)/shard_map/ppermute | solution.py:114
  19.3 15.9 %collective-permute-start.2 = (bf16[64,2560]{1,0:T(8,128)(2,1)}, bf16[64,2560]{1,0:T(8,128)(2,1)S(1)}, u32[]{:S(2)}, u32[]{:S(2)}) collective-permute-start(bf16[64,2560]{1,0:T(8,128)(2,1)} %bitcast.10), channel_id=1, source_target_pairs={{0,4},{2,6},{4,0},{6,2},{8,12},{10,14},{12,8},{14,10},{1,5},{3,7},... | collective-permute-start | bytes 983048 | tf_op jit(solution)/shard_map/ppermute | solution.py:114
  21.2 23.0 %collective-permute-start.10 = (bf16[64,2560]{1,0:T(8,128)(2,1)}, bf16[64,2560]{1,0:T(8,128)(2,1)}, u32[]{:S(2)}, u32[]{:S(2)}) collective-permute-start(bf16[64,2560]{1,0:T(8,128)(2,1)} %bitcast.10), channel_id=1, source_target_pairs={{0,8},{2,10},{4,12},{6,14},{8,0},{10,2},{12,4},{14,6},{16,28},{18,... | collective-permute-start | bytes 983048 | tf_op jit(solution)/shard_map/ppermute | solution.py:155
  22.6 17.2 %collective-permute-start.8 = (bf16[64,2560]{1,0:T(8,128)(2,1)}, bf16[64,2560]{1,0:T(8,128)(2,1)S(1)}, u32[]{:S(2)}, u32[]{:S(2)}) collective-permute-start(bf16[64,2560]{1,0:T(8,128)(2,1)} %collective-permute-done), channel_id=1, source_target_pairs={{0,16},{16,0},{1,17},{17,1},{2,18},{18,2},{3,19},{19,3},{4,20},{20... | collective-permute-start | bytes 983048 | tf_op jit(solution)/shard_map/ppermute | solution.py:154
  35.1 7.5 %collective-permute-start.4 = (f32[1,256]{1,0:T(1,128)S(1)}, f32[1,256]{1,0:T(1,128)S(1)}, u32[]{:S(2)}, u32[]{:S(2)}) collective-permute-start(f32[1,256]{1,0:T(1,128)S(1)} %copy-done.2), channel_id=1, source_target_pairs={{0,8},{2,10},{4,12},{6,14},{8,0},{10,2},{12,4},{14,6},{1,9},{3,11}... | collective-permute-start | bytes 3080 | tf_op jit(solution)/shard_map/ppermute | solution.py:114
  35.2 7.5 %collective-permute-start.5 = (f32[1,256]{1,0:T(1,128)S(1)}, f32[1,256]{1,0:T(1,128)S(1)}, u32[]{:S(2)}, u32[]{:S(2)}) collective-permute-start(f32[1,256]{1,0:T(1,128)S(1)} %copy-done.2), channel_id=1, source_target_pairs={{0,12},{2,14},{4,8},{6,10},{8,4},{10,6},{12,0},{14,2},{1,13},{3,15... | collective-permute-start | bytes 3080 | tf_op jit(solution)/shard_map/ppermute | solution.py:114
  37.2 5.6 %collective-permute-start.3 = (f32[1,256]{1,0:T(1,128)S(1)}, f32[1,256]{1,0:T(1,128)S(1)}, u32[]{:S(2)}, u32[]{:S(2)}) collective-permute-start(f32[1,256]{1,0:T(1,128)S(1)} %copy-done.2), channel_id=1, source_target_pairs={{0,4},{2,6},{4,0},{6,2},{8,12},{10,14},{12,8},{14,10},{1,5},{3,7},... | collective-permute-start | bytes 3080 | tf_op jit(solution)/shard_map/ppermute | solution.py:114
  46.0 10.5 %collective-permute-start.13 = (bf16[64,2560]{1,0:T(8,128)(2,1)S(1)}, bf16[64,2560]{1,0:T(8,128)(2,1)S(1)}, u32[]{:S(2)}, u32[]{:S(2)}) collective-permute-start(bf16[64,2560]{1,0:T(8,128)(2,1)S(1)} %get-tuple-element.35), channel_id=1, source_target_pairs={{0,4},{2,6},{12,8},{14,10},{1,5},{3,7},{13,9},{15,11},{16,20},{18,... | collective-permute-start | bytes 983048 | tf_op jit(solution)/shard_map/ppermute | solution.py:114
  48.5 10.1 %collective-permute-start.11 = (bf16[64,2560]{1,0:T(8,128)(2,1)}, bf16[64,2560]{1,0:T(8,128)(2,1)S(1)}, u32[]{:S(2)}, u32[]{:S(2)}) collective-permute-start(bf16[64,2560]{1,0:T(8,128)(2,1)} %collective-permute-done.10), channel_id=1, source_target_pairs={{0,16},{16,0},{1,17},{17,1},{2,18},{18,2},{3,19},{19,3},{4,20},{20... | collective-permute-start | bytes 983048 | tf_op jit(solution)/shard_map/ppermute | solution.py:157
  49.6 13.9 %collective-permute-start.12 = (bf16[64,2560]{1,0:T(8,128)(2,1)S(1)}, bf16[64,2560]{1,0:T(8,128)(2,1)S(1)}, u32[]{:S(2)}, u32[]{:S(2)}) collective-permute-start(bf16[64,2560]{1,0:T(8,128)(2,1)S(1)} %get-tuple-element.34), channel_id=1, source_target_pairs={{0,4},{2,6},{12,8},{14,10},{1,5},{3,7},{13,9},{15,11},{16,20},{18,... | collective-permute-start | bytes 983048 | tf_op jit(solution)/shard_map/ppermute | solution.py:114
  50.9 19.3 %collective-permute-start.16 = (bf16[64,2560]{1,0:T(8,128)(2,1)S(1)}, bf16[64,2560]{1,0:T(8,128)(2,1)S(1)}, u32[]{:S(2)}, u32[]{:S(2)}) collective-permute-start(bf16[64,2560]{1,0:T(8,128)(2,1)S(1)} %get-tuple-element.37), channel_id=1, source_target_pairs={{0,4},{2,6},{12,8},{14,10},{1,5},{3,7},{13,9},{15,11},{16,20},{18,... | collective-permute-start | bytes 983048 | tf_op jit(solution)/shard_map/ppermute | solution.py:114
  56.5 43.4 %collective-permute-start.25 = (bf16[64,2560]{1,0:T(8,128)(2,1)S(1)}, bf16[64,2560]{1,0:T(8,128)(2,1)S(1)}, u32[]{:S(2)}, u32[]{:S(2)}) collective-permute-start(bf16[64,2560]{1,0:T(8,128)(2,1)S(1)} %add_convert_fusion.1), channel_id=1, source_target_pairs={{4,8},{6,10},{8,4},{10,6},{5,9},{7,11},{9,5},{11,7},{20,24},{22,26... | collective-permute-start | bytes 983048 | tf_op jit(solution)/shard_map/ppermute | solution.py:114
  65.3 4.9 %collective-permute-start.17 = (bf16[64,2560]{1,0:T(8,128)(2,1)S(1)}, bf16[64,2560]{1,0:T(8,128)(2,1)S(1)}, u32[]{:S(2)}, u32[]{:S(2)}) collective-permute-start(bf16[64,2560]{1,0:T(8,128)(2,1)S(1)} %add_convert_fusion.5), channel_id=1, source_target_pairs={{4,8},{6,10},{8,4},{10,6},{5,9},{7,11},{9,5},{11,7},{20,24},{22,26... | collective-permute-start | bytes 983048 | tf_op jit(solution)/shard_map/ppermute | solution.py:114
  67.4 36.3 %collective-permute-start.14 = (bf16[128,2560]{1,0:T(8,128)(2,1)S(1)}, bf16[128,2560]{1,0:T(8,128)(2,1)S(1)}, u32[]{:S(2)}, u32[]{:S(2)}) collective-permute-start(bf16[128,2560]{1,0:T(8,128)(2,1)S(1)} %convolution_convert_fusion.1), channel_id=1, source_target_pairs={{0,2},{2,0},{4,6},{6,4},{8,10},{10,8},{12,14},{14,12},{1,3},{3,1},... | collective-permute-start | bytes 1966088 | tf_op jit(solution)/shard_map/ppermute | solution.py:114
  71.9 19.6 %collective-permute-start.20 = (bf16[64,2560]{1,0:T(8,128)(2,1)S(1)}, bf16[64,2560]{1,0:T(8,128)(2,1)S(1)}, u32[]{:S(2)}, u32[]{:S(2)}) collective-permute-start(bf16[64,2560]{1,0:T(8,128)(2,1)S(1)} %get-tuple-element.43), channel_id=1, source_target_pairs={{0,4},{2,6},{12,8},{14,10},{1,5},{3,7},{13,9},{15,11},{16,20},{18,... | collective-permute-start | bytes 983048 | tf_op jit(solution)/shard_map/ppermute | solution.py:114
  83.5 17.2 %collective-permute-start.26 = (bf16[64,2560]{1,0:T(8,128)(2,1)S(1)}, bf16[64,2560]{1,0:T(8,128)(2,1)S(1)}, u32[]{:S(2)}, u32[]{:S(2)}) collective-permute-start(bf16[64,2560]{1,0:T(8,128)(2,1)S(1)} %add_convert_fusion), channel_id=1, source_target_pairs={{4,0},{6,2},{8,12},{10,14},{5,1},{7,3},{9,13},{11,15},{20,16},{22,... | collective-permute-start | bytes 983048 | tf_op jit(solution)/shard_map/ppermute | solution.py:114
  84.8 13.8 %collective-permute-start.22 = (bf16[64,2560]{1,0:T(8,128)(2,1)S(1)}, bf16[64,2560]{1,0:T(8,128)(2,1)S(1)}, u32[]{:S(2)}, u32[]{:S(2)}) collective-permute-start(bf16[64,2560]{1,0:T(8,128)(2,1)S(1)} %get-tuple-element.46), channel_id=1, source_target_pairs={{0,4},{2,6},{12,8},{14,10},{1,5},{3,7},{13,9},{15,11},{16,20},{18,... | collective-permute-start | bytes 983048 | tf_op jit(solution)/shard_map/ppermute | solution.py:114
  91.5 23.3 %collective-permute-start.19 = (bf16[64,2560]{1,0:T(8,128)(2,1)S(1)}, bf16[64,2560]{1,0:T(8,128)(2,1)S(1)}, u32[]{:S(2)}, u32[]{:S(2)}) collective-permute-start(bf16[64,2560]{1,0:T(8,128)(2,1)S(1)} %get-tuple-element.41), channel_id=1, source_target_pairs={{0,4},{2,6},{12,8},{14,10},{1,5},{3,7},{13,9},{15,11},{16,20},{18,... | collective-permute-start | bytes 983048 | tf_op jit(solution)/shard_map/ppermute | solution.py:114
  98.5 14.2 %collective-permute-start.18 = (bf16[128,2560]{1,0:T(8,128)(2,1)S(1)}, bf16[128,2560]{1,0:T(8,128)(2,1)S(1)}, u32[]{:S(2)}, u32[]{:S(2)}) collective-permute-start(bf16[128,2560]{1,0:T(8,128)(2,1)S(1)} %convolution_convert_fusion), channel_id=1, source_target_pairs={{0,2},{2,0},{4,6},{6,4},{8,10},{10,8},{12,14},{14,12},{1,3},{3,1},... | collective-permute-start | bytes 1966088 | tf_op jit(solution)/shard_map/ppermute | solution.py:114
  100.0 14.9 %collective-permute-start.21 = (bf16[64,2560]{1,0:T(8,128)(2,1)S(1)}, bf16[64,2560]{1,0:T(8,128)(2,1)S(1)}, u32[]{:S(2)}, u32[]{:S(2)}) collective-permute-start(bf16[64,2560]{1,0:T(8,128)(2,1)S(1)} %add_convert_fusion.4), channel_id=1, source_target_pairs={{4,8},{6,10},{8,4},{10,6},{5,9},{7,11},{9,5},{11,7},{20,24},{22,26... | collective-permute-start | bytes 983048 | tf_op jit(solution)/shard_map/ppermute | solution.py:114
  102.3 22.3 %collective-permute-start.24 = (bf16[64,2560]{1,0:T(8,128)(2,1)S(1)}, bf16[64,2560]{1,0:T(8,128)(2,1)S(1)}, u32[]{:S(2)}, u32[]{:S(2)}) collective-permute-start(bf16[64,2560]{1,0:T(8,128)(2,1)S(1)} %add_convert_fusion.2), channel_id=1, source_target_pairs={{4,0},{6,2},{8,12},{10,14},{5,1},{7,3},{9,13},{11,15},{20,16},{22,... | collective-permute-start | bytes 983048 | tf_op jit(solution)/shard_map/ppermute | solution.py:114
  (15 other events, 179.0 us)

commit v5 on v4

--- a/solution.py
+++ b/solution.py
@@ -101,9 +101,6 @@
     return on_line([(a, a ^ bit) for a in range(PLACES)])
 
 
-ENDS_IN = on_line([(0, 1), (3, 2)])
-MIDDLE = on_line([(1, 2), (2, 1)])
-ENDS_OUT = on_line([(1, 0), (2, 3)])
 PARTNER = [(2 * a + side, 2 * a + 1 - side) for a in range(PLACES) for side in (0, 1)]
 SWAP = [(0, 1), (1, 0)]
 OWNERS = 2 * PLACES
@@ -136,6 +133,11 @@
 
 def both_cores(partial):
     return partial + lax.ppermute(partial, "tensor", SWAP)
+
+
+def gather_gates(gating, earlier):
+    later = after(gating, earlier)
+    return [gating] + [move(later, xor_line(bit)) for bit in (1, 2, 3)]
 
 
 def by_pairs(tokens, cotangent, down_adapter, up_adapter, token_lists, gating):
@@ -150,14 +152,12 @@
     far_down = lax.ppermute(down_matrix, ("groups", "adapter"), FAR)
     tokens2 = move(tokens, PARTNER)
     near_down = move(down_matrix, xor_line(1))
-    cot2 = move(cotangent, PARTNER)
+    cot2 = move(after(cotangent, far_down), PARTNER)
     cross_down = lax.ppermute(far_down, "groups", SWAP)
     far_up = lax.ppermute(after(up_matrix, far_down), ("groups", "adapter"), FAR)
     near_up = move(after(up_matrix, near_down), xor_line(1))
     cross_up = lax.ppermute(far_up, "groups", SWAP)
-    later = after(gating, (far_down, near_up))
-    gates = [gating, move(later, xor_line(1)), move(later, xor_line(2)), move(later, xor_line(3))]
-    tokens2, cot2, near_up = lax.optimization_barrier((tokens2, cot2, near_up))
+    gates = gather_gates(gating, (far_down, tokens2))
 
     far_bit = jnp.where(first_group, 2, 3)
     experts = jnp.stack([me, me ^ 2, me ^ (2 * far_bit), me ^ (2 * (far_bit ^ 1))])
@@ -195,30 +195,23 @@
 
     low = low_rank(tokens2, down_all, far_up)
     (own, first, second, third), up_send = partial_sums(for_line(low), cot2)
-    up_1a = move(up_send[2], ENDS_IN)
-    up_1b = move(up_send[1], ENDS_IN)
-    up_1c = move(up_send[0], ENDS_IN)
-
-    cross_up = after(cross_up, (up_1a, up_1b))
+    up_near = move(jnp.concatenate([up_send[0], up_send[2]]), xor_line(1))
+
+    cross_up = after(cross_up, up_send)
     up_all = jnp.concatenate([up_matrix, near_up, far_up, cross_up], axis=0)
-    low_back = low_rank(cot2, up_all)
+    low_back = low_rank(cot2, up_all, up_near)
     branch_back = outward_start(low, up_all)
-    up_2a = move(narrow(add_up(second, up_1a)), MIDDLE)
-    up_2b = move(narrow(add_up(third, up_1b)), MIDDLE)
-    low_back = after(low_back, (up_1c, up_2a))
     (own_b, first_b, second_b, third_b), down_send = partial_sums(for_line(low_back), tokens2)
-    down_1a = move(down_send[2], ENDS_IN)
-    down_1b = move(down_send[1], ENDS_IN)
-    down_1c = move(down_send[0], ENDS_IN)
-    up_3 = move(narrow(add_up(first, up_2a)), ENDS_OUT)
+    down_third = move(down_send[2], xor_line(1))
+    down_first = move(down_send[0], xor_line(1))
     input_back = outward_start(low_back, down_all)
-    down_2a = move(narrow(add_up(second_b, down_1a)), MIDDLE)
-    down_2b = move(narrow(add_up(third_b, down_1b)), MIDDLE)
-    up_grad = add_up(own, up_1c, up_2b, up_3)
+    up_first, up_third = jnp.split(up_near, 2)
+    up_far = move(narrow(add_up(second, up_third)), xor_line(2))
+    down_far = move(narrow(add_up(second_b, down_third)), xor_line(2))
     branch_out = outward_end(low, up_all, branch_back)
-    down_3 = move(narrow(add_up(first_b, down_2a)), ENDS_OUT)
+    up_grad = add_up(own, up_first, up_far)
     input_grad = outward_end(low_back, down_all, input_back)
-    down_grad = add_up(own_b, down_1c, down_2b, down_3)
+    down_grad = add_up(own_b, down_first, down_far)
     down_grad = (down_grad / capacity).astype(jnp.bfloat16)[None]
     up_grad = (up_grad / capacity).astype(jnp.bfloat16)[None]
     return (branch_out, input_grad, down_grad, up_grad)

time: 126 us -> 102 us (0.81)
  starting transfers between devices: 49.9 us -> 25.8 us
    ppermute x21 -> x14, starting transfers between devices: 42.2 us -> 17.5 us  [move(): return lax.ppermute(value, 'adapter', pairs)]
    ppermute x21 -> x14, waiting for transfers between devices: 48.7 us -> 42.3 us  [move(): return lax.ppermute(value, 'adapter', pairs)]
    ppermute x1, waiting for transfers between devices: 0.01 us -> 2.81 us  [by_pairs(): cross_down = lax.ppermute(far_down, 'groups', SWAP)]
    ppermute x1, waiting for transfers between devices: 0.01 us -> 2.02 us  [by_pairs(): lax.ppermute(after(up_matrix, far_down), ('groups', 'adapter'), FAR)]
  transfers between devices with their start and end apart: 27 -> 20, of which waited for: 11 -> 9; matrix products, arithmetic and copies ran while one was open for 15% -> 21% of each run, Pallas kernels for 0% -> 0%
where the time goes in v5:
time: 102 us; the launch traced here: 101 us
  waiting for transfers between devices  52.3 us (51%)
  starting transfers between devices  25.8 us (25%)
  matrix products  14.6 us (14%)
  local copies, waits for them, and re-layouts  4.25 us (4%)
  other arithmetic  3.56 us (3%)
    ppermute x14, waiting for transfers between devices, move(): return lax.ppermute(value, 'adapter', pairs)  42.3 us
    ppermute x14, starting transfers between devices, move(): return lax.ppermute(value, 'adapter', pairs)  17.5 us
    dot_general x2, matrix products, outward_end(): jnp.dot(weights[:tok_local], matrix, preferred_element_type=jnp.float32)  4.71 us
    dot_general x8, matrix products, contract_first(): lax.dot_general(left_op, right_op, (((0,), (0,)), ((), ())), preferred_el...  3.42 us
    dot_general x2, matrix products, contract_last(): lax.dot_general(left_op, right_op, (((1,), (1,)), ((), ())), preferred_el...  3.41 us
    ppermute x1, starting transfers between devices, by_pairs(): cross_down = lax.ppermute(far_down, 'groups', SWAP)  3.16 us
    dot_general x2, matrix products, outward_start(): jnp.dot(weights[tok_local:], matrix, preferred_element_type=jnp.float32)  3.03 us
    ppermute x1, waiting for transfers between devices, by_pairs(): cross_down = lax.ppermute(far_down, 'groups', SWAP)  2.81 us
  transfers between devices with their start and end apart: 20, of which 9 were waited for; matrix products, arithmetic and copies ran while one was open for 21% of the time, Pallas kernels for 0%

profile of v5, /device:TPU:0, one launch (start us, length us, event | category | flops | bytes accessed | tf_op | source)
XLA Modules:
  0.0 101.3 jit_solution(12636334385711672021)
XLA Ops:
  0.6 3.1 %collective-permute-start.5 = (bf16[64,2560]{1,0:T(8,128)(2,1)}, bf16[64,2560]{1,0:T(8,128)(2,1)}, u32[]{:S(2)}, u32[]{:S(2)}) collective-permute-start(bf16[64,2560]{1,0:T(8,128)(2,1)} %bitcast.28), channel_id=1, source_target_pairs={{0,4},{2,6},{4,0},{6,2},{8,12},{10,14},{12,8},{14,10},{1,5},{3,7},... | collective-permute-start | bytes 983048 | tf_op jit(solution)/shard_map/ppermute | solution.py:111
  3.7 2.6 %collective-permute-start = (bf16[64,2560]{1,0:T(8,128)(2,1)}, bf16[64,2560]{1,0:T(8,128)(2,1)}, u32[]{:S(2)}, u32[]{:S(2)}) collective-permute-start(bf16[64,2560]{1,0:T(8,128)(2,1)} %bitcast.29), channel_id=1, source_target_pairs={{0,8},{2,10},{4,12},{6,14},{8,0},{10,2},{12,4},{14,6},{16,28},{18,... | collective-permute-start | bytes 983048 | tf_op jit(solution)/shard_map/ppermute | solution.py:152
  6.3 1.5 %collective-permute-start.1 = (bf16[128,2560]{1,0:T(8,128)(2,1)}, bf16[128,2560]{1,0:T(8,128)(2,1)S(1)}, u32[]{:S(2)}, u32[]{:S(2)}) collective-permute-start(bf16[128,2560]{1,0:T(8,128)(2,1)} %param.6), channel_id=1, source_target_pairs={{0,2},{2,0},{4,6},{6,4},{8,10},{10,8},{12,14},{14,12},{1,3},{3,1},... | collective-permute-start | bytes 1966088 | tf_op jit(solution)/shard_map/ppermute | solution.py:111
  11.0 7.6 %collective-permute-done.5 = bf16[64,2560]{1,0:T(8,128)(2,1)} collective-permute-done((bf16[64,2560]{1,0:T(8,128)(2,1)}, bf16[64,2560]{1,0:T(8,128)(2,1)}, u32[]{:S(2)}, u32[]{:S(2)}) %collective-permute-start.5) | collective-permute-done | bytes 327712 | tf_op jit(solution)/shard_map/ppermute | solution.py:111
  18.7 2.7 %collective-permute-done = bf16[64,2560]{1,0:T(8,128)(2,1)} collective-permute-done((bf16[64,2560]{1,0:T(8,128)(2,1)}, bf16[64,2560]{1,0:T(8,128)(2,1)}, u32[]{:S(2)}, u32[]{:S(2)}) %collective-permute-start) | collective-permute-done | bytes 327712 | tf_op jit(solution)/shard_map/ppermute | solution.py:152
  21.9 1.5 %collective-permute-start.11 = (bf16[128,2560]{1,0:T(8,128)(2,1)}, bf16[128,2560]{1,0:T(8,128)(2,1)}, u32[]{:S(2)}, u32[]{:S(2)}) collective-permute-start(bf16[128,2560]{1,0:T(8,128)(2,1)} %param.7), channel_id=1, source_target_pairs={{0,2},{2,0},{4,6},{6,4},{8,10},{10,8},{12,14},{14,12},{1,3},{3,1},... | collective-permute-start | bytes 1966088 | tf_op jit(solution)/shard_map/ppermute | solution.py:111
  23.4 3.2 %collective-permute-start.6 = (bf16[64,2560]{1,0:T(8,128)(2,1)}, bf16[64,2560]{1,0:T(8,128)(2,1)S(1)}, u32[]{:S(2)}, u32[]{:S(2)}) collective-permute-start(bf16[64,2560]{1,0:T(8,128)(2,1)} %collective-permute-done), channel_id=1, source_target_pairs={{0,16},{16,0},{1,17},{17,1},{2,18},{18,2},{3,19},{19,3},{4,20},{20... | collective-permute-start | bytes 983048 | tf_op jit(solution)/shard_map/ppermute | solution.py:156
  26.5 2.5 %collective-permute-start.4 = (f32[1,256]{1,0:T(1,128)S(1)}, f32[1,256]{1,0:T(1,128)S(1)}, u32[]{:S(2)}, u32[]{:S(2)}) collective-permute-start(f32[1,256]{1,0:T(1,128)S(1)} %copy-done.1), channel_id=1, source_target_pairs={{0,12},{2,14},{4,8},{6,10},{8,4},{10,6},{12,0},{14,2},{1,13},{3,15... | collective-permute-start | bytes 3080 | tf_op jit(solution)/shard_map/ppermute | solution.py:111
  29.1 2.8 %collective-permute-done.6 = bf16[64,2560]{1,0:T(8,128)(2,1)S(1)} collective-permute-done((bf16[64,2560]{1,0:T(8,128)(2,1)}, bf16[64,2560]{1,0:T(8,128)(2,1)S(1)}, u32[]{:S(2)}, u32[]{:S(2)}) %collective-permute-start.6) | collective-permute-done | bytes 327712 | tf_op jit(solution)/shard_map/ppermute | solution.py:156
  33.0 1.6 %fusion.38 = f32[256,256]{1,0:T(8,128)S(1)} fusion(bf16[256,2560]{1,0:T(8,128)(2,1)S(1)} %constant_dynamic-update-slice_fusion, bf16[64,2560]{1,0:T(8,128)(2,1)S(1)} %collective-permute-done.6, bf16[64,2560]{1,0:T(8,128)(2,1)} %collective-permute-done, bf16[64,2560]{1,0:T(8,128)(2,1)} %collective-permute-done.5, bf16[64,2560]{1,0:T(8,128)(2,1)S(1)} %bitcast.30), kind=kOutput, calls=%fused_computation.68 | convolution fusion | flops 340787200 | bytes 2883584 | tf_op jit(solution)/shard_map/dot_general | solution.py:10
  34.6 2.0 %collective-permute-done.8 = bf16[64,2560]{1,0:T(8,128)(2,1)} collective-permute-done((bf16[64,2560]{1,0:T(8,128)(2,1)}, bf16[64,2560]{1,0:T(8,128)(2,1)}, u32[]{:S(2)}, u32[]{:S(2)}) %collective-permute-start.8) | collective-permute-done | bytes 327712 | tf_op jit(solution)/shard_map/ppermute | solution.py:157
  36.7 1.9 %collective-permute-start.10 = (bf16[64,2560]{1,0:T(8,128)(2,1)}, bf16[64,2560]{1,0:T(8,128)(2,1)}, u32[]{:S(2)}, u32[]{:S(2)}) collective-permute-start(bf16[64,2560]{1,0:T(8,128)(2,1)} %collective-permute-done.8), channel_id=1, source_target_pairs={{0,16},{16,0},{1,17},{17,1},{2,18},{18,2},{3,19},{19,3},{4,20},{20... | collective-permute-start | bytes 983048 | tf_op jit(solution)/shard_map/ppermute | solution.py:159
  38.6 1.6 %collective-permute-done.2 = f32[1,256]{1,0:T(1,128)S(1)} collective-permute-done((f32[1,256]{1,0:T(1,128)S(1)}, f32[1,256]{1,0:T(1,128)S(1)}, u32[]{:S(2)}, u32[]{:S(2)}) %collective-permute-start.2) | collective-permute-done | bytes 1056 | tf_op jit(solution)/shard_map/ppermute | solution.py:111
  44.8 2.5 %collective-permute-done.10 = bf16[64,2560]{1,0:T(8,128)(2,1)} collective-permute-done((bf16[64,2560]{1,0:T(8,128)(2,1)}, bf16[64,2560]{1,0:T(8,128)(2,1)}, u32[]{:S(2)}, u32[]{:S(2)}) %collective-permute-start.10) | collective-permute-done | bytes 327712 | tf_op jit(solution)/shard_map/ppermute | solution.py:159
  47.3 1.8 %fusion.37 = f32[256,256]{1,0:T(8,128)S(1)} fusion(bf16[256,2560]{1,0:T(8,128)(2,1)S(1)} %constant_dynamic-update-slice_fusion.2, bf16[64,2560]{1,0:T(8,128)(2,1)} %collective-permute-done.10, bf16[64,2560]{1,0:T(8,128)(2,1)} %collective-permute-done.8, bf16[64,2560]{1,0:T(8,128)(2,1)} %collective-permute-done.9, bf16[64,2560]{1,0:T(8,128)(2,1)} %bitcast.11), kind=kOutput, calls=%fused_computation.67 | convolution fusion | flops 340787200 | bytes 2883584 | tf_op jit(solution)/shard_map/dot_general | solution.py:10
  49.1 1.6 %convolution_convert_fusion.1 = bf16[128,2560]{1,0:T(8,128)(2,1)S(1)} fusion(bf16[256,256]{1,0:T(8,128)(2,1)S(1)} %multiply_convert_fusion.3, bf16[64,2560]{1,0:T(8,128)(2,1)} %collective-permute-done.10, bf16[64,2560]{1,0:T(8,128)(2,1)} %collective-permute-done.8, bf16[64,2560]{1,0:T(8,128)(2,1)} %collective-permute-done.9, bf16[64,2560]{1,0:T(8,128)(2,1)} %bitcast.11), kind=kOutput, calls=%fused_computation.6 | convolution fusion | flops 173342720 | bytes 2031616 | tf_op jit(solution)/shard_map/dot_general | solution.py:189
  50.8 1.5 %collective-permute-start.12 = (bf16[128,2560]{1,0:T(8,128)(2,1)S(1)}, bf16[128,2560]{1,0:T(8,128)(2,1)S(1)}, u32[]{:S(2)}, u32[]{:S(2)}) collective-permute-start(bf16[128,2560]{1,0:T(8,128)(2,1)S(1)} %convolution_convert_fusion.1), channel_id=1, source_target_pairs={{0,2},{2,0},{4,6},{6,4},{8,10},{10,8},{12,14},{14,12},{1,3},{3,1},... | collective-permute-start | bytes 1966088 | tf_op jit(solution)/shard_map/ppermute | solution.py:111
  52.3 7.7 %collective-permute-done.14 = bf16[128,2560]{1,0:T(8,128)(2,1)S(1)} collective-permute-done((bf16[128,2560]{1,0:T(8,128)(2,1)S(1)}, bf16[128,2560]{1,0:T(8,128)(2,1)S(1)}, u32[]{:S(2)}, u32[]{:S(2)}) %collective-permute-start.14) | collective-permute-done | bytes 655392 | tf_op jit(solution)/shard_map/ppermute | solution.py:111
  60.9 2.2 %collective-permute-start.19 = (bf16[64,2560]{1,0:T(8,128)(2,1)S(1)}, bf16[64,2560]{1,0:T(8,128)(2,1)S(1)}, u32[]{:S(2)}, u32[]{:S(2)}) collective-permute-start(bf16[64,2560]{1,0:T(8,128)(2,1)S(1)} %add_convert_fusion), channel_id=1, source_target_pairs={{0,8},{2,10},{4,12},{6,14},{8,0},{10,2},{12,4},{14,6},{1,9},{3,11}... | collective-permute-start | bytes 983048 | tf_op jit(solution)/shard_map/ppermute | solution.py:111
  66.1 1.4 %convolution_convert_fusion = bf16[128,2560]{1,0:T(8,128)(2,1)S(1)} fusion(bf16[256,256]{1,0:T(8,128)(2,1)S(1)} %multiply_convert_fusion.2, bf16[64,2560]{1,0:T(8,128)(2,1)S(1)} %copy-done.5, bf16[64,2560]{1,0:T(8,128)(2,1)} %collective-permute-done, bf16[64,2560]{1,0:T(8,128)(2,1)} %collective-permute-done.5, bf16[64,2560]{1,0:T(8,128)(2,1)S(1)} %bitcast.31), kind=kOutput, calls=%fused_computation.5 | convolution fusion | flops 173342720 | bytes 2031616 | tf_op jit(solution)/shard_map/dot_general | solution.py:189
  68.8 2.5 %fusion = bf16[128,2560]{1,0:T(8,128)(2,1)} fusion(bf16[128,2560]{1,0:T(8,128)(2,1)S(1)} %collective-permute-done.12, bf16[256,256]{1,0:T(8,128)(2,1)S(1)} %multiply_convert_fusion.3, bf16[64,2560]{1,0:T(8,128)(2,1)} %collective-permute-done.10, bf16[64,2560]{1,0:T(8,128)(2,1)} %collective-permute-done.8, bf16[64,2560]{1,0:T(8,128)(2,1)} %collective-permute-done.9, ...), kind=kOutput, calls=%fused_computation.3 | convolution fusion | flops 173998080 | bytes 2686976 | tf_op jit(solution)/shard_map/dot_general | solution.py:193
  71.3 13.8 %collective-permute-done.17 = bf16[64,2560]{1,0:T(8,128)(2,1)S(1)} collective-permute-done((bf16[64,2560]{1,0:T(8,128)(2,1)S(1)}, bf16[64,2560]{1,0:T(8,128)(2,1)S(1)}, u32[]{:S(2)}, u32[]{:S(2)}) %collective-permute-start.17) | collective-permute-done | bytes 327712 | tf_op jit(solution)/shard_map/ppermute | solution.py:111
  86.7 2.3 %fusion.1 = bf16[128,2560]{1,0:T(8,128)(2,1)} fusion(bf16[128,2560]{1,0:T(8,128)(2,1)S(1)} %collective-permute-done.15, bf16[256,256]{1,0:T(8,128)(2,1)S(1)} %multiply_convert_fusion.2, bf16[64,2560]{1,0:T(8,128)(2,1)S(1)} %copy-done.5, bf16[64,2560]{1,0:T(8,128)(2,1)} %collective-permute-done, bf16[64,2560]{1,0:T(8,128)(2,1)} %collective-permute-done.5, ...), kind=kOutput, calls=%fused_computation.4 | convolution fusion | flops 173998080 | bytes 2686976 | tf_op jit(solution)/shard_map/dot_general | solution.py:193
  88.9 11.5 %collective-permute-done.18 = bf16[64,2560]{1,0:T(8,128)(2,1)S(1)} collective-permute-done((bf16[64,2560]{1,0:T(8,128)(2,1)S(1)}, bf16[64,2560]{1,0:T(8,128)(2,1)S(1)}, u32[]{:S(2)}, u32[]{:S(2)}) %collective-permute-start.18) | collective-permute-done | bytes 327712 | tf_op jit(solution)/shard_map/ppermute | solution.py:111
  (67 shorter events, 17.2 us)
Async XLA Ops:
  0.6 7.3 %copy-start = (s32[8,256]{1,0:T(8,128)S(1)}, s32[8,256]{1,0:T(8,128)}, u32[]{:S(2)}) copy-start(s32[8,256]{1,0:T(8,128)} %param.10) | copy-start | bytes 24580
  0.6 18.0 %collective-permute-start.5 = (bf16[64,2560]{1,0:T(8,128)(2,1)}, bf16[64,2560]{1,0:T(8,128)(2,1)}, u32[]{:S(2)}, u32[]{:S(2)}) collective-permute-start(bf16[64,2560]{1,0:T(8,128)(2,1)} %bitcast.28), channel_id=1, source_target_pairs={{0,4},{2,6},{4,0},{6,2},{8,12},{10,14},{12,8},{14,10},{1,5},{3,7},... | collective-permute-start | bytes 983048 | tf_op jit(solution)/shard_map/ppermute | solution.py:111
  3.7 17.6 %collective-permute-start = (bf16[64,2560]{1,0:T(8,128)(2,1)}, bf16[64,2560]{1,0:T(8,128)(2,1)}, u32[]{:S(2)}, u32[]{:S(2)}) collective-permute-start(bf16[64,2560]{1,0:T(8,128)(2,1)} %bitcast.29), channel_id=1, source_target_pairs={{0,8},{2,10},{4,12},{6,14},{8,0},{10,2},{12,4},{14,6},{16,28},{18,... | collective-permute-start | bytes 983048 | tf_op jit(solution)/shard_map/ppermute | solution.py:152
  6.3 20.2 %collective-permute-start.1 = (bf16[128,2560]{1,0:T(8,128)(2,1)}, bf16[128,2560]{1,0:T(8,128)(2,1)S(1)}, u32[]{:S(2)}, u32[]{:S(2)}) collective-permute-start(bf16[128,2560]{1,0:T(8,128)(2,1)} %param.6), channel_id=1, source_target_pairs={{0,2},{2,0},{4,6},{6,4},{8,10},{10,8},{12,14},{14,12},{1,3},{3,1},... | collective-permute-start | bytes 1966088 | tf_op jit(solution)/shard_map/ppermute | solution.py:111
  8.7 17.9 %copy-start.1 = (f32[1,256]{1,0:T(1,128)S(1)}, f32[1,256]{1,0:T(1,128)}, u32[]{:S(2)}) copy-start(f32[1,256]{1,0:T(1,128)} %param.11) | copy-start | bytes 3076
  9.8 23.2 %copy-start.2 = (bf16[1,64,2560]{2,1,0:T(8,128)(2,1)S(1)}, bf16[1,64,2560]{2,1,0:T(8,128)(2,1)}, u32[]{:S(2)}) copy-start(bf16[1,64,2560]{2,1,0:T(8,128)(2,1)} %param.8) | copy-start | bytes 983044
  18.7 28.6 %collective-permute-start.9 = (bf16[64,2560]{1,0:T(8,128)(2,1)}, bf16[64,2560]{1,0:T(8,128)(2,1)}, u32[]{:S(2)}, u32[]{:S(2)}) collective-permute-start(bf16[64,2560]{1,0:T(8,128)(2,1)} %bitcast.11), channel_id=1, source_target_pairs={{0,4},{2,6},{4,0},{6,2},{8,12},{10,14},{12,8},{14,10},{1,5},{3,7},... | collective-permute-start | bytes 983048 | tf_op jit(solution)/shard_map/ppermute | solution.py:111
  21.3 15.4 %collective-permute-start.8 = (bf16[64,2560]{1,0:T(8,128)(2,1)}, bf16[64,2560]{1,0:T(8,128)(2,1)}, u32[]{:S(2)}, u32[]{:S(2)}) collective-permute-start(bf16[64,2560]{1,0:T(8,128)(2,1)} %bitcast.11), channel_id=1, source_target_pairs={{0,8},{2,10},{4,12},{6,14},{8,0},{10,2},{12,4},{14,6},{16,28},{18,... | collective-permute-start | bytes 983048 | tf_op jit(solution)/shard_map/ppermute | solution.py:157
  21.9 19.9 %collective-permute-start.11 = (bf16[128,2560]{1,0:T(8,128)(2,1)}, bf16[128,2560]{1,0:T(8,128)(2,1)}, u32[]{:S(2)}, u32[]{:S(2)}) collective-permute-start(bf16[128,2560]{1,0:T(8,128)(2,1)} %param.7), channel_id=1, source_target_pairs={{0,2},{2,0},{4,6},{6,4},{8,10},{10,8},{12,14},{14,12},{1,3},{3,1},... | collective-permute-start | bytes 1966088 | tf_op jit(solution)/shard_map/ppermute | solution.py:111
  23.4 8.5 %collective-permute-start.6 = (bf16[64,2560]{1,0:T(8,128)(2,1)}, bf16[64,2560]{1,0:T(8,128)(2,1)S(1)}, u32[]{:S(2)}, u32[]{:S(2)}) collective-permute-start(bf16[64,2560]{1,0:T(8,128)(2,1)} %collective-permute-done), channel_id=1, source_target_pairs={{0,16},{16,0},{1,17},{17,1},{2,18},{18,2},{3,19},{19,3},{4,20},{20... | collective-permute-start | bytes 983048 | tf_op jit(solution)/shard_map/ppermute | solution.py:156
  26.5 10.1 %collective-permute-start.4 = (f32[1,256]{1,0:T(1,128)S(1)}, f32[1,256]{1,0:T(1,128)S(1)}, u32[]{:S(2)}, u32[]{:S(2)}) collective-permute-start(f32[1,256]{1,0:T(1,128)S(1)} %copy-done.1), channel_id=1, source_target_pairs={{0,12},{2,14},{4,8},{6,10},{8,4},{10,6},{12,0},{14,2},{1,13},{3,15... | collective-permute-start | bytes 3080 | tf_op jit(solution)/shard_map/ppermute | solution.py:111
  31.9 2.8 %copy-start.4 = (bf16[64,2560]{1,0:T(8,128)(2,1)}, bf16[64,2560]{1,0:T(8,128)(2,1)S(1)}, u32[]{:S(2)}) copy-start(bf16[64,2560]{1,0:T(8,128)(2,1)S(1)} %collective-permute-done.6) | copy-start | bytes 983044
  31.9 4.8 %collective-permute-start.3 = (f32[1,256]{1,0:T(1,128)S(1)}, f32[1,256]{1,0:T(1,128)S(1)}, u32[]{:S(2)}, u32[]{:S(2)}) collective-permute-start(f32[1,256]{1,0:T(1,128)S(1)} %copy-done.1), channel_id=1, source_target_pairs={{0,8},{2,10},{4,12},{6,14},{8,0},{10,2},{12,4},{14,6},{1,9},{3,11}... | collective-permute-start | bytes 3080 | tf_op jit(solution)/shard_map/ppermute | solution.py:111
  36.7 3.6 %collective-permute-start.2 = (f32[1,256]{1,0:T(1,128)S(1)}, f32[1,256]{1,0:T(1,128)S(1)}, u32[]{:S(2)}, u32[]{:S(2)}) collective-permute-start(f32[1,256]{1,0:T(1,128)S(1)} %copy-done.1), channel_id=1, source_target_pairs={{0,4},{2,6},{4,0},{6,2},{8,12},{10,14},{12,8},{14,10},{1,5},{3,7},... | collective-permute-start | bytes 3080 | tf_op jit(solution)/shard_map/ppermute | solution.py:111
  36.7 4.1 %collective-permute-start.7 = (f32[256,256]{1,0:T(8,128)S(1)}, f32[256,256]{1,0:T(8,128)}, u32[]{:S(2)}, u32[]{:S(2)}) collective-permute-start(f32[256,256]{1,0:T(8,128)S(1)} %fusion.38), channel_id=1, source_target_pairs={{0,1},{1,0},{2,3},{3,2},{4,5},{5,4},{6,7},{7,6},{8,9},{9,8},{10,11... | collective-permute-start | bytes 786440 | tf_op jit(solution)/shard_map/ppermute | solution.py:135
  36.7 10.6 %collective-permute-start.10 = (bf16[64,2560]{1,0:T(8,128)(2,1)}, bf16[64,2560]{1,0:T(8,128)(2,1)}, u32[]{:S(2)}, u32[]{:S(2)}) collective-permute-start(bf16[64,2560]{1,0:T(8,128)(2,1)} %collective-permute-done.8), channel_id=1, source_target_pairs={{0,16},{16,0},{1,17},{17,1},{2,18},{18,2},{3,19},{19,3},{4,20},{20... | collective-permute-start | bytes 983048 | tf_op jit(solution)/shard_map/ppermute | solution.py:159
  44.7 15.3 %collective-permute-start.14 = (bf16[128,2560]{1,0:T(8,128)(2,1)S(1)}, bf16[128,2560]{1,0:T(8,128)(2,1)S(1)}, u32[]{:S(2)}, u32[]{:S(2)}) collective-permute-start(bf16[128,2560]{1,0:T(8,128)(2,1)S(1)} %pad_maximum_fusion.2), channel_id=1, source_target_pairs={{0,4},{2,6},{4,0},{6,2},{8,12},{10,14},{12,8},{14,10},{1,5},{3,7},... | collective-permute-start | bytes 1966088 | tf_op jit(solution)/shard_map/ppermute | solution.py:111
  49.1 3.2 %collective-permute-start.13 = (f32[256,256]{1,0:T(8,128)S(1)}, f32[256,256]{1,0:T(8,128)S(1)}, u32[]{:S(2)}, u32[]{:S(2)}) collective-permute-start(f32[256,256]{1,0:T(8,128)S(1)} %fusion.37), channel_id=1, source_target_pairs={{0,1},{1,0},{2,3},{3,2},{4,5},{5,4},{6,7},{7,6},{8,9},{9,8},{10,11... | collective-permute-start | bytes 786440 | tf_op jit(solution)/shard_map/ppermute | solution.py:135
  50.8 18.1 %collective-permute-start.12 = (bf16[128,2560]{1,0:T(8,128)(2,1)S(1)}, bf16[128,2560]{1,0:T(8,128)(2,1)S(1)}, u32[]{:S(2)}, u32[]{:S(2)}) collective-permute-start(bf16[128,2560]{1,0:T(8,128)(2,1)S(1)} %convolution_convert_fusion.1), channel_id=1, source_target_pairs={{0,2},{2,0},{4,6},{6,4},{8,10},{10,8},{12,14},{14,12},{1,3},{3,1},... | collective-permute-start | bytes 1966088 | tf_op jit(solution)/shard_map/ppermute | solution.py:111
  60.9 24.9 %collective-permute-start.19 = (bf16[64,2560]{1,0:T(8,128)(2,1)S(1)}, bf16[64,2560]{1,0:T(8,128)(2,1)S(1)}, u32[]{:S(2)}, u32[]{:S(2)}) collective-permute-start(bf16[64,2560]{1,0:T(8,128)(2,1)S(1)} %add_convert_fusion), channel_id=1, source_target_pairs={{0,8},{2,10},{4,12},{6,14},{8,0},{10,2},{12,4},{14,6},{1,9},{3,11}... | collective-permute-start | bytes 983048 | tf_op jit(solution)/shard_map/ppermute | solution.py:111
  64.0 24.9 %collective-permute-start.16 = (bf16[64,2560]{1,0:T(8,128)(2,1)S(1)}, bf16[64,2560]{1,0:T(8,128)(2,1)S(1)}, u32[]{:S(2)}, u32[]{:S(2)}) collective-permute-start(bf16[64,2560]{1,0:T(8,128)(2,1)S(1)} %fusion.4), channel_id=1, source_target_pairs={{0,4},{2,6},{4,0},{6,2},{8,12},{10,14},{12,8},{14,10},{1,5},{3,7},... | collective-permute-start | bytes 983048 | tf_op jit(solution)/shard_map/ppermute | solution.py:111
  65.1 20.0 %collective-permute-start.17 = (bf16[64,2560]{1,0:T(8,128)(2,1)S(1)}, bf16[64,2560]{1,0:T(8,128)(2,1)S(1)}, u32[]{:S(2)}, u32[]{:S(2)}) collective-permute-start(bf16[64,2560]{1,0:T(8,128)(2,1)S(1)} %fusion.16), channel_id=1, source_target_pairs={{0,4},{2,6},{4,0},{6,2},{8,12},{10,14},{12,8},{14,10},{1,5},{3,7},... | collective-permute-start | bytes 983048 | tf_op jit(solution)/shard_map/ppermute | solution.py:111
  67.5 19.2 %collective-permute-start.15 = (bf16[128,2560]{1,0:T(8,128)(2,1)S(1)}, bf16[128,2560]{1,0:T(8,128)(2,1)S(1)}, u32[]{:S(2)}, u32[]{:S(2)}) collective-permute-start(bf16[128,2560]{1,0:T(8,128)(2,1)S(1)} %convolution_convert_fusion), channel_id=1, source_target_pairs={{0,2},{2,0},{4,6},{6,4},{8,10},{10,8},{12,14},{14,12},{1,3},{3,1},... | collective-permute-start | bytes 1966088 | tf_op jit(solution)/shard_map/ppermute | solution.py:111
  85.2 15.3 %collective-permute-start.18 = (bf16[64,2560]{1,0:T(8,128)(2,1)S(1)}, bf16[64,2560]{1,0:T(8,128)(2,1)S(1)}, u32[]{:S(2)}, u32[]{:S(2)}) collective-permute-start(bf16[64,2560]{1,0:T(8,128)(2,1)S(1)} %add_convert_fusion.1), channel_id=1, source_target_pairs={{0,8},{2,10},{4,12},{6,14},{8,0},{10,2},{12,4},{14,6},{1,9},{3,11}... | collective-permute-start | bytes 983048 | tf_op jit(solution)/shard_map/ppermute | solution.py:111
  (2 other events, 5.0 us)

commit v6 on v5

--- a/solution.py
+++ b/solution.py
@@ -156,6 +156,7 @@
     cross_down = lax.ppermute(far_down, "groups", SWAP)
     far_up = lax.ppermute(after(up_matrix, far_down), ("groups", "adapter"), FAR)
     near_up = move(after(up_matrix, near_down), xor_line(1))
+    cot2, near_up, far_up = lax.optimization_barrier((cot2, near_up, far_up))
     cross_up = lax.ppermute(far_up, "groups", SWAP)
     gates = gather_gates(gating, (far_down, tokens2))
 
@@ -193,19 +194,19 @@
         mine = jnp.dot(weights[:tok_local], matrix, preferred_element_type=jnp.float32)
         return narrow(mine + back.astype(jnp.float32))
 
-    low = low_rank(tokens2, down_all, far_up)
+    low = low_rank(tokens2, down_all)
     (own, first, second, third), up_send = partial_sums(for_line(low), cot2)
-    up_near = move(jnp.concatenate([up_send[0], up_send[2]]), xor_line(1))
-
-    cross_up = after(cross_up, up_send)
+    up_third = move(up_send[2], xor_line(1))
+    up_first = move(up_send[0], xor_line(1))
+
+    cross_up = after(cross_up, up_third)
     up_all = jnp.concatenate([up_matrix, near_up, far_up, cross_up], axis=0)
-    low_back = low_rank(cot2, up_all, up_near)
+    low_back = low_rank(cot2, up_all)
     branch_back = outward_start(low, up_all)
     (own_b, first_b, second_b, third_b), down_send = partial_sums(for_line(low_back), tokens2)
     down_third = move(down_send[2], xor_line(1))
-    down_first = move(down_send[0], xor_line(1))
+    down_first = move(after(down_send[0], (up_first, down_third)), xor_line(1))
     input_back = outward_start(low_back, down_all)
-    up_first, up_third = jnp.split(up_near, 2)
     up_far = move(narrow(add_up(second, up_third)), xor_line(2))
     down_far = move(narrow(add_up(second_b, down_third)), xor_line(2))
     branch_out = outward_end(low, up_all, branch_back)

time: 102 us -> 99.2 us (0.973)
  waiting for transfers between devices: 52.3 us -> 46.6 us
  starting transfers between devices: 25.8 us -> 29.3 us
    ppermute x14 -> x15, waiting for transfers between devices: 42.3 us -> 29.7 us  [move(): return lax.ppermute(value, 'adapter', pairs)]
    ppermute x14 -> x15, starting transfers between devices: 17.5 us -> 23.8 us  [move(): return lax.ppermute(value, 'adapter', pairs)]
    ppermute x1, waiting for transfers between devices: 2.65 us -> 8.91 us  [by_pairs(): far_down = lax.ppermute(down_matrix, ('groups', 'adapter'), FAR)]
    ppermute x1, waiting for transfers between devices: 2.81 us -> 7.62 us  [by_pairs(): cross_down = lax.ppermute(far_down, 'groups', SWAP)]
    ppermute x1, waiting for transfers between devices: 2.5 us -> 0.01 us  [by_pairs(): cross_up = lax.ppermute(far_up, 'groups', SWAP)]
    ppermute x1, waiting for transfers between devices: 2.02 us -> 0.01 us  [by_pairs(): lax.ppermute(after(up_matrix, far_down), ('groups', 'adapter'), FAR)]
    ppermute x1, starting transfers between devices: 1.93 us -> 0.01 us  [by_pairs(): cross_up = lax.ppermute(far_up, 'groups', SWAP)]
    ppermute x1, starting transfers between devices: 3.16 us -> 1.31 us  [by_pairs(): cross_down = lax.ppermute(far_down, 'groups', SWAP)]
  transfers between devices with their start and end apart: 20 -> 21, of which waited for: 9 -> 13; matrix products, arithmetic and copies ran while one was open for 21% -> 19% of each run, Pallas kernels for 0% -> 0%
where the time goes in v6:
time: 99.2 us; the launch traced here: 98.8 us
  waiting for transfers between devices  46.6 us (47%)
  starting transfers between devices  29.3 us (30%)
  matrix products  14.3 us (14%)
  local copies, waits for them, and re-layouts  4.24 us (4%)
  other arithmetic  3.53 us (4%)
    ppermute x15, waiting for transfers between devices, move(): return lax.ppermute(value, 'adapter', pairs)  29.7 us
    ppermute x15, starting transfers between devices, move(): return lax.ppermute(value, 'adapter', pairs)  23.8 us
    ppermute x1, waiting for transfers between devices, by_pairs(): far_down = lax.ppermute(down_matrix, ('groups', 'adapter'), FAR)  8.91 us
    ppermute x1, waiting for transfers between devices, by_pairs(): cross_down = lax.ppermute(far_down, 'groups', SWAP)  7.62 us
    dot_general x2, matrix products, outward_end(): jnp.dot(weights[:tok_local], matrix, preferred_element_type=jnp.float32)  4.62 us
    ppermute x1, starting transfers between devices, by_pairs(): far_down = lax.ppermute(down_matrix, ('groups', 'adapter'), FAR)  4.1 us
    dot_general x8, matrix products, contract_first(): lax.dot_general(left_op, right_op, (((0,), (0,)), ((), ())), preferred_el...  3.41 us
    dot_general x2, matrix products, contract_last(): lax.dot_general(left_op, right_op, (((1,), (1,)), ((), ())), preferred_el...  3.36 us
  transfers between devices with their start and end apart: 21, of which 13 were waited for; matrix products, arithmetic and copies ran while one was open for 19% of the time, Pallas kernels for 0%

profile of v6, /device:TPU:0, one launch (start us, length us, event | category | flops | bytes accessed | tf_op | source)
XLA Modules:
  0.0 98.8 jit_solution(13096838604526318125)
XLA Ops:
  0.6 4.1 %collective-permute-start = (bf16[64,2560]{1,0:T(8,128)(2,1)}, bf16[64,2560]{1,0:T(8,128)(2,1)}, u32[]{:S(2)}, u32[]{:S(2)}) collective-permute-start(bf16[64,2560]{1,0:T(8,128)(2,1)} %bitcast.28), channel_id=1, source_target_pairs={{0,8},{2,10},{4,12},{6,14},{8,0},{10,2},{12,4},{14,6},{16,28},{18,... | collective-permute-start | bytes 983048 | tf_op jit(solution)/shard_map/ppermute | solution.py:152
  4.7 1.6 %collective-permute-start.5 = (bf16[64,2560]{1,0:T(8,128)(2,1)}, bf16[64,2560]{1,0:T(8,128)(2,1)}, u32[]{:S(2)}, u32[]{:S(2)}) collective-permute-start(bf16[64,2560]{1,0:T(8,128)(2,1)} %bitcast.29), channel_id=1, source_target_pairs={{0,4},{2,6},{4,0},{6,2},{8,12},{10,14},{12,8},{14,10},{1,5},{3,7},... | collective-permute-start | bytes 983048 | tf_op jit(solution)/shard_map/ppermute | solution.py:111
  6.3 1.5 %collective-permute-start.1 = (bf16[128,2560]{1,0:T(8,128)(2,1)}, bf16[128,2560]{1,0:T(8,128)(2,1)S(1)}, u32[]{:S(2)}, u32[]{:S(2)}) collective-permute-start(bf16[128,2560]{1,0:T(8,128)(2,1)} %param.6), channel_id=1, source_target_pairs={{0,2},{2,0},{4,6},{6,4},{8,10},{10,8},{12,14},{14,12},{1,3},{3,1},... | collective-permute-start | bytes 1966088 | tf_op jit(solution)/shard_map/ppermute | solution.py:111
  11.0 8.9 %collective-permute-done = bf16[64,2560]{1,0:T(8,128)(2,1)} collective-permute-done((bf16[64,2560]{1,0:T(8,128)(2,1)}, bf16[64,2560]{1,0:T(8,128)(2,1)}, u32[]{:S(2)}, u32[]{:S(2)}) %collective-permute-start) | collective-permute-done | bytes 327712 | tf_op jit(solution)/shard_map/ppermute | solution.py:152
  20.1 3.8 %collective-permute-start.9 = (bf16[64,2560]{1,0:T(8,128)(2,1)}, bf16[64,2560]{1,0:T(8,128)(2,1)}, u32[]{:S(2)}, u32[]{:S(2)}) collective-permute-start(bf16[64,2560]{1,0:T(8,128)(2,1)} %bitcast.11), channel_id=1, source_target_pairs={{0,4},{2,6},{4,0},{6,2},{8,12},{10,14},{12,8},{14,10},{1,5},{3,7},... | collective-permute-start | bytes 983048 | tf_op jit(solution)/shard_map/ppermute | solution.py:111
  23.9 1.5 %collective-permute-start.8 = (bf16[128,2560]{1,0:T(8,128)(2,1)}, bf16[128,2560]{1,0:T(8,128)(2,1)}, u32[]{:S(2)}, u32[]{:S(2)}) collective-permute-start(bf16[128,2560]{1,0:T(8,128)(2,1)} %param.7), channel_id=1, source_target_pairs={{0,2},{2,0},{4,6},{6,4},{8,10},{10,8},{12,14},{14,12},{1,3},{3,1},... | collective-permute-start | bytes 1966088 | tf_op jit(solution)/shard_map/ppermute | solution.py:111
  25.4 1.3 %collective-permute-start.6 = (bf16[64,2560]{1,0:T(8,128)(2,1)}, bf16[64,2560]{1,0:T(8,128)(2,1)S(1)}, u32[]{:S(2)}, u32[]{:S(2)}) collective-permute-start(bf16[64,2560]{1,0:T(8,128)(2,1)} %collective-permute-done), channel_id=1, source_target_pairs={{0,16},{16,0},{1,17},{17,1},{2,18},{18,2},{3,19},{19,3},{4,20},{20... | collective-permute-start | bytes 983048 | tf_op jit(solution)/shard_map/ppermute | solution.py:156
  26.8 7.6 %collective-permute-done.6 = bf16[64,2560]{1,0:T(8,128)(2,1)S(1)} collective-permute-done((bf16[64,2560]{1,0:T(8,128)(2,1)}, bf16[64,2560]{1,0:T(8,128)(2,1)S(1)}, u32[]{:S(2)}, u32[]{:S(2)}) %collective-permute-start.6) | collective-permute-done | bytes 327712 | tf_op jit(solution)/shard_map/ppermute | solution.py:156
  34.5 1.7 %fusion.40 = f32[256,256]{1,0:T(8,128)S(1)} fusion(bf16[256,2560]{1,0:T(8,128)(2,1)S(1)} %constant_dynamic-update-slice_fusion, bf16[64,2560]{1,0:T(8,128)(2,1)S(1)} %collective-permute-done.6, bf16[64,2560]{1,0:T(8,128)(2,1)} %collective-permute-done, bf16[64,2560]{1,0:T(8,128)(2,1)} %collective-permute-done.5, bf16[64,2560]{1,0:T(8,128)(2,1)S(1)} %bitcast.30), kind=kOutput, calls=%fused_computation.67 | convolution fusion | flops 340787200 | bytes 2883584 | tf_op jit(solution)/shard_map/dot_general | solution.py:10
  37.1 2.0 %collective-permute-start.2 = (f32[1,256]{1,0:T(1,128)S(1)}, f32[1,256]{1,0:T(1,128)S(1)}, u32[]{:S(2)}, u32[]{:S(2)}) collective-permute-start(f32[1,256]{1,0:T(1,128)S(1)} %copy-done.1), channel_id=1, source_target_pairs={{0,4},{2,6},{4,0},{6,2},{8,12},{10,14},{12,8},{14,10},{1,5},{3,7},... | collective-permute-start | bytes 3080 | tf_op jit(solution)/shard_map/ppermute | solution.py:111
  45.3 1.8 %collective-permute-start.12 = (bf16[64,2560]{1,0:T(8,128)(2,1)S(1)}, bf16[64,2560]{1,0:T(8,128)(2,1)S(1)}, u32[]{:S(2)}, u32[]{:S(2)}) collective-permute-start(bf16[64,2560]{1,0:T(8,128)(2,1)S(1)} %fusion.22), channel_id=1, source_target_pairs={{0,4},{2,6},{4,0},{6,2},{8,12},{10,14},{12,8},{14,10},{1,5},{3,7},... | collective-permute-start | bytes 983048 | tf_op jit(solution)/shard_map/ppermute | solution.py:111
  47.7 8.2 %collective-permute-done.12 = bf16[64,2560]{1,0:T(8,128)(2,1)S(1)} collective-permute-done((bf16[64,2560]{1,0:T(8,128)(2,1)S(1)}, bf16[64,2560]{1,0:T(8,128)(2,1)S(1)}, u32[]{:S(2)}, u32[]{:S(2)}) %collective-permute-start.12) | collective-permute-done | bytes 327712 | tf_op jit(solution)/shard_map/ppermute | solution.py:111
  56.0 1.7 %fusion.39 = f32[256,256]{1,0:T(8,128)S(1)} fusion(bf16[256,2560]{1,0:T(8,128)(2,1)S(1)} %constant_dynamic-update-slice_fusion.2, bf16[64,2560]{1,0:T(8,128)(2,1)S(1)} %collective-permute-done.11, bf16[64,2560]{1,0:T(8,128)(2,1)} %collective-permute-done.10, bf16[64,2560]{1,0:T(8,128)(2,1)} %collective-permute-done.9, bf16[64,2560]{1,0:T(8,128)(2,1)} %bitcast.11), kind=kOutput, calls=%fused_computation.66 | convolution fusion | flops 340787200 | bytes 2883584 | tf_op jit(solution)/shard_map/dot_general | solution.py:10
  59.0 1.5 %convolution_convert_fusion.1 = bf16[128,2560]{1,0:T(8,128)(2,1)S(1)} fusion(bf16[256,256]{1,0:T(8,128)(2,1)S(1)} %multiply_convert_fusion.3, bf16[64,2560]{1,0:T(8,128)(2,1)S(1)} %collective-permute-done.11, bf16[64,2560]{1,0:T(8,128)(2,1)} %collective-permute-done.10, bf16[64,2560]{1,0:T(8,128)(2,1)} %collective-permute-done.9, bf16[64,2560]{1,0:T(8,128)(2,1)} %bitcast.11), kind=kOutput, calls=%fused_computation.4 | convolution fusion | flops 173342720 | bytes 2031616 | tf_op jit(solution)/shard_map/dot_general | solution.py:190
  63.0 2.1 %collective-permute-start.17 = (bf16[64,2560]{1,0:T(8,128)(2,1)S(1)}, bf16[64,2560]{1,0:T(8,128)(2,1)S(1)}, u32[]{:S(2)}, u32[]{:S(2)}) collective-permute-start(bf16[64,2560]{1,0:T(8,128)(2,1)S(1)} %fusion.18), channel_id=1, source_target_pairs={{0,4},{2,6},{4,0},{6,2},{8,12},{10,14},{12,8},{14,10},{1,5},{3,7},... | collective-permute-start | bytes 983048 | tf_op jit(solution)/shard_map/ppermute | solution.py:111
  65.1 1.4 %convolution_convert_fusion = bf16[128,2560]{1,0:T(8,128)(2,1)S(1)} fusion(bf16[256,256]{1,0:T(8,128)(2,1)S(1)} %multiply_convert_fusion.2, bf16[64,2560]{1,0:T(8,128)(2,1)S(1)} %copy-done.5, bf16[64,2560]{1,0:T(8,128)(2,1)} %collective-permute-done, bf16[64,2560]{1,0:T(8,128)(2,1)} %collective-permute-done.5, bf16[64,2560]{1,0:T(8,128)(2,1)S(1)} %bitcast.31), kind=kOutput, calls=%fused_computation.3 | convolution fusion | flops 173342720 | bytes 2031616 | tf_op jit(solution)/shard_map/dot_general | solution.py:190
  66.5 1.6 %collective-permute-start.15 = (bf16[128,2560]{1,0:T(8,128)(2,1)S(1)}, bf16[128,2560]{1,0:T(8,128)(2,1)S(1)}, u32[]{:S(2)}, u32[]{:S(2)}) collective-permute-start(bf16[128,2560]{1,0:T(8,128)(2,1)S(1)} %convolution_convert_fusion), channel_id=1, source_target_pairs={{0,2},{2,0},{4,6},{6,4},{8,10},{10,8},{12,14},{14,12},{1,3},{3,1},... | collective-permute-start | bytes 1966088 | tf_op jit(solution)/shard_map/ppermute | solution.py:111
  68.1 8.0 %collective-permute-done.20 = bf16[64,2560]{1,0:T(8,128)(2,1)S(1)} collective-permute-done((bf16[64,2560]{1,0:T(8,128)(2,1)S(1)}, bf16[64,2560]{1,0:T(8,128)(2,1)S(1)}, u32[]{:S(2)}, u32[]{:S(2)}) %collective-permute-start.20) | collective-permute-done | bytes 327712 | tf_op jit(solution)/shard_map/ppermute | solution.py:111
  76.9 1.7 %collective-permute-done.17 = bf16[64,2560]{1,0:T(8,128)(2,1)S(1)} collective-permute-done((bf16[64,2560]{1,0:T(8,128)(2,1)S(1)}, bf16[64,2560]{1,0:T(8,128)(2,1)S(1)}, u32[]{:S(2)}, u32[]{:S(2)}) %collective-permute-start.17) | collective-permute-done | bytes 327712 | tf_op jit(solution)/shard_map/ppermute | solution.py:111
  78.7 5.5 %collective-permute-start.19 = (bf16[64,2560]{1,0:T(8,128)(2,1)S(1)}, bf16[64,2560]{1,0:T(8,128)(2,1)S(1)}, u32[]{:S(2)}, u32[]{:S(2)}) collective-permute-start(bf16[64,2560]{1,0:T(8,128)(2,1)S(1)} %add_convert_fusion.2), channel_id=1, source_target_pairs={{0,8},{2,10},{4,12},{6,14},{8,0},{10,2},{12,4},{14,6},{1,9},{3,11}... | collective-permute-start | bytes 983048 | tf_op jit(solution)/shard_map/ppermute | solution.py:111
  84.2 2.4 %add_convert_fusion = bf16[128,2560]{1,0:T(8,128)(2,1)} fusion(bf16[128,2560]{1,0:T(8,128)(2,1)S(1)} %collective-permute-done.13, bf16[256,256]{1,0:T(8,128)(2,1)S(1)} %multiply_convert_fusion.3, bf16[64,2560]{1,0:T(8,128)(2,1)S(1)} %collective-permute-done.11, bf16[64,2560]{1,0:T(8,128)(2,1)} %collective-permute-done.10, ...), kind=kOutput, calls=%fused_computation.7 | convolution fusion | flops 173998080 | bytes 2686976 | tf_op jit(solution)/shard_map/dot_general | solution.py:194
  86.6 5.0 %collective-permute-done.15 = bf16[128,2560]{1,0:T(8,128)(2,1)S(1)} collective-permute-done((bf16[128,2560]{1,0:T(8,128)(2,1)S(1)}, bf16[128,2560]{1,0:T(8,128)(2,1)S(1)}, u32[]{:S(2)}, u32[]{:S(2)}) %collective-permute-start.15) | collective-permute-done | bytes 655392 | tf_op jit(solution)/shard_map/ppermute | solution.py:111
  91.5 2.3 %fusion = bf16[128,2560]{1,0:T(8,128)(2,1)} fusion(bf16[128,2560]{1,0:T(8,128)(2,1)S(1)} %collective-permute-done.15, bf16[256,256]{1,0:T(8,128)(2,1)S(1)} %multiply_convert_fusion.2, bf16[64,2560]{1,0:T(8,128)(2,1)S(1)} %copy-done.5, bf16[64,2560]{1,0:T(8,128)(2,1)} %collective-permute-done, bf16[64,2560]{1,0:T(8,128)(2,1)} %collective-permute-done.5, ...), kind=kOutput, calls=%fused_computation.2 | convolution fusion | flops 173998080 | bytes 2686976 | tf_op jit(solution)/shard_map/dot_general | solution.py:194
  94.3 3.7 %collective-permute-done.19 = bf16[64,2560]{1,0:T(8,128)(2,1)S(1)} collective-permute-done((bf16[64,2560]{1,0:T(8,128)(2,1)S(1)}, bf16[64,2560]{1,0:T(8,128)(2,1)S(1)}, u32[]{:S(2)}, u32[]{:S(2)}) %collective-permute-start.19) | collective-permute-done | bytes 327712 | tf_op jit(solution)/shard_map/ppermute | solution.py:111
  (68 shorter events, 17.2 us)
Async XLA Ops:
  0.6 7.3 %copy-start = (s32[8,256]{1,0:T(8,128)S(1)}, s32[8,256]{1,0:T(8,128)}, u32[]{:S(2)}) copy-start(s32[8,256]{1,0:T(8,128)} %param.10) | copy-start | bytes 24580
  0.6 19.3 %collective-permute-start = (bf16[64,2560]{1,0:T(8,128)(2,1)}, bf16[64,2560]{1,0:T(8,128)(2,1)}, u32[]{:S(2)}, u32[]{:S(2)}) collective-permute-start(bf16[64,2560]{1,0:T(8,128)(2,1)} %bitcast.28), channel_id=1, source_target_pairs={{0,8},{2,10},{4,12},{6,14},{8,0},{10,2},{12,4},{14,6},{16,28},{18,... | collective-permute-start | bytes 983048 | tf_op jit(solution)/shard_map/ppermute | solution.py:152
  4.7 15.3 %collective-permute-start.5 = (bf16[64,2560]{1,0:T(8,128)(2,1)}, bf16[64,2560]{1,0:T(8,128)(2,1)}, u32[]{:S(2)}, u32[]{:S(2)}) collective-permute-start(bf16[64,2560]{1,0:T(8,128)(2,1)} %bitcast.29), channel_id=1, source_target_pairs={{0,4},{2,6},{4,0},{6,2},{8,12},{10,14},{12,8},{14,10},{1,5},{3,7},... | collective-permute-start | bytes 983048 | tf_op jit(solution)/shard_map/ppermute | solution.py:111
  6.3 20.4 %collective-permute-start.1 = (bf16[128,2560]{1,0:T(8,128)(2,1)}, bf16[128,2560]{1,0:T(8,128)(2,1)S(1)}, u32[]{:S(2)}, u32[]{:S(2)}) collective-permute-start(bf16[128,2560]{1,0:T(8,128)(2,1)} %param.6), channel_id=1, source_target_pairs={{0,2},{2,0},{4,6},{6,4},{8,10},{10,8},{12,14},{14,12},{1,3},{3,1},... | collective-permute-start | bytes 1966088 | tf_op jit(solution)/shard_map/ppermute | solution.py:111
  8.7 18.1 %copy-start.1 = (f32[1,256]{1,0:T(1,128)S(1)}, f32[1,256]{1,0:T(1,128)}, u32[]{:S(2)}) copy-start(f32[1,256]{1,0:T(1,128)} %param.11) | copy-start | bytes 3076
  9.8 24.7 %copy-start.2 = (bf16[1,64,2560]{2,1,0:T(8,128)(2,1)S(1)}, bf16[1,64,2560]{2,1,0:T(8,128)(2,1)}, u32[]{:S(2)}) copy-start(bf16[1,64,2560]{2,1,0:T(8,128)(2,1)} %param.8) | copy-start | bytes 983044
  19.9 22.6 %collective-permute-start.10 = (bf16[64,2560]{1,0:T(8,128)(2,1)}, bf16[64,2560]{1,0:T(8,128)(2,1)}, u32[]{:S(2)}, u32[]{:S(2)}) collective-permute-start(bf16[64,2560]{1,0:T(8,128)(2,1)} %bitcast.11), channel_id=1, source_target_pairs={{0,8},{2,10},{4,12},{6,14},{8,0},{10,2},{12,4},{14,6},{16,28},{18,... | collective-permute-start | bytes 983048 | tf_op jit(solution)/shard_map/ppermute | solution.py:157
  20.1 22.4 %collective-permute-start.9 = (bf16[64,2560]{1,0:T(8,128)(2,1)}, bf16[64,2560]{1,0:T(8,128)(2,1)}, u32[]{:S(2)}, u32[]{:S(2)}) collective-permute-start(bf16[64,2560]{1,0:T(8,128)(2,1)} %bitcast.11), channel_id=1, source_target_pairs={{0,4},{2,6},{4,0},{6,2},{8,12},{10,14},{12,8},{14,10},{1,5},{3,7},... | collective-permute-start | bytes 983048 | tf_op jit(solution)/shard_map/ppermute | solution.py:111
  23.9 18.6 %collective-permute-start.8 = (bf16[128,2560]{1,0:T(8,128)(2,1)}, bf16[128,2560]{1,0:T(8,128)(2,1)}, u32[]{:S(2)}, u32[]{:S(2)}) collective-permute-start(bf16[128,2560]{1,0:T(8,128)(2,1)} %param.7), channel_id=1, source_target_pairs={{0,2},{2,0},{4,6},{6,4},{8,10},{10,8},{12,14},{14,12},{1,3},{3,1},... | collective-permute-start | bytes 1966088 | tf_op jit(solution)/shard_map/ppermute | solution.py:111
  25.4 9.0 %collective-permute-start.6 = (bf16[64,2560]{1,0:T(8,128)(2,1)}, bf16[64,2560]{1,0:T(8,128)(2,1)S(1)}, u32[]{:S(2)}, u32[]{:S(2)}) collective-permute-start(bf16[64,2560]{1,0:T(8,128)(2,1)} %collective-permute-done), channel_id=1, source_target_pairs={{0,16},{16,0},{1,17},{17,1},{2,18},{18,2},{3,19},{19,3},{4,20},{20... | collective-permute-start | bytes 983048 | tf_op jit(solution)/shard_map/ppermute | solution.py:156
  26.7 10.4 %collective-permute-start.3 = (f32[1,256]{1,0:T(1,128)S(1)}, f32[1,256]{1,0:T(1,128)S(1)}, u32[]{:S(2)}, u32[]{:S(2)}) collective-permute-start(f32[1,256]{1,0:T(1,128)S(1)} %copy-done.1), channel_id=1, source_target_pairs={{0,8},{2,10},{4,12},{6,14},{8,0},{10,2},{12,4},{14,6},{1,9},{3,11}... | collective-permute-start | bytes 3080 | tf_op jit(solution)/shard_map/ppermute | solution.py:111
  34.4 5.4 %collective-permute-start.4 = (f32[1,256]{1,0:T(1,128)S(1)}, f32[1,256]{1,0:T(1,128)S(1)}, u32[]{:S(2)}, u32[]{:S(2)}) collective-permute-start(f32[1,256]{1,0:T(1,128)S(1)} %copy-done.1), channel_id=1, source_target_pairs={{0,12},{2,14},{4,8},{6,10},{8,4},{10,6},{12,0},{14,2},{1,13},{3,15... | collective-permute-start | bytes 3080 | tf_op jit(solution)/shard_map/ppermute | solution.py:111
  37.1 3.6 %collective-permute-start.2 = (f32[1,256]{1,0:T(1,128)S(1)}, f32[1,256]{1,0:T(1,128)S(1)}, u32[]{:S(2)}, u32[]{:S(2)}) collective-permute-start(f32[1,256]{1,0:T(1,128)S(1)} %copy-done.1), channel_id=1, source_target_pairs={{0,4},{2,6},{4,0},{6,2},{8,12},{10,14},{12,8},{14,10},{1,5},{3,7},... | collective-permute-start | bytes 3080 | tf_op jit(solution)/shard_map/ppermute | solution.py:111
  39.8 1.7 %collective-permute-start.7 = (f32[256,256]{1,0:T(8,128)S(1)}, f32[256,256]{1,0:T(8,128)}, u32[]{:S(2)}, u32[]{:S(2)}) collective-permute-start(f32[256,256]{1,0:T(8,128)S(1)} %fusion.40), channel_id=1, source_target_pairs={{0,1},{1,0},{2,3},{3,2},{4,5},{5,4},{6,7},{7,6},{8,9},{9,8},{10,11... | collective-permute-start | bytes 786440 | tf_op jit(solution)/shard_map/ppermute | solution.py:135
  45.3 10.6 %collective-permute-start.12 = (bf16[64,2560]{1,0:T(8,128)(2,1)S(1)}, bf16[64,2560]{1,0:T(8,128)(2,1)S(1)}, u32[]{:S(2)}, u32[]{:S(2)}) collective-permute-start(bf16[64,2560]{1,0:T(8,128)(2,1)S(1)} %fusion.22), channel_id=1, source_target_pairs={{0,4},{2,6},{4,0},{6,2},{8,12},{10,14},{12,8},{14,10},{1,5},{3,7},... | collective-permute-start | bytes 983048 | tf_op jit(solution)/shard_map/ppermute | solution.py:111
  47.1 8.8 %collective-permute-start.11 = (bf16[64,2560]{1,0:T(8,128)(2,1)}, bf16[64,2560]{1,0:T(8,128)(2,1)S(1)}, u32[]{:S(2)}, u32[]{:S(2)}) collective-permute-start(bf16[64,2560]{1,0:T(8,128)(2,1)} %collective-permute-done.10), channel_id=1, source_target_pairs={{0,16},{16,0},{1,17},{17,1},{2,18},{18,2},{3,19},{19,3},{4,20},{20... | collective-permute-start | bytes 983048 | tf_op jit(solution)/shard_map/ppermute | solution.py:160
  47.1 21.0 %collective-permute-start.16 = (bf16[64,2560]{1,0:T(8,128)(2,1)S(1)}, bf16[64,2560]{1,0:T(8,128)(2,1)S(1)}, u32[]{:S(2)}, u32[]{:S(2)}) collective-permute-start(bf16[64,2560]{1,0:T(8,128)(2,1)S(1)} %fusion.10), channel_id=1, source_target_pairs={{0,4},{2,6},{4,0},{6,2},{8,12},{10,14},{12,8},{14,10},{1,5},{3,7},... | collective-permute-start | bytes 983048 | tf_op jit(solution)/shard_map/ppermute | solution.py:111
  57.7 3.5 %collective-permute-start.14 = (f32[256,256]{1,0:T(8,128)S(1)}, f32[256,256]{1,0:T(8,128)S(1)}, u32[]{:S(2)}, u32[]{:S(2)}) collective-permute-start(f32[256,256]{1,0:T(8,128)S(1)} %fusion.39), channel_id=1, source_target_pairs={{0,1},{1,0},{2,3},{3,2},{4,5},{5,4},{6,7},{7,6},{8,9},{9,8},{10,11... | collective-permute-start | bytes 786440 | tf_op jit(solution)/shard_map/ppermute | solution.py:135
  57.8 18.2 %collective-permute-start.20 = (bf16[64,2560]{1,0:T(8,128)(2,1)S(1)}, bf16[64,2560]{1,0:T(8,128)(2,1)S(1)}, u32[]{:S(2)}, u32[]{:S(2)}) collective-permute-start(bf16[64,2560]{1,0:T(8,128)(2,1)S(1)} %add_convert_fusion.1), channel_id=1, source_target_pairs={{0,8},{2,10},{4,12},{6,14},{8,0},{10,2},{12,4},{14,6},{1,9},{3,11}... | collective-permute-start | bytes 983048 | tf_op jit(solution)/shard_map/ppermute | solution.py:111
  60.6 23.6 %collective-permute-start.13 = (bf16[128,2560]{1,0:T(8,128)(2,1)S(1)}, bf16[128,2560]{1,0:T(8,128)(2,1)S(1)}, u32[]{:S(2)}, u32[]{:S(2)}) collective-permute-start(bf16[128,2560]{1,0:T(8,128)(2,1)S(1)} %convolution_convert_fusion.1), channel_id=1, source_target_pairs={{0,2},{2,0},{4,6},{6,4},{8,10},{10,8},{12,14},{14,12},{1,3},{3,1},... | collective-permute-start | bytes 1966088 | tf_op jit(solution)/shard_map/ppermute | solution.py:111
  63.0 15.6 %collective-permute-start.17 = (bf16[64,2560]{1,0:T(8,128)(2,1)S(1)}, bf16[64,2560]{1,0:T(8,128)(2,1)S(1)}, u32[]{:S(2)}, u32[]{:S(2)}) collective-permute-start(bf16[64,2560]{1,0:T(8,128)(2,1)S(1)} %fusion.18), channel_id=1, source_target_pairs={{0,4},{2,6},{4,0},{6,2},{8,12},{10,14},{12,8},{14,10},{1,5},{3,7},... | collective-permute-start | bytes 983048 | tf_op jit(solution)/shard_map/ppermute | solution.py:111
  66.5 25.0 %collective-permute-start.15 = (bf16[128,2560]{1,0:T(8,128)(2,1)S(1)}, bf16[128,2560]{1,0:T(8,128)(2,1)S(1)}, u32[]{:S(2)}, u32[]{:S(2)}) collective-permute-start(bf16[128,2560]{1,0:T(8,128)(2,1)S(1)} %convolution_convert_fusion), channel_id=1, source_target_pairs={{0,2},{2,0},{4,6},{6,4},{8,10},{10,8},{12,14},{14,12},{1,3},{3,1},... | collective-permute-start | bytes 1966088 | tf_op jit(solution)/shard_map/ppermute | solution.py:111
  78.6 15.7 %collective-permute-start.18 = (bf16[64,2560]{1,0:T(8,128)(2,1)S(1)}, bf16[64,2560]{1,0:T(8,128)(2,1)S(1)}, u32[]{:S(2)}, u32[]{:S(2)}) collective-permute-start(bf16[64,2560]{1,0:T(8,128)(2,1)S(1)} %fusion.3), channel_id=1, source_target_pairs={{0,4},{2,6},{4,0},{6,2},{8,12},{10,14},{12,8},{14,10},{1,5},{3,7},... | collective-permute-start | bytes 983048 | tf_op jit(solution)/shard_map/ppermute | solution.py:111
  78.7 19.2 %collective-permute-start.19 = (bf16[64,2560]{1,0:T(8,128)(2,1)S(1)}, bf16[64,2560]{1,0:T(8,128)(2,1)S(1)}, u32[]{:S(2)}, u32[]{:S(2)}) collective-permute-start(bf16[64,2560]{1,0:T(8,128)(2,1)S(1)} %add_convert_fusion.2), channel_id=1, source_target_pairs={{0,8},{2,10},{4,12},{6,14},{8,0},{10,2},{12,4},{14,6},{1,9},{3,11}... | collective-permute-start | bytes 983048 | tf_op jit(solution)/shard_map/ppermute | solution.py:111
  (3 other events, 6.9 us)

commit v7 on v6

--- a/solution.py
+++ b/solution.py
@@ -127,7 +127,7 @@
 
 
 def partial_sums(weights, rows):
-    parts = [contract_first(weight, rows) for weight in weights]
+    parts = [jnp.dot(weight, rows, preferred_element_type=jnp.float32) for weight in weights]
     return lax.optimization_barrier((parts, [narrow(part) for part in parts[1:]]))
 
 
@@ -135,66 +135,79 @@
     return partial + lax.ppermute(partial, "tensor", SWAP)
 
 
-def gather_gates(gating, earlier):
-    later = after(gating, earlier)
-    return [gating] + [move(later, xor_line(bit)) for bit in (1, 2, 3)]
+LANES = 128
+
+
+def gate_columns(gating, rows):
+    pieces, rest = [], gating
+    for _ in range(3):
+        piece = lax.reduce_precision(rest, exponent_bits=8, mantissa_bits=7)
+        pieces.append(narrow(piece).reshape(-1, LANES))
+        rest = rest - piece
+    columns = jnp.concatenate(pieces)
+    return jnp.pad(columns, ((0, rows - columns.shape[0]), (0, 0)))
+
+
+def gates_of(columns, capacity):
+    pieces = columns[: 3 * capacity // LANES].reshape(3, 1, capacity)
+    return jnp.sum(pieces.astype(jnp.float32), axis=0)
 
 
 def by_pairs(tokens, cotangent, down_adapter, up_adapter, token_lists, gating):
     me = lax.axis_index("adapter")
     first_group = lax.axis_index("groups") == 0
-    tok_local = tokens.shape[0]
+    tok_local, width = tokens.shape
     capacity = gating.shape[1]
     down_matrix = down_adapter[0]
     up_matrix = up_adapter[0]
     rank = down_matrix.shape[0]
 
-    far_down = lax.ppermute(down_matrix, ("groups", "adapter"), FAR)
+    message = jnp.concatenate([down_matrix, gate_columns(gating, rank)], axis=1)
+    far_down = lax.ppermute(message, ("groups", "adapter"), FAR)
     tokens2 = move(tokens, PARTNER)
-    near_down = move(down_matrix, xor_line(1))
-    cot2 = move(after(cotangent, far_down), PARTNER)
+    near_down = move(message, xor_line(1))
+    cot2 = move(cotangent, PARTNER)
+    far_up = lax.ppermute(up_matrix, ("groups", "adapter"), FAR)
     cross_down = lax.ppermute(far_down, "groups", SWAP)
-    far_up = lax.ppermute(after(up_matrix, far_down), ("groups", "adapter"), FAR)
-    near_up = move(after(up_matrix, near_down), xor_line(1))
-    cot2, near_up, far_up = lax.optimization_barrier((cot2, near_up, far_up))
-    cross_up = lax.ppermute(far_up, "groups", SWAP)
-    gates = gather_gates(gating, (far_down, tokens2))
-
+    near_up = move(jnp.concatenate([up_matrix, far_down[:, width:]], axis=1), xor_line(1))
+
+    gates = [gating] + [gates_of(m[:, width:], capacity) for m in (near_down, far_down, near_up)]
+    near_down, far_down, cross_down, near_up = (
+        m[:, :width] for m in (near_down, far_down, cross_down, near_up)
+    )
     far_bit = jnp.where(first_group, 2, 3)
     experts = jnp.stack([me, me ^ 2, me ^ (2 * far_bit), me ^ (2 * (far_bit ^ 1))])
     lists = jnp.take(token_lists, experts, axis=0)
-    far_gate = jnp.where(first_group, gates[2], gates[3])
-    cross_gate = jnp.where(first_group, gates[3], gates[2])
-    gate_rows = adapter_scale_factor * jnp.concatenate([gates[0], gates[1], far_gate, cross_gate])
+    gate_rows = adapter_scale_factor * jnp.concatenate(gates)
     token_ids = jnp.arange(tok_local, dtype=jnp.int32)
     ids = jnp.concatenate([me * tok_local + token_ids, (me ^ 1) * tok_local + token_ids])
-    taken = ids[:, None, None] == lists[None, :, :]
-    scale = jnp.sum(jnp.where(taken, gate_rows[None, :, :], 0.0), axis=2)
-    scale = jnp.repeat(scale, rank, axis=1)
+    taken = lists[:, :, None] == ids[None, None, :]
+    scale = jnp.sum(jnp.where(taken, gate_rows[:, :, None], 0.0), axis=1)
 
     tokens2 = jnp.concatenate([tokens, tokens2], axis=0)
+    down_all = jnp.concatenate([down_matrix, near_down, far_down, cross_down], axis=0)
+
+    def low_rank(rows, matrices):
+        product = both_cores(contract_last(matrices, rows))
+        return narrow(scale[:, None, :] * product.reshape(-1, rank, 2 * tok_local))
+
+    def for_line(low):
+        second = jnp.where(first_group, low[2], low[3])
+        third = jnp.where(first_group, low[3], low[2])
+        return low[0], low[1], second, third
+
+    def outward_start(low, matrix):
+        weights = low[:, :, tok_local:].reshape(-1, tok_local)
+        return move(narrow(contract_first(weights, matrix)), PARTNER)
+
+    def outward_end(low, matrix, back):
+        weights = low[:, :, :tok_local].reshape(-1, tok_local)
+        return narrow(contract_first(weights, matrix) + back.astype(jnp.float32))
+
+    low = low_rank(tokens2, down_all)
+    cot2, far_up, low = lax.optimization_barrier((cot2, far_up, low))
+    cross_up = lax.ppermute(far_up, "groups", SWAP)
     cot2 = jnp.concatenate([cotangent, cot2], axis=0)
-    down_all = jnp.concatenate([down_matrix, near_down, far_down, cross_down], axis=0)
-
-    def low_rank(rows, matrices, *earlier):
-        product = both_cores(contract_last(rows, matrices))
-        return narrow(scale * after(product, earlier))
-
-    def for_line(low):
-        own, near, far, cross = (low[:, k * rank : (k + 1) * rank] for k in range(4))
-        second = jnp.where(first_group, far, cross)
-        third = jnp.where(first_group, cross, far)
-        return own, near, second, third
-
-    def outward_start(weights, matrix):
-        theirs = jnp.dot(weights[tok_local:], matrix, preferred_element_type=jnp.float32)
-        return move(narrow(theirs), PARTNER)
-
-    def outward_end(weights, matrix, back):
-        mine = jnp.dot(weights[:tok_local], matrix, preferred_element_type=jnp.float32)
-        return narrow(mine + back.astype(jnp.float32))
-
-    low = low_rank(tokens2, down_all)
     (own, first, second, third), up_send = partial_sums(for_line(low), cot2)
     up_third = move(up_send[2], xor_line(1))
     up_first = move(up_send[0], xor_line(1))

time: 99.2 us -> 99.8 us (level)
  other arithmetic: 3.53 us -> 8.15 us
  matrix products: 14.3 us -> 9.93 us
  local copies, waits for them, and re-layouts: 4.24 us -> 8.3 us
  starting transfers between devices: 29.3 us -> 25.7 us
    ppermute x15 -> x12, starting transfers between devices: 23.8 us -> 17.2 us  [move(): return lax.ppermute(value, 'adapter', pairs)]
    dot_general x4 -> x8, matrix products: 7.55 us -> 2.84 us  [partial_sums(): jnp.dot(weight, rows, preferred_element_type=jnp.float32)]
    ppermute x1, waiting for transfers between devices: 7.62 us -> 3.44 us  [by_pairs(): cross_down = lax.ppermute(far_down, 'groups', SWAP)]
    slice x0 -> x7, local copies, waits for them, and re-layouts: none -> 3.93 us  [the longest x4 3.16 us: by_pairs(): m[:, :width]]
    concatenate x0 -> x3, other arithmetic: none -> 2.74 us  [the longest x1 1.73 us: by_pairs(): message = jnp.concatenate([down_matrix, gate_columns(gating, rank)], axis=1)]
    ppermute x2, waiting for transfers between devices: 8.91 us -> 11.5 us  [the longest x1 11.5 us: by_pairs(): far_down = lax.ppermute(message, ('groups', 'adapter'), FAR)]
    convert_element_type x0 -> x3, other arithmetic: none -> 2.01 us  [gates_of(): return jnp.sum(pieces.astype(jnp.float32), axis=0)]
    dot_general x8 -> x4, matrix products: 3.41 us -> 5.06 us  [contract_first(): lax.dot_general(left_op, right_op, (((0,), (0,)), ((), ())), preferred_el...]
  transfers between devices with their start and end apart: 21 -> 18, of which waited for: 13 -> 9; matrix products, arithmetic and copies ran while one was open for 19% -> 20% of each run, Pallas kernels for 0% -> 0%
where the time goes in v7:
time: 99.8 us; the launch traced here: 99.1 us
  waiting for transfers between devices  46.1 us (46%)
  starting transfers between devices  25.7 us (26%)
  matrix products  9.93 us (10%)
  local copies, waits for them, and re-layouts  8.3 us (8%)
  other arithmetic  8.15 us (8%)
  between operations  1 us (1%)
    ppermute x12, waiting for transfers between devices, move(): return lax.ppermute(value, 'adapter', pairs)  31.1 us
    ppermute x12, starting transfers between devices, move(): return lax.ppermute(value, 'adapter', pairs)  17.2 us
    ppermute x1, waiting for transfers between devices, by_pairs(): far_down = lax.ppermute(message, ('groups', 'adapter'), FAR)  11.5 us
    dot_general x4, matrix products, contract_first(): lax.dot_general(left_op, right_op, (((0,), (0,)), ((), ())), preferred_el...  5.06 us
    ppermute x1, starting transfers between devices, by_pairs(): far_down = lax.ppermute(message, ('groups', 'adapter'), FAR)  4.04 us
    ppermute x1, waiting for transfers between devices, by_pairs(): cross_down = lax.ppermute(far_down, 'groups', SWAP)  3.44 us
    slice x4, local copies, waits for them, and re-layouts, by_pairs(): m[:, :width]  3.16 us
    dot_general x8, matrix products, partial_sums(): jnp.dot(weight, rows, preferred_element_type=jnp.float32)  2.84 us
  transfers between devices with their start and end apart: 18, of which 9 were waited for; matrix products, arithmetic and copies ran while one was open for 20% of the time, Pallas kernels for 0%

profile of v7, /device:TPU:0, one launch (start us, length us, event | category | flops | bytes accessed | tf_op | source)
XLA Modules:
  0.0 99.1 jit_solution(4055527185096806352)
XLA Ops:
  1.4 1.7 %pad_maximum_fusion.2 = bf16[64,2688]{1,0:T(8,128)(2,1)} fusion(bf16[64,128]{1,0:T(8,128)(2,1)S(1)} %fusion.39, bf16[64,2560]{1,0:T(8,128)(2,1)} %bitcast.73), kind=kLoop, calls=%fused_computation.13 | loop fusion | flops 688128 | bytes 688128 | tf_op jit(solution)/shard_map/concatenate | solution.py:165
  3.2 4.0 %collective-permute-start.3 = (bf16[64,2688]{1,0:T(8,128)(2,1)}, bf16[64,2688]{1,0:T(8,128)(2,1)}, u32[]{:S(2)}, u32[]{:S(2)}) collective-permute-start(bf16[64,2688]{1,0:T(8,128)(2,1)} %pad_maximum_fusion.2), channel_id=1, source_target_pairs={{0,8},{2,10},{4,12},{6,14},{8,0},{10,2},{12,4},{14,6},{16,28},{18,... | collective-permute-start | bytes 1032200 | tf_op jit(solution)/shard_map/ppermute | solution.py:166
  7.2 1.6 %collective-permute-start.2 = (bf16[64,2688]{1,0:T(8,128)(2,1)}, bf16[64,2688]{1,0:T(8,128)(2,1)}, u32[]{:S(2)}, u32[]{:S(2)}) collective-permute-start(bf16[64,2688]{1,0:T(8,128)(2,1)} %pad_maximum_fusion.2), channel_id=1, source_target_pairs={{0,4},{2,6},{4,0},{6,2},{8,12},{10,14},{12,8},{14,10},{1,5},{3,7},... | collective-permute-start | bytes 1032200 | tf_op jit(solution)/shard_map/ppermute | solution.py:111
  8.8 1.5 %collective-permute-start.6 = (bf16[128,2560]{1,0:T(8,128)(2,1)}, bf16[128,2560]{1,0:T(8,128)(2,1)}, u32[]{:S(2)}, u32[]{:S(2)}) collective-permute-start(bf16[128,2560]{1,0:T(8,128)(2,1)} %param.6), channel_id=1, source_target_pairs={{0,2},{2,0},{4,6},{6,4},{8,10},{10,8},{12,14},{14,12},{1,3},{3,1},... | collective-permute-start | bytes 1966088 | tf_op jit(solution)/shard_map/ppermute | solution.py:111
  13.2 11.5 %collective-permute-done.3 = bf16[64,2688]{1,0:T(8,128)(2,1)} collective-permute-done((bf16[64,2688]{1,0:T(8,128)(2,1)}, bf16[64,2688]{1,0:T(8,128)(2,1)}, u32[]{:S(2)}, u32[]{:S(2)}) %collective-permute-start.3) | collective-permute-done | bytes 344096 | tf_op jit(solution)/shard_map/ppermute | solution.py:166
  27.9 2.6 %collective-permute-start.5 = (bf16[64,2688]{1,0:T(8,128)(2,1)}, bf16[64,2688]{1,0:T(8,128)(2,1)S(1)}, u32[]{:S(2)}, u32[]{:S(2)}) collective-permute-start(bf16[64,2688]{1,0:T(8,128)(2,1)} %collective-permute-done.3), channel_id=1, source_target_pairs={{0,16},{16,0},{1,17},{17,1},{2,18},{18,2},{3,19},{19,3},{4,20},{20... | collective-permute-start | bytes 1032200 | tf_op jit(solution)/shard_map/ppermute | solution.py:171
  32.7 1.2 %constant_dynamic-update-slice_fusion = bf16[256,2560]{1,0:T(8,128)(2,1)S(1)} fusion(bf16[256,2560]{1,0:T(8,128)(2,1)S(1)} %constant_dynamic-update-slice_fusion.1, bf16[128,2560]{1,0:T(8,128)(2,1)} %collective-permute-done.6), kind=kLoop, calls=%fused_computation.59 | loop fusion | bytes 1310720 | tf_op jit(solution)/shard_map/concatenate | solution.py:187
  33.9 3.4 %collective-permute-done.5 = bf16[64,2688]{1,0:T(8,128)(2,1)S(1)} collective-permute-done((bf16[64,2688]{1,0:T(8,128)(2,1)}, bf16[64,2688]{1,0:T(8,128)(2,1)S(1)}, u32[]{:S(2)}, u32[]{:S(2)}) %collective-permute-start.5) | collective-permute-done | bytes 344096 | tf_op jit(solution)/shard_map/ppermute | solution.py:171
  38.1 2.1 %collective-permute-done.4 = bf16[64,2688]{1,0:T(8,128)(2,1)} collective-permute-done((bf16[64,2688]{1,0:T(8,128)(2,1)S(1)}, bf16[64,2688]{1,0:T(8,128)(2,1)}, u32[]{:S(2)}, u32[]{:S(2)}) %collective-permute-start.4) | collective-permute-done | bytes 344096 | tf_op jit(solution)/shard_map/ppermute | solution.py:111
  44.0 1.5 %collective-permute-start.8 = (bf16[64,2560]{1,0:T(8,128)(2,1)}, bf16[64,2560]{1,0:T(8,128)(2,1)S(1)}, u32[]{:S(2)}, u32[]{:S(2)}) collective-permute-start(bf16[64,2560]{1,0:T(8,128)(2,1)} %collective-permute-done.1), channel_id=1, source_target_pairs={{0,16},{16,0},{1,17},{17,1},{2,18},{18,2},{3,19},{19,3},{4,20},{20... | collective-permute-start | bytes 983048 | tf_op jit(solution)/shard_map/ppermute | solution.py:209
  47.1 7.5 %collective-permute-done.9 = bf16[64,2560]{1,0:T(8,128)(2,1)S(1)} collective-permute-done((bf16[64,2560]{1,0:T(8,128)(2,1)S(1)}, bf16[64,2560]{1,0:T(8,128)(2,1)S(1)}, u32[]{:S(2)}, u32[]{:S(2)}) %collective-permute-start.9) | collective-permute-done | bytes 327712 | tf_op jit(solution)/shard_map/ppermute | solution.py:111
  54.6 1.5 %fusion.47 = f32[256,256]{1,0:T(8,128)S(1)} fusion(bf16[256,2560]{1,0:T(8,128)(2,1)S(1)} %constant_dynamic-update-slice_fusion.2, bf16[64,2560]{1,0:T(8,128)(2,1)S(1)} %collective-permute-done.8, bf16[64,2560]{1,0:T(8,128)(2,1)} %collective-permute-done.1, bf16[64,2560]{1,0:T(8,128)(2,1)S(1)} %slice.99, bf16[64,2560]{1,0:T(8,128)(2,1)S(1)} %bitcast.70), kind=kOutput, calls=%fused_computation.86 | convolution fusion | flops 340787200 | bytes 2883584 | tf_op jit(solution)/shard_map/dot_general | solution.py:10
  56.3 4.8 %collective-permute-start.17 = (bf16[64,2560]{1,0:T(8,128)(2,1)S(1)}, bf16[64,2560]{1,0:T(8,128)(2,1)S(1)}, u32[]{:S(2)}, u32[]{:S(2)}) collective-permute-start(bf16[64,2560]{1,0:T(8,128)(2,1)S(1)} %add_convert_fusion.1), channel_id=1, source_target_pairs={{0,8},{2,10},{4,12},{6,14},{8,0},{10,2},{12,4},{14,6},{1,9},{3,11}... | collective-permute-start | bytes 983048 | tf_op jit(solution)/shard_map/ppermute | solution.py:111
  61.1 1.3 %convolution_convert_fusion.1 = bf16[128,2560]{1,0:T(8,128)(2,1)S(1)} fusion(bf16[256,128]{1,0:T(8,128)(2,1)S(1)} %bitcast.79, bf16[64,2560]{1,0:T(8,128)(2,1)S(1)} %collective-permute-done.8, bf16[64,2560]{1,0:T(8,128)(2,1)} %collective-permute-done.1, bf16[64,2560]{1,0:T(8,128)(2,1)S(1)} %slice.99, bf16[64,2560]{1,0:T(8,128)(2,1)S(1)} %bitcast.71), kind=kOutput, calls=%fused_computation.4 | convolution fusion | flops 173342720 | bytes 2031616 | tf_op jit(solution)/shard_map/dot_general | solution.py:16
  62.4 1.6 %collective-permute-start.10 = (bf16[128,2560]{1,0:T(8,128)(2,1)S(1)}, bf16[128,2560]{1,0:T(8,128)(2,1)S(1)}, u32[]{:S(2)}, u32[]{:S(2)}) collective-permute-start(bf16[128,2560]{1,0:T(8,128)(2,1)S(1)} %convolution_convert_fusion.1), channel_id=1, source_target_pairs={{0,2},{2,0},{4,6},{6,4},{8,10},{10,8},{12,14},{14,12},{1,3},{3,1},... | collective-permute-start | bytes 1966088 | tf_op jit(solution)/shard_map/ppermute | solution.py:111
  65.6 2.0 %collective-permute-start.14 = (bf16[64,2560]{1,0:T(8,128)(2,1)S(1)}, bf16[64,2560]{1,0:T(8,128)(2,1)S(1)}, u32[]{:S(2)}, u32[]{:S(2)}) collective-permute-start(bf16[64,2560]{1,0:T(8,128)(2,1)S(1)} %fusion.8), channel_id=1, source_target_pairs={{0,4},{2,6},{4,0},{6,2},{8,12},{10,14},{12,8},{14,10},{1,5},{3,7},... | collective-permute-start | bytes 983048 | tf_op jit(solution)/shard_map/ppermute | solution.py:111
  68.5 8.1 %collective-permute-done.17 = bf16[64,2560]{1,0:T(8,128)(2,1)S(1)} collective-permute-done((bf16[64,2560]{1,0:T(8,128)(2,1)S(1)}, bf16[64,2560]{1,0:T(8,128)(2,1)S(1)}, u32[]{:S(2)}, u32[]{:S(2)}) %collective-permute-start.17) | collective-permute-done | bytes 327712 | tf_op jit(solution)/shard_map/ppermute | solution.py:111
  77.4 3.1 %collective-permute-done.14 = bf16[64,2560]{1,0:T(8,128)(2,1)S(1)} collective-permute-done((bf16[64,2560]{1,0:T(8,128)(2,1)S(1)}, bf16[64,2560]{1,0:T(8,128)(2,1)S(1)}, u32[]{:S(2)}, u32[]{:S(2)}) %collective-permute-start.14) | collective-permute-done | bytes 327712 | tf_op jit(solution)/shard_map/ppermute | solution.py:111
  80.6 3.9 %collective-permute-start.16 = (bf16[64,2560]{1,0:T(8,128)(2,1)S(1)}, bf16[64,2560]{1,0:T(8,128)(2,1)S(1)}, u32[]{:S(2)}, u32[]{:S(2)}) collective-permute-start(bf16[64,2560]{1,0:T(8,128)(2,1)S(1)} %add_convert_fusion.2), channel_id=1, source_target_pairs={{0,8},{2,10},{4,12},{6,14},{8,0},{10,2},{12,4},{14,6},{1,9},{3,11}... | collective-permute-start | bytes 983048 | tf_op jit(solution)/shard_map/ppermute | solution.py:111
  84.6 2.2 %add_convert_fusion = bf16[128,2560]{1,0:T(8,128)(2,1)} fusion(bf16[128,2560]{1,0:T(8,128)(2,1)S(1)} %collective-permute-done.10, bf16[256,128]{1,0:T(8,128)(2,1)S(1)} %bitcast.77, bf16[64,2560]{1,0:T(8,128)(2,1)S(1)} %collective-permute-done.8, bf16[64,2560]{1,0:T(8,128)(2,1)} %collective-permute-done.1, bf16[64,2560]{1,0:T(8,128)(2,1)S(1)} %slice.99, ...), kind=kOutput, calls=%fused_computation.7 | convolution fusion | flops 173998080 | bytes 2686976 | tf_op jit(solution)/shard_map/dot_general | solution.py:16
  86.7 6.7 %collective-permute-done.12 = bf16[128,2560]{1,0:T(8,128)(2,1)S(1)} collective-permute-done((bf16[128,2560]{1,0:T(8,128)(2,1)S(1)}, bf16[128,2560]{1,0:T(8,128)(2,1)S(1)}, u32[]{:S(2)}, u32[]{:S(2)}) %collective-permute-start.12) | collective-permute-done | bytes 655392 | tf_op jit(solution)/shard_map/ppermute | solution.py:111
  93.4 1.2 %fusion = bf16[128,2560]{1,0:T(8,128)(2,1)} fusion(bf16[256,128]{1,0:T(8,128)(2,1)S(1)} %bitcast.78, bf16[128,2560]{1,0:T(8,128)(2,1)S(1)} %collective-permute-done.12, bf16[64,2560]{1,0:T(8,128)(2,1)S(1)} %copy-done.10, bf16[64,2560]{1,0:T(8,128)(2,1)S(1)} %copy-done.6, bf16[64,2560]{1,0:T(8,128)(2,1)S(1)} %copy-done.8, bf16[64,2560]{1,0:T(8,128)(2,1)S(1)} %bitcast.76), kind=kOutput, calls=%fused_computation.2 | convolution fusion | flops 173998080 | bytes 2686976 | tf_op jit(solution)/shard_map/dot_general | solution.py:16
  94.6 1.5 %collective-permute-done.15 = bf16[64,2560]{1,0:T(8,128)(2,1)S(1)} collective-permute-done((bf16[64,2560]{1,0:T(8,128)(2,1)S(1)}, bf16[64,2560]{1,0:T(8,128)(2,1)S(1)}, u32[]{:S(2)}, u32[]{:S(2)}) %collective-permute-start.15) | collective-permute-done | bytes 327712 | tf_op jit(solution)/shard_map/ppermute | solution.py:111
  96.1 2.2 %collective-permute-done.16 = bf16[64,2560]{1,0:T(8,128)(2,1)S(1)} collective-permute-done((bf16[64,2560]{1,0:T(8,128)(2,1)S(1)}, bf16[64,2560]{1,0:T(8,128)(2,1)S(1)}, u32[]{:S(2)}, u32[]{:S(2)}) %collective-permute-start.16) | collective-permute-done | bytes 327712 | tf_op jit(solution)/shard_map/ppermute | solution.py:111
  (91 shorter events, 19.5 us)
Async XLA Ops:
  0.6 11.8 %copy-start = (s32[8,256]{1,0:T(8,128)S(1)}, s32[8,256]{1,0:T(8,128)}, u32[]{:S(2)}) copy-start(s32[8,256]{1,0:T(8,128)} %param.10) | copy-start | bytes 24580
  0.6 12.5 %copy-start.1 = (bf16[128,2560]{1,0:T(8,128)(2,1)S(1)}, bf16[128,2560]{1,0:T(8,128)(2,1)}, u32[]{:S(2)}) copy-start(bf16[128,2560]{1,0:T(8,128)(2,1)} %param.7) | copy-start | bytes 1966084
  3.2 21.5 %collective-permute-start.3 = (bf16[64,2688]{1,0:T(8,128)(2,1)}, bf16[64,2688]{1,0:T(8,128)(2,1)}, u32[]{:S(2)}, u32[]{:S(2)}) collective-permute-start(bf16[64,2688]{1,0:T(8,128)(2,1)} %pad_maximum_fusion.2), channel_id=1, source_target_pairs={{0,8},{2,10},{4,12},{6,14},{8,0},{10,2},{12,4},{14,6},{16,28},{18,... | collective-permute-start | bytes 1032200 | tf_op jit(solution)/shard_map/ppermute | solution.py:166
  7.2 20.0 %collective-permute-start.2 = (bf16[64,2688]{1,0:T(8,128)(2,1)}, bf16[64,2688]{1,0:T(8,128)(2,1)}, u32[]{:S(2)}, u32[]{:S(2)}) collective-permute-start(bf16[64,2688]{1,0:T(8,128)(2,1)} %pad_maximum_fusion.2), channel_id=1, source_target_pairs={{0,4},{2,6},{4,0},{6,2},{8,12},{10,14},{12,8},{14,10},{1,5},{3,7},... | collective-permute-start | bytes 1032200 | tf_op jit(solution)/shard_map/ppermute | solution.py:111
  8.8 23.9 %collective-permute-start.6 = (bf16[128,2560]{1,0:T(8,128)(2,1)}, bf16[128,2560]{1,0:T(8,128)(2,1)}, u32[]{:S(2)}, u32[]{:S(2)}) collective-permute-start(bf16[128,2560]{1,0:T(8,128)(2,1)} %param.6), channel_id=1, source_target_pairs={{0,2},{2,0},{4,6},{6,4},{8,10},{10,8},{12,14},{14,12},{1,3},{3,1},... | collective-permute-start | bytes 1966088 | tf_op jit(solution)/shard_map/ppermute | solution.py:111
  10.3 31.1 %collective-permute-start.1 = (bf16[64,2560]{1,0:T(8,128)(2,1)}, bf16[64,2560]{1,0:T(8,128)(2,1)}, u32[]{:S(2)}, u32[]{:S(2)}) collective-permute-start(bf16[64,2560]{1,0:T(8,128)(2,1)} %bitcast.68), channel_id=1, source_target_pairs={{0,8},{2,10},{4,12},{6,14},{8,0},{10,2},{12,4},{14,6},{16,28},{18,... | collective-permute-start | bytes 983048 | tf_op jit(solution)/shard_map/ppermute | solution.py:170
  10.6 30.7 %collective-permute-start = (bf16[128,2560]{1,0:T(8,128)(2,1)}, bf16[128,2560]{1,0:T(8,128)(2,1)}, u32[]{:S(2)}, u32[]{:S(2)}) collective-permute-start(bf16[128,2560]{1,0:T(8,128)(2,1)} %param.7), channel_id=1, source_target_pairs={{0,2},{2,0},{4,6},{6,4},{8,10},{10,8},{12,14},{14,12},{1,3},{3,1},... | collective-permute-start | bytes 1966088 | tf_op jit(solution)/shard_map/ppermute | solution.py:111
  26.4 13.8 %collective-permute-start.4 = (bf16[64,2688]{1,0:T(8,128)(2,1)S(1)}, bf16[64,2688]{1,0:T(8,128)(2,1)}, u32[]{:S(2)}, u32[]{:S(2)}) collective-permute-start(bf16[64,2688]{1,0:T(8,128)(2,1)S(1)} %pad_maximum_fusion.3), channel_id=1, source_target_pairs={{0,4},{2,6},{4,0},{6,2},{8,12},{10,14},{12,8},{14,10},{1,5},{3,7},... | collective-permute-start | bytes 1032200 | tf_op jit(solution)/shard_map/ppermute | solution.py:111
  27.9 9.5 %collective-permute-start.5 = (bf16[64,2688]{1,0:T(8,128)(2,1)}, bf16[64,2688]{1,0:T(8,128)(2,1)S(1)}, u32[]{:S(2)}, u32[]{:S(2)}) collective-permute-start(bf16[64,2688]{1,0:T(8,128)(2,1)} %collective-permute-done.3), channel_id=1, source_target_pairs={{0,16},{16,0},{1,17},{17,1},{2,18},{18,2},{3,19},{19,3},{4,20},{20... | collective-permute-start | bytes 1032200 | tf_op jit(solution)/shard_map/ppermute | solution.py:171
  31.5 6.5 %copy-start.5 = (bf16[64,2560]{1,0:T(8,128)(2,1)}, bf16[64,2560]{1,0:T(8,128)(2,1)S(1)}, u32[]{:S(2)}) copy-start(bf16[64,2560]{1,0:T(8,128)(2,1)S(1)} %slice.97) | copy-start | bytes 983044
  31.5 5.9 %copy-start.3 = (bf16[1,64,2560]{2,1,0:T(8,128)(2,1)S(1)}, bf16[1,64,2560]{2,1,0:T(8,128)(2,1)}, u32[]{:S(2)}) copy-start(bf16[1,64,2560]{2,1,0:T(8,128)(2,1)} %param.8) | copy-start | bytes 983044
  32.6 5.3 %copy-start.7 = (bf16[64,2560]{1,0:T(8,128)(2,1)}, bf16[64,2560]{1,0:T(8,128)(2,1)S(1)}, u32[]{:S(2)}) copy-start(bf16[64,2560]{1,0:T(8,128)(2,1)S(1)} %slice.96) | copy-start | bytes 983044
  38.1 3.1 %collective-permute-start.7 = (f32[256,256]{1,0:T(8,128)S(1)}, f32[256,256]{1,0:T(8,128)S(1)}, u32[]{:S(2)}, u32[]{:S(2)}) collective-permute-start(f32[256,256]{1,0:T(8,128)S(1)} %fusion.46), channel_id=1, source_target_pairs={{0,1},{1,0},{2,3},{3,2},{4,5},{5,4},{6,7},{7,6},{8,9},{9,8},{10,11... | collective-permute-start | bytes 786440 | tf_op jit(solution)/shard_map/ppermute | solution.py:135
  43.6 11.1 %copy-start.2 = (bf16[1,64,2560]{2,1,0:T(8,128)(2,1)S(1)}, bf16[1,64,2560]{2,1,0:T(8,128)(2,1)}, u32[]{:S(2)}) copy-start(bf16[1,64,2560]{2,1,0:T(8,128)(2,1)} %param.9) | copy-start | bytes 983044
  43.9 10.7 %collective-permute-start.9 = (bf16[64,2560]{1,0:T(8,128)(2,1)S(1)}, bf16[64,2560]{1,0:T(8,128)(2,1)S(1)}, u32[]{:S(2)}, u32[]{:S(2)}) collective-permute-start(bf16[64,2560]{1,0:T(8,128)(2,1)S(1)} %fusion.12), channel_id=1, source_target_pairs={{0,4},{2,6},{4,0},{6,2},{8,12},{10,14},{12,8},{14,10},{1,5},{3,7},... | collective-permute-start | bytes 983048 | tf_op jit(solution)/shard_map/ppermute | solution.py:111
  44.0 10.6 %collective-permute-start.8 = (bf16[64,2560]{1,0:T(8,128)(2,1)}, bf16[64,2560]{1,0:T(8,128)(2,1)S(1)}, u32[]{:S(2)}, u32[]{:S(2)}) collective-permute-start(bf16[64,2560]{1,0:T(8,128)(2,1)} %collective-permute-done.1), channel_id=1, source_target_pairs={{0,16},{16,0},{1,17},{17,1},{2,18},{18,2},{3,19},{19,3},{4,20},{20... | collective-permute-start | bytes 983048 | tf_op jit(solution)/shard_map/ppermute | solution.py:209
  46.5 22.0 %collective-permute-start.13 = (bf16[64,2560]{1,0:T(8,128)(2,1)S(1)}, bf16[64,2560]{1,0:T(8,128)(2,1)S(1)}, u32[]{:S(2)}, u32[]{:S(2)}) collective-permute-start(bf16[64,2560]{1,0:T(8,128)(2,1)S(1)} %fusion.16), channel_id=1, source_target_pairs={{0,4},{2,6},{4,0},{6,2},{8,12},{10,14},{12,8},{14,10},{1,5},{3,7},... | collective-permute-start | bytes 983048 | tf_op jit(solution)/shard_map/ppermute | solution.py:111
  56.1 7.9 %collective-permute-start.11 = (f32[256,256]{1,0:T(8,128)S(1)}, f32[256,256]{1,0:T(8,128)S(1)}, u32[]{:S(2)}, u32[]{:S(2)}) collective-permute-start(f32[256,256]{1,0:T(8,128)S(1)} %fusion.47), channel_id=1, source_target_pairs={{0,1},{1,0},{2,3},{3,2},{4,5},{5,4},{6,7},{7,6},{8,9},{9,8},{10,11... | collective-permute-start | bytes 786440 | tf_op jit(solution)/shard_map/ppermute | solution.py:135
  56.3 20.3 %collective-permute-start.17 = (bf16[64,2560]{1,0:T(8,128)(2,1)S(1)}, bf16[64,2560]{1,0:T(8,128)(2,1)S(1)}, u32[]{:S(2)}, u32[]{:S(2)}) collective-permute-start(bf16[64,2560]{1,0:T(8,128)(2,1)S(1)} %add_convert_fusion.1), channel_id=1, source_target_pairs={{0,8},{2,10},{4,12},{6,14},{8,0},{10,2},{12,4},{14,6},{1,9},{3,11}... | collective-permute-start | bytes 983048 | tf_op jit(solution)/shard_map/ppermute | solution.py:111
  62.4 22.1 %collective-permute-start.10 = (bf16[128,2560]{1,0:T(8,128)(2,1)S(1)}, bf16[128,2560]{1,0:T(8,128)(2,1)S(1)}, u32[]{:S(2)}, u32[]{:S(2)}) collective-permute-start(bf16[128,2560]{1,0:T(8,128)(2,1)S(1)} %convolution_convert_fusion.1), channel_id=1, source_target_pairs={{0,2},{2,0},{4,6},{6,4},{8,10},{10,8},{12,14},{14,12},{1,3},{3,1},... | collective-permute-start | bytes 1966088 | tf_op jit(solution)/shard_map/ppermute | solution.py:111
  65.6 15.0 %collective-permute-start.14 = (bf16[64,2560]{1,0:T(8,128)(2,1)S(1)}, bf16[64,2560]{1,0:T(8,128)(2,1)S(1)}, u32[]{:S(2)}, u32[]{:S(2)}) collective-permute-start(bf16[64,2560]{1,0:T(8,128)(2,1)S(1)} %fusion.8), channel_id=1, source_target_pairs={{0,4},{2,6},{4,0},{6,2},{8,12},{10,14},{12,8},{14,10},{1,5},{3,7},... | collective-permute-start | bytes 983048 | tf_op jit(solution)/shard_map/ppermute | solution.py:111
  67.9 25.5 %collective-permute-start.12 = (bf16[128,2560]{1,0:T(8,128)(2,1)S(1)}, bf16[128,2560]{1,0:T(8,128)(2,1)S(1)}, u32[]{:S(2)}, u32[]{:S(2)}) collective-permute-start(bf16[128,2560]{1,0:T(8,128)(2,1)S(1)} %convolution_convert_fusion), channel_id=1, source_target_pairs={{0,2},{2,0},{4,6},{6,4},{8,10},{10,8},{12,14},{14,12},{1,3},{3,1},... | collective-permute-start | bytes 1966088 | tf_op jit(solution)/shard_map/ppermute | solution.py:111
  80.6 15.5 %collective-permute-start.15 = (bf16[64,2560]{1,0:T(8,128)(2,1)S(1)}, bf16[64,2560]{1,0:T(8,128)(2,1)S(1)}, u32[]{:S(2)}, u32[]{:S(2)}) collective-permute-start(bf16[64,2560]{1,0:T(8,128)(2,1)S(1)} %fusion.3), channel_id=1, source_target_pairs={{0,4},{2,6},{4,0},{6,2},{8,12},{10,14},{12,8},{14,10},{1,5},{3,7},... | collective-permute-start | bytes 983048 | tf_op jit(solution)/shard_map/ppermute | solution.py:111
  80.6 17.6 %collective-permute-start.16 = (bf16[64,2560]{1,0:T(8,128)(2,1)S(1)}, bf16[64,2560]{1,0:T(8,128)(2,1)S(1)}, u32[]{:S(2)}, u32[]{:S(2)}) collective-permute-start(bf16[64,2560]{1,0:T(8,128)(2,1)S(1)} %add_convert_fusion.2), channel_id=1, source_target_pairs={{0,8},{2,10},{4,12},{6,14},{8,0},{10,2},{12,4},{14,6},{1,9},{3,11}... | collective-permute-start | bytes 983048 | tf_op jit(solution)/shard_map/ppermute | solution.py:111
  (6 other events, 13.8 us)

commit v8 on v7

--- a/solution.py
+++ b/solution.py
@@ -135,56 +135,42 @@
     return partial + lax.ppermute(partial, "tensor", SWAP)
 
 
-LANES = 128
-
-
-def gate_columns(gating, rows):
-    pieces, rest = [], gating
-    for _ in range(3):
-        piece = lax.reduce_precision(rest, exponent_bits=8, mantissa_bits=7)
-        pieces.append(narrow(piece).reshape(-1, LANES))
-        rest = rest - piece
-    columns = jnp.concatenate(pieces)
-    return jnp.pad(columns, ((0, rows - columns.shape[0]), (0, 0)))
-
-
-def gates_of(columns, capacity):
-    pieces = columns[: 3 * capacity // LANES].reshape(3, 1, capacity)
-    return jnp.sum(pieces.astype(jnp.float32), axis=0)
+def gather_gates(gating):
+    pair = jnp.concatenate([gating, move(gating, xor_line(1))])
+    return jnp.concatenate([pair, move(pair, xor_line(2))])
 
 
 def by_pairs(tokens, cotangent, down_adapter, up_adapter, token_lists, gating):
     me = lax.axis_index("adapter")
     first_group = lax.axis_index("groups") == 0
-    tok_local, width = tokens.shape
+    tok_local = tokens.shape[0]
     capacity = gating.shape[1]
     down_matrix = down_adapter[0]
     up_matrix = up_adapter[0]
     rank = down_matrix.shape[0]
 
-    message = jnp.concatenate([down_matrix, gate_columns(gating, rank)], axis=1)
-    far_down = lax.ppermute(message, ("groups", "adapter"), FAR)
+    far_down = lax.ppermute(down_matrix, ("groups", "adapter"), FAR)
     tokens2 = move(tokens, PARTNER)
-    near_down = move(message, xor_line(1))
+    near_down = move(down_matrix, xor_line(1))
     cot2 = move(cotangent, PARTNER)
-    far_up = lax.ppermute(up_matrix, ("groups", "adapter"), FAR)
-    cross_down = lax.ppermute(far_down, "groups", SWAP)
-    near_up = move(jnp.concatenate([up_matrix, far_down[:, width:]], axis=1), xor_line(1))
-
-    gates = [gating] + [gates_of(m[:, width:], capacity) for m in (near_down, far_down, near_up)]
-    near_down, far_down, cross_down, near_up = (
-        m[:, :width] for m in (near_down, far_down, cross_down, near_up)
-    )
+    near_up = move(up_matrix, xor_line(1))
+    gates = gather_gates(gating)
+
     far_bit = jnp.where(first_group, 2, 3)
     experts = jnp.stack([me, me ^ 2, me ^ (2 * far_bit), me ^ (2 * (far_bit ^ 1))])
     lists = jnp.take(token_lists, experts, axis=0)
-    gate_rows = adapter_scale_factor * jnp.concatenate(gates)
+    crossed = jnp.concatenate([gates[:2], gates[3:], gates[2:3]])
+    gate_rows = adapter_scale_factor * jnp.where(first_group, gates, crossed)
     token_ids = jnp.arange(tok_local, dtype=jnp.int32)
     ids = jnp.concatenate([me * tok_local + token_ids, (me ^ 1) * tok_local + token_ids])
     taken = lists[:, :, None] == ids[None, None, :]
     scale = jnp.sum(jnp.where(taken, gate_rows[:, :, None], 0.0), axis=1)
 
     tokens2 = jnp.concatenate([tokens, tokens2], axis=0)
+    up_later, scale = lax.optimization_barrier((up_matrix, scale))
+    far_up = lax.ppermute(up_later, ("groups", "adapter"), FAR)
+    ready, scale = lax.optimization_barrier((far_down, scale))
+    cross_down = lax.ppermute(ready, "groups", SWAP)
     down_all = jnp.concatenate([down_matrix, near_down, far_down, cross_down], axis=0)
 
     def low_rank(rows, matrices):
@@ -205,7 +191,7 @@
         return narrow(contract_first(weights, matrix) + back.astype(jnp.float32))
 
     low = low_rank(tokens2, down_all)
-    cot2, far_up, low = lax.optimization_barrier((cot2, far_up, low))
+    cot2, far_up, near_up, low = lax.optimization_barrier((cot2, far_up, near_up, low))
     cross_up = lax.ppermute(far_up, "groups", SWAP)
     cot2 = jnp.concatenate([cotangent, cot2], axis=0)
     (own, first, second, third), up_send = partial_sums(for_line(low), cot2)
@@ -215,13 +201,14 @@
     cross_up = after(cross_up, up_third)
     up_all = jnp.concatenate([up_matrix, near_up, far_up, cross_up], axis=0)
     low_back = low_rank(cot2, up_all)
-    branch_back = outward_start(low, up_all)
     (own_b, first_b, second_b, third_b), down_send = partial_sums(for_line(low_back), tokens2)
     down_third = move(down_send[2], xor_line(1))
-    down_first = move(after(down_send[0], (up_first, down_third)), xor_line(1))
+    branch_back = outward_start(after(low, down_send), up_all)
     input_back = outward_start(low_back, down_all)
     up_far = move(narrow(add_up(second, up_third)), xor_line(2))
-    down_far = move(narrow(add_up(second_b, down_third)), xor_line(2))
+    down_sum = narrow(add_up(second_b, down_third))
+    down_far = move(down_sum, xor_line(2))
+    down_first = move(after(down_send[0], (up_first, down_sum)), xor_line(1))
     branch_out = outward_end(low, up_all, branch_back)
     up_grad = add_up(own, up_first, up_far)
     input_grad = outward_end(low_back, down_all, input_back)

time: 99.8 us -> 97.7 us (0.979)
  waiting for transfers between devices: 46.1 us -> 54.9 us
  local copies, waits for them, and re-layouts: 8.3 us -> 1.95 us
  other arithmetic: 8.15 us -> 2.55 us
  matrix products: 9.93 us -> 13.2 us
  starting transfers between devices: 25.7 us -> 23.8 us
    ppermute x12 -> x14, waiting for transfers between devices: 31.1 us -> 42.9 us  [move(): return lax.ppermute(value, 'adapter', pairs)]
    ppermute x3, waiting for transfers between devices: 14.9 us -> 9.25 us  [the longest x1 7.22 us: by_pairs(): cross_down = lax.ppermute(ready, 'groups', SWAP)]
    ppermute x12 -> x14, starting transfers between devices: 17.2 us -> 12.5 us  [move(): return lax.ppermute(value, 'adapter', pairs)]
    slice x5 -> x1, local copies, waits for them, and re-layouts: 3.88 us -> 0.01 us  [by_pairs(): crossed = jnp.concatenate([gates[:2], gates[3:], gates[2:3]])]
    ppermute x2, waiting for transfers between devices: 0.01 us -> 2.8 us  [both_cores(): return partial + lax.ppermute(partial, 'tensor', SWAP)]
    concatenate x3 -> x1, other arithmetic: 2.74 us -> 0.01 us  [gather_gates(): pair = jnp.concatenate([gating, move(gating, xor_line(1))])]
    dot_general x4, matrix products: 5.06 us -> 7.25 us  [contract_first(): lax.dot_general(left_op, right_op, (((0,), (0,)), ((), ())), preferred_el...]
    convert_element_type x3 -> x0, other arithmetic: 2.01 us -> none  [gates_of(): return jnp.sum(pieces.astype(jnp.float32), axis=0)]
  transfers between devices with their start and end apart: 18 -> 20, of which waited for: 9 -> 11; matrix products, arithmetic and copies ran while one was open for 20% -> 16% of each run, Pallas kernels for 0% -> 0%
where the time goes in v8:
time: 97.7 us; the launch traced here: 97.4 us
  waiting for transfers between devices  54.9 us (56%)
  starting transfers between devices  23.8 us (24%)
  matrix products  13.2 us (14%)
  other arithmetic  2.55 us (3%)
  local copies, waits for them, and re-layouts  1.95 us (2%)
    ppermute x14, waiting for transfers between devices, move(): return lax.ppermute(value, 'adapter', pairs)  42.9 us
    ppermute x14, starting transfers between devices, move(): return lax.ppermute(value, 'adapter', pairs)  12.5 us
    dot_general x4, matrix products, contract_first(): lax.dot_general(left_op, right_op, (((0,), (0,)), ((), ())), preferred_el...  7.25 us
    ppermute x1, waiting for transfers between devices, by_pairs(): cross_down = lax.ppermute(ready, 'groups', SWAP)  7.22 us
    ppermute x1, starting transfers between devices, by_pairs(): far_down = lax.ppermute(down_matrix, ('groups', 'adapter'), FAR)  4.1 us
    ppermute x1, starting transfers between devices, by_pairs(): far_up = lax.ppermute(up_later, ('groups', 'adapter'), FAR)  3.26 us
    ppermute x1, starting transfers between devices, by_pairs(): cross_up = lax.ppermute(far_up, 'groups', SWAP)  3.13 us
    dot_general x2, matrix products, contract_last(): lax.dot_general(left_op, right_op, (((1,), (1,)), ((), ())), preferred_el...  3.11 us
  transfers between devices with their start and end apart: 20, of which 11 were waited for; matrix products, arithmetic and copies ran while one was open for 16% of the time, Pallas kernels for 0%

profile of v8, /device:TPU:0, one launch (start us, length us, event | category | flops | bytes accessed | tf_op | source)
XLA Modules:
  0.0 97.4 jit_solution(3194969896071619373)
XLA Ops:
  0.7 4.1 %collective-permute-start.5 = (bf16[64,2560]{1,0:T(8,128)(2,1)}, bf16[64,2560]{1,0:T(8,128)(2,1)}, u32[]{:S(2)}, u32[]{:S(2)}) collective-permute-start(bf16[64,2560]{1,0:T(8,128)(2,1)} %bitcast.66), channel_id=1, source_target_pairs={{0,8},{2,10},{4,12},{6,14},{8,0},{10,2},{12,4},{14,6},{16,28},{18,... | collective-permute-start | bytes 983048 | tf_op jit(solution)/shard_map/ppermute | solution.py:152
  4.8 1.6 %collective-permute-start.6 = (bf16[64,2560]{1,0:T(8,128)(2,1)}, bf16[64,2560]{1,0:T(8,128)(2,1)}, u32[]{:S(2)}, u32[]{:S(2)}) collective-permute-start(bf16[64,2560]{1,0:T(8,128)(2,1)} %bitcast.67), channel_id=1, source_target_pairs={{0,4},{2,6},{4,0},{6,2},{8,12},{10,14},{12,8},{14,10},{1,5},{3,7},... | collective-permute-start | bytes 983048 | tf_op jit(solution)/shard_map/ppermute | solution.py:111
  6.8 1.5 %collective-permute-start.8 = (bf16[128,2560]{1,0:T(8,128)(2,1)}, bf16[128,2560]{1,0:T(8,128)(2,1)S(1)}, u32[]{:S(2)}, u32[]{:S(2)}) collective-permute-start(bf16[128,2560]{1,0:T(8,128)(2,1)} %param.6), channel_id=1, source_target_pairs={{0,2},{2,0},{4,6},{6,4},{8,10},{10,8},{12,14},{14,12},{1,3},{3,1},... | collective-permute-start | bytes 1966088 | tf_op jit(solution)/shard_map/ppermute | solution.py:111
  8.3 1.6 %collective-permute-start.4 = (bf16[64,2560]{1,0:T(8,128)(2,1)}, bf16[64,2560]{1,0:T(8,128)(2,1)}, u32[]{:S(2)}, u32[]{:S(2)}) collective-permute-start(bf16[64,2560]{1,0:T(8,128)(2,1)} %bitcast.71), channel_id=1, source_target_pairs={{0,4},{2,6},{4,0},{6,2},{8,12},{10,14},{12,8},{14,10},{1,5},{3,7},... | collective-permute-start | bytes 983048 | tf_op jit(solution)/shard_map/ppermute | solution.py:111
  11.9 9.7 %collective-permute-done.1 = f32[1,256]{1,0:T(1,128)S(1)} collective-permute-done((f32[1,256]{1,0:T(1,128)}, f32[1,256]{1,0:T(1,128)S(1)}, u32[]{:S(2)}, u32[]{:S(2)}) %collective-permute-start.1) | collective-permute-done | bytes 1056 | tf_op jit(solution)/shard_map/ppermute | solution.py:111
  22.7 3.6 %collective-permute-done.2 = f32[2,256]{1,0:T(2,128)S(1)} collective-permute-done((f32[2,256]{1,0:T(2,128)S(1)}, f32[2,256]{1,0:T(2,128)S(1)}, u32[]{:S(2)}, u32[]{:S(2)}) %collective-permute-start.2) | collective-permute-done | bytes 2080 | tf_op jit(solution)/shard_map/ppermute | solution.py:111
  26.3 1.5 %collective-permute-start = (bf16[128,2560]{1,0:T(8,128)(2,1)S(1)}, bf16[128,2560]{1,0:T(8,128)(2,1)S(1)}, u32[]{:S(2)}, u32[]{:S(2)}) collective-permute-start(bf16[128,2560]{1,0:T(8,128)(2,1)S(1)} %copy-done.2), channel_id=1, source_target_pairs={{0,2},{2,0},{4,6},{6,4},{8,10},{10,8},{12,14},{14,12},{1,3},{3,1},... | collective-permute-start | bytes 1966088 | tf_op jit(solution)/shard_map/ppermute | solution.py:111
  28.2 3.3 %collective-permute-start.3 = (bf16[64,2560]{1,0:T(8,128)(2,1)S(1)}, bf16[64,2560]{1,0:T(8,128)(2,1)S(1)}, u32[]{:S(2)}, u32[]{:S(2)}) collective-permute-start(bf16[64,2560]{1,0:T(8,128)(2,1)S(1)} %bitcast.72), channel_id=1, source_target_pairs={{0,8},{2,10},{4,12},{6,14},{8,0},{10,2},{12,4},{14,6},{16,28},{18,... | collective-permute-start | bytes 983048 | tf_op jit(solution)/shard_map/ppermute | solution.py:171
  32.2 7.2 %collective-permute-done.7 = bf16[64,2560]{1,0:T(8,128)(2,1)S(1)} collective-permute-done((bf16[64,2560]{1,0:T(8,128)(2,1)}, bf16[64,2560]{1,0:T(8,128)(2,1)S(1)}, u32[]{:S(2)}, u32[]{:S(2)}) %collective-permute-start.7) | collective-permute-done | bytes 327712 | tf_op jit(solution)/shard_map/ppermute | solution.py:173
  39.4 1.6 %fusion.37 = f32[256,256]{1,0:T(8,128)S(1)} fusion(bf16[256,2560]{1,0:T(8,128)(2,1)S(1)} %constant_dynamic-update-slice_fusion, bf16[64,2560]{1,0:T(8,128)(2,1)S(1)} %collective-permute-done.7, bf16[64,2560]{1,0:T(8,128)(2,1)} %collective-permute-done.5, bf16[64,2560]{1,0:T(8,128)(2,1)} %collective-permute-done.6, bf16[64,2560]{1,0:T(8,128)(2,1)S(1)} %bitcast.68), kind=kOutput, calls=%fused_computation.68 | convolution fusion | flops 340787200 | bytes 2883584 | tf_op jit(solution)/shard_map/dot_general | solution.py:10
  41.1 1.5 %collective-permute-done.9 = f32[256,256]{1,0:T(8,128)S(1)} collective-permute-done((f32[256,256]{1,0:T(8,128)S(1)}, f32[256,256]{1,0:T(8,128)S(1)}, u32[]{:S(2)}, u32[]{:S(2)}) %collective-permute-start.9) | collective-permute-done | bytes 262176 | tf_op jit(solution)/shard_map/ppermute | solution.py:135
  42.7 2.0 %collective-permute-done.3 = bf16[64,2560]{1,0:T(8,128)(2,1)S(1)} collective-permute-done((bf16[64,2560]{1,0:T(8,128)(2,1)S(1)}, bf16[64,2560]{1,0:T(8,128)(2,1)S(1)}, u32[]{:S(2)}, u32[]{:S(2)}) %collective-permute-start.3) | collective-permute-done | bytes 327712 | tf_op jit(solution)/shard_map/ppermute | solution.py:171
  46.3 3.1 %collective-permute-start.10 = (bf16[64,2560]{1,0:T(8,128)(2,1)S(1)}, bf16[64,2560]{1,0:T(8,128)(2,1)S(1)}, u32[]{:S(2)}, u32[]{:S(2)}) collective-permute-start(bf16[64,2560]{1,0:T(8,128)(2,1)S(1)} %collective-permute-done.3), channel_id=1, source_target_pairs={{0,16},{16,0},{1,17},{17,1},{2,18},{18,2},{3,19},{19,3},{4,20},{20... | collective-permute-start | bytes 983048 | tf_op jit(solution)/shard_map/ppermute | solution.py:195
  49.5 7.4 %collective-permute-done.11 = bf16[64,2560]{1,0:T(8,128)(2,1)S(1)} collective-permute-done((bf16[64,2560]{1,0:T(8,128)(2,1)S(1)}, bf16[64,2560]{1,0:T(8,128)(2,1)S(1)}, u32[]{:S(2)}, u32[]{:S(2)}) %collective-permute-start.11) | collective-permute-done | bytes 327712 | tf_op jit(solution)/shard_map/ppermute | solution.py:111
  56.9 1.5 %fusion.38 = f32[256,256]{1,0:T(8,128)S(1)} fusion(bf16[256,2560]{1,0:T(8,128)(2,1)S(1)} %constant_dynamic-update-slice_fusion.2, bf16[64,2560]{1,0:T(8,128)(2,1)S(1)} %collective-permute-done.10, bf16[64,2560]{1,0:T(8,128)(2,1)S(1)} %collective-permute-done.3, bf16[64,2560]{1,0:T(8,128)(2,1)} %collective-permute-done.4, bf16[64,2560]{1,0:T(8,128)(2,1)S(1)} %bitcast.73), kind=kOutput, calls=%fused_computation.69 | convolution fusion | flops 340787200 | bytes 2883584 | tf_op jit(solution)/shard_map/dot_general | solution.py:10
  58.7 1.3 %collective-permute-done.12 = f32[256,256]{1,0:T(8,128)S(1)} collective-permute-done((f32[256,256]{1,0:T(8,128)S(1)}, f32[256,256]{1,0:T(8,128)S(1)}, u32[]{:S(2)}, u32[]{:S(2)}) %collective-permute-start.12) | collective-permute-done | bytes 262176 | tf_op jit(solution)/shard_map/ppermute | solution.py:135
  62.2 1.4 %convolution_convert_fusion = bf16[128,2560]{1,0:T(8,128)(2,1)S(1)} fusion(bf16[256,128]{1,0:T(8,128)(2,1)S(1)} %bitcast.65, bf16[64,2560]{1,0:T(8,128)(2,1)S(1)} %collective-permute-done.7, bf16[64,2560]{1,0:T(8,128)(2,1)} %collective-permute-done.5, bf16[64,2560]{1,0:T(8,128)(2,1)} %collective-permute-done.6, bf16[64,2560]{1,0:T(8,128)(2,1)S(1)} %bitcast.69), kind=kOutput, calls=%fused_computation.3 | convolution fusion | flops 173342720 | bytes 2031616 | tf_op jit(solution)/shard_map/dot_general | solution.py:16
  64.3 1.3 %convolution_convert_fusion.1 = bf16[128,2560]{1,0:T(8,128)(2,1)S(1)} fusion(bf16[256,128]{1,0:T(8,128)(2,1)S(1)} %bitcast.63, bf16[64,2560]{1,0:T(8,128)(2,1)S(1)} %collective-permute-done.10, bf16[64,2560]{1,0:T(8,128)(2,1)S(1)} %collective-permute-done.3, bf16[64,2560]{1,0:T(8,128)(2,1)} %collective-permute-done.4, bf16[64,2560]{1,0:T(8,128)(2,1)S(1)} %bitcast.74), kind=kOutput, calls=%fused_computation.4 | convolution fusion | flops 173342720 | bytes 2031616 | tf_op jit(solution)/shard_map/dot_general | solution.py:16
  65.6 1.6 %collective-permute-start.13 = (bf16[128,2560]{1,0:T(8,128)(2,1)S(1)}, bf16[128,2560]{1,0:T(8,128)(2,1)S(1)}, u32[]{:S(2)}, u32[]{:S(2)}) collective-permute-start(bf16[128,2560]{1,0:T(8,128)(2,1)S(1)} %convolution_convert_fusion.1), channel_id=1, source_target_pairs={{0,2},{2,0},{4,6},{6,4},{8,10},{10,8},{12,14},{14,12},{1,3},{3,1},... | collective-permute-start | bytes 1966088 | tf_op jit(solution)/shard_map/ppermute | solution.py:111
  67.2 9.0 %collective-permute-done.19 = bf16[64,2560]{1,0:T(8,128)(2,1)S(1)} collective-permute-done((bf16[64,2560]{1,0:T(8,128)(2,1)S(1)}, bf16[64,2560]{1,0:T(8,128)(2,1)S(1)}, u32[]{:S(2)}, u32[]{:S(2)}) %collective-permute-start.19) | collective-permute-done | bytes 327712 | tf_op jit(solution)/shard_map/ppermute | solution.py:111
  78.4 1.7 %collective-permute-start.17 = (bf16[64,2560]{1,0:T(8,128)(2,1)S(1)}, bf16[64,2560]{1,0:T(8,128)(2,1)S(1)}, u32[]{:S(2)}, u32[]{:S(2)}) collective-permute-start(bf16[64,2560]{1,0:T(8,128)(2,1)S(1)} %fusion.3), channel_id=1, source_target_pairs={{0,4},{2,6},{4,0},{6,2},{8,12},{10,14},{12,8},{14,10},{1,5},{3,7},... | collective-permute-start | bytes 983048 | tf_op jit(solution)/shard_map/ppermute | solution.py:111
  81.3 2.3 %fusion = bf16[128,2560]{1,0:T(8,128)(2,1)} fusion(bf16[256,128]{1,0:T(8,128)(2,1)S(1)} %bitcast.64, bf16[128,2560]{1,0:T(8,128)(2,1)S(1)} %collective-permute-done.14, bf16[64,2560]{1,0:T(8,128)(2,1)S(1)} %collective-permute-done.7, bf16[64,2560]{1,0:T(8,128)(2,1)} %collective-permute-done.5, bf16[64,2560]{1,0:T(8,128)(2,1)} %collective-permute-done.6, ...), kind=kOutput, calls=%fused_computation.2 | convolution fusion | flops 173998080 | bytes 2686976 | tf_op jit(solution)/shard_map/dot_general | solution.py:16
  83.6 10.7 %collective-permute-done.13 = bf16[128,2560]{1,0:T(8,128)(2,1)S(1)} collective-permute-done((bf16[128,2560]{1,0:T(8,128)(2,1)S(1)}, bf16[128,2560]{1,0:T(8,128)(2,1)S(1)}, u32[]{:S(2)}, u32[]{:S(2)}) %collective-permute-start.13) | collective-permute-done | bytes 655392 | tf_op jit(solution)/shard_map/ppermute | solution.py:111
  94.3 2.2 %add_convert_fusion = bf16[128,2560]{1,0:T(8,128)(2,1)} fusion(bf16[128,2560]{1,0:T(8,128)(2,1)S(1)} %collective-permute-done.13, bf16[256,128]{1,0:T(8,128)(2,1)S(1)} %bitcast.60, bf16[64,2560]{1,0:T(8,128)(2,1)S(1)} %collective-permute-done.10, bf16[64,2560]{1,0:T(8,128)(2,1)S(1)} %collective-permute-done.3, bf16[64,2560]{1,0:T(8,128)(2,1)} %collective-permute-done.4, ...), kind=kOutput, calls=%fused_computation.7 | convolution fusion | flops 173998080 | bytes 2686976 | tf_op jit(solution)/shard_map/dot_general | solution.py:16
  (69 shorter events, 13.7 us)
Async XLA Ops:
  0.7 27.5 %copy-start.5 = (bf16[1,64,2560]{2,1,0:T(8,128)(2,1)S(1)}, bf16[1,64,2560]{2,1,0:T(8,128)(2,1)}, u32[]{:S(2)}) copy-start(bf16[1,64,2560]{2,1,0:T(8,128)(2,1)} %param.9) | copy-start | bytes 983044
  0.7 25.6 %copy-start.2 = (bf16[128,2560]{1,0:T(8,128)(2,1)S(1)}, bf16[128,2560]{1,0:T(8,128)(2,1)}, u32[]{:S(2)}) copy-start(bf16[128,2560]{1,0:T(8,128)(2,1)} %param.7) | copy-start | bytes 1966084
  0.7 27.5 %collective-permute-start.5 = (bf16[64,2560]{1,0:T(8,128)(2,1)}, bf16[64,2560]{1,0:T(8,128)(2,1)}, u32[]{:S(2)}, u32[]{:S(2)}) collective-permute-start(bf16[64,2560]{1,0:T(8,128)(2,1)} %bitcast.66), channel_id=1, source_target_pairs={{0,8},{2,10},{4,12},{6,14},{8,0},{10,2},{12,4},{14,6},{16,28},{18,... | collective-permute-start | bytes 983048 | tf_op jit(solution)/shard_map/ppermute | solution.py:152
  4.8 27.4 %collective-permute-start.6 = (bf16[64,2560]{1,0:T(8,128)(2,1)}, bf16[64,2560]{1,0:T(8,128)(2,1)}, u32[]{:S(2)}, u32[]{:S(2)}) collective-permute-start(bf16[64,2560]{1,0:T(8,128)(2,1)} %bitcast.67), channel_id=1, source_target_pairs={{0,4},{2,6},{4,0},{6,2},{8,12},{10,14},{12,8},{14,10},{1,5},{3,7},... | collective-permute-start | bytes 983048 | tf_op jit(solution)/shard_map/ppermute | solution.py:111
  6.4 15.2 %collective-permute-start.1 = (f32[1,256]{1,0:T(1,128)}, f32[1,256]{1,0:T(1,128)S(1)}, u32[]{:S(2)}, u32[]{:S(2)}) collective-permute-start(f32[1,256]{1,0:T(1,128)} %param.11), channel_id=1, source_target_pairs={{0,4},{2,6},{4,0},{6,2},{8,12},{10,14},{12,8},{14,10},{1,5},{3,7},... | collective-permute-start | bytes 3080 | tf_op jit(solution)/shard_map/ppermute | solution.py:111
  6.8 24.6 %collective-permute-start.8 = (bf16[128,2560]{1,0:T(8,128)(2,1)}, bf16[128,2560]{1,0:T(8,128)(2,1)S(1)}, u32[]{:S(2)}, u32[]{:S(2)}) collective-permute-start(bf16[128,2560]{1,0:T(8,128)(2,1)} %param.6), channel_id=1, source_target_pairs={{0,2},{2,0},{4,6},{6,4},{8,10},{10,8},{12,14},{14,12},{1,3},{3,1},... | collective-permute-start | bytes 1966088 | tf_op jit(solution)/shard_map/ppermute | solution.py:111
  8.3 34.4 %collective-permute-start.4 = (bf16[64,2560]{1,0:T(8,128)(2,1)}, bf16[64,2560]{1,0:T(8,128)(2,1)}, u32[]{:S(2)}, u32[]{:S(2)}) collective-permute-start(bf16[64,2560]{1,0:T(8,128)(2,1)} %bitcast.71), channel_id=1, source_target_pairs={{0,4},{2,6},{4,0},{6,2},{8,12},{10,14},{12,8},{14,10},{1,5},{3,7},... | collective-permute-start | bytes 983048 | tf_op jit(solution)/shard_map/ppermute | solution.py:111
  9.9 29.5 %copy-start.4 = (bf16[1,64,2560]{2,1,0:T(8,128)(2,1)S(1)}, bf16[1,64,2560]{2,1,0:T(8,128)(2,1)}, u32[]{:S(2)}) copy-start(bf16[1,64,2560]{2,1,0:T(8,128)(2,1)} %param.8) | copy-start | bytes 983044
  21.6 4.6 %collective-permute-start.2 = (f32[2,256]{1,0:T(2,128)S(1)}, f32[2,256]{1,0:T(2,128)S(1)}, u32[]{:S(2)}, u32[]{:S(2)}) collective-permute-start(f32[2,256]{1,0:T(2,128)S(1)} %pad_maximum_fusion.3), channel_id=1, source_target_pairs={{0,8},{2,10},{4,12},{6,14},{8,0},{10,2},{12,4},{14,6},{1,9},{3,11}... | collective-permute-start | bytes 6152 | tf_op jit(solution)/shard_map/ppermute | solution.py:111
  26.3 18.5 %collective-permute-start = (bf16[128,2560]{1,0:T(8,128)(2,1)S(1)}, bf16[128,2560]{1,0:T(8,128)(2,1)S(1)}, u32[]{:S(2)}, u32[]{:S(2)}) collective-permute-start(bf16[128,2560]{1,0:T(8,128)(2,1)S(1)} %copy-done.2), channel_id=1, source_target_pairs={{0,2},{2,0},{4,6},{6,4},{8,10},{10,8},{12,14},{14,12},{1,3},{3,1},... | collective-permute-start | bytes 1966088 | tf_op jit(solution)/shard_map/ppermute | solution.py:111
  28.2 16.5 %collective-permute-start.3 = (bf16[64,2560]{1,0:T(8,128)(2,1)S(1)}, bf16[64,2560]{1,0:T(8,128)(2,1)S(1)}, u32[]{:S(2)}, u32[]{:S(2)}) collective-permute-start(bf16[64,2560]{1,0:T(8,128)(2,1)S(1)} %bitcast.72), channel_id=1, source_target_pairs={{0,8},{2,10},{4,12},{6,14},{8,0},{10,2},{12,4},{14,6},{16,28},{18,... | collective-permute-start | bytes 983048 | tf_op jit(solution)/shard_map/ppermute | solution.py:171
  31.4 7.9 %collective-permute-start.7 = (bf16[64,2560]{1,0:T(8,128)(2,1)}, bf16[64,2560]{1,0:T(8,128)(2,1)S(1)}, u32[]{:S(2)}, u32[]{:S(2)}) collective-permute-start(bf16[64,2560]{1,0:T(8,128)(2,1)} %collective-permute-done.5), channel_id=1, source_target_pairs={{0,16},{16,0},{1,17},{17,1},{2,18},{18,2},{3,19},{19,3},{4,20},{20... | collective-permute-start | bytes 983048 | tf_op jit(solution)/shard_map/ppermute | solution.py:173
  41.0 1.6 %collective-permute-start.9 = (f32[256,256]{1,0:T(8,128)S(1)}, f32[256,256]{1,0:T(8,128)S(1)}, u32[]{:S(2)}, u32[]{:S(2)}) collective-permute-start(f32[256,256]{1,0:T(8,128)S(1)} %fusion.37), channel_id=1, source_target_pairs={{0,1},{1,0},{2,3},{3,2},{4,5},{5,4},{6,7},{7,6},{8,9},{9,8},{10,11... | collective-permute-start | bytes 786440 | tf_op jit(solution)/shard_map/ppermute | solution.py:135
  42.7 21.6 %copy-start.1 = (bf16[4,64,256]{2,1,0:T(8,128)(2,1)}, bf16[4,64,256]{2,1,0:T(8,128)(2,1)S(1)}, u32[]{:S(2)}) copy-start(bf16[4,64,256]{2,1,0:T(8,128)(2,1)S(1)} %multiply_convert_fusion.3) | copy-start | bytes 393220
  46.2 10.7 %collective-permute-start.11 = (bf16[64,2560]{1,0:T(8,128)(2,1)S(1)}, bf16[64,2560]{1,0:T(8,128)(2,1)S(1)}, u32[]{:S(2)}, u32[]{:S(2)}) collective-permute-start(bf16[64,2560]{1,0:T(8,128)(2,1)S(1)} %fusion.9), channel_id=1, source_target_pairs={{0,4},{2,6},{4,0},{6,2},{8,12},{10,14},{12,8},{14,10},{1,5},{3,7},... | collective-permute-start | bytes 983048 | tf_op jit(solution)/shard_map/ppermute | solution.py:111
  46.3 10.6 %collective-permute-start.10 = (bf16[64,2560]{1,0:T(8,128)(2,1)S(1)}, bf16[64,2560]{1,0:T(8,128)(2,1)S(1)}, u32[]{:S(2)}, u32[]{:S(2)}) collective-permute-start(bf16[64,2560]{1,0:T(8,128)(2,1)S(1)} %collective-permute-done.3), channel_id=1, source_target_pairs={{0,16},{16,0},{1,17},{17,1},{2,18},{18,2},{3,19},{19,3},{4,20},{20... | collective-permute-start | bytes 983048 | tf_op jit(solution)/shard_map/ppermute | solution.py:195
  49.4 17.8 %collective-permute-start.15 = (bf16[64,2560]{1,0:T(8,128)(2,1)S(1)}, bf16[64,2560]{1,0:T(8,128)(2,1)S(1)}, u32[]{:S(2)}, u32[]{:S(2)}) collective-permute-start(bf16[64,2560]{1,0:T(8,128)(2,1)S(1)} %fusion.13), channel_id=1, source_target_pairs={{0,4},{2,6},{4,0},{6,2},{8,12},{10,14},{12,8},{14,10},{1,5},{3,7},... | collective-permute-start | bytes 983048 | tf_op jit(solution)/shard_map/ppermute | solution.py:111
  58.4 1.6 %collective-permute-start.12 = (f32[256,256]{1,0:T(8,128)S(1)}, f32[256,256]{1,0:T(8,128)S(1)}, u32[]{:S(2)}, u32[]{:S(2)}) collective-permute-start(f32[256,256]{1,0:T(8,128)S(1)} %fusion.38), channel_id=1, source_target_pairs={{0,1},{1,0},{2,3},{3,2},{4,5},{5,4},{6,7},{7,6},{8,9},{9,8},{10,11... | collective-permute-start | bytes 786440 | tf_op jit(solution)/shard_map/ppermute | solution.py:135
  58.6 17.6 %collective-permute-start.19 = (bf16[64,2560]{1,0:T(8,128)(2,1)S(1)}, bf16[64,2560]{1,0:T(8,128)(2,1)S(1)}, u32[]{:S(2)}, u32[]{:S(2)}) collective-permute-start(bf16[64,2560]{1,0:T(8,128)(2,1)S(1)} %add_convert_fusion.1), channel_id=1, source_target_pairs={{0,8},{2,10},{4,12},{6,14},{8,0},{10,2},{12,4},{14,6},{1,9},{3,11}... | collective-permute-start | bytes 983048 | tf_op jit(solution)/shard_map/ppermute | solution.py:111
  61.6 16.7 %collective-permute-start.16 = (bf16[64,2560]{1,0:T(8,128)(2,1)S(1)}, bf16[64,2560]{1,0:T(8,128)(2,1)S(1)}, u32[]{:S(2)}, u32[]{:S(2)}) collective-permute-start(bf16[64,2560]{1,0:T(8,128)(2,1)S(1)} %fusion.5), channel_id=1, source_target_pairs={{0,4},{2,6},{4,0},{6,2},{8,12},{10,14},{12,8},{14,10},{1,5},{3,7},... | collective-permute-start | bytes 983048 | tf_op jit(solution)/shard_map/ppermute | solution.py:111
  63.6 17.7 %collective-permute-start.14 = (bf16[128,2560]{1,0:T(8,128)(2,1)S(1)}, bf16[128,2560]{1,0:T(8,128)(2,1)S(1)}, u32[]{:S(2)}, u32[]{:S(2)}) collective-permute-start(bf16[128,2560]{1,0:T(8,128)(2,1)S(1)} %convolution_convert_fusion), channel_id=1, source_target_pairs={{0,2},{2,0},{4,6},{6,4},{8,10},{10,8},{12,14},{14,12},{1,3},{3,1},... | collective-permute-start | bytes 1966088 | tf_op jit(solution)/shard_map/ppermute | solution.py:111
  65.6 28.7 %collective-permute-start.13 = (bf16[128,2560]{1,0:T(8,128)(2,1)S(1)}, bf16[128,2560]{1,0:T(8,128)(2,1)S(1)}, u32[]{:S(2)}, u32[]{:S(2)}) collective-permute-start(bf16[128,2560]{1,0:T(8,128)(2,1)S(1)} %convolution_convert_fusion.1), channel_id=1, source_target_pairs={{0,2},{2,0},{4,6},{6,4},{8,10},{10,8},{12,14},{14,12},{1,3},{3,1},... | collective-permute-start | bytes 1966088 | tf_op jit(solution)/shard_map/ppermute | solution.py:111
  78.4 18.1 %collective-permute-start.18 = (bf16[64,2560]{1,0:T(8,128)(2,1)S(1)}, bf16[64,2560]{1,0:T(8,128)(2,1)S(1)}, u32[]{:S(2)}, u32[]{:S(2)}) collective-permute-start(bf16[64,2560]{1,0:T(8,128)(2,1)S(1)} %add_convert_fusion.2), channel_id=1, source_target_pairs={{0,8},{2,10},{4,12},{6,14},{8,0},{10,2},{12,4},{14,6},{1,9},{3,11}... | collective-permute-start | bytes 983048 | tf_op jit(solution)/shard_map/ppermute | solution.py:111
  78.4 18.1 %collective-permute-start.17 = (bf16[64,2560]{1,0:T(8,128)(2,1)S(1)}, bf16[64,2560]{1,0:T(8,128)(2,1)S(1)}, u32[]{:S(2)}, u32[]{:S(2)}) collective-permute-start(bf16[64,2560]{1,0:T(8,128)(2,1)S(1)} %fusion.3), channel_id=1, source_target_pairs={{0,4},{2,6},{4,0},{6,2},{8,12},{10,14},{12,8},{14,10},{1,5},{3,7},... | collective-permute-start | bytes 983048 | tf_op jit(solution)/shard_map/ppermute | solution.py:111
  (3 other events, 44.5 us)

commit v9 on v8

--- a/solution.py
+++ b/solution.py
@@ -135,11 +135,6 @@
     return partial + lax.ppermute(partial, "tensor", SWAP)
 
 
-def gather_gates(gating):
-    pair = jnp.concatenate([gating, move(gating, xor_line(1))])
-    return jnp.concatenate([pair, move(pair, xor_line(2))])
-
-
 def by_pairs(tokens, cotangent, down_adapter, up_adapter, token_lists, gating):
     me = lax.axis_index("adapter")
     first_group = lax.axis_index("groups") == 0
@@ -151,10 +146,12 @@
 
     far_down = lax.ppermute(down_matrix, ("groups", "adapter"), FAR)
     tokens2 = move(tokens, PARTNER)
-    near_down = move(down_matrix, xor_line(1))
+    near_gate, down_later = lax.optimization_barrier((move(gating, xor_line(1)), down_matrix))
+    near_down = move(down_later, xor_line(1))
     cot2 = move(cotangent, PARTNER)
     near_up = move(up_matrix, xor_line(1))
-    gates = gather_gates(gating)
+    gates = jnp.concatenate([gating, near_gate])
+    gates = jnp.concatenate([gates, move(gates, xor_line(2))])
 
     far_bit = jnp.where(first_group, 2, 3)
     experts = jnp.stack([me, me ^ 2, me ^ (2 * far_bit), me ^ (2 * (far_bit ^ 1))])
@@ -203,7 +200,7 @@
     low_back = low_rank(cot2, up_all)
     (own_b, first_b, second_b, third_b), down_send = partial_sums(for_line(low_back), tokens2)
     down_third = move(down_send[2], xor_line(1))
-    branch_back = outward_start(after(low, down_send), up_all)
+    branch_back = outward_start(low, up_all)
     input_back = outward_start(low_back, down_all)
     up_far = move(narrow(add_up(second, up_third)), xor_line(2))
     down_sum = narrow(add_up(second_b, down_third))

time: 97.7 us -> 92.5 us (0.947)
  waiting for transfers between devices: 54.9 us -> 51.3 us
  starting transfers between devices: 23.8 us -> 22.5 us
    ppermute x1, waiting for transfers between devices: 7.22 us -> 0.01 us  [by_pairs(): cross_down = lax.ppermute(ready, 'groups', SWAP)]
    ppermute x14, waiting for transfers between devices: 42.9 us -> 49.8 us  [move(): return lax.ppermute(value, 'adapter', pairs)]
    ppermute x1, starting transfers between devices: 3.13 us -> 0.07 us  [by_pairs(): cross_up = lax.ppermute(far_up, 'groups', SWAP)]
    ppermute x14, starting transfers between devices: 12.5 us -> 14.6 us  [move(): return lax.ppermute(value, 'adapter', pairs)]
    ppermute x1, waiting for transfers between devices: 2.04 us -> 0.01 us  [by_pairs(): far_up = lax.ppermute(up_later, ('groups', 'adapter'), FAR)]
    ppermute x1, starting transfers between devices: 0.66 us -> 2.41 us  [by_pairs(): cross_down = lax.ppermute(ready, 'groups', SWAP)]
    ppermute x1, starting transfers between devices: 4.1 us -> 2.59 us  [by_pairs(): far_down = lax.ppermute(down_matrix, ('groups', 'adapter'), FAR)]
    ppermute x2, waiting for transfers between devices: 2.8 us -> 1.46 us  [both_cores(): return partial + lax.ppermute(partial, 'tensor', SWAP)]
  transfers between devices with their start and end apart: 20 -> 20, of which waited for: 11 -> 8; matrix products, arithmetic and copies ran while one was open for 16% -> 16% of each run, Pallas kernels for 0% -> 0%
where the time goes in v9:
time: 92.5 us; the launch traced here: 92.1 us
  waiting for transfers between devices  51.3 us (55%)
  starting transfers between devices  22.5 us (24%)
  matrix products  12.9 us (14%)
  other arithmetic  2.55 us (3%)
  local copies, waits for them, and re-layouts  1.9 us (2%)
  between operations  0.93 us (1%)
    ppermute x14, waiting for transfers between devices, move(): return lax.ppermute(value, 'adapter', pairs)  49.8 us
    ppermute x14, starting transfers between devices, move(): return lax.ppermute(value, 'adapter', pairs)  14.6 us
    dot_general x4, matrix products, contract_first(): lax.dot_general(left_op, right_op, (((0,), (0,)), ((), ())), preferred_el...  7.01 us
    dot_general x2, matrix products, contract_last(): lax.dot_general(left_op, right_op, (((1,), (1,)), ((), ())), preferred_el...  3.02 us
    dot_general x8, matrix products, partial_sums(): jnp.dot(weight, rows, preferred_element_type=jnp.float32)  2.85 us
    ppermute x1, starting transfers between devices, by_pairs(): far_up = lax.ppermute(up_later, ('groups', 'adapter'), FAR)  2.72 us
    ppermute x1, starting transfers between devices, by_pairs(): far_down = lax.ppermute(down_matrix, ('groups', 'adapter'), FAR)  2.59 us
    ppermute x1, starting transfers between devices, by_pairs(): cross_down = lax.ppermute(ready, 'groups', SWAP)  2.41 us
  transfers between devices with their start and end apart: 20, of which 8 were waited for; matrix products, arithmetic and copies ran while one was open for 16% of the time, Pallas kernels for 0%

profile of v9, /device:TPU:0, one launch (start us, length us, event | category | flops | bytes accessed | tf_op | source)
XLA Modules:
  0.0 92.1 jit_solution(14225797966268141602)
XLA Ops:
  0.7 3.1 %collective-permute-start.1 = (f32[1,256]{1,0:T(1,128)}, f32[1,256]{1,0:T(1,128)S(1)}, u32[]{:S(2)}, u32[]{:S(2)}) collective-permute-start(f32[1,256]{1,0:T(1,128)} %param.11), channel_id=1, source_target_pairs={{0,4},{2,6},{4,0},{6,2},{8,12},{10,14},{12,8},{14,10},{1,5},{3,7},... | collective-permute-start | bytes 3080 | tf_op jit(solution)/shard_map/ppermute | solution.py:111
  3.8 2.6 %collective-permute-start.5 = (bf16[64,2560]{1,0:T(8,128)(2,1)}, bf16[64,2560]{1,0:T(8,128)(2,1)}, u32[]{:S(2)}, u32[]{:S(2)}) collective-permute-start(bf16[64,2560]{1,0:T(8,128)(2,1)} %bitcast.71), channel_id=1, source_target_pairs={{0,8},{2,10},{4,12},{6,14},{8,0},{10,2},{12,4},{14,6},{16,28},{18,... | collective-permute-start | bytes 983048 | tf_op jit(solution)/shard_map/ppermute | solution.py:147
  6.4 1.5 %collective-permute-start.8 = (bf16[128,2560]{1,0:T(8,128)(2,1)}, bf16[128,2560]{1,0:T(8,128)(2,1)S(1)}, u32[]{:S(2)}, u32[]{:S(2)}) collective-permute-start(bf16[128,2560]{1,0:T(8,128)(2,1)} %param.6), channel_id=1, source_target_pairs={{0,2},{2,0},{4,6},{6,4},{8,10},{10,8},{12,14},{14,12},{1,3},{3,1},... | collective-permute-start | bytes 1966088 | tf_op jit(solution)/shard_map/ppermute | solution.py:111
  8.8 1.1 %constant_dynamic-update-slice_fusion.1 = bf16[256,2560]{1,0:T(8,128)(2,1)S(1)} fusion(bf16[128,2560]{1,0:T(8,128)(2,1)} %param.6), kind=kLoop, calls=%fused_computation.52 | loop fusion | bytes 1310720
  10.9 10.2 %collective-permute-done.2 = f32[2,256]{1,0:T(2,128)S(1)} collective-permute-done((f32[2,256]{1,0:T(2,128)S(1)}, f32[2,256]{1,0:T(2,128)S(1)}, u32[]{:S(2)}, u32[]{:S(2)}) %collective-permute-start.2) | collective-permute-done | bytes 2080 | tf_op jit(solution)/shard_map/ppermute | solution.py:111
  22.0 2.7 %collective-permute-start.3 = (bf16[64,2560]{1,0:T(8,128)(2,1)S(1)}, bf16[64,2560]{1,0:T(8,128)(2,1)S(1)}, u32[]{:S(2)}, u32[]{:S(2)}) collective-permute-start(bf16[64,2560]{1,0:T(8,128)(2,1)S(1)} %bitcast.67), channel_id=1, source_target_pairs={{0,8},{2,10},{4,12},{6,14},{8,0},{10,2},{12,4},{14,6},{16,28},{18,... | collective-permute-start | bytes 983048 | tf_op jit(solution)/shard_map/ppermute | solution.py:168
  24.7 2.4 %collective-permute-start.7 = (bf16[64,2560]{1,0:T(8,128)(2,1)}, bf16[64,2560]{1,0:T(8,128)(2,1)S(1)}, u32[]{:S(2)}, u32[]{:S(2)}) collective-permute-start(bf16[64,2560]{1,0:T(8,128)(2,1)} %collective-permute-done.5), channel_id=1, source_target_pairs={{0,16},{16,0},{1,17},{17,1},{2,18},{18,2},{3,19},{19,3},{4,20},{20... | collective-permute-start | bytes 983048 | tf_op jit(solution)/shard_map/ppermute | solution.py:170
  27.2 9.7 %collective-permute-done.6 = bf16[64,2560]{1,0:T(8,128)(2,1)S(1)} collective-permute-done((bf16[64,2560]{1,0:T(8,128)(2,1)S(1)}, bf16[64,2560]{1,0:T(8,128)(2,1)S(1)}, u32[]{:S(2)}, u32[]{:S(2)}) %collective-permute-start.6) | collective-permute-done | bytes 327712 | tf_op jit(solution)/shard_map/ppermute | solution.py:111
  36.9 1.5 %fusion.37 = f32[256,256]{1,0:T(8,128)S(1)} fusion(bf16[256,2560]{1,0:T(8,128)(2,1)S(1)} %constant_dynamic-update-slice_fusion, bf16[64,2560]{1,0:T(8,128)(2,1)S(1)} %collective-permute-done.7, bf16[64,2560]{1,0:T(8,128)(2,1)} %collective-permute-done.5, bf16[64,2560]{1,0:T(8,128)(2,1)S(1)} %collective-permute-done.6, bf16[64,2560]{1,0:T(8,128)(2,1)S(1)} %bitcast.73), kind=kOutput, calls=%fused_computation.68 | convolution fusion | flops 340787200 | bytes 2883584 | tf_op jit(solution)/shard_map/dot_general | solution.py:10
  38.6 1.5 %collective-permute-done.9 = f32[256,256]{1,0:T(8,128)S(1)} collective-permute-done((f32[256,256]{1,0:T(8,128)S(1)}, f32[256,256]{1,0:T(8,128)S(1)}, u32[]{:S(2)}, u32[]{:S(2)}) %collective-permute-start.9) | collective-permute-done | bytes 262176 | tf_op jit(solution)/shard_map/ppermute | solution.py:135
  41.8 1.9 %collective-permute-start.15 = (bf16[64,2560]{1,0:T(8,128)(2,1)S(1)}, bf16[64,2560]{1,0:T(8,128)(2,1)S(1)}, u32[]{:S(2)}, u32[]{:S(2)}) collective-permute-start(bf16[64,2560]{1,0:T(8,128)(2,1)S(1)} %fusion.13), channel_id=1, source_target_pairs={{0,4},{2,6},{4,0},{6,2},{8,12},{10,14},{12,8},{14,10},{1,5},{3,7},... | collective-permute-start | bytes 983048 | tf_op jit(solution)/shard_map/ppermute | solution.py:111
  43.7 8.5 %collective-permute-done.11 = bf16[64,2560]{1,0:T(8,128)(2,1)S(1)} collective-permute-done((bf16[64,2560]{1,0:T(8,128)(2,1)S(1)}, bf16[64,2560]{1,0:T(8,128)(2,1)S(1)}, u32[]{:S(2)}, u32[]{:S(2)}) %collective-permute-start.11) | collective-permute-done | bytes 327712 | tf_op jit(solution)/shard_map/ppermute | solution.py:111
  52.2 1.5 %fusion.38 = f32[256,256]{1,0:T(8,128)S(1)} fusion(bf16[256,2560]{1,0:T(8,128)(2,1)S(1)} %constant_dynamic-update-slice_fusion.2, bf16[64,2560]{1,0:T(8,128)(2,1)S(1)} %collective-permute-done.10, bf16[64,2560]{1,0:T(8,128)(2,1)S(1)} %collective-permute-done.3, bf16[64,2560]{1,0:T(8,128)(2,1)} %collective-permute-done.4, bf16[64,2560]{1,0:T(8,128)(2,1)S(1)} %bitcast.68), kind=kOutput, calls=%fused_computation.69 | convolution fusion | flops 340787200 | bytes 2883584 | tf_op jit(solution)/shard_map/dot_general | solution.py:10
  54.4 1.3 %convolution_convert_fusion.1 = bf16[128,2560]{1,0:T(8,128)(2,1)S(1)} fusion(bf16[256,128]{1,0:T(8,128)(2,1)S(1)} %bitcast.64, bf16[64,2560]{1,0:T(8,128)(2,1)S(1)} %collective-permute-done.10, bf16[64,2560]{1,0:T(8,128)(2,1)S(1)} %collective-permute-done.3, bf16[64,2560]{1,0:T(8,128)(2,1)} %collective-permute-done.4, bf16[64,2560]{1,0:T(8,128)(2,1)S(1)} %bitcast.69), kind=kOutput, calls=%fused_computation.4 | convolution fusion | flops 173342720 | bytes 2031616 | tf_op jit(solution)/shard_map/dot_general | solution.py:16
  55.7 1.7 %collective-permute-start.12 = (bf16[128,2560]{1,0:T(8,128)(2,1)S(1)}, bf16[128,2560]{1,0:T(8,128)(2,1)S(1)}, u32[]{:S(2)}, u32[]{:S(2)}) collective-permute-start(bf16[128,2560]{1,0:T(8,128)(2,1)S(1)} %convolution_convert_fusion.1), channel_id=1, source_target_pairs={{0,2},{2,0},{4,6},{6,4},{8,10},{10,8},{12,14},{14,12},{1,3},{3,1},... | collective-permute-start | bytes 1966088 | tf_op jit(solution)/shard_map/ppermute | solution.py:111
  59.0 1.3 %collective-permute-start.16 = (bf16[64,2560]{1,0:T(8,128)(2,1)S(1)}, bf16[64,2560]{1,0:T(8,128)(2,1)S(1)}, u32[]{:S(2)}, u32[]{:S(2)}) collective-permute-start(bf16[64,2560]{1,0:T(8,128)(2,1)S(1)} %fusion.5), channel_id=1, source_target_pairs={{0,4},{2,6},{4,0},{6,2},{8,12},{10,14},{12,8},{14,10},{1,5},{3,7},... | collective-permute-start | bytes 983048 | tf_op jit(solution)/shard_map/ppermute | solution.py:111
  60.3 1.3 %convolution_convert_fusion = bf16[128,2560]{1,0:T(8,128)(2,1)S(1)} fusion(bf16[256,128]{1,0:T(8,128)(2,1)S(1)} %bitcast.65, bf16[64,2560]{1,0:T(8,128)(2,1)S(1)} %collective-permute-done.7, bf16[64,2560]{1,0:T(8,128)(2,1)} %collective-permute-done.5, bf16[64,2560]{1,0:T(8,128)(2,1)S(1)} %collective-permute-done.6, bf16[64,2560]{1,0:T(8,128)(2,1)S(1)} %bitcast.74), kind=kOutput, calls=%fused_computation.3 | convolution fusion | flops 173342720 | bytes 2031616 | tf_op jit(solution)/shard_map/dot_general | solution.py:16
  62.2 9.9 %collective-permute-done.19 = bf16[64,2560]{1,0:T(8,128)(2,1)S(1)} collective-permute-done((bf16[64,2560]{1,0:T(8,128)(2,1)S(1)}, bf16[64,2560]{1,0:T(8,128)(2,1)S(1)}, u32[]{:S(2)}, u32[]{:S(2)}) %collective-permute-start.19) | collective-permute-done | bytes 327712 | tf_op jit(solution)/shard_map/ppermute | solution.py:111
  72.9 2.2 %collective-permute-done.16 = bf16[64,2560]{1,0:T(8,128)(2,1)S(1)} collective-permute-done((bf16[64,2560]{1,0:T(8,128)(2,1)S(1)}, bf16[64,2560]{1,0:T(8,128)(2,1)S(1)}, u32[]{:S(2)}, u32[]{:S(2)}) %collective-permute-start.16) | collective-permute-done | bytes 327712 | tf_op jit(solution)/shard_map/ppermute | solution.py:111
  75.2 2.3 %collective-permute-start.17 = (bf16[64,2560]{1,0:T(8,128)(2,1)S(1)}, bf16[64,2560]{1,0:T(8,128)(2,1)S(1)}, u32[]{:S(2)}, u32[]{:S(2)}) collective-permute-start(bf16[64,2560]{1,0:T(8,128)(2,1)S(1)} %fusion.3), channel_id=1, source_target_pairs={{0,4},{2,6},{4,0},{6,2},{8,12},{10,14},{12,8},{14,10},{1,5},{3,7},... | collective-permute-start | bytes 983048 | tf_op jit(solution)/shard_map/ppermute | solution.py:111
  77.6 2.2 %add_convert_fusion = bf16[128,2560]{1,0:T(8,128)(2,1)} fusion(bf16[128,2560]{1,0:T(8,128)(2,1)S(1)} %collective-permute-done.12, bf16[256,128]{1,0:T(8,128)(2,1)S(1)} %bitcast.62, bf16[64,2560]{1,0:T(8,128)(2,1)S(1)} %collective-permute-done.10, bf16[64,2560]{1,0:T(8,128)(2,1)S(1)} %collective-permute-done.3, bf16[64,2560]{1,0:T(8,128)(2,1)} %collective-permute-done.4, ...), kind=kOutput, calls=%fused_computation.7 | convolution fusion | flops 173998080 | bytes 2686976 | tf_op jit(solution)/shard_map/dot_general | solution.py:16
  79.8 6.9 %collective-permute-done.14 = bf16[128,2560]{1,0:T(8,128)(2,1)S(1)} collective-permute-done((bf16[128,2560]{1,0:T(8,128)(2,1)S(1)}, bf16[128,2560]{1,0:T(8,128)(2,1)S(1)}, u32[]{:S(2)}, u32[]{:S(2)}) %collective-permute-start.14) | collective-permute-done | bytes 655392 | tf_op jit(solution)/shard_map/ppermute | solution.py:111
  86.7 2.2 %fusion = bf16[128,2560]{1,0:T(8,128)(2,1)} fusion(bf16[256,128]{1,0:T(8,128)(2,1)S(1)} %bitcast.63, bf16[128,2560]{1,0:T(8,128)(2,1)S(1)} %collective-permute-done.14, bf16[64,2560]{1,0:T(8,128)(2,1)S(1)} %collective-permute-done.7, bf16[64,2560]{1,0:T(8,128)(2,1)} %collective-permute-done.5, bf16[64,2560]{1,0:T(8,128)(2,1)S(1)} %collective-permute-done.6, ...), kind=kOutput, calls=%fused_computation.2 | convolution fusion | flops 173998080 | bytes 2686976 | tf_op jit(solution)/shard_map/dot_general | solution.py:16
  88.9 2.4 %collective-permute-done.17 = bf16[64,2560]{1,0:T(8,128)(2,1)S(1)} collective-permute-done((bf16[64,2560]{1,0:T(8,128)(2,1)S(1)}, bf16[64,2560]{1,0:T(8,128)(2,1)S(1)}, u32[]{:S(2)}, u32[]{:S(2)}) %collective-permute-start.17) | collective-permute-done | bytes 327712 | tf_op jit(solution)/shard_map/ppermute | solution.py:111
  (65 shorter events, 9.2 us)
Async XLA Ops:
  0.6 10.2 %copy-start.2 = (f32[1,256]{1,0:T(1,128)S(1)}, f32[1,256]{1,0:T(1,128)}, u32[]{:S(2)}) copy-start(f32[1,256]{1,0:T(1,128)} %param.11) | copy-start | bytes 3076
  0.7 20.5 %copy-start.4 = (bf16[1,64,2560]{2,1,0:T(8,128)(2,1)S(1)}, bf16[1,64,2560]{2,1,0:T(8,128)(2,1)}, u32[]{:S(2)}) copy-start(bf16[1,64,2560]{2,1,0:T(8,128)(2,1)} %param.8) | copy-start | bytes 983044
  0.7 21.3 %copy-start.3 = (bf16[1,64,2560]{2,1,0:T(8,128)(2,1)S(1)}, bf16[1,64,2560]{2,1,0:T(8,128)(2,1)}, u32[]{:S(2)}) copy-start(bf16[1,64,2560]{2,1,0:T(8,128)(2,1)} %param.9) | copy-start | bytes 983044
  0.7 10.1 %collective-permute-start.1 = (f32[1,256]{1,0:T(1,128)}, f32[1,256]{1,0:T(1,128)S(1)}, u32[]{:S(2)}, u32[]{:S(2)}) collective-permute-start(f32[1,256]{1,0:T(1,128)} %param.11), channel_id=1, source_target_pairs={{0,4},{2,6},{4,0},{6,2},{8,12},{10,14},{12,8},{14,10},{1,5},{3,7},... | collective-permute-start | bytes 3080 | tf_op jit(solution)/shard_map/ppermute | solution.py:111
  3.8 18.2 %collective-permute-start.5 = (bf16[64,2560]{1,0:T(8,128)(2,1)}, bf16[64,2560]{1,0:T(8,128)(2,1)}, u32[]{:S(2)}, u32[]{:S(2)}) collective-permute-start(bf16[64,2560]{1,0:T(8,128)(2,1)} %bitcast.71), channel_id=1, source_target_pairs={{0,8},{2,10},{4,12},{6,14},{8,0},{10,2},{12,4},{14,6},{16,28},{18,... | collective-permute-start | bytes 983048 | tf_op jit(solution)/shard_map/ppermute | solution.py:147
  6.4 18.4 %collective-permute-start.8 = (bf16[128,2560]{1,0:T(8,128)(2,1)}, bf16[128,2560]{1,0:T(8,128)(2,1)S(1)}, u32[]{:S(2)}, u32[]{:S(2)}) collective-permute-start(bf16[128,2560]{1,0:T(8,128)(2,1)} %param.6), channel_id=1, source_target_pairs={{0,2},{2,0},{4,6},{6,4},{8,10},{10,8},{12,14},{14,12},{1,3},{3,1},... | collective-permute-start | bytes 1966088 | tf_op jit(solution)/shard_map/ppermute | solution.py:111
  7.8 32.3 %collective-permute-start.4 = (bf16[64,2560]{1,0:T(8,128)(2,1)}, bf16[64,2560]{1,0:T(8,128)(2,1)}, u32[]{:S(2)}, u32[]{:S(2)}) collective-permute-start(bf16[64,2560]{1,0:T(8,128)(2,1)} %bitcast.66), channel_id=1, source_target_pairs={{0,4},{2,6},{4,0},{6,2},{8,12},{10,14},{12,8},{14,10},{1,5},{3,7},... | collective-permute-start | bytes 983048 | tf_op jit(solution)/shard_map/ppermute | solution.py:111
  8.3 31.8 %collective-permute-start = (bf16[128,2560]{1,0:T(8,128)(2,1)}, bf16[128,2560]{1,0:T(8,128)(2,1)S(1)}, u32[]{:S(2)}, u32[]{:S(2)}) collective-permute-start(bf16[128,2560]{1,0:T(8,128)(2,1)} %param.7), channel_id=1, source_target_pairs={{0,2},{2,0},{4,6},{6,4},{8,10},{10,8},{12,14},{14,12},{1,3},{3,1},... | collective-permute-start | bytes 1966088 | tf_op jit(solution)/shard_map/ppermute | solution.py:111
  10.8 10.3 %collective-permute-start.2 = (f32[2,256]{1,0:T(2,128)S(1)}, f32[2,256]{1,0:T(2,128)S(1)}, u32[]{:S(2)}, u32[]{:S(2)}) collective-permute-start(f32[2,256]{1,0:T(2,128)S(1)} %pad_maximum_fusion.3), channel_id=1, source_target_pairs={{0,8},{2,10},{4,12},{6,14},{8,0},{10,2},{12,4},{14,6},{1,9},{3,11}... | collective-permute-start | bytes 6152 | tf_op jit(solution)/shard_map/ppermute | solution.py:111
  21.2 15.7 %collective-permute-start.6 = (bf16[64,2560]{1,0:T(8,128)(2,1)S(1)}, bf16[64,2560]{1,0:T(8,128)(2,1)S(1)}, u32[]{:S(2)}, u32[]{:S(2)}) collective-permute-start(bf16[64,2560]{1,0:T(8,128)(2,1)S(1)} %bitcast.72), channel_id=1, source_target_pairs={{0,4},{2,6},{4,0},{6,2},{8,12},{10,14},{12,8},{14,10},{1,5},{3,7},... | collective-permute-start | bytes 983048 | tf_op jit(solution)/shard_map/ppermute | solution.py:111
  22.0 18.1 %collective-permute-start.3 = (bf16[64,2560]{1,0:T(8,128)(2,1)S(1)}, bf16[64,2560]{1,0:T(8,128)(2,1)S(1)}, u32[]{:S(2)}, u32[]{:S(2)}) collective-permute-start(bf16[64,2560]{1,0:T(8,128)(2,1)S(1)} %bitcast.67), channel_id=1, source_target_pairs={{0,8},{2,10},{4,12},{6,14},{8,0},{10,2},{12,4},{14,6},{16,28},{18,... | collective-permute-start | bytes 983048 | tf_op jit(solution)/shard_map/ppermute | solution.py:168
  24.7 12.2 %collective-permute-start.7 = (bf16[64,2560]{1,0:T(8,128)(2,1)}, bf16[64,2560]{1,0:T(8,128)(2,1)S(1)}, u32[]{:S(2)}, u32[]{:S(2)}) collective-permute-start(bf16[64,2560]{1,0:T(8,128)(2,1)} %collective-permute-done.5), channel_id=1, source_target_pairs={{0,16},{16,0},{1,17},{17,1},{2,18},{18,2},{3,19},{19,3},{4,20},{20... | collective-permute-start | bytes 983048 | tf_op jit(solution)/shard_map/ppermute | solution.py:170
  27.2 11.3 %copy-start.1 = (bf16[128,2560]{1,0:T(8,128)(2,1)S(1)}, bf16[128,2560]{1,0:T(8,128)(2,1)}, u32[]{:S(2)}) copy-start(bf16[128,2560]{1,0:T(8,128)(2,1)} %param.7) | copy-start | bytes 1966084
  38.4 1.6 %collective-permute-start.9 = (f32[256,256]{1,0:T(8,128)S(1)}, f32[256,256]{1,0:T(8,128)S(1)}, u32[]{:S(2)}, u32[]{:S(2)}) collective-permute-start(f32[256,256]{1,0:T(8,128)S(1)} %fusion.37), channel_id=1, source_target_pairs={{0,1},{1,0},{2,3},{3,2},{4,5},{5,4},{6,7},{7,6},{8,9},{9,8},{10,11... | collective-permute-start | bytes 786440 | tf_op jit(solution)/shard_map/ppermute | solution.py:135
  41.6 10.6 %collective-permute-start.11 = (bf16[64,2560]{1,0:T(8,128)(2,1)S(1)}, bf16[64,2560]{1,0:T(8,128)(2,1)S(1)}, u32[]{:S(2)}, u32[]{:S(2)}) collective-permute-start(bf16[64,2560]{1,0:T(8,128)(2,1)S(1)} %fusion.9), channel_id=1, source_target_pairs={{0,4},{2,6},{4,0},{6,2},{8,12},{10,14},{12,8},{14,10},{1,5},{3,7},... | collective-permute-start | bytes 983048 | tf_op jit(solution)/shard_map/ppermute | solution.py:111
  41.7 10.5 %collective-permute-start.10 = (bf16[64,2560]{1,0:T(8,128)(2,1)S(1)}, bf16[64,2560]{1,0:T(8,128)(2,1)S(1)}, u32[]{:S(2)}, u32[]{:S(2)}) collective-permute-start(bf16[64,2560]{1,0:T(8,128)(2,1)S(1)} %collective-permute-done.3), channel_id=1, source_target_pairs={{0,16},{16,0},{1,17},{17,1},{2,18},{18,2},{3,19},{19,3},{4,20},{20... | collective-permute-start | bytes 983048 | tf_op jit(solution)/shard_map/ppermute | solution.py:192
  41.8 20.5 %collective-permute-start.15 = (bf16[64,2560]{1,0:T(8,128)(2,1)S(1)}, bf16[64,2560]{1,0:T(8,128)(2,1)S(1)}, u32[]{:S(2)}, u32[]{:S(2)}) collective-permute-start(bf16[64,2560]{1,0:T(8,128)(2,1)S(1)} %fusion.13), channel_id=1, source_target_pairs={{0,4},{2,6},{4,0},{6,2},{8,12},{10,14},{12,8},{14,10},{1,5},{3,7},... | collective-permute-start | bytes 983048 | tf_op jit(solution)/shard_map/ppermute | solution.py:111
  53.7 3.7 %collective-permute-start.13 = (f32[256,256]{1,0:T(8,128)S(1)}, f32[256,256]{1,0:T(8,128)S(1)}, u32[]{:S(2)}, u32[]{:S(2)}) collective-permute-start(f32[256,256]{1,0:T(8,128)S(1)} %fusion.38), channel_id=1, source_target_pairs={{0,1},{1,0},{2,3},{3,2},{4,5},{5,4},{6,7},{7,6},{8,9},{9,8},{10,11... | collective-permute-start | bytes 786440 | tf_op jit(solution)/shard_map/ppermute | solution.py:135
  53.9 18.2 %collective-permute-start.19 = (bf16[64,2560]{1,0:T(8,128)(2,1)S(1)}, bf16[64,2560]{1,0:T(8,128)(2,1)S(1)}, u32[]{:S(2)}, u32[]{:S(2)}) collective-permute-start(bf16[64,2560]{1,0:T(8,128)(2,1)S(1)} %add_convert_fusion.1), channel_id=1, source_target_pairs={{0,8},{2,10},{4,12},{6,14},{8,0},{10,2},{12,4},{14,6},{1,9},{3,11}... | collective-permute-start | bytes 983048 | tf_op jit(solution)/shard_map/ppermute | solution.py:111
  55.7 21.8 %collective-permute-start.12 = (bf16[128,2560]{1,0:T(8,128)(2,1)S(1)}, bf16[128,2560]{1,0:T(8,128)(2,1)S(1)}, u32[]{:S(2)}, u32[]{:S(2)}) collective-permute-start(bf16[128,2560]{1,0:T(8,128)(2,1)S(1)} %convolution_convert_fusion.1), channel_id=1, source_target_pairs={{0,2},{2,0},{4,6},{6,4},{8,10},{10,8},{12,14},{14,12},{1,3},{3,1},... | collective-permute-start | bytes 1966088 | tf_op jit(solution)/shard_map/ppermute | solution.py:111
  59.0 16.2 %collective-permute-start.16 = (bf16[64,2560]{1,0:T(8,128)(2,1)S(1)}, bf16[64,2560]{1,0:T(8,128)(2,1)S(1)}, u32[]{:S(2)}, u32[]{:S(2)}) collective-permute-start(bf16[64,2560]{1,0:T(8,128)(2,1)S(1)} %fusion.5), channel_id=1, source_target_pairs={{0,4},{2,6},{4,0},{6,2},{8,12},{10,14},{12,8},{14,10},{1,5},{3,7},... | collective-permute-start | bytes 983048 | tf_op jit(solution)/shard_map/ppermute | solution.py:111
  61.6 25.1 %collective-permute-start.14 = (bf16[128,2560]{1,0:T(8,128)(2,1)S(1)}, bf16[128,2560]{1,0:T(8,128)(2,1)S(1)}, u32[]{:S(2)}, u32[]{:S(2)}) collective-permute-start(bf16[128,2560]{1,0:T(8,128)(2,1)S(1)} %convolution_convert_fusion), channel_id=1, source_target_pairs={{0,2},{2,0},{4,6},{6,4},{8,10},{10,8},{12,14},{14,12},{1,3},{3,1},... | collective-permute-start | bytes 1966088 | tf_op jit(solution)/shard_map/ppermute | solution.py:111
  75.2 16.1 %collective-permute-start.18 = (bf16[64,2560]{1,0:T(8,128)(2,1)S(1)}, bf16[64,2560]{1,0:T(8,128)(2,1)S(1)}, u32[]{:S(2)}, u32[]{:S(2)}) collective-permute-start(bf16[64,2560]{1,0:T(8,128)(2,1)S(1)} %add_convert_fusion.2), channel_id=1, source_target_pairs={{0,8},{2,10},{4,12},{6,14},{8,0},{10,2},{12,4},{14,6},{1,9},{3,11}... | collective-permute-start | bytes 983048 | tf_op jit(solution)/shard_map/ppermute | solution.py:111
  75.2 16.0 %collective-permute-start.17 = (bf16[64,2560]{1,0:T(8,128)(2,1)S(1)}, bf16[64,2560]{1,0:T(8,128)(2,1)S(1)}, u32[]{:S(2)}, u32[]{:S(2)}) collective-permute-start(bf16[64,2560]{1,0:T(8,128)(2,1)S(1)} %fusion.3), channel_id=1, source_target_pairs={{0,4},{2,6},{4,0},{6,2},{8,12},{10,14},{12,8},{14,10},{1,5},{3,7},... | collective-permute-start | bytes 983048 | tf_op jit(solution)/shard_map/ppermute | solution.py:111
  (1 other events, 9.4 us)

commit v10 on v9

--- a/solution.py
+++ b/solution.py
@@ -149,7 +149,6 @@
     near_gate, down_later = lax.optimization_barrier((move(gating, xor_line(1)), down_matrix))
     near_down = move(down_later, xor_line(1))
     cot2 = move(cotangent, PARTNER)
-    near_up = move(up_matrix, xor_line(1))
     gates = jnp.concatenate([gating, near_gate])
     gates = jnp.concatenate([gates, move(gates, xor_line(2))])
 
@@ -163,16 +162,21 @@
     taken = lists[:, :, None] == ids[None, None, :]
     scale = jnp.sum(jnp.where(taken, gate_rows[:, :, None], 0.0), axis=1)
 
+    up_later, tokens2, scale = lax.optimization_barrier((up_matrix, tokens2, scale))
+    far_up = lax.ppermute(up_later, ("groups", "adapter"), FAR)
+    near_up = move(up_later, xor_line(1))
+    ready, near_down, scale = lax.optimization_barrier((far_down, near_down, scale))
+    cross_down = lax.ppermute(ready, "groups", SWAP)
     tokens2 = jnp.concatenate([tokens, tokens2], axis=0)
-    up_later, scale = lax.optimization_barrier((up_matrix, scale))
-    far_up = lax.ppermute(up_later, ("groups", "adapter"), FAR)
-    ready, scale = lax.optimization_barrier((far_down, scale))
-    cross_down = lax.ppermute(ready, "groups", SWAP)
     down_all = jnp.concatenate([down_matrix, near_down, far_down, cross_down], axis=0)
 
-    def low_rank(rows, matrices):
-        product = both_cores(contract_last(matrices, rows))
-        return narrow(scale[:, None, :] * product.reshape(-1, rank, 2 * tok_local))
+    def most_products(rows, *matrices):
+        return both_cores(contract_last(jnp.concatenate(matrices), rows))
+
+    def low_rank(most, rows, matrix):
+        products = [most[k * rank : (k + 1) * rank] for k in range(3)]
+        products.append(both_cores(contract_last(matrix, rows)))
+        return [narrow(scale[k] * product) for k, product in enumerate(products)]
 
     def for_line(low):
         second = jnp.where(first_group, low[2], low[3])
@@ -180,24 +184,27 @@
         return low[0], low[1], second, third
 
     def outward_start(low, matrix):
-        weights = low[:, :, tok_local:].reshape(-1, tok_local)
+        weights = jnp.concatenate([slot[:, tok_local:] for slot in low])
         return move(narrow(contract_first(weights, matrix)), PARTNER)
 
     def outward_end(low, matrix, back):
-        weights = low[:, :, :tok_local].reshape(-1, tok_local)
+        weights = jnp.concatenate([slot[:, :tok_local] for slot in low])
         return narrow(contract_first(weights, matrix) + back.astype(jnp.float32))
 
-    low = low_rank(tokens2, down_all)
+    most = most_products(tokens2, down_matrix, near_down, far_down)
+    low = low_rank(most, tokens2, cross_down)
     cot2, far_up, near_up, low = lax.optimization_barrier((cot2, far_up, near_up, low))
     cross_up = lax.ppermute(far_up, "groups", SWAP)
     cot2 = jnp.concatenate([cotangent, cot2], axis=0)
     (own, first, second, third), up_send = partial_sums(for_line(low), cot2)
     up_third = move(up_send[2], xor_line(1))
-    up_first = move(up_send[0], xor_line(1))
+    most = most_products(cot2, up_matrix, near_up, far_up)
+    most, up_next = lax.optimization_barrier((most, up_send[0]))
+    up_first = move(up_next, xor_line(1))
 
     cross_up = after(cross_up, up_third)
     up_all = jnp.concatenate([up_matrix, near_up, far_up, cross_up], axis=0)
-    low_back = low_rank(cot2, up_all)
+    low_back = low_rank(most, cot2, cross_up)
     (own_b, first_b, second_b, third_b), down_send = partial_sums(for_line(low_back), tokens2)
     down_third = move(down_send[2], xor_line(1))
     branch_back = outward_start(low, up_all)

time: 92.5 us -> 92.9 us (level)
  local copies, waits for them, and re-layouts: 1.9 us -> 4.08 us
  matrix products: 12.9 us -> 11 us
  starting transfers between devices: 22.5 us -> 24.2 us
  waiting for transfers between devices: 51.3 us -> 49.8 us
    ppermute x14, waiting for transfers between devices: 49.8 us -> 39.1 us  [move(): return lax.ppermute(value, 'adapter', pairs)]
    ppermute x1, waiting for transfers between devices: 0.01 us -> 3.52 us  [by_pairs(): far_up = lax.ppermute(up_later, ('groups', 'adapter'), FAR)]
    ppermute x1, waiting for transfers between devices: 0.01 us -> 2.89 us  [by_pairs(): cross_down = lax.ppermute(ready, 'groups', SWAP)]
    ppermute x2 -> x4, waiting for transfers between devices: 1.46 us -> 4.25 us  [both_cores(): return partial + lax.ppermute(partial, 'tensor', SWAP)]
    ppermute x1, starting transfers between devices: 0.07 us -> 2.48 us  [by_pairs(): cross_up = lax.ppermute(far_up, 'groups', SWAP)]
    ppermute x14, starting transfers between devices: 14.6 us -> 16.7 us  [move(): return lax.ppermute(value, 'adapter', pairs)]
    dot_general x4, matrix products: 7.01 us -> 5.06 us  [contract_first(): lax.dot_general(left_op, right_op, (((0,), (0,)), ((), ())), preferred_el...]
    ppermute x1, starting transfers between devices: 2.41 us -> 0.68 us  [by_pairs(): cross_down = lax.ppermute(ready, 'groups', SWAP)]
  transfers between devices with their start and end apart: 20 -> 22, of which waited for: 8 -> 13; matrix products, arithmetic and copies ran while one was open for 16% -> 14% of each run, Pallas kernels for 0% -> 0%
where the time goes in v10:
time: 92.9 us; the launch traced here: 92.6 us
  waiting for transfers between devices  49.8 us (54%)
  starting transfers between devices  24.2 us (26%)
  matrix products  11 us (12%)
  local copies, waits for them, and re-layouts  4.08 us (4%)
  other arithmetic  2.54 us (3%)
  between operations  0.93 us (1%)
    ppermute x14, waiting for transfers between devices, move(): return lax.ppermute(value, 'adapter', pairs)  39.1 us
    ppermute x14, starting transfers between devices, move(): return lax.ppermute(value, 'adapter', pairs)  16.7 us
    dot_general x4, matrix products, contract_first(): lax.dot_general(left_op, right_op, (((0,), (0,)), ((), ())), preferred_el...  5.06 us
    ppermute x4, waiting for transfers between devices, both_cores(): return partial + lax.ppermute(partial, 'tensor', SWAP)  4.25 us
    ppermute x1, waiting for transfers between devices, by_pairs(): far_up = lax.ppermute(up_later, ('groups', 'adapter'), FAR)  3.52 us
    dot_general x4, matrix products, contract_last(): lax.dot_general(left_op, right_op, (((1,), (1,)), ((), ())), preferred_el...  3.13 us
    ppermute x1, waiting for transfers between devices, by_pairs(): cross_down = lax.ppermute(ready, 'groups', SWAP)  2.89 us
    dot_general x8, matrix products, partial_sums(): jnp.dot(weight, rows, preferred_element_type=jnp.float32)  2.84 us
  transfers between devices with their start and end apart: 22, of which 13 were waited for; matrix products, arithmetic and copies ran while one was open for 14% of the time, Pallas kernels for 0%

profile of v10, /device:TPU:0, one launch (start us, length us, event | category | flops | bytes accessed | tf_op | source)
XLA Modules:
  0.0 92.6 jit_solution(808047573381828819)
XLA Ops:
  0.7 3.1 %collective-permute-start.2 = (f32[1,256]{1,0:T(1,128)}, f32[1,256]{1,0:T(1,128)S(1)}, u32[]{:S(2)}, u32[]{:S(2)}) collective-permute-start(f32[1,256]{1,0:T(1,128)} %param.11), channel_id=1, source_target_pairs={{0,4},{2,6},{4,0},{6,2},{8,12},{10,14},{12,8},{14,10},{1,5},{3,7},... | collective-permute-start | bytes 3080 | tf_op jit(solution)/shard_map/ppermute | solution.py:111
  3.7 1.5 %collective-permute-start.1 = (bf16[128,2560]{1,0:T(8,128)(2,1)}, bf16[128,2560]{1,0:T(8,128)(2,1)}, u32[]{:S(2)}, u32[]{:S(2)}) collective-permute-start(bf16[128,2560]{1,0:T(8,128)(2,1)} %param.6), channel_id=1, source_target_pairs={{0,2},{2,0},{4,6},{6,4},{8,10},{10,8},{12,14},{14,12},{1,3},{3,1},... | collective-permute-start | bytes 1966088 | tf_op jit(solution)/shard_map/ppermute | solution.py:111
  5.2 2.6 %collective-permute-start.6 = (bf16[64,2560]{1,0:T(8,128)(2,1)}, bf16[64,2560]{1,0:T(8,128)(2,1)}, u32[]{:S(2)}, u32[]{:S(2)}) collective-permute-start(bf16[64,2560]{1,0:T(8,128)(2,1)} %bitcast.51), channel_id=1, source_target_pairs={{0,8},{2,10},{4,12},{6,14},{8,0},{10,2},{12,4},{14,6},{16,28},{18,... | collective-permute-start | bytes 983048 | tf_op jit(solution)/shard_map/ppermute | solution.py:147
  11.1 11.4 %collective-permute-done.3 = f32[2,256]{1,0:T(2,128)S(1)} collective-permute-done((f32[2,256]{1,0:T(2,128)S(1)}, f32[2,256]{1,0:T(2,128)S(1)}, u32[]{:S(2)}, u32[]{:S(2)}) %collective-permute-start.3) | collective-permute-done | bytes 2080 | tf_op jit(solution)/shard_map/ppermute | solution.py:111
  22.8 1.5 %collective-permute-start.4 = (bf16[64,2560]{1,0:T(8,128)(2,1)}, bf16[64,2560]{1,0:T(8,128)(2,1)S(1)}, u32[]{:S(2)}, u32[]{:S(2)}) collective-permute-start(bf16[64,2560]{1,0:T(8,128)(2,1)} %bitcast.46), channel_id=1, source_target_pairs={{0,8},{2,10},{4,12},{6,14},{8,0},{10,2},{12,4},{14,6},{16,28},{18,... | collective-permute-start | bytes 983048 | tf_op jit(solution)/shard_map/ppermute | solution.py:166
  24.3 1.7 %collective-permute-start.5 = (bf16[64,2560]{1,0:T(8,128)(2,1)}, bf16[64,2560]{1,0:T(8,128)(2,1)S(1)}, u32[]{:S(2)}, u32[]{:S(2)}) collective-permute-start(bf16[64,2560]{1,0:T(8,128)(2,1)} %bitcast.47), channel_id=1, source_target_pairs={{0,4},{2,6},{4,0},{6,2},{8,12},{10,14},{12,8},{14,10},{1,5},{3,7},... | collective-permute-start | bytes 983048 | tf_op jit(solution)/shard_map/ppermute | solution.py:111
  28.2 1.5 %fusion.1 = f32[192,256]{1,0:T(8,128)S(1)} fusion(bf16[256,2560]{1,0:T(8,128)(2,1)S(1)} %constant_dynamic-update-slice_fusion, bf16[64,2560]{1,0:T(8,128)(2,1)} %collective-permute-done.6, bf16[64,2560]{1,0:T(8,128)(2,1)S(1)} %collective-permute-done.7, bf16[64,2560]{1,0:T(8,128)(2,1)S(1)} %bitcast.53), kind=kOutput, calls=%fused_computation.9 | convolution fusion | flops 254607360 | bytes 2490368 | tf_op jit(solution)/shard_map/dot_general | solution.py:10
  29.9 1.4 %collective-permute-done.8 = f32[192,256]{1,0:T(8,128)S(1)} collective-permute-done((f32[192,256]{1,0:T(8,128)S(1)}, f32[192,256]{1,0:T(8,128)S(1)}, u32[]{:S(2)}, u32[]{:S(2)}) %collective-permute-start.8) | collective-permute-done | bytes 196640 | tf_op jit(solution)/shard_map/ppermute | solution.py:135
  31.3 2.9 %collective-permute-done.9 = bf16[64,2560]{1,0:T(8,128)(2,1)S(1)} collective-permute-done((bf16[64,2560]{1,0:T(8,128)(2,1)}, bf16[64,2560]{1,0:T(8,128)(2,1)S(1)}, u32[]{:S(2)}, u32[]{:S(2)}) %collective-permute-start.9) | collective-permute-done | bytes 327712 | tf_op jit(solution)/shard_map/ppermute | solution.py:169
  34.8 1.2 %collective-permute-done.10 = f32[64,256]{1,0:T(8,128)S(1)} collective-permute-done((f32[64,256]{1,0:T(8,128)S(1)}, f32[64,256]{1,0:T(8,128)S(1)}, u32[]{:S(2)}, u32[]{:S(2)}) %collective-permute-start.10) | collective-permute-done | bytes 65568 | tf_op jit(solution)/shard_map/ppermute | solution.py:135
  36.1 3.5 %collective-permute-done.4 = bf16[64,2560]{1,0:T(8,128)(2,1)S(1)} collective-permute-done((bf16[64,2560]{1,0:T(8,128)(2,1)}, bf16[64,2560]{1,0:T(8,128)(2,1)S(1)}, u32[]{:S(2)}, u32[]{:S(2)}) %collective-permute-start.4) | collective-permute-done | bytes 327712 | tf_op jit(solution)/shard_map/ppermute | solution.py:166
  42.8 2.5 %collective-permute-start.11 = (bf16[64,2560]{1,0:T(8,128)(2,1)S(1)}, bf16[64,2560]{1,0:T(8,128)(2,1)S(1)}, u32[]{:S(2)}, u32[]{:S(2)}) collective-permute-start(bf16[64,2560]{1,0:T(8,128)(2,1)S(1)} %collective-permute-done.4), channel_id=1, source_target_pairs={{0,16},{16,0},{1,17},{17,1},{2,18},{18,2},{3,19},{19,3},{4,20},{20... | collective-permute-start | bytes 983048 | tf_op jit(solution)/shard_map/ppermute | solution.py:197
  46.0 1.4 %collective-permute-done.14 = f32[192,256]{1,0:T(8,128)S(1)} collective-permute-done((f32[192,256]{1,0:T(8,128)S(1)}, f32[192,256]{1,0:T(8,128)S(1)}, u32[]{:S(2)}, u32[]{:S(2)}) %collective-permute-start.14) | collective-permute-done | bytes 196640 | tf_op jit(solution)/shard_map/ppermute | solution.py:135
  47.8 1.2 %collective-permute-start.17 = (bf16[64,2560]{1,0:T(8,128)(2,1)S(1)}, bf16[64,2560]{1,0:T(8,128)(2,1)S(1)}, u32[]{:S(2)}, u32[]{:S(2)}) collective-permute-start(bf16[64,2560]{1,0:T(8,128)(2,1)S(1)} %fusion.79), channel_id=1, source_target_pairs={{0,4},{2,6},{4,0},{6,2},{8,12},{10,14},{12,8},{14,10},{1,5},{3,7},... | collective-permute-start | bytes 983048 | tf_op jit(solution)/shard_map/ppermute | solution.py:111
  49.3 3.6 %collective-permute-done.12 = bf16[64,2560]{1,0:T(8,128)(2,1)S(1)} collective-permute-done((bf16[64,2560]{1,0:T(8,128)(2,1)S(1)}, bf16[64,2560]{1,0:T(8,128)(2,1)S(1)}, u32[]{:S(2)}, u32[]{:S(2)}) %collective-permute-start.12) | collective-permute-done | bytes 327712 | tf_op jit(solution)/shard_map/ppermute | solution.py:111
  56.6 2.3 %collective-permute-start.18 = (bf16[64,2560]{1,0:T(8,128)(2,1)S(1)}, bf16[64,2560]{1,0:T(8,128)(2,1)S(1)}, u32[]{:S(2)}, u32[]{:S(2)}) collective-permute-start(bf16[64,2560]{1,0:T(8,128)(2,1)S(1)} %fusion.47), channel_id=1, source_target_pairs={{0,4},{2,6},{4,0},{6,2},{8,12},{10,14},{12,8},{14,10},{1,5},{3,7},... | collective-permute-start | bytes 983048 | tf_op jit(solution)/shard_map/ppermute | solution.py:111
  58.9 1.3 %convolution_convert_fusion = bf16[128,2560]{1,0:T(8,128)(2,1)S(1)} fusion(bf16[64,2560]{1,0:T(8,128)(2,1)S(1)} %collective-permute-done.9, bf16[64,2560]{1,0:T(8,128)(2,1)} %collective-permute-done.6, bf16[64,2560]{1,0:T(8,128)(2,1)S(1)} %collective-permute-done.7, bf16[64,2560]{1,0:T(8,128)(2,1)S(1)} %bitcast.54, ...), kind=kOutput, calls=%fused_computation.3 | convolution fusion | flops 173604864 | bytes 2031616 | tf_op jit(solution)/shard_map/dot_general | solution.py:16
  61.3 11.6 %collective-permute-done.18 = bf16[64,2560]{1,0:T(8,128)(2,1)S(1)} collective-permute-done((bf16[64,2560]{1,0:T(8,128)(2,1)S(1)}, bf16[64,2560]{1,0:T(8,128)(2,1)S(1)}, u32[]{:S(2)}, u32[]{:S(2)}) %collective-permute-start.18) | collective-permute-done | bytes 327712 | tf_op jit(solution)/shard_map/ppermute | solution.py:111
  72.9 1.2 %collective-permute-start.20 = (bf16[64,2560]{1,0:T(8,128)(2,1)S(1)}, bf16[64,2560]{1,0:T(8,128)(2,1)S(1)}, u32[]{:S(2)}, u32[]{:S(2)}) collective-permute-start(bf16[64,2560]{1,0:T(8,128)(2,1)S(1)} %add_convert_fusion.2), channel_id=1, source_target_pairs={{0,8},{2,10},{4,12},{6,14},{8,0},{10,2},{12,4},{14,6},{1,9},{3,11}... | collective-permute-start | bytes 983048 | tf_op jit(solution)/shard_map/ppermute | solution.py:111
  74.2 1.7 %collective-permute-start.19 = (bf16[64,2560]{1,0:T(8,128)(2,1)S(1)}, bf16[64,2560]{1,0:T(8,128)(2,1)S(1)}, u32[]{:S(2)}, u32[]{:S(2)}) collective-permute-start(bf16[64,2560]{1,0:T(8,128)(2,1)S(1)} %fusion.82), channel_id=1, source_target_pairs={{0,4},{2,6},{4,0},{6,2},{8,12},{10,14},{12,8},{14,10},{1,5},{3,7},... | collective-permute-start | bytes 983048 | tf_op jit(solution)/shard_map/ppermute | solution.py:111
  76.7 1.2 %add_convert_fusion = bf16[128,2560]{1,0:T(8,128)(2,1)} fusion(bf16[128,2560]{1,0:T(8,128)(2,1)S(1)} %collective-permute-done.13, bf16[64,2560]{1,0:T(8,128)(2,1)S(1)} %collective-permute-done.11, bf16[64,2560]{1,0:T(8,128)(2,1)S(1)} %collective-permute-done.4, bf16[64,2560]{1,0:T(8,128)(2,1)S(1)} %collective-permute-done.5, ...), kind=kOutput, calls=%fused_computation.7 | convolution fusion | flops 174260224 | bytes 2686976 | tf_op jit(solution)/shard_map/dot_general | solution.py:16
  77.9 9.6 %collective-permute-done.19 = bf16[64,2560]{1,0:T(8,128)(2,1)S(1)} collective-permute-done((bf16[64,2560]{1,0:T(8,128)(2,1)S(1)}, bf16[64,2560]{1,0:T(8,128)(2,1)S(1)}, u32[]{:S(2)}, u32[]{:S(2)}) %collective-permute-start.19) | collective-permute-done | bytes 327712 | tf_op jit(solution)/shard_map/ppermute | solution.py:111
  87.6 1.9 %collective-permute-done.20 = bf16[64,2560]{1,0:T(8,128)(2,1)S(1)} collective-permute-done((bf16[64,2560]{1,0:T(8,128)(2,1)S(1)}, bf16[64,2560]{1,0:T(8,128)(2,1)S(1)}, u32[]{:S(2)}, u32[]{:S(2)}) %collective-permute-start.20) | collective-permute-done | bytes 327712 | tf_op jit(solution)/shard_map/ppermute | solution.py:111
  90.4 2.2 %fusion = bf16[128,2560]{1,0:T(8,128)(2,1)} fusion(bf16[128,2560]{1,0:T(8,128)(2,1)S(1)} %collective-permute-done.16, bf16[64,2560]{1,0:T(8,128)(2,1)S(1)} %collective-permute-done.9, bf16[64,2560]{1,0:T(8,128)(2,1)} %collective-permute-done.6, bf16[64,2560]{1,0:T(8,128)(2,1)S(1)} %collective-permute-done.7, bf16[64,2560]{1,0:T(8,128)(2,1)S(1)} %bitcast.55, ...), kind=kOutput, calls=%fused_computation.2 | convolution fusion | flops 174260224 | bytes 2686976 | tf_op jit(solution)/shard_map/dot_general | solution.py:16
  (80 shorter events, 17.5 us)
Async XLA Ops:
  0.6 9.1 %copy-start = (s32[8,256]{1,0:T(8,128)S(1)}, s32[8,256]{1,0:T(8,128)}, u32[]{:S(2)}) copy-start(s32[8,256]{1,0:T(8,128)} %param.10) | copy-start | bytes 24580
  0.7 9.8 %collective-permute-start.2 = (f32[1,256]{1,0:T(1,128)}, f32[1,256]{1,0:T(1,128)S(1)}, u32[]{:S(2)}, u32[]{:S(2)}) collective-permute-start(f32[1,256]{1,0:T(1,128)} %param.11), channel_id=1, source_target_pairs={{0,4},{2,6},{4,0},{6,2},{8,12},{10,14},{12,8},{14,10},{1,5},{3,7},... | collective-permute-start | bytes 3080 | tf_op jit(solution)/shard_map/ppermute | solution.py:111
  3.7 19.0 %collective-permute-start.1 = (bf16[128,2560]{1,0:T(8,128)(2,1)}, bf16[128,2560]{1,0:T(8,128)(2,1)}, u32[]{:S(2)}, u32[]{:S(2)}) collective-permute-start(bf16[128,2560]{1,0:T(8,128)(2,1)} %param.6), channel_id=1, source_target_pairs={{0,2},{2,0},{4,6},{6,4},{8,10},{10,8},{12,14},{14,12},{1,3},{3,1},... | collective-permute-start | bytes 1966088 | tf_op jit(solution)/shard_map/ppermute | solution.py:111
  5.2 20.8 %collective-permute-start.6 = (bf16[64,2560]{1,0:T(8,128)(2,1)}, bf16[64,2560]{1,0:T(8,128)(2,1)}, u32[]{:S(2)}, u32[]{:S(2)}) collective-permute-start(bf16[64,2560]{1,0:T(8,128)(2,1)} %bitcast.51), channel_id=1, source_target_pairs={{0,8},{2,10},{4,12},{6,14},{8,0},{10,2},{12,4},{14,6},{16,28},{18,... | collective-permute-start | bytes 983048 | tf_op jit(solution)/shard_map/ppermute | solution.py:147
  7.8 28.2 %collective-permute-start = (bf16[128,2560]{1,0:T(8,128)(2,1)}, bf16[128,2560]{1,0:T(8,128)(2,1)}, u32[]{:S(2)}, u32[]{:S(2)}) collective-permute-start(bf16[128,2560]{1,0:T(8,128)(2,1)} %param.7), channel_id=1, source_target_pairs={{0,2},{2,0},{4,6},{6,4},{8,10},{10,8},{12,14},{14,12},{1,3},{3,1},... | collective-permute-start | bytes 1966088 | tf_op jit(solution)/shard_map/ppermute | solution.py:111
  9.6 18.6 %copy-start.4 = (bf16[1,64,2560]{2,1,0:T(8,128)(2,1)S(1)}, bf16[1,64,2560]{2,1,0:T(8,128)(2,1)}, u32[]{:S(2)}) copy-start(bf16[1,64,2560]{2,1,0:T(8,128)(2,1)} %param.8) | copy-start | bytes 983044
  10.4 12.0 %collective-permute-start.3 = (f32[2,256]{1,0:T(2,128)S(1)}, f32[2,256]{1,0:T(2,128)S(1)}, u32[]{:S(2)}, u32[]{:S(2)}) collective-permute-start(f32[2,256]{1,0:T(2,128)S(1)} %pad_maximum_fusion.9), channel_id=1, source_target_pairs={{0,8},{2,10},{4,12},{6,14},{8,0},{10,2},{12,4},{14,6},{1,9},{3,11}... | collective-permute-start | bytes 6152 | tf_op jit(solution)/shard_map/ppermute | solution.py:111
  10.9 15.5 %collective-permute-start.7 = (bf16[64,2560]{1,0:T(8,128)(2,1)}, bf16[64,2560]{1,0:T(8,128)(2,1)S(1)}, u32[]{:S(2)}, u32[]{:S(2)}) collective-permute-start(bf16[64,2560]{1,0:T(8,128)(2,1)} %bitcast.52), channel_id=1, source_target_pairs={{0,4},{2,6},{4,0},{6,2},{8,12},{10,14},{12,8},{14,10},{1,5},{3,7},... | collective-permute-start | bytes 983048 | tf_op jit(solution)/shard_map/ppermute | solution.py:111
  22.8 16.8 %collective-permute-start.4 = (bf16[64,2560]{1,0:T(8,128)(2,1)}, bf16[64,2560]{1,0:T(8,128)(2,1)S(1)}, u32[]{:S(2)}, u32[]{:S(2)}) collective-permute-start(bf16[64,2560]{1,0:T(8,128)(2,1)} %bitcast.46), channel_id=1, source_target_pairs={{0,8},{2,10},{4,12},{6,14},{8,0},{10,2},{12,4},{14,6},{16,28},{18,... | collective-permute-start | bytes 983048 | tf_op jit(solution)/shard_map/ppermute | solution.py:166
  24.3 15.9 %collective-permute-start.5 = (bf16[64,2560]{1,0:T(8,128)(2,1)}, bf16[64,2560]{1,0:T(8,128)(2,1)S(1)}, u32[]{:S(2)}, u32[]{:S(2)}) collective-permute-start(bf16[64,2560]{1,0:T(8,128)(2,1)} %bitcast.47), channel_id=1, source_target_pairs={{0,4},{2,6},{4,0},{6,2},{8,12},{10,14},{12,8},{14,10},{1,5},{3,7},... | collective-permute-start | bytes 983048 | tf_op jit(solution)/shard_map/ppermute | solution.py:111
  26.4 7.8 %collective-permute-start.9 = (bf16[64,2560]{1,0:T(8,128)(2,1)}, bf16[64,2560]{1,0:T(8,128)(2,1)S(1)}, u32[]{:S(2)}, u32[]{:S(2)}) collective-permute-start(bf16[64,2560]{1,0:T(8,128)(2,1)} %collective-permute-done.6), channel_id=1, source_target_pairs={{0,16},{16,0},{1,17},{17,1},{2,18},{18,2},{3,19},{19,3},{4,20},{20... | collective-permute-start | bytes 983048 | tf_op jit(solution)/shard_map/ppermute | solution.py:169
  29.8 1.5 %collective-permute-start.8 = (f32[192,256]{1,0:T(8,128)S(1)}, f32[192,256]{1,0:T(8,128)S(1)}, u32[]{:S(2)}, u32[]{:S(2)}) collective-permute-start(f32[192,256]{1,0:T(8,128)S(1)} %fusion.1), channel_id=1, source_target_pairs={{0,1},{1,0},{2,3},{3,2},{4,5},{5,4},{6,7},{7,6},{8,9},{9,8},{10,11... | collective-permute-start | bytes 589832 | tf_op jit(solution)/shard_map/ppermute | solution.py:135
  34.7 1.3 %collective-permute-start.10 = (f32[64,256]{1,0:T(8,128)S(1)}, f32[64,256]{1,0:T(8,128)S(1)}, u32[]{:S(2)}, u32[]{:S(2)}) collective-permute-start(f32[64,256]{1,0:T(8,128)S(1)} %fusion.77), channel_id=1, source_target_pairs={{0,1},{1,0},{2,3},{3,2},{4,5},{5,4},{6,7},{7,6},{8,9},{9,8},{10,11... | collective-permute-start | bytes 196616 | tf_op jit(solution)/shard_map/ppermute | solution.py:135
  42.8 10.2 %collective-permute-start.12 = (bf16[64,2560]{1,0:T(8,128)(2,1)S(1)}, bf16[64,2560]{1,0:T(8,128)(2,1)S(1)}, u32[]{:S(2)}, u32[]{:S(2)}) collective-permute-start(bf16[64,2560]{1,0:T(8,128)(2,1)S(1)} %fusion.51), channel_id=1, source_target_pairs={{0,4},{2,6},{4,0},{6,2},{8,12},{10,14},{12,8},{14,10},{1,5},{3,7},... | collective-permute-start | bytes 983048 | tf_op jit(solution)/shard_map/ppermute | solution.py:111
  42.8 11.2 %collective-permute-start.11 = (bf16[64,2560]{1,0:T(8,128)(2,1)S(1)}, bf16[64,2560]{1,0:T(8,128)(2,1)S(1)}, u32[]{:S(2)}, u32[]{:S(2)}) collective-permute-start(bf16[64,2560]{1,0:T(8,128)(2,1)S(1)} %collective-permute-done.4), channel_id=1, source_target_pairs={{0,16},{16,0},{1,17},{17,1},{2,18},{18,2},{3,19},{19,3},{4,20},{20... | collective-permute-start | bytes 983048 | tf_op jit(solution)/shard_map/ppermute | solution.py:197
  45.9 1.5 %collective-permute-start.14 = (f32[192,256]{1,0:T(8,128)S(1)}, f32[192,256]{1,0:T(8,128)S(1)}, u32[]{:S(2)}, u32[]{:S(2)}) collective-permute-start(f32[192,256]{1,0:T(8,128)S(1)} %fusion.7), channel_id=1, source_target_pairs={{0,1},{1,0},{2,3},{3,2},{4,5},{5,4},{6,7},{7,6},{8,9},{9,8},{10,11... | collective-permute-start | bytes 589832 | tf_op jit(solution)/shard_map/ppermute | solution.py:135
  47.8 26.4 %collective-permute-start.17 = (bf16[64,2560]{1,0:T(8,128)(2,1)S(1)}, bf16[64,2560]{1,0:T(8,128)(2,1)S(1)}, u32[]{:S(2)}, u32[]{:S(2)}) collective-permute-start(bf16[64,2560]{1,0:T(8,128)(2,1)S(1)} %fusion.79), channel_id=1, source_target_pairs={{0,4},{2,6},{4,0},{6,2},{8,12},{10,14},{12,8},{14,10},{1,5},{3,7},... | collective-permute-start | bytes 983048 | tf_op jit(solution)/shard_map/ppermute | solution.py:111
  53.0 22.9 %collective-permute-start.21 = (bf16[64,2560]{1,0:T(8,128)(2,1)S(1)}, bf16[64,2560]{1,0:T(8,128)(2,1)S(1)}, u32[]{:S(2)}, u32[]{:S(2)}) collective-permute-start(bf16[64,2560]{1,0:T(8,128)(2,1)S(1)} %add_convert_fusion.1), channel_id=1, source_target_pairs={{0,8},{2,10},{4,12},{6,14},{8,0},{10,2},{12,4},{14,6},{1,9},{3,11}... | collective-permute-start | bytes 983048 | tf_op jit(solution)/shard_map/ppermute | solution.py:111
  54.5 1.3 %collective-permute-start.15 = (f32[64,256]{1,0:T(8,128)S(1)}, f32[64,256]{1,0:T(8,128)S(1)}, u32[]{:S(2)}, u32[]{:S(2)}) collective-permute-start(f32[64,256]{1,0:T(8,128)S(1)} %fusion.80), channel_id=1, source_target_pairs={{0,1},{1,0},{2,3},{3,2},{4,5},{5,4},{6,7},{7,6},{8,9},{9,8},{10,11... | collective-permute-start | bytes 196616 | tf_op jit(solution)/shard_map/ppermute | solution.py:135
  55.0 21.8 %collective-permute-start.13 = (bf16[128,2560]{1,0:T(8,128)(2,1)S(1)}, bf16[128,2560]{1,0:T(8,128)(2,1)S(1)}, u32[]{:S(2)}, u32[]{:S(2)}) collective-permute-start(bf16[128,2560]{1,0:T(8,128)(2,1)S(1)} %convolution_convert_fusion.1), channel_id=1, source_target_pairs={{0,2},{2,0},{4,6},{6,4},{8,10},{10,8},{12,14},{14,12},{1,3},{3,1},... | collective-permute-start | bytes 1966088 | tf_op jit(solution)/shard_map/ppermute | solution.py:111
  56.6 16.3 %collective-permute-start.18 = (bf16[64,2560]{1,0:T(8,128)(2,1)S(1)}, bf16[64,2560]{1,0:T(8,128)(2,1)S(1)}, u32[]{:S(2)}, u32[]{:S(2)}) collective-permute-start(bf16[64,2560]{1,0:T(8,128)(2,1)S(1)} %fusion.47), channel_id=1, source_target_pairs={{0,4},{2,6},{4,0},{6,2},{8,12},{10,14},{12,8},{14,10},{1,5},{3,7},... | collective-permute-start | bytes 983048 | tf_op jit(solution)/shard_map/ppermute | solution.py:111
  60.2 30.1 %collective-permute-start.16 = (bf16[128,2560]{1,0:T(8,128)(2,1)S(1)}, bf16[128,2560]{1,0:T(8,128)(2,1)S(1)}, u32[]{:S(2)}, u32[]{:S(2)}) collective-permute-start(bf16[128,2560]{1,0:T(8,128)(2,1)S(1)} %convolution_convert_fusion), channel_id=1, source_target_pairs={{0,2},{2,0},{4,6},{6,4},{8,10},{10,8},{12,14},{14,12},{1,3},{3,1},... | collective-permute-start | bytes 1966088 | tf_op jit(solution)/shard_map/ppermute | solution.py:111
  72.9 16.6 %collective-permute-start.20 = (bf16[64,2560]{1,0:T(8,128)(2,1)S(1)}, bf16[64,2560]{1,0:T(8,128)(2,1)S(1)}, u32[]{:S(2)}, u32[]{:S(2)}) collective-permute-start(bf16[64,2560]{1,0:T(8,128)(2,1)S(1)} %add_convert_fusion.2), channel_id=1, source_target_pairs={{0,8},{2,10},{4,12},{6,14},{8,0},{10,2},{12,4},{14,6},{1,9},{3,11}... | collective-permute-start | bytes 983048 | tf_op jit(solution)/shard_map/ppermute | solution.py:111
  74.2 13.4 %collective-permute-start.19 = (bf16[64,2560]{1,0:T(8,128)(2,1)S(1)}, bf16[64,2560]{1,0:T(8,128)(2,1)S(1)}, u32[]{:S(2)}, u32[]{:S(2)}) collective-permute-start(bf16[64,2560]{1,0:T(8,128)(2,1)S(1)} %fusion.82), channel_id=1, source_target_pairs={{0,4},{2,6},{4,0},{6,2},{8,12},{10,14},{12,8},{14,10},{1,5},{3,7},... | collective-permute-start | bytes 983048 | tf_op jit(solution)/shard_map/ppermute | solution.py:111
  (3 other events, 13.9 us)

commit v11 on v10

--- a/solution.py
+++ b/solution.py
@@ -146,8 +146,11 @@
 
     far_down = lax.ppermute(down_matrix, ("groups", "adapter"), FAR)
     tokens2 = move(tokens, PARTNER)
-    near_gate, down_later = lax.optimization_barrier((move(gating, xor_line(1)), down_matrix))
-    near_down = move(down_later, xor_line(1))
+    near_gate, down_later, up_later = lax.optimization_barrier(
+        (move(gating, xor_line(1)), down_matrix, up_matrix)
+    )
+    near_down, up_last = lax.optimization_barrier((move(down_later, xor_line(1)), up_matrix))
+    near_up = move(up_last, xor_line(1))
     cot2 = move(cotangent, PARTNER)
     gates = jnp.concatenate([gating, near_gate])
     gates = jnp.concatenate([gates, move(gates, xor_line(2))])
@@ -162,10 +165,8 @@
     taken = lists[:, :, None] == ids[None, None, :]
     scale = jnp.sum(jnp.where(taken, gate_rows[:, :, None], 0.0), axis=1)
 
-    up_later, tokens2, scale = lax.optimization_barrier((up_matrix, tokens2, scale))
     far_up = lax.ppermute(up_later, ("groups", "adapter"), FAR)
-    near_up = move(up_later, xor_line(1))
-    ready, near_down, scale = lax.optimization_barrier((far_down, near_down, scale))
+    ready, scale = lax.optimization_barrier((far_down, scale))
     cross_down = lax.ppermute(ready, "groups", SWAP)
     tokens2 = jnp.concatenate([tokens, tokens2], axis=0)
     down_all = jnp.concatenate([down_matrix, near_down, far_down, cross_down], axis=0)
@@ -192,8 +193,9 @@
         return narrow(contract_first(weights, matrix) + back.astype(jnp.float32))
 
     most = most_products(tokens2, down_matrix, near_down, far_down)
+    most, tokens2 = lax.optimization_barrier((most, tokens2))
     low = low_rank(most, tokens2, cross_down)
-    cot2, far_up, near_up, low = lax.optimization_barrier((cot2, far_up, near_up, low))
+    cot2, far_up, low = lax.optimization_barrier((cot2, far_up, low))
     cross_up = lax.ppermute(far_up, "groups", SWAP)
     cot2 = jnp.concatenate([cotangent, cot2], axis=0)
     (own, first, second, third), up_send = partial_sums(for_line(low), cot2)

time: 92.9 us -> 93.9 us (1.011)
  waiting for transfers between devices: 49.8 us -> 52.8 us
  starting transfers between devices: 24.2 us -> 22.1 us
    ppermute x14, waiting for transfers between devices: 39.1 us -> 43.3 us  [move(): return lax.ppermute(value, 'adapter', pairs)]
    ppermute x1, starting transfers between devices: 0.68 us -> 4.26 us  [by_pairs(): cross_down = lax.ppermute(ready, 'groups', SWAP)]
    ppermute x14, starting transfers between devices: 16.7 us -> 14.2 us  [move(): return lax.ppermute(value, 'adapter', pairs)]
    ppermute x1, starting transfers between devices: 2.48 us -> 0.76 us  [by_pairs(): cross_up = lax.ppermute(far_up, 'groups', SWAP)]
    ppermute x1, starting transfers between devices: 1.51 us -> 0.01 us  [by_pairs(): far_up = lax.ppermute(up_later, ('groups', 'adapter'), FAR)]
    ppermute x1, waiting for transfers between devices: 2.89 us -> 1.86 us  [by_pairs(): cross_down = lax.ppermute(ready, 'groups', SWAP)]
  transfers between devices with their start and end apart: 22 -> 22, of which waited for: 13 -> 11; matrix products, arithmetic and copies ran while one was open for 14% -> 17% of each run, Pallas kernels for 0% -> 0%
where the time goes in v11:
time: 93.9 us; the launch traced here: 93.6 us
  waiting for transfers between devices  52.8 us (56%)
  starting transfers between devices  22.1 us (24%)
  matrix products  11.1 us (12%)
  local copies, waits for them, and re-layouts  4.09 us (4%)
  other arithmetic  2.54 us (3%)
    ppermute x14, waiting for transfers between devices, move(): return lax.ppermute(value, 'adapter', pairs)  43.3 us
    ppermute x14, starting transfers between devices, move(): return lax.ppermute(value, 'adapter', pairs)  14.2 us
    dot_general x4, matrix products, contract_first(): lax.dot_general(left_op, right_op, (((0,), (0,)), ((), ())), preferred_el...  5.07 us
    ppermute x1, starting transfers between devices, by_pairs(): cross_down = lax.ppermute(ready, 'groups', SWAP)  4.26 us
    ppermute x4, waiting for transfers between devices, both_cores(): return partial + lax.ppermute(partial, 'tensor', SWAP)  3.94 us
    ppermute x1, waiting for transfers between devices, by_pairs(): far_up = lax.ppermute(up_later, ('groups', 'adapter'), FAR)  3.69 us
    dot_general x4, matrix products, contract_last(): lax.dot_general(left_op, right_op, (((1,), (1,)), ((), ())), preferred_el...  3.18 us
    dot_general x8, matrix products, partial_sums(): jnp.dot(weight, rows, preferred_element_type=jnp.float32)  2.84 us
  transfers between devices with their start and end apart: 22, of which 11 were waited for; matrix products, arithmetic and copies ran while one was open for 17% of the time, Pallas kernels for 0%

profile of v11, /device:TPU:0, one launch (start us, length us, event | category | flops | bytes accessed | tf_op | source)
XLA Modules:
  0.0 93.6 jit_solution(14137120983708377057)
XLA Ops:
  0.7 3.1 %collective-permute-start.1 = (f32[1,256]{1,0:T(1,128)}, f32[1,256]{1,0:T(1,128)S(1)}, u32[]{:S(2)}, u32[]{:S(2)}) collective-permute-start(f32[1,256]{1,0:T(1,128)} %param.11), channel_id=1, source_target_pairs={{0,4},{2,6},{4,0},{6,2},{8,12},{10,14},{12,8},{14,10},{1,5},{3,7},... | collective-permute-start | bytes 3080 | tf_op jit(solution)/shard_map/ppermute | solution.py:111
  3.7 2.6 %collective-permute-start.3 = (bf16[64,2560]{1,0:T(8,128)(2,1)}, bf16[64,2560]{1,0:T(8,128)(2,1)}, u32[]{:S(2)}, u32[]{:S(2)}) collective-permute-start(bf16[64,2560]{1,0:T(8,128)(2,1)} %bitcast.51), channel_id=1, source_target_pairs={{0,8},{2,10},{4,12},{6,14},{8,0},{10,2},{12,4},{14,6},{16,28},{18,... | collective-permute-start | bytes 983048 | tf_op jit(solution)/shard_map/ppermute | solution.py:147
  6.3 1.5 %collective-permute-start.6 = (bf16[128,2560]{1,0:T(8,128)(2,1)}, bf16[128,2560]{1,0:T(8,128)(2,1)}, u32[]{:S(2)}, u32[]{:S(2)}) collective-permute-start(bf16[128,2560]{1,0:T(8,128)(2,1)} %param.6), channel_id=1, source_target_pairs={{0,2},{2,0},{4,6},{6,4},{8,10},{10,8},{12,14},{14,12},{1,3},{3,1},... | collective-permute-start | bytes 1966088 | tf_op jit(solution)/shard_map/ppermute | solution.py:111
  8.4 1.1 %constant_dynamic-update-slice_fusion.1 = bf16[256,2560]{1,0:T(8,128)(2,1)S(1)} fusion(bf16[128,2560]{1,0:T(8,128)(2,1)} %param.6), kind=kLoop, calls=%fused_computation.77 | loop fusion | bytes 1310720
  11.1 10.1 %collective-permute-done.4 = f32[2,256]{1,0:T(2,128)S(1)} collective-permute-done((f32[2,256]{1,0:T(2,128)S(1)}, f32[2,256]{1,0:T(2,128)S(1)}, u32[]{:S(2)}, u32[]{:S(2)}) %collective-permute-start.4) | collective-permute-done | bytes 2080 | tf_op jit(solution)/shard_map/ppermute | solution.py:111
  21.5 4.3 %collective-permute-start.8 = (bf16[64,2560]{1,0:T(8,128)(2,1)}, bf16[64,2560]{1,0:T(8,128)(2,1)S(1)}, u32[]{:S(2)}, u32[]{:S(2)}) collective-permute-start(bf16[64,2560]{1,0:T(8,128)(2,1)} %collective-permute-done.3), channel_id=1, source_target_pairs={{0,16},{16,0},{1,17},{17,1},{2,18},{18,2},{3,19},{19,3},{4,20},{20... | collective-permute-start | bytes 983048 | tf_op jit(solution)/shard_map/ppermute | solution.py:170
  26.2 1.1 %constant_dynamic-update-slice_fusion = bf16[256,2560]{1,0:T(8,128)(2,1)S(1)} fusion(bf16[256,2560]{1,0:T(8,128)(2,1)S(1)} %constant_dynamic-update-slice_fusion.1, bf16[128,2560]{1,0:T(8,128)(2,1)} %collective-permute-done.6), kind=kLoop, calls=%fused_computation.76 | loop fusion | bytes 1310720 | tf_op jit(solution)/shard_map/concatenate | solution.py:171
  27.4 1.6 %fusion.2 = f32[192,256]{1,0:T(8,128)S(1)} fusion(bf16[256,2560]{1,0:T(8,128)(2,1)S(1)} %constant_dynamic-update-slice_fusion, bf16[64,2560]{1,0:T(8,128)(2,1)} %collective-permute-done.3, bf16[64,2560]{1,0:T(8,128)(2,1)S(1)} %collective-permute-done.5, bf16[64,2560]{1,0:T(8,128)(2,1)S(1)} %bitcast.53), kind=kOutput, calls=%fused_computation.10 | convolution fusion | flops 254607360 | bytes 2490368 | tf_op jit(solution)/shard_map/dot_general | solution.py:10
  29.2 1.3 %collective-permute-done.7 = f32[192,256]{1,0:T(8,128)S(1)} collective-permute-done((f32[192,256]{1,0:T(8,128)S(1)}, f32[192,256]{1,0:T(8,128)S(1)}, u32[]{:S(2)}, u32[]{:S(2)}) %collective-permute-start.7) | collective-permute-done | bytes 196640 | tf_op jit(solution)/shard_map/ppermute | solution.py:135
  30.5 1.9 %collective-permute-done.8 = bf16[64,2560]{1,0:T(8,128)(2,1)S(1)} collective-permute-done((bf16[64,2560]{1,0:T(8,128)(2,1)}, bf16[64,2560]{1,0:T(8,128)(2,1)S(1)}, u32[]{:S(2)}, u32[]{:S(2)}) %collective-permute-start.8) | collective-permute-done | bytes 327712 | tf_op jit(solution)/shard_map/ppermute | solution.py:170
  33.0 1.2 %collective-permute-done.9 = f32[64,256]{1,0:T(8,128)S(1)} collective-permute-done((f32[64,256]{1,0:T(8,128)S(1)}, f32[64,256]{1,0:T(8,128)S(1)}, u32[]{:S(2)}, u32[]{:S(2)}) %collective-permute-start.9) | collective-permute-done | bytes 65568 | tf_op jit(solution)/shard_map/ppermute | solution.py:135
  34.2 3.7 %collective-permute-done.2 = bf16[64,2560]{1,0:T(8,128)(2,1)S(1)} collective-permute-done((bf16[64,2560]{1,0:T(8,128)(2,1)}, bf16[64,2560]{1,0:T(8,128)(2,1)S(1)}, u32[]{:S(2)}, u32[]{:S(2)}) %collective-permute-start.2) | collective-permute-done | bytes 327712 | tf_op jit(solution)/shard_map/ppermute | solution.py:168
  37.9 1.1 %constant_dynamic-update-slice_fusion.2 = bf16[256,2560]{1,0:T(8,128)(2,1)S(1)} fusion(bf16[256,2560]{1,0:T(8,128)(2,1)S(1)} %constant_dynamic-update-slice_fusion.3, bf16[128,2560]{1,0:T(8,128)(2,1)} %collective-permute-done), kind=kLoop, calls=%fused_computation.78 | loop fusion | bytes 1310720 | tf_op jit(solution)/shard_map/concatenate | solution.py:200
  41.3 3.5 %collective-permute-done.10 = bf16[64,2560]{1,0:T(8,128)(2,1)S(1)} collective-permute-done((bf16[64,2560]{1,0:T(8,128)(2,1)S(1)}, bf16[64,2560]{1,0:T(8,128)(2,1)S(1)}, u32[]{:S(2)}, u32[]{:S(2)}) %collective-permute-start.10) | collective-permute-done | bytes 327712 | tf_op jit(solution)/shard_map/ppermute | solution.py:111
  45.6 1.4 %collective-permute-done.14 = f32[192,256]{1,0:T(8,128)S(1)} collective-permute-done((f32[192,256]{1,0:T(8,128)S(1)}, f32[192,256]{1,0:T(8,128)S(1)}, u32[]{:S(2)}, u32[]{:S(2)}) %collective-permute-start.14) | collective-permute-done | bytes 196640 | tf_op jit(solution)/shard_map/ppermute | solution.py:135
  47.8 4.1 %collective-permute-done.12 = bf16[64,2560]{1,0:T(8,128)(2,1)S(1)} collective-permute-done((bf16[64,2560]{1,0:T(8,128)(2,1)S(1)}, bf16[64,2560]{1,0:T(8,128)(2,1)S(1)}, u32[]{:S(2)}, u32[]{:S(2)}) %collective-permute-start.12) | collective-permute-done | bytes 327712 | tf_op jit(solution)/shard_map/ppermute | solution.py:111
  53.3 1.6 %collective-permute-start.13 = (bf16[128,2560]{1,0:T(8,128)(2,1)S(1)}, bf16[128,2560]{1,0:T(8,128)(2,1)S(1)}, u32[]{:S(2)}, u32[]{:S(2)}) collective-permute-start(bf16[128,2560]{1,0:T(8,128)(2,1)S(1)} %convolution_convert_fusion.1), channel_id=1, source_target_pairs={{0,2},{2,0},{4,6},{6,4},{8,10},{10,8},{12,14},{14,12},{1,3},{3,1},... | collective-permute-start | bytes 1966088 | tf_op jit(solution)/shard_map/ppermute | solution.py:111
  55.6 2.5 %collective-permute-start.18 = (bf16[64,2560]{1,0:T(8,128)(2,1)S(1)}, bf16[64,2560]{1,0:T(8,128)(2,1)S(1)}, u32[]{:S(2)}, u32[]{:S(2)}) collective-permute-start(bf16[64,2560]{1,0:T(8,128)(2,1)S(1)} %fusion.44), channel_id=1, source_target_pairs={{0,4},{2,6},{4,0},{6,2},{8,12},{10,14},{12,8},{14,10},{1,5},{3,7},... | collective-permute-start | bytes 983048 | tf_op jit(solution)/shard_map/ppermute | solution.py:111
  58.2 1.3 %convolution_convert_fusion = bf16[128,2560]{1,0:T(8,128)(2,1)S(1)} fusion(bf16[64,2560]{1,0:T(8,128)(2,1)S(1)} %collective-permute-done.8, bf16[64,2560]{1,0:T(8,128)(2,1)} %collective-permute-done.3, bf16[64,2560]{1,0:T(8,128)(2,1)S(1)} %collective-permute-done.5, bf16[64,2560]{1,0:T(8,128)(2,1)S(1)} %bitcast.54, ...), kind=kOutput, calls=%fused_computation.5 | convolution fusion | flops 173604864 | bytes 2031616 | tf_op jit(solution)/shard_map/dot_general | solution.py:16
  60.4 12.5 %collective-permute-done.18 = bf16[64,2560]{1,0:T(8,128)(2,1)S(1)} collective-permute-done((bf16[64,2560]{1,0:T(8,128)(2,1)S(1)}, bf16[64,2560]{1,0:T(8,128)(2,1)S(1)}, u32[]{:S(2)}, u32[]{:S(2)}) %collective-permute-start.18) | collective-permute-done | bytes 327712 | tf_op jit(solution)/shard_map/ppermute | solution.py:111
  73.4 2.5 %collective-permute-start.19 = (bf16[64,2560]{1,0:T(8,128)(2,1)S(1)}, bf16[64,2560]{1,0:T(8,128)(2,1)S(1)}, u32[]{:S(2)}, u32[]{:S(2)}) collective-permute-start(bf16[64,2560]{1,0:T(8,128)(2,1)S(1)} %fusion.79), channel_id=1, source_target_pairs={{0,4},{2,6},{4,0},{6,2},{8,12},{10,14},{12,8},{14,10},{1,5},{3,7},... | collective-permute-start | bytes 983048 | tf_op jit(solution)/shard_map/ppermute | solution.py:111
  76.7 1.2 %fusion = bf16[128,2560]{1,0:T(8,128)(2,1)} fusion(bf16[128,2560]{1,0:T(8,128)(2,1)S(1)} %collective-permute-done.13, bf16[64,2560]{1,0:T(8,128)(2,1)S(1)} %collective-permute-done.11, bf16[64,2560]{1,0:T(8,128)(2,1)S(1)} %collective-permute-done.2, bf16[64,2560]{1,0:T(8,128)(2,1)S(1)} %collective-permute-done.10, bf16[64,2560]{1,0:T(8,128)(2,1)S(1)} %bitcast.50, ...), kind=kOutput, calls=%fused_computation.3 | convolution fusion | flops 174260224 | bytes 2686976 | tf_op jit(solution)/shard_map/dot_general | solution.py:16
  77.9 12.6 %collective-permute-done.19 = bf16[64,2560]{1,0:T(8,128)(2,1)S(1)} collective-permute-done((bf16[64,2560]{1,0:T(8,128)(2,1)S(1)}, bf16[64,2560]{1,0:T(8,128)(2,1)S(1)}, u32[]{:S(2)}, u32[]{:S(2)}) %collective-permute-start.19) | collective-permute-done | bytes 327712 | tf_op jit(solution)/shard_map/ppermute | solution.py:111
  91.4 2.2 %fusion.1 = bf16[128,2560]{1,0:T(8,128)(2,1)} fusion(bf16[128,2560]{1,0:T(8,128)(2,1)S(1)} %collective-permute-done.16, bf16[64,2560]{1,0:T(8,128)(2,1)S(1)} %collective-permute-done.8, bf16[64,2560]{1,0:T(8,128)(2,1)} %collective-permute-done.3, bf16[64,2560]{1,0:T(8,128)(2,1)S(1)} %collective-permute-done.5, bf16[64,2560]{1,0:T(8,128)(2,1)S(1)} %bitcast.55, ...), kind=kOutput, calls=%fused_computation.4 | convolution fusion | flops 174260224 | bytes 2686976 | tf_op jit(solution)/shard_map/dot_general | solution.py:16
  (80 shorter events, 12.5 us)
Async XLA Ops:
  0.6 9.1 %copy-start = (s32[8,256]{1,0:T(8,128)S(1)}, s32[8,256]{1,0:T(8,128)}, u32[]{:S(2)}) copy-start(s32[8,256]{1,0:T(8,128)} %param.10) | copy-start | bytes 24580
  0.7 9.8 %collective-permute-start.1 = (f32[1,256]{1,0:T(1,128)}, f32[1,256]{1,0:T(1,128)S(1)}, u32[]{:S(2)}, u32[]{:S(2)}) collective-permute-start(f32[1,256]{1,0:T(1,128)} %param.11), channel_id=1, source_target_pairs={{0,4},{2,6},{4,0},{6,2},{8,12},{10,14},{12,8},{14,10},{1,5},{3,7},... | collective-permute-start | bytes 3080 | tf_op jit(solution)/shard_map/ppermute | solution.py:111
  3.7 17.8 %collective-permute-start.3 = (bf16[64,2560]{1,0:T(8,128)(2,1)}, bf16[64,2560]{1,0:T(8,128)(2,1)}, u32[]{:S(2)}, u32[]{:S(2)}) collective-permute-start(bf16[64,2560]{1,0:T(8,128)(2,1)} %bitcast.51), channel_id=1, source_target_pairs={{0,8},{2,10},{4,12},{6,14},{8,0},{10,2},{12,4},{14,6},{16,28},{18,... | collective-permute-start | bytes 983048 | tf_op jit(solution)/shard_map/ppermute | solution.py:147
  6.3 19.9 %collective-permute-start.6 = (bf16[128,2560]{1,0:T(8,128)(2,1)}, bf16[128,2560]{1,0:T(8,128)(2,1)}, u32[]{:S(2)}, u32[]{:S(2)}) collective-permute-start(bf16[128,2560]{1,0:T(8,128)(2,1)} %param.6), channel_id=1, source_target_pairs={{0,2},{2,0},{4,6},{6,4},{8,10},{10,8},{12,14},{14,12},{1,3},{3,1},... | collective-permute-start | bytes 1966088 | tf_op jit(solution)/shard_map/ppermute | solution.py:111
  7.8 30.1 %collective-permute-start = (bf16[128,2560]{1,0:T(8,128)(2,1)}, bf16[128,2560]{1,0:T(8,128)(2,1)}, u32[]{:S(2)}, u32[]{:S(2)}) collective-permute-start(bf16[128,2560]{1,0:T(8,128)(2,1)} %param.7), channel_id=1, source_target_pairs={{0,2},{2,0},{4,6},{6,4},{8,10},{10,8},{12,14},{14,12},{1,3},{3,1},... | collective-permute-start | bytes 1966088 | tf_op jit(solution)/shard_map/ppermute | solution.py:111
  9.6 17.8 %copy-start.4 = (bf16[1,64,2560]{2,1,0:T(8,128)(2,1)S(1)}, bf16[1,64,2560]{2,1,0:T(8,128)(2,1)}, u32[]{:S(2)}) copy-start(bf16[1,64,2560]{2,1,0:T(8,128)(2,1)} %param.8) | copy-start | bytes 983044
  10.4 10.7 %collective-permute-start.4 = (f32[2,256]{1,0:T(2,128)S(1)}, f32[2,256]{1,0:T(2,128)S(1)}, u32[]{:S(2)}, u32[]{:S(2)}) collective-permute-start(f32[2,256]{1,0:T(2,128)S(1)} %pad_maximum_fusion.7), channel_id=1, source_target_pairs={{0,8},{2,10},{4,12},{6,14},{8,0},{10,2},{12,4},{14,6},{1,9},{3,11}... | collective-permute-start | bytes 6152 | tf_op jit(solution)/shard_map/ppermute | solution.py:111
  10.9 15.4 %collective-permute-start.5 = (bf16[64,2560]{1,0:T(8,128)(2,1)}, bf16[64,2560]{1,0:T(8,128)(2,1)S(1)}, u32[]{:S(2)}, u32[]{:S(2)}) collective-permute-start(bf16[64,2560]{1,0:T(8,128)(2,1)} %bitcast.52), channel_id=1, source_target_pairs={{0,4},{2,6},{4,0},{6,2},{8,12},{10,14},{12,8},{14,10},{1,5},{3,7},... | collective-permute-start | bytes 983048 | tf_op jit(solution)/shard_map/ppermute | solution.py:111
  21.1 16.8 %collective-permute-start.2 = (bf16[64,2560]{1,0:T(8,128)(2,1)}, bf16[64,2560]{1,0:T(8,128)(2,1)S(1)}, u32[]{:S(2)}, u32[]{:S(2)}) collective-permute-start(bf16[64,2560]{1,0:T(8,128)(2,1)} %bitcast.46), channel_id=1, source_target_pairs={{0,8},{2,10},{4,12},{6,14},{8,0},{10,2},{12,4},{14,6},{16,28},{18,... | collective-permute-start | bytes 983048 | tf_op jit(solution)/shard_map/ppermute | solution.py:168
  21.5 10.9 %collective-permute-start.8 = (bf16[64,2560]{1,0:T(8,128)(2,1)}, bf16[64,2560]{1,0:T(8,128)(2,1)S(1)}, u32[]{:S(2)}, u32[]{:S(2)}) collective-permute-start(bf16[64,2560]{1,0:T(8,128)(2,1)} %collective-permute-done.3), channel_id=1, source_target_pairs={{0,16},{16,0},{1,17},{17,1},{2,18},{18,2},{3,19},{19,3},{4,20},{20... | collective-permute-start | bytes 983048 | tf_op jit(solution)/shard_map/ppermute | solution.py:170
  29.0 1.5 %collective-permute-start.7 = (f32[192,256]{1,0:T(8,128)S(1)}, f32[192,256]{1,0:T(8,128)S(1)}, u32[]{:S(2)}, u32[]{:S(2)}) collective-permute-start(f32[192,256]{1,0:T(8,128)S(1)} %fusion.2), channel_id=1, source_target_pairs={{0,1},{1,0},{2,3},{3,2},{4,5},{5,4},{6,7},{7,6},{8,9},{9,8},{10,11... | collective-permute-start | bytes 589832 | tf_op jit(solution)/shard_map/ppermute | solution.py:135
  29.1 15.8 %collective-permute-start.10 = (bf16[64,2560]{1,0:T(8,128)(2,1)S(1)}, bf16[64,2560]{1,0:T(8,128)(2,1)S(1)}, u32[]{:S(2)}, u32[]{:S(2)}) collective-permute-start(bf16[64,2560]{1,0:T(8,128)(2,1)S(1)} %bitcast.47), channel_id=1, source_target_pairs={{0,4},{2,6},{4,0},{6,2},{8,12},{10,14},{12,8},{14,10},{1,5},{3,7},... | collective-permute-start | bytes 983048 | tf_op jit(solution)/shard_map/ppermute | solution.py:111
  32.9 1.3 %collective-permute-start.9 = (f32[64,256]{1,0:T(8,128)S(1)}, f32[64,256]{1,0:T(8,128)S(1)}, u32[]{:S(2)}, u32[]{:S(2)}) collective-permute-start(f32[64,256]{1,0:T(8,128)S(1)} %fusion.74), channel_id=1, source_target_pairs={{0,1},{1,0},{2,3},{3,2},{4,5},{5,4},{6,7},{7,6},{8,9},{9,8},{10,11... | collective-permute-start | bytes 196616 | tf_op jit(solution)/shard_map/ppermute | solution.py:135
  40.5 11.4 %collective-permute-start.12 = (bf16[64,2560]{1,0:T(8,128)(2,1)S(1)}, bf16[64,2560]{1,0:T(8,128)(2,1)S(1)}, u32[]{:S(2)}, u32[]{:S(2)}) collective-permute-start(bf16[64,2560]{1,0:T(8,128)(2,1)S(1)} %fusion.48), channel_id=1, source_target_pairs={{0,4},{2,6},{4,0},{6,2},{8,12},{10,14},{12,8},{14,10},{1,5},{3,7},... | collective-permute-start | bytes 983048 | tf_op jit(solution)/shard_map/ppermute | solution.py:111
  40.6 11.8 %collective-permute-start.11 = (bf16[64,2560]{1,0:T(8,128)(2,1)S(1)}, bf16[64,2560]{1,0:T(8,128)(2,1)S(1)}, u32[]{:S(2)}, u32[]{:S(2)}) collective-permute-start(bf16[64,2560]{1,0:T(8,128)(2,1)S(1)} %collective-permute-done.2), channel_id=1, source_target_pairs={{0,16},{16,0},{1,17},{17,1},{2,18},{18,2},{3,19},{19,3},{4,20},{20... | collective-permute-start | bytes 983048 | tf_op jit(solution)/shard_map/ppermute | solution.py:199
  45.4 1.5 %collective-permute-start.14 = (f32[192,256]{1,0:T(8,128)S(1)}, f32[192,256]{1,0:T(8,128)S(1)}, u32[]{:S(2)}, u32[]{:S(2)}) collective-permute-start(f32[192,256]{1,0:T(8,128)S(1)} %fusion.8), channel_id=1, source_target_pairs={{0,1},{1,0},{2,3},{3,2},{4,5},{5,4},{6,7},{7,6},{8,9},{9,8},{10,11... | collective-permute-start | bytes 589832 | tf_op jit(solution)/shard_map/ppermute | solution.py:135
  47.4 26.0 %collective-permute-start.17 = (bf16[64,2560]{1,0:T(8,128)(2,1)S(1)}, bf16[64,2560]{1,0:T(8,128)(2,1)S(1)}, u32[]{:S(2)}, u32[]{:S(2)}) collective-permute-start(bf16[64,2560]{1,0:T(8,128)(2,1)S(1)} %fusion.76), channel_id=1, source_target_pairs={{0,4},{2,6},{4,0},{6,2},{8,12},{10,14},{12,8},{14,10},{1,5},{3,7},... | collective-permute-start | bytes 983048 | tf_op jit(solution)/shard_map/ppermute | solution.py:111
  52.0 23.9 %collective-permute-start.21 = (bf16[64,2560]{1,0:T(8,128)(2,1)S(1)}, bf16[64,2560]{1,0:T(8,128)(2,1)S(1)}, u32[]{:S(2)}, u32[]{:S(2)}) collective-permute-start(bf16[64,2560]{1,0:T(8,128)(2,1)S(1)} %add_convert_fusion), channel_id=1, source_target_pairs={{0,8},{2,10},{4,12},{6,14},{8,0},{10,2},{12,4},{14,6},{1,9},{3,11}... | collective-permute-start | bytes 983048 | tf_op jit(solution)/shard_map/ppermute | solution.py:111
  52.9 2.1 %collective-permute-start.15 = (f32[64,256]{1,0:T(8,128)S(1)}, f32[64,256]{1,0:T(8,128)S(1)}, u32[]{:S(2)}, u32[]{:S(2)}) collective-permute-start(f32[64,256]{1,0:T(8,128)S(1)} %fusion.77), channel_id=1, source_target_pairs={{0,1},{1,0},{2,3},{3,2},{4,5},{5,4},{6,7},{7,6},{8,9},{9,8},{10,11... | collective-permute-start | bytes 196616 | tf_op jit(solution)/shard_map/ppermute | solution.py:135
  53.3 23.4 %collective-permute-start.13 = (bf16[128,2560]{1,0:T(8,128)(2,1)S(1)}, bf16[128,2560]{1,0:T(8,128)(2,1)S(1)}, u32[]{:S(2)}, u32[]{:S(2)}) collective-permute-start(bf16[128,2560]{1,0:T(8,128)(2,1)S(1)} %convolution_convert_fusion.1), channel_id=1, source_target_pairs={{0,2},{2,0},{4,6},{6,4},{8,10},{10,8},{12,14},{14,12},{1,3},{3,1},... | collective-permute-start | bytes 1966088 | tf_op jit(solution)/shard_map/ppermute | solution.py:111
  55.6 17.3 %collective-permute-start.18 = (bf16[64,2560]{1,0:T(8,128)(2,1)S(1)}, bf16[64,2560]{1,0:T(8,128)(2,1)S(1)}, u32[]{:S(2)}, u32[]{:S(2)}) collective-permute-start(bf16[64,2560]{1,0:T(8,128)(2,1)S(1)} %fusion.44), channel_id=1, source_target_pairs={{0,4},{2,6},{4,0},{6,2},{8,12},{10,14},{12,8},{14,10},{1,5},{3,7},... | collective-permute-start | bytes 983048 | tf_op jit(solution)/shard_map/ppermute | solution.py:111
  59.5 31.9 %collective-permute-start.16 = (bf16[128,2560]{1,0:T(8,128)(2,1)S(1)}, bf16[128,2560]{1,0:T(8,128)(2,1)S(1)}, u32[]{:S(2)}, u32[]{:S(2)}) collective-permute-start(bf16[128,2560]{1,0:T(8,128)(2,1)S(1)} %convolution_convert_fusion), channel_id=1, source_target_pairs={{0,2},{2,0},{4,6},{6,4},{8,10},{10,8},{12,14},{14,12},{1,3},{3,1},... | collective-permute-start | bytes 1966088 | tf_op jit(solution)/shard_map/ppermute | solution.py:111
  73.0 17.6 %collective-permute-start.20 = (bf16[64,2560]{1,0:T(8,128)(2,1)S(1)}, bf16[64,2560]{1,0:T(8,128)(2,1)S(1)}, u32[]{:S(2)}, u32[]{:S(2)}) collective-permute-start(bf16[64,2560]{1,0:T(8,128)(2,1)S(1)} %add_convert_fusion.1), channel_id=1, source_target_pairs={{0,8},{2,10},{4,12},{6,14},{8,0},{10,2},{12,4},{14,6},{1,9},{3,11}... | collective-permute-start | bytes 983048 | tf_op jit(solution)/shard_map/ppermute | solution.py:111
  73.4 17.1 %collective-permute-start.19 = (bf16[64,2560]{1,0:T(8,128)(2,1)S(1)}, bf16[64,2560]{1,0:T(8,128)(2,1)S(1)}, u32[]{:S(2)}, u32[]{:S(2)}) collective-permute-start(bf16[64,2560]{1,0:T(8,128)(2,1)S(1)} %fusion.79), channel_id=1, source_target_pairs={{0,4},{2,6},{4,0},{6,2},{8,12},{10,14},{12,8},{14,10},{1,5},{3,7},... | collective-permute-start | bytes 983048 | tf_op jit(solution)/shard_map/ppermute | solution.py:111
  (3 other events, 12.6 us)

commit v12 on v11

--- a/solution.py
+++ b/solution.py
@@ -104,11 +104,18 @@
 PARTNER = [(2 * a + side, 2 * a + 1 - side) for a in range(PLACES) for side in (0, 1)]
 SWAP = [(0, 1), (1, 0)]
 OWNERS = 2 * PLACES
-FAR = xor_line(2) + [(OWNERS + a, OWNERS + b) for a, b in xor_line(3)]
+AROUND = on_line([(0, 1), (1, 3), (3, 2), (2, 0)])
+DOWNWARD = on_line([(0, 3), (1, 0), (2, 1), (3, 2)])
+FIRST_TURN = AROUND + [(OWNERS + a, OWNERS + b) for a, b in DOWNWARD]
+SECOND_TURN = [(b, a) for a, b in FIRST_TURN]
 
 
 def move(value, pairs):
     return lax.ppermute(value, "adapter", pairs)
+
+
+def turn(value, pairs):
+    return lax.ppermute(value, ("groups", "adapter"), pairs)
 
 
 def after(value, earlier):
@@ -127,8 +134,13 @@
 
 
 def partial_sums(weights, rows):
-    parts = [jnp.dot(weight, rows, preferred_element_type=jnp.float32) for weight in weights]
-    return lax.optimization_barrier((parts, [narrow(part) for part in parts[1:]]))
+    parts, sent = [], []
+    for weight in weights[::-1]:
+        part = jnp.dot(weight, rows, preferred_element_type=jnp.float32)
+        part, send, rows = lax.optimization_barrier((part, narrow(part), rows))
+        parts.append(part)
+        sent.append(send)
+    return parts[::-1], sent[::-1]
 
 
 def both_cores(partial):
@@ -144,32 +156,33 @@
     up_matrix = up_adapter[0]
     rank = down_matrix.shape[0]
 
-    far_down = lax.ppermute(down_matrix, ("groups", "adapter"), FAR)
+    near_gate, down_later = lax.optimization_barrier((move(gating, xor_line(1)), down_matrix))
+    turn_down = turn(down_matrix, FIRST_TURN)
     tokens2 = move(tokens, PARTNER)
-    near_gate, down_later, up_later = lax.optimization_barrier(
-        (move(gating, xor_line(1)), down_matrix, up_matrix)
-    )
-    near_down, up_last = lax.optimization_barrier((move(down_later, xor_line(1)), up_matrix))
-    near_up = move(up_last, xor_line(1))
     cot2 = move(cotangent, PARTNER)
+    back_down = turn(down_later, SECOND_TURN)
+
+    place = me // 2
+    near_first = jnp.where(first_group, (place == 1) | (place == 2), place % 2 == 0)
+    far_bit = jnp.where(first_group, 2, 3)
+    first_bit = jnp.where(near_first, 1, far_bit)
+    bits = jnp.stack([jnp.zeros_like(me), first_bit, first_bit ^ far_bit ^ 1, far_bit ^ 1])
     gates = jnp.concatenate([gating, near_gate])
     gates = jnp.concatenate([gates, move(gates, xor_line(2))])
-
-    far_bit = jnp.where(first_group, 2, 3)
-    experts = jnp.stack([me, me ^ 2, me ^ (2 * far_bit), me ^ (2 * (far_bit ^ 1))])
-    lists = jnp.take(token_lists, experts, axis=0)
-    crossed = jnp.concatenate([gates[:2], gates[3:], gates[2:3]])
-    gate_rows = adapter_scale_factor * jnp.where(first_group, gates, crossed)
+    gate_rows = adapter_scale_factor * jnp.take(gates, bits, axis=0)
+    lists = jnp.take(token_lists, me ^ (2 * bits), axis=0)
     token_ids = jnp.arange(tok_local, dtype=jnp.int32)
     ids = jnp.concatenate([me * tok_local + token_ids, (me ^ 1) * tok_local + token_ids])
     taken = lists[:, :, None] == ids[None, None, :]
     scale = jnp.sum(jnp.where(taken, gate_rows[:, :, None], 0.0), axis=1)
 
-    far_up = lax.ppermute(up_later, ("groups", "adapter"), FAR)
-    ready, scale = lax.optimization_barrier((far_down, scale))
-    cross_down = lax.ppermute(ready, "groups", SWAP)
+    up_later, scale = lax.optimization_barrier((up_matrix, scale))
+    turn_up = turn(up_later, FIRST_TURN)
+    back_up = turn(up_later, SECOND_TURN)
+    far_down, scale = lax.optimization_barrier((jnp.where(near_first, back_down, turn_down), scale))
+    cross_down = lax.ppermute(far_down, "groups", SWAP)
     tokens2 = jnp.concatenate([tokens, tokens2], axis=0)
-    down_all = jnp.concatenate([down_matrix, near_down, far_down, cross_down], axis=0)
+    down_all = jnp.concatenate([down_matrix, turn_down, back_down, cross_down], axis=0)
 
     def most_products(rows, *matrices):
         return both_cores(contract_last(jnp.concatenate(matrices), rows))
@@ -180,41 +193,46 @@
         return [narrow(scale[k] * product) for k, product in enumerate(products)]
 
     def for_line(low):
-        second = jnp.where(first_group, low[2], low[3])
-        third = jnp.where(first_group, low[3], low[2])
-        return low[0], low[1], second, third
-
-    def outward_start(low, matrix):
+        near = jnp.where(near_first, low[1], low[2])
+        far = jnp.where(near_first, low[2], low[1])
+        second = jnp.where(first_group, far, low[3])
+        third = jnp.where(first_group, low[3], far)
+        return low[0], near, second, third
+
+    def theirs(low, matrix):
         weights = jnp.concatenate([slot[:, tok_local:] for slot in low])
-        return move(narrow(contract_first(weights, matrix)), PARTNER)
+        return narrow(contract_first(weights, matrix))
 
     def outward_end(low, matrix, back):
         weights = jnp.concatenate([slot[:, :tok_local] for slot in low])
         return narrow(contract_first(weights, matrix) + back.astype(jnp.float32))
 
-    most = most_products(tokens2, down_matrix, near_down, far_down)
+    most = most_products(tokens2, down_matrix, turn_down, back_down)
     most, tokens2 = lax.optimization_barrier((most, tokens2))
     low = low_rank(most, tokens2, cross_down)
-    cot2, far_up, low = lax.optimization_barrier((cot2, far_up, low))
-    cross_up = lax.ppermute(far_up, "groups", SWAP)
+    cot2, turn_up, back_up, low = lax.optimization_barrier((cot2, turn_up, back_up, low))
+    cross_up = lax.ppermute(jnp.where(near_first, back_up, turn_up), "groups", SWAP)
     cot2 = jnp.concatenate([cotangent, cot2], axis=0)
     (own, first, second, third), up_send = partial_sums(for_line(low), cot2)
-    up_third = move(up_send[2], xor_line(1))
-    most = most_products(cot2, up_matrix, near_up, far_up)
-    most, up_next = lax.optimization_barrier((most, up_send[0]))
+    up_third = move(up_send[3], xor_line(1))
+    most = most_products(cot2, up_matrix, turn_up, back_up)
+    most, up_next = lax.optimization_barrier((most, up_send[1]))
     up_first = move(up_next, xor_line(1))
 
     cross_up = after(cross_up, up_third)
-    up_all = jnp.concatenate([up_matrix, near_up, far_up, cross_up], axis=0)
+    up_all = jnp.concatenate([up_matrix, turn_up, back_up, cross_up], axis=0)
     low_back = low_rank(most, cot2, cross_up)
     (own_b, first_b, second_b, third_b), down_send = partial_sums(for_line(low_back), tokens2)
-    down_third = move(down_send[2], xor_line(1))
-    branch_back = outward_start(low, up_all)
-    input_back = outward_start(low_back, down_all)
-    up_far = move(narrow(add_up(second, up_third)), xor_line(2))
+    down_third = move(down_send[3], xor_line(1))
+    branch_back = move(theirs(low, up_all), PARTNER)
+    input_theirs, up_sum = lax.optimization_barrier(
+        (theirs(low_back, down_all), narrow(add_up(second, up_third)))
+    )
+    input_back = move(input_theirs, PARTNER)
+    up_far = move(up_sum, xor_line(2))
     down_sum = narrow(add_up(second_b, down_third))
     down_far = move(down_sum, xor_line(2))
-    down_first = move(after(down_send[0], (up_first, down_sum)), xor_line(1))
+    down_first = move(after(down_send[1], (up_first, down_sum)), xor_line(1))
     branch_out = outward_end(low, up_all, branch_back)
     up_grad = add_up(own, up_first, up_far)
     input_grad = outward_end(low_back, down_all, input_back)

time: 93.9 us -> 97.6 us (1.039)
  starting transfers between devices: 22.1 us -> 30.7 us
  waiting for transfers between devices: 52.8 us -> 45.4 us
  other arithmetic: 2.54 us -> 3.75 us
  local copies, waits for them, and re-layouts: 4.09 us -> 5.22 us
    ppermute x14 -> x12, waiting for transfers between devices: 43.3 us -> 36.9 us  [move(): return lax.ppermute(value, 'adapter', pairs)]
    ppermute x14 -> x12, starting transfers between devices: 14.2 us -> 19.7 us  [move(): return lax.ppermute(value, 'adapter', pairs)]
    ppermute x4 -> x6, starting transfers between devices: 7.61 us -> 10.7 us  [the longest x4 6.82 us: turn(): return lax.ppermute(value, ('groups', 'adapter'), pairs)]
    ppermute x4 -> x6, waiting for transfers between devices: 5.56 us -> 4.43 us  [the longest x1 4.41 us: by_pairs(): lax.ppermute(jnp.where(near_first, back_up, turn_up), 'groups', SWAP)]
    select_n x2 -> x5, other arithmetic: 0.15 us -> 1.23 us  [the longest x1 1.03 us: by_pairs(): jnp.where(near_first, back_down, turn_down)]
  transfers between devices with their start and end apart: 22 -> 22, of which waited for: 11 -> 11; matrix products, arithmetic and copies ran while one was open for 17% -> 16% of each run, Pallas kernels for 0% -> 0%
where the time goes in v12:
time: 97.6 us; the launch traced here: 97.2 us
  waiting for transfers between devices  45.4 us (47%)
  starting transfers between devices  30.7 us (31%)
  matrix products  11.1 us (11%)
  local copies, waits for them, and re-layouts  5.22 us (5%)
  other arithmetic  3.75 us (4%)
  between operations  0.98 us (1%)
    ppermute x12, waiting for transfers between devices, move(): return lax.ppermute(value, 'adapter', pairs)  36.9 us
    ppermute x12, starting transfers between devices, move(): return lax.ppermute(value, 'adapter', pairs)  19.7 us
    ppermute x4, starting transfers between devices, turn(): return lax.ppermute(value, ('groups', 'adapter'), pairs)  6.82 us
    dot_general x4, matrix products, contract_first(): lax.dot_general(left_op, right_op, (((0,), (0,)), ((), ())), preferred_el...  5.07 us
    ppermute x1, waiting for transfers between devices, by_pairs(): lax.ppermute(jnp.where(near_first, back_up, turn_up), 'groups', SWAP)  4.41 us
    ppermute x4, waiting for transfers between devices, both_cores(): return partial + lax.ppermute(partial, 'tensor', SWAP)  4.05 us
    dot_general x4, matrix products, contract_last(): lax.dot_general(left_op, right_op, (((1,), (1,)), ((), ())), preferred_el...  3.24 us
    dot_general x8, matrix products, partial_sums(): part = jnp.dot(weight, rows, preferred_element_type=jnp.float32)  2.84 us
  transfers between devices with their start and end apart: 22, of which 11 were waited for; matrix products, arithmetic and copies ran while one was open for 16% of the time, Pallas kernels for 0%

profile of v12, /device:TPU:0, one launch (start us, length us, event | category | flops | bytes accessed | tf_op | source)
XLA Modules:
  0.0 97.2 jit_solution(5986916993957081245)
XLA Ops:
  0.7 3.0 %collective-permute-start = (bf16[128,2560]{1,0:T(8,128)(2,1)}, bf16[128,2560]{1,0:T(8,128)(2,1)}, u32[]{:S(2)}, u32[]{:S(2)}) collective-permute-start(bf16[128,2560]{1,0:T(8,128)(2,1)} %param.7), channel_id=1, source_target_pairs={{0,2},{2,0},{4,6},{6,4},{8,10},{10,8},{12,14},{14,12},{1,3},{3,1},... | collective-permute-start | bytes 1966088 | tf_op jit(solution)/shard_map/ppermute | solution.py:114
  3.7 1.6 %collective-permute-start.1 = (f32[1,256]{1,0:T(1,128)}, f32[1,256]{1,0:T(1,128)S(1)}, u32[]{:S(2)}, u32[]{:S(2)}) collective-permute-start(f32[1,256]{1,0:T(1,128)} %param.11), channel_id=1, source_target_pairs={{0,4},{2,6},{4,0},{6,2},{8,12},{10,14},{12,8},{14,10},{1,5},{3,7},... | collective-permute-start | bytes 3080 | tf_op jit(solution)/shard_map/ppermute | solution.py:114
  7.9 3.0 %collective-permute-start.2 = (f32[2,256]{1,0:T(2,128)S(1)}, f32[2,256]{1,0:T(2,128)S(1)}, u32[]{:S(2)}, u32[]{:S(2)}) collective-permute-start(f32[2,256]{1,0:T(2,128)S(1)} %pad_maximum_fusion.9), channel_id=1, source_target_pairs={{0,8},{2,10},{4,12},{6,14},{8,0},{10,2},{12,4},{14,6},{1,9},{3,11}... | collective-permute-start | bytes 6152 | tf_op jit(solution)/shard_map/ppermute | solution.py:114
  11.0 5.7 %collective-permute-done.2 = f32[2,256]{1,0:T(2,128)S(1)} collective-permute-done((f32[2,256]{1,0:T(2,128)S(1)}, f32[2,256]{1,0:T(2,128)S(1)}, u32[]{:S(2)}, u32[]{:S(2)}) %collective-permute-start.2) | collective-permute-done | bytes 2080 | tf_op jit(solution)/shard_map/ppermute | solution.py:114
  17.6 6.7 %collective-permute-start.3 = (bf16[64,2560]{1,0:T(8,128)(2,1)}, bf16[64,2560]{1,0:T(8,128)(2,1)S(1)}, u32[]{:S(2)}, u32[]{:S(2)}) collective-permute-start(bf16[64,2560]{1,0:T(8,128)(2,1)} %bitcast.44), channel_id=1, source_target_pairs={{0,4},{2,6},{4,12},{6,14},{12,8},{14,10},{8,0},{10,2},{16,28},{18,... | collective-permute-start | bytes 983048 | tf_op jit(solution)/shard_map/ppermute | solution.py:118
  25.4 2.0 %collective-permute-start.9 = (bf16[64,2560]{1,0:T(8,128)(2,1)S(1)}, bf16[64,2560]{1,0:T(8,128)(2,1)S(1)}, u32[]{:S(2)}, u32[]{:S(2)}) collective-permute-start(bf16[64,2560]{1,0:T(8,128)(2,1)S(1)} %broadcast_select_fusion.1), channel_id=1, source_target_pairs={{0,16},{16,0},{1,17},{17,1},{2,18},{18,2},{3,19},{19,3},{4,20},{20... | collective-permute-start | bytes 983048 | tf_op jit(solution)/shard_map/ppermute | solution.py:183
  27.5 5.3 %collective-permute-done.7 = bf16[128,2560]{1,0:T(8,128)(2,1)} collective-permute-done((bf16[128,2560]{1,0:T(8,128)(2,1)}, bf16[128,2560]{1,0:T(8,128)(2,1)}, u32[]{:S(2)}, u32[]{:S(2)}) %collective-permute-start.7) | collective-permute-done | bytes 655392 | tf_op jit(solution)/shard_map/ppermute | solution.py:114
  33.9 1.6 %fusion.1 = f32[192,256]{1,0:T(8,128)S(1)} fusion(bf16[256,2560]{1,0:T(8,128)(2,1)S(1)} %constant_dynamic-update-slice_fusion, bf16[64,2560]{1,0:T(8,128)(2,1)S(1)} %collective-permute-done.5, bf16[64,2560]{1,0:T(8,128)(2,1)} %collective-permute-done.6, bf16[64,2560]{1,0:T(8,128)(2,1)} %bitcast.51), kind=kOutput, calls=%fused_computation.10 | convolution fusion | flops 254607360 | bytes 2490368 | tf_op jit(solution)/shard_map/dot_general | solution.py:10
  35.6 1.4 %collective-permute-done.8 = f32[192,256]{1,0:T(8,128)S(1)} collective-permute-done((f32[192,256]{1,0:T(8,128)S(1)}, f32[192,256]{1,0:T(8,128)S(1)}, u32[]{:S(2)}, u32[]{:S(2)}) %collective-permute-start.8) | collective-permute-done | bytes 196640 | tf_op jit(solution)/shard_map/ppermute | solution.py:147
  41.7 1.8 %collective-permute-start.11 = (bf16[64,2560]{1,0:T(8,128)(2,1)S(1)}, bf16[64,2560]{1,0:T(8,128)(2,1)S(1)}, u32[]{:S(2)}, u32[]{:S(2)}) collective-permute-start(bf16[64,2560]{1,0:T(8,128)(2,1)S(1)} %broadcast_select_fusion), channel_id=1, source_target_pairs={{0,16},{16,0},{1,17},{17,1},{2,18},{18,2},{3,19},{19,3},{4,20},{20... | collective-permute-start | bytes 983048 | tf_op jit(solution)/shard_map/ppermute | solution.py:214
  43.5 1.6 %collective-permute-start.12 = (bf16[64,2560]{1,0:T(8,128)(2,1)S(1)}, bf16[64,2560]{1,0:T(8,128)(2,1)S(1)}, u32[]{:S(2)}, u32[]{:S(2)}) collective-permute-start(bf16[64,2560]{1,0:T(8,128)(2,1)S(1)} %fusion.54), channel_id=1, source_target_pairs={{0,4},{2,6},{4,0},{6,2},{8,12},{10,14},{12,8},{14,10},{1,5},{3,7},... | collective-permute-start | bytes 983048 | tf_op jit(solution)/shard_map/ppermute | solution.py:114
  47.1 4.4 %collective-permute-done.11 = bf16[64,2560]{1,0:T(8,128)(2,1)S(1)} collective-permute-done((bf16[64,2560]{1,0:T(8,128)(2,1)S(1)}, bf16[64,2560]{1,0:T(8,128)(2,1)S(1)}, u32[]{:S(2)}, u32[]{:S(2)}) %collective-permute-start.11) | collective-permute-done | bytes 327712 | tf_op jit(solution)/shard_map/ppermute | solution.py:214
  51.6 2.6 %collective-permute-done.12 = bf16[64,2560]{1,0:T(8,128)(2,1)S(1)} collective-permute-done((bf16[64,2560]{1,0:T(8,128)(2,1)S(1)}, bf16[64,2560]{1,0:T(8,128)(2,1)S(1)}, u32[]{:S(2)}, u32[]{:S(2)}) %collective-permute-start.12) | collective-permute-done | bytes 327712 | tf_op jit(solution)/shard_map/ppermute | solution.py:114
  55.0 1.6 %collective-permute-start.13 = (bf16[128,2560]{1,0:T(8,128)(2,1)S(1)}, bf16[128,2560]{1,0:T(8,128)(2,1)S(1)}, u32[]{:S(2)}, u32[]{:S(2)}) collective-permute-start(bf16[128,2560]{1,0:T(8,128)(2,1)S(1)} %convolution_convert_fusion.1), channel_id=1, source_target_pairs={{0,2},{2,0},{4,6},{6,4},{8,10},{10,8},{12,14},{14,12},{1,3},{3,1},... | collective-permute-start | bytes 1966088 | tf_op jit(solution)/shard_map/ppermute | solution.py:114
  56.6 1.2 %collective-permute-done.15 = f32[64,256]{1,0:T(8,128)S(1)} collective-permute-done((f32[64,256]{1,0:T(8,128)S(1)}, f32[64,256]{1,0:T(8,128)S(1)}, u32[]{:S(2)}, u32[]{:S(2)}) %collective-permute-start.15) | collective-permute-done | bytes 65568 | tf_op jit(solution)/shard_map/ppermute | solution.py:147
  58.2 1.3 %convolution_convert_fusion = bf16[128,2560]{1,0:T(8,128)(2,1)S(1)} fusion(bf16[64,2560]{1,0:T(8,128)(2,1)S(1)} %collective-permute-done.9, bf16[64,2560]{1,0:T(8,128)(2,1)S(1)} %collective-permute-done.5, bf16[64,2560]{1,0:T(8,128)(2,1)} %collective-permute-done.6, bf16[64,2560]{1,0:T(8,128)(2,1)S(1)} %bitcast.52, ...), kind=kOutput, calls=%fused_computation.4 | convolution fusion | flops 173604864 | bytes 2031616 | tf_op jit(solution)/shard_map/dot_general | solution.py:16
  60.5 1.6 %collective-permute-start.18 = (bf16[64,2560]{1,0:T(8,128)(2,1)S(1)}, bf16[64,2560]{1,0:T(8,128)(2,1)S(1)}, u32[]{:S(2)}, u32[]{:S(2)}) collective-permute-start(bf16[64,2560]{1,0:T(8,128)(2,1)S(1)} %fusion.44), channel_id=1, source_target_pairs={{0,4},{2,6},{4,0},{6,2},{8,12},{10,14},{12,8},{14,10},{1,5},{3,7},... | collective-permute-start | bytes 983048 | tf_op jit(solution)/shard_map/ppermute | solution.py:114
  62.8 2.6 %collective-permute-start.21 = (bf16[64,2560]{1,0:T(8,128)(2,1)S(1)}, bf16[64,2560]{1,0:T(8,128)(2,1)S(1)}, u32[]{:S(2)}, u32[]{:S(2)}) collective-permute-start(bf16[64,2560]{1,0:T(8,128)(2,1)S(1)} %add_convert_fusion.2), channel_id=1, source_target_pairs={{0,8},{2,10},{4,12},{6,14},{8,0},{10,2},{12,4},{14,6},{1,9},{3,11}... | collective-permute-start | bytes 983048 | tf_op jit(solution)/shard_map/ppermute | solution.py:114
  65.5 10.7 %collective-permute-done.18 = bf16[64,2560]{1,0:T(8,128)(2,1)S(1)} collective-permute-done((bf16[64,2560]{1,0:T(8,128)(2,1)S(1)}, bf16[64,2560]{1,0:T(8,128)(2,1)S(1)}, u32[]{:S(2)}, u32[]{:S(2)}) %collective-permute-start.18) | collective-permute-done | bytes 327712 | tf_op jit(solution)/shard_map/ppermute | solution.py:114
  76.9 2.5 %collective-permute-start.19 = (bf16[64,2560]{1,0:T(8,128)(2,1)S(1)}, bf16[64,2560]{1,0:T(8,128)(2,1)S(1)}, u32[]{:S(2)}, u32[]{:S(2)}) collective-permute-start(bf16[64,2560]{1,0:T(8,128)(2,1)S(1)} %fusion.48), channel_id=1, source_target_pairs={{0,4},{2,6},{4,0},{6,2},{8,12},{10,14},{12,8},{14,10},{1,5},{3,7},... | collective-permute-start | bytes 983048 | tf_op jit(solution)/shard_map/ppermute | solution.py:114
  79.4 8.6 %collective-permute-done.21 = bf16[64,2560]{1,0:T(8,128)(2,1)S(1)} collective-permute-done((bf16[64,2560]{1,0:T(8,128)(2,1)S(1)}, bf16[64,2560]{1,0:T(8,128)(2,1)S(1)}, u32[]{:S(2)}, u32[]{:S(2)}) %collective-permute-start.21) | collective-permute-done | bytes 327712 | tf_op jit(solution)/shard_map/ppermute | solution.py:114
  88.8 1.2 %add_convert_fusion = bf16[128,2560]{1,0:T(8,128)(2,1)} fusion(bf16[128,2560]{1,0:T(8,128)(2,1)S(1)} %collective-permute-done.13, bf16[64,2560]{1,0:T(8,128)(2,1)S(1)} %collective-permute-done.11, bf16[64,2560]{1,0:T(8,128)(2,1)S(1)} %collective-permute-done.4, bf16[64,2560]{1,0:T(8,128)(2,1)S(1)} %collective-permute-done.3, ...), kind=kOutput, calls=%fused_computation.8 | convolution fusion | flops 174260224 | bytes 2686976 | tf_op jit(solution)/shard_map/dot_general | solution.py:16
  90.0 4.1 %collective-permute-done.20 = bf16[64,2560]{1,0:T(8,128)(2,1)S(1)} collective-permute-done((bf16[64,2560]{1,0:T(8,128)(2,1)S(1)}, bf16[64,2560]{1,0:T(8,128)(2,1)S(1)}, u32[]{:S(2)}, u32[]{:S(2)}) %collective-permute-start.20) | collective-permute-done | bytes 327712 | tf_op jit(solution)/shard_map/ppermute | solution.py:114
  95.0 2.2 %fusion = bf16[128,2560]{1,0:T(8,128)(2,1)} fusion(bf16[128,2560]{1,0:T(8,128)(2,1)S(1)} %collective-permute-done.16, bf16[64,2560]{1,0:T(8,128)(2,1)S(1)} %collective-permute-done.9, bf16[64,2560]{1,0:T(8,128)(2,1)S(1)} %collective-permute-done.5, bf16[64,2560]{1,0:T(8,128)(2,1)} %collective-permute-done.6, bf16[64,2560]{1,0:T(8,128)(2,1)S(1)} %bitcast.53, ...), kind=kOutput, calls=%fused_computation.3 | convolution fusion | flops 174260224 | bytes 2686976 | tf_op jit(solution)/shard_map/dot_general | solution.py:16
  (86 shorter events, 17.9 us)
Async XLA Ops:
  0.6 6.6 %copy-start = (s32[8,256]{1,0:T(8,128)S(1)}, s32[8,256]{1,0:T(8,128)}, u32[]{:S(2)}) copy-start(s32[8,256]{1,0:T(8,128)} %param.10) | copy-start | bytes 24580
  0.6 6.3 %copy-start.1 = (bf16[128,2560]{1,0:T(8,128)(2,1)S(1)}, bf16[128,2560]{1,0:T(8,128)(2,1)}, u32[]{:S(2)}) copy-start(bf16[128,2560]{1,0:T(8,128)(2,1)} %param.7) | copy-start | bytes 1966084
  0.7 38.3 %collective-permute-start = (bf16[128,2560]{1,0:T(8,128)(2,1)}, bf16[128,2560]{1,0:T(8,128)(2,1)}, u32[]{:S(2)}, u32[]{:S(2)}) collective-permute-start(bf16[128,2560]{1,0:T(8,128)(2,1)} %param.7), channel_id=1, source_target_pairs={{0,2},{2,0},{4,6},{6,4},{8,10},{10,8},{12,14},{14,12},{1,3},{3,1},... | collective-permute-start | bytes 1966088 | tf_op jit(solution)/shard_map/ppermute | solution.py:114
  3.7 4.2 %collective-permute-start.1 = (f32[1,256]{1,0:T(1,128)}, f32[1,256]{1,0:T(1,128)S(1)}, u32[]{:S(2)}, u32[]{:S(2)}) collective-permute-start(f32[1,256]{1,0:T(1,128)} %param.11), channel_id=1, source_target_pairs={{0,4},{2,6},{4,0},{6,2},{8,12},{10,14},{12,8},{14,10},{1,5},{3,7},... | collective-permute-start | bytes 3080 | tf_op jit(solution)/shard_map/ppermute | solution.py:114
  5.2 27.5 %collective-permute-start.7 = (bf16[128,2560]{1,0:T(8,128)(2,1)}, bf16[128,2560]{1,0:T(8,128)(2,1)}, u32[]{:S(2)}, u32[]{:S(2)}) collective-permute-start(bf16[128,2560]{1,0:T(8,128)(2,1)} %param.6), channel_id=1, source_target_pairs={{0,2},{2,0},{4,6},{6,4},{8,10},{10,8},{12,14},{14,12},{1,3},{3,1},... | collective-permute-start | bytes 1966088 | tf_op jit(solution)/shard_map/ppermute | solution.py:114
  5.8 18.6 %collective-permute-start.6 = (bf16[64,2560]{1,0:T(8,128)(2,1)}, bf16[64,2560]{1,0:T(8,128)(2,1)}, u32[]{:S(2)}, u32[]{:S(2)}) collective-permute-start(bf16[64,2560]{1,0:T(8,128)(2,1)} %bitcast.49), channel_id=1, source_target_pairs={{0,4},{2,6},{4,12},{6,14},{12,8},{14,10},{8,0},{10,2},{16,28},{18,... | collective-permute-start | bytes 983048 | tf_op jit(solution)/shard_map/ppermute | solution.py:118
  7.9 8.7 %collective-permute-start.2 = (f32[2,256]{1,0:T(2,128)S(1)}, f32[2,256]{1,0:T(2,128)S(1)}, u32[]{:S(2)}, u32[]{:S(2)}) collective-permute-start(f32[2,256]{1,0:T(2,128)S(1)} %pad_maximum_fusion.9), channel_id=1, source_target_pairs={{0,8},{2,10},{4,12},{6,14},{8,0},{10,2},{12,4},{14,6},{1,9},{3,11}... | collective-permute-start | bytes 6152 | tf_op jit(solution)/shard_map/ppermute | solution.py:114
  10.9 13.5 %collective-permute-start.5 = (bf16[64,2560]{1,0:T(8,128)(2,1)}, bf16[64,2560]{1,0:T(8,128)(2,1)S(1)}, u32[]{:S(2)}, u32[]{:S(2)}) collective-permute-start(bf16[64,2560]{1,0:T(8,128)(2,1)} %bitcast.50), channel_id=1, source_target_pairs={{4,0},{6,2},{12,4},{14,6},{8,12},{10,14},{0,8},{2,10},{28,16},{30,... | collective-permute-start | bytes 983048 | tf_op jit(solution)/shard_map/ppermute | solution.py:118
  17.6 21.3 %collective-permute-start.3 = (bf16[64,2560]{1,0:T(8,128)(2,1)}, bf16[64,2560]{1,0:T(8,128)(2,1)S(1)}, u32[]{:S(2)}, u32[]{:S(2)}) collective-permute-start(bf16[64,2560]{1,0:T(8,128)(2,1)} %bitcast.44), channel_id=1, source_target_pairs={{0,4},{2,6},{4,12},{6,14},{12,8},{14,10},{8,0},{10,2},{16,28},{18,... | collective-permute-start | bytes 983048 | tf_op jit(solution)/shard_map/ppermute | solution.py:118
  24.4 14.6 %collective-permute-start.4 = (bf16[64,2560]{1,0:T(8,128)(2,1)}, bf16[64,2560]{1,0:T(8,128)(2,1)S(1)}, u32[]{:S(2)}, u32[]{:S(2)}) collective-permute-start(bf16[64,2560]{1,0:T(8,128)(2,1)} %bitcast.45), channel_id=1, source_target_pairs={{4,0},{6,2},{12,4},{14,6},{8,12},{10,14},{0,8},{2,10},{28,16},{30,... | collective-permute-start | bytes 983048 | tf_op jit(solution)/shard_map/ppermute | solution.py:118
  25.4 11.6 %collective-permute-start.9 = (bf16[64,2560]{1,0:T(8,128)(2,1)S(1)}, bf16[64,2560]{1,0:T(8,128)(2,1)S(1)}, u32[]{:S(2)}, u32[]{:S(2)}) collective-permute-start(bf16[64,2560]{1,0:T(8,128)(2,1)S(1)} %broadcast_select_fusion.1), channel_id=1, source_target_pairs={{0,16},{16,0},{1,17},{17,1},{2,18},{18,2},{3,19},{19,3},{4,20},{20... | collective-permute-start | bytes 983048 | tf_op jit(solution)/shard_map/ppermute | solution.py:183
  35.5 1.5 %collective-permute-start.8 = (f32[192,256]{1,0:T(8,128)S(1)}, f32[192,256]{1,0:T(8,128)S(1)}, u32[]{:S(2)}, u32[]{:S(2)}) collective-permute-start(f32[192,256]{1,0:T(8,128)S(1)} %fusion.1), channel_id=1, source_target_pairs={{0,1},{1,0},{2,3},{3,2},{4,5},{5,4},{6,7},{7,6},{8,9},{9,8},{10,11... | collective-permute-start | bytes 589832 | tf_op jit(solution)/shard_map/ppermute | solution.py:147
  37.6 1.3 %collective-permute-start.10 = (f32[64,256]{1,0:T(8,128)S(1)}, f32[64,256]{1,0:T(8,128)S(1)}, u32[]{:S(2)}, u32[]{:S(2)}) collective-permute-start(f32[64,256]{1,0:T(8,128)S(1)} %fusion.79), channel_id=1, source_target_pairs={{0,1},{1,0},{2,3},{3,2},{4,5},{5,4},{6,7},{7,6},{8,9},{9,8},{10,11... | collective-permute-start | bytes 196616 | tf_op jit(solution)/shard_map/ppermute | solution.py:147
  41.7 9.9 %collective-permute-start.11 = (bf16[64,2560]{1,0:T(8,128)(2,1)S(1)}, bf16[64,2560]{1,0:T(8,128)(2,1)S(1)}, u32[]{:S(2)}, u32[]{:S(2)}) collective-permute-start(bf16[64,2560]{1,0:T(8,128)(2,1)S(1)} %broadcast_select_fusion), channel_id=1, source_target_pairs={{0,16},{16,0},{1,17},{17,1},{2,18},{18,2},{3,19},{19,3},{4,20},{20... | collective-permute-start | bytes 983048 | tf_op jit(solution)/shard_map/ppermute | solution.py:214
  43.5 10.6 %collective-permute-start.12 = (bf16[64,2560]{1,0:T(8,128)(2,1)S(1)}, bf16[64,2560]{1,0:T(8,128)(2,1)S(1)}, u32[]{:S(2)}, u32[]{:S(2)}) collective-permute-start(bf16[64,2560]{1,0:T(8,128)(2,1)S(1)} %fusion.54), channel_id=1, source_target_pairs={{0,4},{2,6},{4,0},{6,2},{8,12},{10,14},{12,8},{14,10},{1,5},{3,7},... | collective-permute-start | bytes 983048 | tf_op jit(solution)/shard_map/ppermute | solution.py:114
  45.1 1.4 %collective-permute-start.14 = (f32[192,256]{1,0:T(8,128)S(1)}, f32[192,256]{1,0:T(8,128)S(1)}, u32[]{:S(2)}, u32[]{:S(2)}) collective-permute-start(f32[192,256]{1,0:T(8,128)S(1)} %fusion.7), channel_id=1, source_target_pairs={{0,1},{1,0},{2,3},{3,2},{4,5},{5,4},{6,7},{7,6},{8,9},{9,8},{10,11... | collective-permute-start | bytes 589832 | tf_op jit(solution)/shard_map/ppermute | solution.py:147
  46.6 30.3 %collective-permute-start.17 = (bf16[64,2560]{1,0:T(8,128)(2,1)S(1)}, bf16[64,2560]{1,0:T(8,128)(2,1)S(1)}, u32[]{:S(2)}, u32[]{:S(2)}) collective-permute-start(bf16[64,2560]{1,0:T(8,128)(2,1)S(1)} %fusion.52), channel_id=1, source_target_pairs={{0,4},{2,6},{4,0},{6,2},{8,12},{10,14},{12,8},{14,10},{1,5},{3,7},... | collective-permute-start | bytes 983048 | tf_op jit(solution)/shard_map/ppermute | solution.py:114
  55.0 33.8 %collective-permute-start.13 = (bf16[128,2560]{1,0:T(8,128)(2,1)S(1)}, bf16[128,2560]{1,0:T(8,128)(2,1)S(1)}, u32[]{:S(2)}, u32[]{:S(2)}) collective-permute-start(bf16[128,2560]{1,0:T(8,128)(2,1)S(1)} %convolution_convert_fusion.1), channel_id=1, source_target_pairs={{0,2},{2,0},{4,6},{6,4},{8,10},{10,8},{12,14},{14,12},{1,3},{3,1},... | collective-permute-start | bytes 1966088 | tf_op jit(solution)/shard_map/ppermute | solution.py:114
  56.6 1.3 %collective-permute-start.15 = (f32[64,256]{1,0:T(8,128)S(1)}, f32[64,256]{1,0:T(8,128)S(1)}, u32[]{:S(2)}, u32[]{:S(2)}) collective-permute-start(f32[64,256]{1,0:T(8,128)S(1)} %fusion.80), channel_id=1, source_target_pairs={{0,1},{1,0},{2,3},{3,2},{4,5},{5,4},{6,7},{7,6},{8,9},{9,8},{10,11... | collective-permute-start | bytes 196616 | tf_op jit(solution)/shard_map/ppermute | solution.py:147
  59.5 35.5 %collective-permute-start.16 = (bf16[128,2560]{1,0:T(8,128)(2,1)S(1)}, bf16[128,2560]{1,0:T(8,128)(2,1)S(1)}, u32[]{:S(2)}, u32[]{:S(2)}) collective-permute-start(bf16[128,2560]{1,0:T(8,128)(2,1)S(1)} %convolution_convert_fusion), channel_id=1, source_target_pairs={{0,2},{2,0},{4,6},{6,4},{8,10},{10,8},{12,14},{14,12},{1,3},{3,1},... | collective-permute-start | bytes 1966088 | tf_op jit(solution)/shard_map/ppermute | solution.py:114
  60.5 15.7 %collective-permute-start.18 = (bf16[64,2560]{1,0:T(8,128)(2,1)S(1)}, bf16[64,2560]{1,0:T(8,128)(2,1)S(1)}, u32[]{:S(2)}, u32[]{:S(2)}) collective-permute-start(bf16[64,2560]{1,0:T(8,128)(2,1)S(1)} %fusion.44), channel_id=1, source_target_pairs={{0,4},{2,6},{4,0},{6,2},{8,12},{10,14},{12,8},{14,10},{1,5},{3,7},... | collective-permute-start | bytes 983048 | tf_op jit(solution)/shard_map/ppermute | solution.py:114
  62.8 25.1 %collective-permute-start.21 = (bf16[64,2560]{1,0:T(8,128)(2,1)S(1)}, bf16[64,2560]{1,0:T(8,128)(2,1)S(1)}, u32[]{:S(2)}, u32[]{:S(2)}) collective-permute-start(bf16[64,2560]{1,0:T(8,128)(2,1)S(1)} %add_convert_fusion.2), channel_id=1, source_target_pairs={{0,8},{2,10},{4,12},{6,14},{8,0},{10,2},{12,4},{14,6},{1,9},{3,11}... | collective-permute-start | bytes 983048 | tf_op jit(solution)/shard_map/ppermute | solution.py:114
  76.3 17.9 %collective-permute-start.20 = (bf16[64,2560]{1,0:T(8,128)(2,1)S(1)}, bf16[64,2560]{1,0:T(8,128)(2,1)S(1)}, u32[]{:S(2)}, u32[]{:S(2)}) collective-permute-start(bf16[64,2560]{1,0:T(8,128)(2,1)S(1)} %add_convert_fusion.1), channel_id=1, source_target_pairs={{0,8},{2,10},{4,12},{6,14},{8,0},{10,2},{12,4},{14,6},{1,9},{3,11}... | collective-permute-start | bytes 983048 | tf_op jit(solution)/shard_map/ppermute | solution.py:114
  76.9 17.2 %collective-permute-start.19 = (bf16[64,2560]{1,0:T(8,128)(2,1)S(1)}, bf16[64,2560]{1,0:T(8,128)(2,1)S(1)}, u32[]{:S(2)}, u32[]{:S(2)}) collective-permute-start(bf16[64,2560]{1,0:T(8,128)(2,1)S(1)} %fusion.48), channel_id=1, source_target_pairs={{0,4},{2,6},{4,0},{6,2},{8,12},{10,14},{12,8},{14,10},{1,5},{3,7},... | collective-permute-start | bytes 983048 | tf_op jit(solution)/shard_map/ppermute | solution.py:114
  (3 other events, 4.7 us)

commit v13 on v12

--- a/solution.py
+++ b/solution.py
@@ -156,10 +156,12 @@
     up_matrix = up_adapter[0]
     rank = down_matrix.shape[0]
 
-    near_gate, down_later = lax.optimization_barrier((move(gating, xor_line(1)), down_matrix))
+    near_gate, down_later, cot_later = lax.optimization_barrier(
+        (move(gating, xor_line(1)), down_matrix, cotangent)
+    )
     turn_down = turn(down_matrix, FIRST_TURN)
     tokens2 = move(tokens, PARTNER)
-    cot2 = move(cotangent, PARTNER)
+    cot2 = move(cot_later, PARTNER)
     back_down = turn(down_later, SECOND_TURN)
 
     place = me // 2

time: 97.6 us -> 96.3 us (0.987)
    ppermute x12, starting transfers between devices: 19.7 us -> 16.8 us  [move(): return lax.ppermute(value, 'adapter', pairs)]
    ppermute x1, waiting for transfers between devices: 4.41 us -> 2.69 us  [by_pairs(): lax.ppermute(jnp.where(near_first, back_up, turn_up), 'groups', SWAP)]
    ppermute x1, waiting for transfers between devices: 0.01 us -> 1.41 us  [by_pairs(): cross_down = lax.ppermute(far_down, 'groups', SWAP)]
    ppermute x12, waiting for transfers between devices: 36.9 us -> 35.7 us  [move(): return lax.ppermute(value, 'adapter', pairs)]
    ppermute x1, starting transfers between devices: 2.02 us -> 3.04 us  [by_pairs(): cross_down = lax.ppermute(far_down, 'groups', SWAP)]
where the time goes in v13:
time: 96.3 us; the launch traced here: 96 us
  waiting for transfers between devices  44.8 us (47%)
  starting transfers between devices  30 us (31%)
  matrix products  11.3 us (12%)
  local copies, waits for them, and re-layouts  5.21 us (5%)
  other arithmetic  3.7 us (4%)
  between operations  0.98 us (1%)
    ppermute x12, waiting for transfers between devices, move(): return lax.ppermute(value, 'adapter', pairs)  35.7 us
    ppermute x12, starting transfers between devices, move(): return lax.ppermute(value, 'adapter', pairs)  16.8 us
    ppermute x4, starting transfers between devices, turn(): return lax.ppermute(value, ('groups', 'adapter'), pairs)  7.27 us
    dot_general x4, matrix products, contract_first(): lax.dot_general(left_op, right_op, (((0,), (0,)), ((), ())), preferred_el...  5.27 us
    ppermute x4, waiting for transfers between devices, both_cores(): return partial + lax.ppermute(partial, 'tensor', SWAP)  4.19 us
    dot_general x4, matrix products, contract_last(): lax.dot_general(left_op, right_op, (((1,), (1,)), ((), ())), preferred_el...  3.23 us
    ppermute x1, starting transfers between devices, by_pairs(): cross_down = lax.ppermute(far_down, 'groups', SWAP)  3.04 us
    dot_general x8, matrix products, partial_sums(): part = jnp.dot(weight, rows, preferred_element_type=jnp.float32)  2.82 us
  transfers between devices with their start and end apart: 22, of which 11 were waited for; matrix products, arithmetic and copies ran while one was open for 16% of the time, Pallas kernels for 0%

profile of v13, /device:TPU:0, one launch (start us, length us, event | category | flops | bytes accessed | tf_op | source)
XLA Modules:
  0.0 96.0 jit_solution(5977030141396164832)
XLA Ops:
  0.7 3.1 %collective-permute-start = (f32[1,256]{1,0:T(1,128)}, f32[1,256]{1,0:T(1,128)S(1)}, u32[]{:S(2)}, u32[]{:S(2)}) collective-permute-start(f32[1,256]{1,0:T(1,128)} %param.11), channel_id=1, source_target_pairs={{0,4},{2,6},{4,0},{6,2},{8,12},{10,14},{12,8},{14,10},{1,5},{3,7},... | collective-permute-start | bytes 3080 | tf_op jit(solution)/shard_map/ppermute | solution.py:114
  3.7 1.5 %collective-permute-start.7 = (bf16[128,2560]{1,0:T(8,128)(2,1)}, bf16[128,2560]{1,0:T(8,128)(2,1)}, u32[]{:S(2)}, u32[]{:S(2)}) collective-permute-start(bf16[128,2560]{1,0:T(8,128)(2,1)} %param.6), channel_id=1, source_target_pairs={{0,2},{2,0},{4,6},{6,4},{8,10},{10,8},{12,14},{14,12},{1,3},{3,1},... | collective-permute-start | bytes 1966088 | tf_op jit(solution)/shard_map/ppermute | solution.py:114
  5.7 1.1 %constant_dynamic-update-slice_fusion.1 = bf16[256,2560]{1,0:T(8,128)(2,1)S(1)} fusion(bf16[128,2560]{1,0:T(8,128)(2,1)} %param.6), kind=kLoop, calls=%fused_computation.88 | loop fusion | bytes 1310720
  7.8 2.5 %collective-permute-start.2 = (f32[2,256]{1,0:T(2,128)S(1)}, f32[2,256]{1,0:T(2,128)S(1)}, u32[]{:S(2)}, u32[]{:S(2)}) collective-permute-start(f32[2,256]{1,0:T(2,128)S(1)} %pad_maximum_fusion.9), channel_id=1, source_target_pairs={{0,8},{2,10},{4,12},{6,14},{8,0},{10,2},{12,4},{14,6},{1,9},{3,11}... | collective-permute-start | bytes 6152 | tf_op jit(solution)/shard_map/ppermute | solution.py:114
  11.0 5.1 %collective-permute-done.2 = f32[2,256]{1,0:T(2,128)S(1)} collective-permute-done((f32[2,256]{1,0:T(2,128)S(1)}, f32[2,256]{1,0:T(2,128)S(1)}, u32[]{:S(2)}, u32[]{:S(2)}) %collective-permute-start.2) | collective-permute-done | bytes 2080 | tf_op jit(solution)/shard_map/ppermute | solution.py:114
  17.1 6.7 %collective-permute-start.3 = (bf16[64,2560]{1,0:T(8,128)(2,1)}, bf16[64,2560]{1,0:T(8,128)(2,1)S(1)}, u32[]{:S(2)}, u32[]{:S(2)}) collective-permute-start(bf16[64,2560]{1,0:T(8,128)(2,1)} %bitcast.44), channel_id=1, source_target_pairs={{0,4},{2,6},{4,12},{6,14},{12,8},{14,10},{8,0},{10,2},{16,28},{18,... | collective-permute-start | bytes 983048 | tf_op jit(solution)/shard_map/ppermute | solution.py:118
  24.9 3.0 %collective-permute-start.9 = (bf16[64,2560]{1,0:T(8,128)(2,1)S(1)}, bf16[64,2560]{1,0:T(8,128)(2,1)S(1)}, u32[]{:S(2)}, u32[]{:S(2)}) collective-permute-start(bf16[64,2560]{1,0:T(8,128)(2,1)S(1)} %broadcast_select_fusion.1), channel_id=1, source_target_pairs={{0,16},{16,0},{1,17},{17,1},{2,18},{18,2},{3,19},{19,3},{4,20},{20... | collective-permute-start | bytes 983048 | tf_op jit(solution)/shard_map/ppermute | solution.py:185
  29.1 1.6 %fusion.1 = f32[192,256]{1,0:T(8,128)S(1)} fusion(bf16[256,2560]{1,0:T(8,128)(2,1)S(1)} %constant_dynamic-update-slice_fusion, bf16[64,2560]{1,0:T(8,128)(2,1)} %collective-permute-done.5, bf16[64,2560]{1,0:T(8,128)(2,1)} %collective-permute-done.6, bf16[64,2560]{1,0:T(8,128)(2,1)S(1)} %bitcast.51), kind=kOutput, calls=%fused_computation.10 | convolution fusion | flops 254607360 | bytes 2490368 | tf_op jit(solution)/shard_map/dot_general | solution.py:10
  30.8 1.4 %collective-permute-done.8 = f32[192,256]{1,0:T(8,128)S(1)} collective-permute-done((f32[192,256]{1,0:T(8,128)S(1)}, f32[192,256]{1,0:T(8,128)S(1)}, u32[]{:S(2)}, u32[]{:S(2)}) %collective-permute-start.8) | collective-permute-done | bytes 196640 | tf_op jit(solution)/shard_map/ppermute | solution.py:147
  32.3 1.4 %collective-permute-done.9 = bf16[64,2560]{1,0:T(8,128)(2,1)S(1)} collective-permute-done((bf16[64,2560]{1,0:T(8,128)(2,1)S(1)}, bf16[64,2560]{1,0:T(8,128)(2,1)S(1)}, u32[]{:S(2)}, u32[]{:S(2)}) %collective-permute-start.9) | collective-permute-done | bytes 327712 | tf_op jit(solution)/shard_map/ppermute | solution.py:185
  34.3 1.2 %collective-permute-done.10 = f32[64,256]{1,0:T(8,128)S(1)} collective-permute-done((f32[64,256]{1,0:T(8,128)S(1)}, f32[64,256]{1,0:T(8,128)S(1)}, u32[]{:S(2)}, u32[]{:S(2)}) %collective-permute-start.10) | collective-permute-done | bytes 65568 | tf_op jit(solution)/shard_map/ppermute | solution.py:147
  39.1 2.8 %collective-permute-start.11 = (bf16[64,2560]{1,0:T(8,128)(2,1)S(1)}, bf16[64,2560]{1,0:T(8,128)(2,1)S(1)}, u32[]{:S(2)}, u32[]{:S(2)}) collective-permute-start(bf16[64,2560]{1,0:T(8,128)(2,1)S(1)} %broadcast_select_fusion), channel_id=1, source_target_pairs={{0,16},{16,0},{1,17},{17,1},{2,18},{18,2},{3,19},{19,3},{4,20},{20... | collective-permute-start | bytes 983048 | tf_op jit(solution)/shard_map/ppermute | solution.py:216
  41.8 1.5 %collective-permute-start.12 = (bf16[64,2560]{1,0:T(8,128)(2,1)S(1)}, bf16[64,2560]{1,0:T(8,128)(2,1)S(1)}, u32[]{:S(2)}, u32[]{:S(2)}) collective-permute-start(bf16[64,2560]{1,0:T(8,128)(2,1)S(1)} %fusion.54), channel_id=1, source_target_pairs={{0,4},{2,6},{4,0},{6,2},{8,12},{10,14},{12,8},{14,10},{1,5},{3,7},... | collective-permute-start | bytes 983048 | tf_op jit(solution)/shard_map/ppermute | solution.py:114
  45.4 2.7 %collective-permute-done.11 = bf16[64,2560]{1,0:T(8,128)(2,1)S(1)} collective-permute-done((bf16[64,2560]{1,0:T(8,128)(2,1)S(1)}, bf16[64,2560]{1,0:T(8,128)(2,1)S(1)}, u32[]{:S(2)}, u32[]{:S(2)}) %collective-permute-start.11) | collective-permute-done | bytes 327712 | tf_op jit(solution)/shard_map/ppermute | solution.py:216
  48.1 4.3 %collective-permute-done.12 = bf16[64,2560]{1,0:T(8,128)(2,1)S(1)} collective-permute-done((bf16[64,2560]{1,0:T(8,128)(2,1)S(1)}, bf16[64,2560]{1,0:T(8,128)(2,1)S(1)}, u32[]{:S(2)}, u32[]{:S(2)}) %collective-permute-start.12) | collective-permute-done | bytes 327712 | tf_op jit(solution)/shard_map/ppermute | solution.py:114
  54.3 1.2 %collective-permute-done.15 = f32[64,256]{1,0:T(8,128)S(1)} collective-permute-done((f32[64,256]{1,0:T(8,128)S(1)}, f32[64,256]{1,0:T(8,128)S(1)}, u32[]{:S(2)}, u32[]{:S(2)}) %collective-permute-start.15) | collective-permute-done | bytes 65568 | tf_op jit(solution)/shard_map/ppermute | solution.py:147
  55.9 1.4 %convolution_convert_fusion = bf16[128,2560]{1,0:T(8,128)(2,1)S(1)} fusion(bf16[64,2560]{1,0:T(8,128)(2,1)S(1)} %collective-permute-done.9, bf16[64,2560]{1,0:T(8,128)(2,1)} %collective-permute-done.5, bf16[64,2560]{1,0:T(8,128)(2,1)} %collective-permute-done.6, bf16[64,2560]{1,0:T(8,128)(2,1)S(1)} %bitcast.52, bf16[64,128]{1,0:T(8,128)(2,1)S(1)} %get-tuple-element.93, ...), kind=kOutput, calls=%fused_computation.4 | convolution fusion | flops 173604864 | bytes 2031616 | tf_op jit(solution)/shard_map/dot_general | solution.py:16
  57.4 1.2 %collective-permute-start.16 = (bf16[128,2560]{1,0:T(8,128)(2,1)S(1)}, bf16[128,2560]{1,0:T(8,128)(2,1)S(1)}, u32[]{:S(2)}, u32[]{:S(2)}) collective-permute-start(bf16[128,2560]{1,0:T(8,128)(2,1)S(1)} %convolution_convert_fusion), channel_id=1, source_target_pairs={{0,2},{2,0},{4,6},{6,4},{8,10},{10,8},{12,14},{14,12},{1,3},{3,1},... | collective-permute-start | bytes 1966088 | tf_op jit(solution)/shard_map/ppermute | solution.py:114
  58.9 1.5 %collective-permute-start.18 = (bf16[64,2560]{1,0:T(8,128)(2,1)S(1)}, bf16[64,2560]{1,0:T(8,128)(2,1)S(1)}, u32[]{:S(2)}, u32[]{:S(2)}) collective-permute-start(bf16[64,2560]{1,0:T(8,128)(2,1)S(1)} %fusion.44), channel_id=1, source_target_pairs={{0,4},{2,6},{4,0},{6,2},{8,12},{10,14},{12,8},{14,10},{1,5},{3,7},... | collective-permute-start | bytes 983048 | tf_op jit(solution)/shard_map/ppermute | solution.py:114
  61.1 2.5 %collective-permute-start.21 = (bf16[64,2560]{1,0:T(8,128)(2,1)S(1)}, bf16[64,2560]{1,0:T(8,128)(2,1)S(1)}, u32[]{:S(2)}, u32[]{:S(2)}) collective-permute-start(bf16[64,2560]{1,0:T(8,128)(2,1)S(1)} %add_convert_fusion.2), channel_id=1, source_target_pairs={{0,8},{2,10},{4,12},{6,14},{8,0},{10,2},{12,4},{14,6},{1,9},{3,11}... | collective-permute-start | bytes 983048 | tf_op jit(solution)/shard_map/ppermute | solution.py:114
  63.6 11.8 %collective-permute-done.18 = bf16[64,2560]{1,0:T(8,128)(2,1)S(1)} collective-permute-done((bf16[64,2560]{1,0:T(8,128)(2,1)S(1)}, bf16[64,2560]{1,0:T(8,128)(2,1)S(1)}, u32[]{:S(2)}, u32[]{:S(2)}) %collective-permute-start.18) | collective-permute-done | bytes 327712 | tf_op jit(solution)/shard_map/ppermute | solution.py:114
  77.2 1.2 %add_convert_fusion = bf16[128,2560]{1,0:T(8,128)(2,1)} fusion(bf16[128,2560]{1,0:T(8,128)(2,1)S(1)} %collective-permute-done.13, bf16[64,2560]{1,0:T(8,128)(2,1)S(1)} %collective-permute-done.11, bf16[64,2560]{1,0:T(8,128)(2,1)S(1)} %collective-permute-done.4, bf16[64,2560]{1,0:T(8,128)(2,1)S(1)} %collective-permute-done.3, ...), kind=kOutput, calls=%fused_computation.8 | convolution fusion | flops 174260224 | bytes 2686976 | tf_op jit(solution)/shard_map/dot_general | solution.py:16
  78.4 14.4 %collective-permute-done.20 = bf16[64,2560]{1,0:T(8,128)(2,1)S(1)} collective-permute-done((bf16[64,2560]{1,0:T(8,128)(2,1)S(1)}, bf16[64,2560]{1,0:T(8,128)(2,1)S(1)}, u32[]{:S(2)}, u32[]{:S(2)}) %collective-permute-start.20) | collective-permute-done | bytes 327712 | tf_op jit(solution)/shard_map/ppermute | solution.py:114
  93.7 2.3 %fusion = bf16[128,2560]{1,0:T(8,128)(2,1)} fusion(bf16[128,2560]{1,0:T(8,128)(2,1)S(1)} %collective-permute-done.16, bf16[64,2560]{1,0:T(8,128)(2,1)S(1)} %collective-permute-done.9, bf16[64,2560]{1,0:T(8,128)(2,1)} %collective-permute-done.5, bf16[64,2560]{1,0:T(8,128)(2,1)} %collective-permute-done.6, bf16[64,2560]{1,0:T(8,128)(2,1)S(1)} %bitcast.53, ...), kind=kOutput, calls=%fused_computation.3 | convolution fusion | flops 174260224 | bytes 2686976 | tf_op jit(solution)/shard_map/dot_general | solution.py:16
  (86 shorter events, 17.3 us)
Async XLA Ops:
  0.6 6.5 %copy-start = (s32[8,256]{1,0:T(8,128)S(1)}, s32[8,256]{1,0:T(8,128)}, u32[]{:S(2)}) copy-start(s32[8,256]{1,0:T(8,128)} %param.10) | copy-start | bytes 24580
  0.7 7.1 %collective-permute-start = (f32[1,256]{1,0:T(1,128)}, f32[1,256]{1,0:T(1,128)S(1)}, u32[]{:S(2)}, u32[]{:S(2)}) collective-permute-start(f32[1,256]{1,0:T(1,128)} %param.11), channel_id=1, source_target_pairs={{0,4},{2,6},{4,0},{6,2},{8,12},{10,14},{12,8},{14,10},{1,5},{3,7},... | collective-permute-start | bytes 3080 | tf_op jit(solution)/shard_map/ppermute | solution.py:114
  3.7 24.2 %collective-permute-start.7 = (bf16[128,2560]{1,0:T(8,128)(2,1)}, bf16[128,2560]{1,0:T(8,128)(2,1)}, u32[]{:S(2)}, u32[]{:S(2)}) collective-permute-start(bf16[128,2560]{1,0:T(8,128)(2,1)} %param.6), channel_id=1, source_target_pairs={{0,2},{2,0},{4,6},{6,4},{8,10},{10,8},{12,14},{14,12},{1,3},{3,1},... | collective-permute-start | bytes 1966088 | tf_op jit(solution)/shard_map/ppermute | solution.py:114
  5.2 18.6 %collective-permute-start.6 = (bf16[64,2560]{1,0:T(8,128)(2,1)}, bf16[64,2560]{1,0:T(8,128)(2,1)}, u32[]{:S(2)}, u32[]{:S(2)}) collective-permute-start(bf16[64,2560]{1,0:T(8,128)(2,1)} %bitcast.49), channel_id=1, source_target_pairs={{0,4},{2,6},{4,12},{6,14},{12,8},{14,10},{8,0},{10,2},{16,28},{18,... | collective-permute-start | bytes 983048 | tf_op jit(solution)/shard_map/ppermute | solution.py:118
  7.8 8.3 %collective-permute-start.2 = (f32[2,256]{1,0:T(2,128)S(1)}, f32[2,256]{1,0:T(2,128)S(1)}, u32[]{:S(2)}, u32[]{:S(2)}) collective-permute-start(f32[2,256]{1,0:T(2,128)S(1)} %pad_maximum_fusion.9), channel_id=1, source_target_pairs={{0,8},{2,10},{4,12},{6,14},{8,0},{10,2},{12,4},{14,6},{1,9},{3,11}... | collective-permute-start | bytes 6152 | tf_op jit(solution)/shard_map/ppermute | solution.py:114
  10.4 26.0 %collective-permute-start.1 = (bf16[128,2560]{1,0:T(8,128)(2,1)S(1)}, bf16[128,2560]{1,0:T(8,128)(2,1)}, u32[]{:S(2)}, u32[]{:S(2)}) collective-permute-start(bf16[128,2560]{1,0:T(8,128)(2,1)S(1)} %copy-done.1), channel_id=1, source_target_pairs={{0,2},{2,0},{4,6},{6,4},{8,10},{10,8},{12,14},{14,12},{1,3},{3,1},... | collective-permute-start | bytes 1966088 | tf_op jit(solution)/shard_map/ppermute | solution.py:114
  10.9 12.9 %collective-permute-start.5 = (bf16[64,2560]{1,0:T(8,128)(2,1)}, bf16[64,2560]{1,0:T(8,128)(2,1)}, u32[]{:S(2)}, u32[]{:S(2)}) collective-permute-start(bf16[64,2560]{1,0:T(8,128)(2,1)} %bitcast.50), channel_id=1, source_target_pairs={{4,0},{6,2},{12,4},{14,6},{8,12},{10,14},{0,8},{2,10},{28,16},{30,... | collective-permute-start | bytes 983048 | tf_op jit(solution)/shard_map/ppermute | solution.py:118
  16.7 12.4 %copy-start.4 = (bf16[1,64,2560]{2,1,0:T(8,128)(2,1)S(1)}, bf16[1,64,2560]{2,1,0:T(8,128)(2,1)}, u32[]{:S(2)}) copy-start(bf16[1,64,2560]{2,1,0:T(8,128)(2,1)} %param.8) | copy-start | bytes 983044
  17.1 18.4 %collective-permute-start.3 = (bf16[64,2560]{1,0:T(8,128)(2,1)}, bf16[64,2560]{1,0:T(8,128)(2,1)S(1)}, u32[]{:S(2)}, u32[]{:S(2)}) collective-permute-start(bf16[64,2560]{1,0:T(8,128)(2,1)} %bitcast.44), channel_id=1, source_target_pairs={{0,4},{2,6},{4,12},{6,14},{12,8},{14,10},{8,0},{10,2},{16,28},{18,... | collective-permute-start | bytes 983048 | tf_op jit(solution)/shard_map/ppermute | solution.py:118
  23.9 12.5 %collective-permute-start.4 = (bf16[64,2560]{1,0:T(8,128)(2,1)}, bf16[64,2560]{1,0:T(8,128)(2,1)S(1)}, u32[]{:S(2)}, u32[]{:S(2)}) collective-permute-start(bf16[64,2560]{1,0:T(8,128)(2,1)} %bitcast.45), channel_id=1, source_target_pairs={{4,0},{6,2},{12,4},{14,6},{8,12},{10,14},{0,8},{2,10},{28,16},{30,... | collective-permute-start | bytes 983048 | tf_op jit(solution)/shard_map/ppermute | solution.py:118
  24.9 8.8 %collective-permute-start.9 = (bf16[64,2560]{1,0:T(8,128)(2,1)S(1)}, bf16[64,2560]{1,0:T(8,128)(2,1)S(1)}, u32[]{:S(2)}, u32[]{:S(2)}) collective-permute-start(bf16[64,2560]{1,0:T(8,128)(2,1)S(1)} %broadcast_select_fusion.1), channel_id=1, source_target_pairs={{0,16},{16,0},{1,17},{17,1},{2,18},{18,2},{3,19},{19,3},{4,20},{20... | collective-permute-start | bytes 983048 | tf_op jit(solution)/shard_map/ppermute | solution.py:185
  30.7 1.5 %collective-permute-start.8 = (f32[192,256]{1,0:T(8,128)S(1)}, f32[192,256]{1,0:T(8,128)S(1)}, u32[]{:S(2)}, u32[]{:S(2)}) collective-permute-start(f32[192,256]{1,0:T(8,128)S(1)} %fusion.1), channel_id=1, source_target_pairs={{0,1},{1,0},{2,3},{3,2},{4,5},{5,4},{6,7},{7,6},{8,9},{9,8},{10,11... | collective-permute-start | bytes 589832 | tf_op jit(solution)/shard_map/ppermute | solution.py:147
  34.2 1.3 %collective-permute-start.10 = (f32[64,256]{1,0:T(8,128)S(1)}, f32[64,256]{1,0:T(8,128)S(1)}, u32[]{:S(2)}, u32[]{:S(2)}) collective-permute-start(f32[64,256]{1,0:T(8,128)S(1)} %fusion.79), channel_id=1, source_target_pairs={{0,1},{1,0},{2,3},{3,2},{4,5},{5,4},{6,7},{7,6},{8,9},{9,8},{10,11... | collective-permute-start | bytes 196616 | tf_op jit(solution)/shard_map/ppermute | solution.py:147
  39.1 9.1 %collective-permute-start.11 = (bf16[64,2560]{1,0:T(8,128)(2,1)S(1)}, bf16[64,2560]{1,0:T(8,128)(2,1)S(1)}, u32[]{:S(2)}, u32[]{:S(2)}) collective-permute-start(bf16[64,2560]{1,0:T(8,128)(2,1)S(1)} %broadcast_select_fusion), channel_id=1, source_target_pairs={{0,16},{16,0},{1,17},{17,1},{2,18},{18,2},{3,19},{19,3},{4,20},{20... | collective-permute-start | bytes 983048 | tf_op jit(solution)/shard_map/ppermute | solution.py:216
  41.8 10.6 %collective-permute-start.12 = (bf16[64,2560]{1,0:T(8,128)(2,1)S(1)}, bf16[64,2560]{1,0:T(8,128)(2,1)S(1)}, u32[]{:S(2)}, u32[]{:S(2)}) collective-permute-start(bf16[64,2560]{1,0:T(8,128)(2,1)S(1)} %fusion.54), channel_id=1, source_target_pairs={{0,4},{2,6},{4,0},{6,2},{8,12},{10,14},{12,8},{14,10},{1,5},{3,7},... | collective-permute-start | bytes 983048 | tf_op jit(solution)/shard_map/ppermute | solution.py:114
  43.3 1.4 %collective-permute-start.14 = (f32[192,256]{1,0:T(8,128)S(1)}, f32[192,256]{1,0:T(8,128)S(1)}, u32[]{:S(2)}, u32[]{:S(2)}) collective-permute-start(f32[192,256]{1,0:T(8,128)S(1)} %fusion.7), channel_id=1, source_target_pairs={{0,1},{1,0},{2,3},{3,2},{4,5},{5,4},{6,7},{7,6},{8,9},{9,8},{10,11... | collective-permute-start | bytes 589832 | tf_op jit(solution)/shard_map/ppermute | solution.py:147
  44.8 30.8 %collective-permute-start.17 = (bf16[64,2560]{1,0:T(8,128)(2,1)S(1)}, bf16[64,2560]{1,0:T(8,128)(2,1)S(1)}, u32[]{:S(2)}, u32[]{:S(2)}) collective-permute-start(bf16[64,2560]{1,0:T(8,128)(2,1)S(1)} %fusion.52), channel_id=1, source_target_pairs={{0,4},{2,6},{4,0},{6,2},{8,12},{10,14},{12,8},{14,10},{1,5},{3,7},... | collective-permute-start | bytes 983048 | tf_op jit(solution)/shard_map/ppermute | solution.py:114
  53.3 23.9 %collective-permute-start.13 = (bf16[128,2560]{1,0:T(8,128)(2,1)S(1)}, bf16[128,2560]{1,0:T(8,128)(2,1)S(1)}, u32[]{:S(2)}, u32[]{:S(2)}) collective-permute-start(bf16[128,2560]{1,0:T(8,128)(2,1)S(1)} %convolution_convert_fusion.1), channel_id=1, source_target_pairs={{0,2},{2,0},{4,6},{6,4},{8,10},{10,8},{12,14},{14,12},{1,3},{3,1},... | collective-permute-start | bytes 1966088 | tf_op jit(solution)/shard_map/ppermute | solution.py:114
  54.3 1.3 %collective-permute-start.15 = (f32[64,256]{1,0:T(8,128)S(1)}, f32[64,256]{1,0:T(8,128)S(1)}, u32[]{:S(2)}, u32[]{:S(2)}) collective-permute-start(f32[64,256]{1,0:T(8,128)S(1)} %fusion.80), channel_id=1, source_target_pairs={{0,1},{1,0},{2,3},{3,2},{4,5},{5,4},{6,7},{7,6},{8,9},{9,8},{10,11... | collective-permute-start | bytes 196616 | tf_op jit(solution)/shard_map/ppermute | solution.py:147
  57.4 36.3 %collective-permute-start.16 = (bf16[128,2560]{1,0:T(8,128)(2,1)S(1)}, bf16[128,2560]{1,0:T(8,128)(2,1)S(1)}, u32[]{:S(2)}, u32[]{:S(2)}) collective-permute-start(bf16[128,2560]{1,0:T(8,128)(2,1)S(1)} %convolution_convert_fusion), channel_id=1, source_target_pairs={{0,2},{2,0},{4,6},{6,4},{8,10},{10,8},{12,14},{14,12},{1,3},{3,1},... | collective-permute-start | bytes 1966088 | tf_op jit(solution)/shard_map/ppermute | solution.py:114
  58.9 16.6 %collective-permute-start.18 = (bf16[64,2560]{1,0:T(8,128)(2,1)S(1)}, bf16[64,2560]{1,0:T(8,128)(2,1)S(1)}, u32[]{:S(2)}, u32[]{:S(2)}) collective-permute-start(bf16[64,2560]{1,0:T(8,128)(2,1)S(1)} %fusion.44), channel_id=1, source_target_pairs={{0,4},{2,6},{4,0},{6,2},{8,12},{10,14},{12,8},{14,10},{1,5},{3,7},... | collective-permute-start | bytes 983048 | tf_op jit(solution)/shard_map/ppermute | solution.py:114
  61.1 15.2 %collective-permute-start.21 = (bf16[64,2560]{1,0:T(8,128)(2,1)S(1)}, bf16[64,2560]{1,0:T(8,128)(2,1)S(1)}, u32[]{:S(2)}, u32[]{:S(2)}) collective-permute-start(bf16[64,2560]{1,0:T(8,128)(2,1)S(1)} %add_convert_fusion.2), channel_id=1, source_target_pairs={{0,8},{2,10},{4,12},{6,14},{8,0},{10,2},{12,4},{14,6},{1,9},{3,11}... | collective-permute-start | bytes 983048 | tf_op jit(solution)/shard_map/ppermute | solution.py:114
  75.5 17.3 %collective-permute-start.20 = (bf16[64,2560]{1,0:T(8,128)(2,1)S(1)}, bf16[64,2560]{1,0:T(8,128)(2,1)S(1)}, u32[]{:S(2)}, u32[]{:S(2)}) collective-permute-start(bf16[64,2560]{1,0:T(8,128)(2,1)S(1)} %add_convert_fusion.1), channel_id=1, source_target_pairs={{0,8},{2,10},{4,12},{6,14},{8,0},{10,2},{12,4},{14,6},{1,9},{3,11}... | collective-permute-start | bytes 983048 | tf_op jit(solution)/shard_map/ppermute | solution.py:114
  75.6 17.2 %collective-permute-start.19 = (bf16[64,2560]{1,0:T(8,128)(2,1)S(1)}, bf16[64,2560]{1,0:T(8,128)(2,1)S(1)}, u32[]{:S(2)}, u32[]{:S(2)}) collective-permute-start(bf16[64,2560]{1,0:T(8,128)(2,1)S(1)} %fusion.48), channel_id=1, source_target_pairs={{0,4},{2,6},{4,0},{6,2},{8,12},{10,14},{12,8},{14,10},{1,5},{3,7},... | collective-permute-start | bytes 983048 | tf_op jit(solution)/shard_map/ppermute | solution.py:114
  (3 other events, 9.5 us)

commit v14 on v11

--- a/solution.py
+++ b/solution.py
@@ -195,11 +195,12 @@
     most = most_products(tokens2, down_matrix, near_down, far_down)
     most, tokens2 = lax.optimization_barrier((most, tokens2))
     low = low_rank(most, tokens2, cross_down)
-    cot2, far_up, low = lax.optimization_barrier((cot2, far_up, low))
-    cross_up = lax.ppermute(far_up, "groups", SWAP)
+    cot2, low = lax.optimization_barrier((cot2, low))
     cot2 = jnp.concatenate([cotangent, cot2], axis=0)
     (own, first, second, third), up_send = partial_sums(for_line(low), cot2)
     up_third = move(up_send[2], xor_line(1))
+    far_up = after(far_up, up_send)
+    cross_up = lax.ppermute(far_up, "groups", SWAP)
     most = most_products(cot2, up_matrix, near_up, far_up)
     most, up_next = lax.optimization_barrier((most, up_send[0]))
     up_first = move(up_next, xor_line(1))
@@ -216,8 +217,9 @@
     down_far = move(down_sum, xor_line(2))
     down_first = move(after(down_send[0], (up_first, down_sum)), xor_line(1))
     branch_out = outward_end(low, up_all, branch_back)
-    up_grad = add_up(own, up_first, up_far)
+    up_grad = add_up(own, up_first, after(up_far, down_sum))
     input_grad = outward_end(low_back, down_all, input_back)
+    input_grad, down_far = lax.optimization_barrier((input_grad, down_far))
     down_grad = add_up(own_b, down_first, down_far)
     down_grad = (down_grad / capacity).astype(jnp.bfloat16)[None]
     up_grad = (up_grad / capacity).astype(jnp.bfloat16)[None]

time: 93.9 us -> 91.7 us (0.977)
  waiting for transfers between devices: 52.8 us -> 49.3 us
  starting transfers between devices: 22.1 us -> 23.4 us
    ppermute x1, waiting for transfers between devices: 3.69 us -> 0.01 us  [by_pairs(): far_up = lax.ppermute(up_later, ('groups', 'adapter'), FAR)]
  transfers between devices with their start and end apart: 22 -> 22, of which waited for: 11 -> 13; matrix products, arithmetic and copies ran while one was open for 17% -> 18% of each run, Pallas kernels for 0% -> 0%
where the time goes in v14:
time: 91.7 us; the launch traced here: 91.4 us
  waiting for transfers between devices  49.3 us (54%)
  starting transfers between devices  23.4 us (26%)
  matrix products  11.1 us (12%)
  local copies, waits for them, and re-layouts  4.09 us (4%)
  other arithmetic  2.54 us (3%)
  between operations  0.93 us (1%)
    ppermute x14, waiting for transfers between devices, move(): return lax.ppermute(value, 'adapter', pairs)  43.5 us
    ppermute x14, starting transfers between devices, move(): return lax.ppermute(value, 'adapter', pairs)  14.6 us
    dot_general x4, matrix products, contract_first(): lax.dot_general(left_op, right_op, (((0,), (0,)), ((), ())), preferred_el...  5.07 us
    ppermute x1, starting transfers between devices, by_pairs(): cross_down = lax.ppermute(ready, 'groups', SWAP)  4.26 us
    ppermute x4, waiting for transfers between devices, both_cores(): return partial + lax.ppermute(partial, 'tensor', SWAP)  3.94 us
    dot_general x4, matrix products, contract_last(): lax.dot_general(left_op, right_op, (((1,), (1,)), ((), ())), preferred_el...  3.18 us
    dot_general x8, matrix products, partial_sums(): jnp.dot(weight, rows, preferred_element_type=jnp.float32)  2.84 us
    ppermute x1, starting transfers between devices, by_pairs(): far_down = lax.ppermute(down_matrix, ('groups', 'adapter'), FAR)  2.59 us
  transfers between devices with their start and end apart: 22, of which 13 were waited for; matrix products, arithmetic and copies ran while one was open for 18% of the time, Pallas kernels for 0%

profile of v14, /device:TPU:0, one launch (start us, length us, event | category | flops | bytes accessed | tf_op | source)
XLA Modules:
  0.0 91.4 jit_solution(1665875333710038245)
XLA Ops:
  0.7 3.1 %collective-permute-start.2 = (f32[1,256]{1,0:T(1,128)}, f32[1,256]{1,0:T(1,128)S(1)}, u32[]{:S(2)}, u32[]{:S(2)}) collective-permute-start(f32[1,256]{1,0:T(1,128)} %param.11), channel_id=1, source_target_pairs={{0,4},{2,6},{4,0},{6,2},{8,12},{10,14},{12,8},{14,10},{1,5},{3,7},... | collective-permute-start | bytes 3080 | tf_op jit(solution)/shard_map/ppermute | solution.py:111
  3.7 2.6 %collective-permute-start.1 = (bf16[64,2560]{1,0:T(8,128)(2,1)}, bf16[64,2560]{1,0:T(8,128)(2,1)}, u32[]{:S(2)}, u32[]{:S(2)}) collective-permute-start(bf16[64,2560]{1,0:T(8,128)(2,1)} %bitcast.51), channel_id=1, source_target_pairs={{0,8},{2,10},{4,12},{6,14},{8,0},{10,2},{12,4},{14,6},{16,28},{18,... | collective-permute-start | bytes 983048 | tf_op jit(solution)/shard_map/ppermute | solution.py:147
  6.3 1.5 %collective-permute-start.5 = (bf16[128,2560]{1,0:T(8,128)(2,1)}, bf16[128,2560]{1,0:T(8,128)(2,1)}, u32[]{:S(2)}, u32[]{:S(2)}) collective-permute-start(bf16[128,2560]{1,0:T(8,128)(2,1)} %param.6), channel_id=1, source_target_pairs={{0,2},{2,0},{4,6},{6,4},{8,10},{10,8},{12,14},{14,12},{1,3},{3,1},... | collective-permute-start | bytes 1966088 | tf_op jit(solution)/shard_map/ppermute | solution.py:111
  8.4 1.1 %constant_dynamic-update-slice_fusion.1 = bf16[256,2560]{1,0:T(8,128)(2,1)S(1)} fusion(bf16[128,2560]{1,0:T(8,128)(2,1)} %param.6), kind=kLoop, calls=%fused_computation.77 | loop fusion | bytes 1310720
  11.1 10.1 %collective-permute-done.3 = f32[2,256]{1,0:T(2,128)S(1)} collective-permute-done((f32[2,256]{1,0:T(2,128)S(1)}, f32[2,256]{1,0:T(2,128)S(1)}, u32[]{:S(2)}, u32[]{:S(2)}) %collective-permute-start.3) | collective-permute-done | bytes 2080 | tf_op jit(solution)/shard_map/ppermute | solution.py:111
  21.5 4.3 %collective-permute-start.7 = (bf16[64,2560]{1,0:T(8,128)(2,1)}, bf16[64,2560]{1,0:T(8,128)(2,1)S(1)}, u32[]{:S(2)}, u32[]{:S(2)}) collective-permute-start(bf16[64,2560]{1,0:T(8,128)(2,1)} %collective-permute-done.1), channel_id=1, source_target_pairs={{0,16},{16,0},{1,17},{17,1},{2,18},{18,2},{3,19},{19,3},{4,20},{20... | collective-permute-start | bytes 983048 | tf_op jit(solution)/shard_map/ppermute | solution.py:170
  27.4 1.6 %fusion.2 = f32[192,256]{1,0:T(8,128)S(1)} fusion(bf16[256,2560]{1,0:T(8,128)(2,1)S(1)} %constant_dynamic-update-slice_fusion, bf16[64,2560]{1,0:T(8,128)(2,1)} %collective-permute-done.1, bf16[64,2560]{1,0:T(8,128)(2,1)S(1)} %collective-permute-done.4, bf16[64,2560]{1,0:T(8,128)(2,1)S(1)} %bitcast.53), kind=kOutput, calls=%fused_computation.10 | convolution fusion | flops 254607360 | bytes 2490368 | tf_op jit(solution)/shard_map/dot_general | solution.py:10
  29.2 1.3 %collective-permute-done.6 = f32[192,256]{1,0:T(8,128)S(1)} collective-permute-done((f32[192,256]{1,0:T(8,128)S(1)}, f32[192,256]{1,0:T(8,128)S(1)}, u32[]{:S(2)}, u32[]{:S(2)}) %collective-permute-start.6) | collective-permute-done | bytes 196640 | tf_op jit(solution)/shard_map/ppermute | solution.py:135
  30.5 1.9 %collective-permute-done.7 = bf16[64,2560]{1,0:T(8,128)(2,1)S(1)} collective-permute-done((bf16[64,2560]{1,0:T(8,128)(2,1)}, bf16[64,2560]{1,0:T(8,128)(2,1)S(1)}, u32[]{:S(2)}, u32[]{:S(2)}) %collective-permute-start.7) | collective-permute-done | bytes 327712 | tf_op jit(solution)/shard_map/ppermute | solution.py:170
  33.0 1.2 %collective-permute-done.8 = f32[64,256]{1,0:T(8,128)S(1)} collective-permute-done((f32[64,256]{1,0:T(8,128)S(1)}, f32[64,256]{1,0:T(8,128)S(1)}, u32[]{:S(2)}, u32[]{:S(2)}) %collective-permute-start.8) | collective-permute-done | bytes 65568 | tf_op jit(solution)/shard_map/ppermute | solution.py:135
  34.2 2.4 %collective-permute-done = bf16[128,2560]{1,0:T(8,128)(2,1)} collective-permute-done((bf16[128,2560]{1,0:T(8,128)(2,1)}, bf16[128,2560]{1,0:T(8,128)(2,1)}, u32[]{:S(2)}, u32[]{:S(2)}) %collective-permute-start) | collective-permute-done | bytes 655392 | tf_op jit(solution)/shard_map/ppermute | solution.py:111
  39.7 1.6 %collective-permute-start.11 = (bf16[64,2560]{1,0:T(8,128)(2,1)S(1)}, bf16[64,2560]{1,0:T(8,128)(2,1)S(1)}, u32[]{:S(2)}, u32[]{:S(2)}) collective-permute-start(bf16[64,2560]{1,0:T(8,128)(2,1)S(1)} %collective-permute-done.10), channel_id=1, source_target_pairs={{0,16},{16,0},{1,17},{17,1},{2,18},{18,2},{3,19},{19,3},{4,20},{20... | collective-permute-start | bytes 983048 | tf_op jit(solution)/shard_map/ppermute | solution.py:203
  41.3 3.5 %collective-permute-done.9 = bf16[64,2560]{1,0:T(8,128)(2,1)S(1)} collective-permute-done((bf16[64,2560]{1,0:T(8,128)(2,1)S(1)}, bf16[64,2560]{1,0:T(8,128)(2,1)S(1)}, u32[]{:S(2)}, u32[]{:S(2)}) %collective-permute-start.9) | collective-permute-done | bytes 327712 | tf_op jit(solution)/shard_map/ppermute | solution.py:111
  45.6 1.4 %collective-permute-done.14 = f32[192,256]{1,0:T(8,128)S(1)} collective-permute-done((f32[192,256]{1,0:T(8,128)S(1)}, f32[192,256]{1,0:T(8,128)S(1)}, u32[]{:S(2)}, u32[]{:S(2)}) %collective-permute-start.14) | collective-permute-done | bytes 196640 | tf_op jit(solution)/shard_map/ppermute | solution.py:135
  47.8 4.1 %collective-permute-done.12 = bf16[64,2560]{1,0:T(8,128)(2,1)S(1)} collective-permute-done((bf16[64,2560]{1,0:T(8,128)(2,1)S(1)}, bf16[64,2560]{1,0:T(8,128)(2,1)S(1)}, u32[]{:S(2)}, u32[]{:S(2)}) %collective-permute-start.12) | collective-permute-done | bytes 327712 | tf_op jit(solution)/shard_map/ppermute | solution.py:111
  53.3 1.6 %collective-permute-start.13 = (bf16[128,2560]{1,0:T(8,128)(2,1)S(1)}, bf16[128,2560]{1,0:T(8,128)(2,1)S(1)}, u32[]{:S(2)}, u32[]{:S(2)}) collective-permute-start(bf16[128,2560]{1,0:T(8,128)(2,1)S(1)} %convolution_convert_fusion.1), channel_id=1, source_target_pairs={{0,2},{2,0},{4,6},{6,4},{8,10},{10,8},{12,14},{14,12},{1,3},{3,1},... | collective-permute-start | bytes 1966088 | tf_op jit(solution)/shard_map/ppermute | solution.py:111
  55.6 2.5 %collective-permute-start.17 = (bf16[64,2560]{1,0:T(8,128)(2,1)S(1)}, bf16[64,2560]{1,0:T(8,128)(2,1)S(1)}, u32[]{:S(2)}, u32[]{:S(2)}) collective-permute-start(bf16[64,2560]{1,0:T(8,128)(2,1)S(1)} %fusion.44), channel_id=1, source_target_pairs={{0,4},{2,6},{4,0},{6,2},{8,12},{10,14},{12,8},{14,10},{1,5},{3,7},... | collective-permute-start | bytes 983048 | tf_op jit(solution)/shard_map/ppermute | solution.py:111
  58.2 1.3 %convolution_convert_fusion = bf16[128,2560]{1,0:T(8,128)(2,1)S(1)} fusion(bf16[64,2560]{1,0:T(8,128)(2,1)S(1)} %collective-permute-done.7, bf16[64,2560]{1,0:T(8,128)(2,1)} %collective-permute-done.1, bf16[64,2560]{1,0:T(8,128)(2,1)S(1)} %collective-permute-done.4, bf16[64,2560]{1,0:T(8,128)(2,1)S(1)} %bitcast.54, ...), kind=kOutput, calls=%fused_computation.5 | convolution fusion | flops 173604864 | bytes 2031616 | tf_op jit(solution)/shard_map/dot_general | solution.py:16
  60.4 12.5 %collective-permute-done.17 = bf16[64,2560]{1,0:T(8,128)(2,1)S(1)} collective-permute-done((bf16[64,2560]{1,0:T(8,128)(2,1)S(1)}, bf16[64,2560]{1,0:T(8,128)(2,1)S(1)}, u32[]{:S(2)}, u32[]{:S(2)}) %collective-permute-start.17) | collective-permute-done | bytes 327712 | tf_op jit(solution)/shard_map/ppermute | solution.py:111
  73.4 2.5 %collective-permute-start.20 = (bf16[64,2560]{1,0:T(8,128)(2,1)S(1)}, bf16[64,2560]{1,0:T(8,128)(2,1)S(1)}, u32[]{:S(2)}, u32[]{:S(2)}) collective-permute-start(bf16[64,2560]{1,0:T(8,128)(2,1)S(1)} %fusion.79), channel_id=1, source_target_pairs={{0,4},{2,6},{4,0},{6,2},{8,12},{10,14},{12,8},{14,10},{1,5},{3,7},... | collective-permute-start | bytes 983048 | tf_op jit(solution)/shard_map/ppermute | solution.py:111
  76.7 1.2 %fusion = bf16[128,2560]{1,0:T(8,128)(2,1)} fusion(bf16[128,2560]{1,0:T(8,128)(2,1)S(1)} %collective-permute-done.13, bf16[64,2560]{1,0:T(8,128)(2,1)S(1)} %collective-permute-done.11, bf16[64,2560]{1,0:T(8,128)(2,1)S(1)} %collective-permute-done.10, bf16[64,2560]{1,0:T(8,128)(2,1)S(1)} %collective-permute-done.9, bf16[64,2560]{1,0:T(8,128)(2,1)S(1)} %bitcast.50, ...), kind=kOutput, calls=%fused_computation.3 | convolution fusion | flops 174260224 | bytes 2686976 | tf_op jit(solution)/shard_map/dot_general | solution.py:16
  77.9 6.6 %collective-permute-done.16 = bf16[128,2560]{1,0:T(8,128)(2,1)S(1)} collective-permute-done((bf16[128,2560]{1,0:T(8,128)(2,1)S(1)}, bf16[128,2560]{1,0:T(8,128)(2,1)S(1)}, u32[]{:S(2)}, u32[]{:S(2)}) %collective-permute-start.16) | collective-permute-done | bytes 655392 | tf_op jit(solution)/shard_map/ppermute | solution.py:111
  84.5 2.2 %fusion.1 = bf16[128,2560]{1,0:T(8,128)(2,1)} fusion(bf16[128,2560]{1,0:T(8,128)(2,1)S(1)} %collective-permute-done.16, bf16[64,2560]{1,0:T(8,128)(2,1)S(1)} %collective-permute-done.7, bf16[64,2560]{1,0:T(8,128)(2,1)} %collective-permute-done.1, bf16[64,2560]{1,0:T(8,128)(2,1)S(1)} %collective-permute-done.4, bf16[64,2560]{1,0:T(8,128)(2,1)S(1)} %bitcast.55, ...), kind=kOutput, calls=%fused_computation.4 | convolution fusion | flops 174260224 | bytes 2686976 | tf_op jit(solution)/shard_map/dot_general | solution.py:16
  86.7 3.6 %collective-permute-done.18 = bf16[64,2560]{1,0:T(8,128)(2,1)S(1)} collective-permute-done((bf16[64,2560]{1,0:T(8,128)(2,1)S(1)}, bf16[64,2560]{1,0:T(8,128)(2,1)S(1)}, u32[]{:S(2)}, u32[]{:S(2)}) %collective-permute-start.18) | collective-permute-done | bytes 327712 | tf_op jit(solution)/shard_map/ppermute | solution.py:111
  (80 shorter events, 14.7 us)
Async XLA Ops:
  0.6 9.1 %copy-start = (s32[8,256]{1,0:T(8,128)S(1)}, s32[8,256]{1,0:T(8,128)}, u32[]{:S(2)}) copy-start(s32[8,256]{1,0:T(8,128)} %param.10) | copy-start | bytes 24580
  0.7 9.8 %collective-permute-start.2 = (f32[1,256]{1,0:T(1,128)}, f32[1,256]{1,0:T(1,128)S(1)}, u32[]{:S(2)}, u32[]{:S(2)}) collective-permute-start(f32[1,256]{1,0:T(1,128)} %param.11), channel_id=1, source_target_pairs={{0,4},{2,6},{4,0},{6,2},{8,12},{10,14},{12,8},{14,10},{1,5},{3,7},... | collective-permute-start | bytes 3080 | tf_op jit(solution)/shard_map/ppermute | solution.py:111
  3.7 17.8 %collective-permute-start.1 = (bf16[64,2560]{1,0:T(8,128)(2,1)}, bf16[64,2560]{1,0:T(8,128)(2,1)}, u32[]{:S(2)}, u32[]{:S(2)}) collective-permute-start(bf16[64,2560]{1,0:T(8,128)(2,1)} %bitcast.51), channel_id=1, source_target_pairs={{0,8},{2,10},{4,12},{6,14},{8,0},{10,2},{12,4},{14,6},{16,28},{18,... | collective-permute-start | bytes 983048 | tf_op jit(solution)/shard_map/ppermute | solution.py:147
  6.3 19.9 %collective-permute-start.5 = (bf16[128,2560]{1,0:T(8,128)(2,1)}, bf16[128,2560]{1,0:T(8,128)(2,1)}, u32[]{:S(2)}, u32[]{:S(2)}) collective-permute-start(bf16[128,2560]{1,0:T(8,128)(2,1)} %param.6), channel_id=1, source_target_pairs={{0,2},{2,0},{4,6},{6,4},{8,10},{10,8},{12,14},{14,12},{1,3},{3,1},... | collective-permute-start | bytes 1966088 | tf_op jit(solution)/shard_map/ppermute | solution.py:111
  7.8 28.8 %collective-permute-start = (bf16[128,2560]{1,0:T(8,128)(2,1)}, bf16[128,2560]{1,0:T(8,128)(2,1)}, u32[]{:S(2)}, u32[]{:S(2)}) collective-permute-start(bf16[128,2560]{1,0:T(8,128)(2,1)} %param.7), channel_id=1, source_target_pairs={{0,2},{2,0},{4,6},{6,4},{8,10},{10,8},{12,14},{14,12},{1,3},{3,1},... | collective-permute-start | bytes 1966088 | tf_op jit(solution)/shard_map/ppermute | solution.py:111
  9.6 17.8 %copy-start.4 = (bf16[1,64,2560]{2,1,0:T(8,128)(2,1)S(1)}, bf16[1,64,2560]{2,1,0:T(8,128)(2,1)}, u32[]{:S(2)}) copy-start(bf16[1,64,2560]{2,1,0:T(8,128)(2,1)} %param.8) | copy-start | bytes 983044
  10.4 10.7 %collective-permute-start.3 = (f32[2,256]{1,0:T(2,128)S(1)}, f32[2,256]{1,0:T(2,128)S(1)}, u32[]{:S(2)}, u32[]{:S(2)}) collective-permute-start(f32[2,256]{1,0:T(2,128)S(1)} %pad_maximum_fusion.7), channel_id=1, source_target_pairs={{0,8},{2,10},{4,12},{6,14},{8,0},{10,2},{12,4},{14,6},{1,9},{3,11}... | collective-permute-start | bytes 6152 | tf_op jit(solution)/shard_map/ppermute | solution.py:111
  10.9 15.4 %collective-permute-start.4 = (bf16[64,2560]{1,0:T(8,128)(2,1)}, bf16[64,2560]{1,0:T(8,128)(2,1)S(1)}, u32[]{:S(2)}, u32[]{:S(2)}) collective-permute-start(bf16[64,2560]{1,0:T(8,128)(2,1)} %bitcast.52), channel_id=1, source_target_pairs={{0,4},{2,6},{4,0},{6,2},{8,12},{10,14},{12,8},{14,10},{1,5},{3,7},... | collective-permute-start | bytes 983048 | tf_op jit(solution)/shard_map/ppermute | solution.py:111
  21.1 18.6 %collective-permute-start.10 = (bf16[64,2560]{1,0:T(8,128)(2,1)}, bf16[64,2560]{1,0:T(8,128)(2,1)S(1)}, u32[]{:S(2)}, u32[]{:S(2)}) collective-permute-start(bf16[64,2560]{1,0:T(8,128)(2,1)} %bitcast.46), channel_id=1, source_target_pairs={{0,8},{2,10},{4,12},{6,14},{8,0},{10,2},{12,4},{14,6},{16,28},{18,... | collective-permute-start | bytes 983048 | tf_op jit(solution)/shard_map/ppermute | solution.py:168
  21.5 10.9 %collective-permute-start.7 = (bf16[64,2560]{1,0:T(8,128)(2,1)}, bf16[64,2560]{1,0:T(8,128)(2,1)S(1)}, u32[]{:S(2)}, u32[]{:S(2)}) collective-permute-start(bf16[64,2560]{1,0:T(8,128)(2,1)} %collective-permute-done.1), channel_id=1, source_target_pairs={{0,16},{16,0},{1,17},{17,1},{2,18},{18,2},{3,19},{19,3},{4,20},{20... | collective-permute-start | bytes 983048 | tf_op jit(solution)/shard_map/ppermute | solution.py:170
  29.0 1.5 %collective-permute-start.6 = (f32[192,256]{1,0:T(8,128)S(1)}, f32[192,256]{1,0:T(8,128)S(1)}, u32[]{:S(2)}, u32[]{:S(2)}) collective-permute-start(f32[192,256]{1,0:T(8,128)S(1)} %fusion.2), channel_id=1, source_target_pairs={{0,1},{1,0},{2,3},{3,2},{4,5},{5,4},{6,7},{7,6},{8,9},{9,8},{10,11... | collective-permute-start | bytes 589832 | tf_op jit(solution)/shard_map/ppermute | solution.py:135
  29.1 15.8 %collective-permute-start.9 = (bf16[64,2560]{1,0:T(8,128)(2,1)S(1)}, bf16[64,2560]{1,0:T(8,128)(2,1)S(1)}, u32[]{:S(2)}, u32[]{:S(2)}) collective-permute-start(bf16[64,2560]{1,0:T(8,128)(2,1)S(1)} %bitcast.47), channel_id=1, source_target_pairs={{0,4},{2,6},{4,0},{6,2},{8,12},{10,14},{12,8},{14,10},{1,5},{3,7},... | collective-permute-start | bytes 983048 | tf_op jit(solution)/shard_map/ppermute | solution.py:111
  32.9 1.3 %collective-permute-start.8 = (f32[64,256]{1,0:T(8,128)S(1)}, f32[64,256]{1,0:T(8,128)S(1)}, u32[]{:S(2)}, u32[]{:S(2)}) collective-permute-start(f32[64,256]{1,0:T(8,128)S(1)} %fusion.74), channel_id=1, source_target_pairs={{0,1},{1,0},{2,3},{3,2},{4,5},{5,4},{6,7},{7,6},{8,9},{9,8},{10,11... | collective-permute-start | bytes 196616 | tf_op jit(solution)/shard_map/ppermute | solution.py:135
  39.2 12.7 %collective-permute-start.12 = (bf16[64,2560]{1,0:T(8,128)(2,1)S(1)}, bf16[64,2560]{1,0:T(8,128)(2,1)S(1)}, u32[]{:S(2)}, u32[]{:S(2)}) collective-permute-start(bf16[64,2560]{1,0:T(8,128)(2,1)S(1)} %fusion.48), channel_id=1, source_target_pairs={{0,4},{2,6},{4,0},{6,2},{8,12},{10,14},{12,8},{14,10},{1,5},{3,7},... | collective-permute-start | bytes 983048 | tf_op jit(solution)/shard_map/ppermute | solution.py:111
  39.7 12.6 %collective-permute-start.11 = (bf16[64,2560]{1,0:T(8,128)(2,1)S(1)}, bf16[64,2560]{1,0:T(8,128)(2,1)S(1)}, u32[]{:S(2)}, u32[]{:S(2)}) collective-permute-start(bf16[64,2560]{1,0:T(8,128)(2,1)S(1)} %collective-permute-done.10), channel_id=1, source_target_pairs={{0,16},{16,0},{1,17},{17,1},{2,18},{18,2},{3,19},{19,3},{4,20},{20... | collective-permute-start | bytes 983048 | tf_op jit(solution)/shard_map/ppermute | solution.py:203
  45.4 1.5 %collective-permute-start.14 = (f32[192,256]{1,0:T(8,128)S(1)}, f32[192,256]{1,0:T(8,128)S(1)}, u32[]{:S(2)}, u32[]{:S(2)}) collective-permute-start(f32[192,256]{1,0:T(8,128)S(1)} %fusion.8), channel_id=1, source_target_pairs={{0,1},{1,0},{2,3},{3,2},{4,5},{5,4},{6,7},{7,6},{8,9},{9,8},{10,11... | collective-permute-start | bytes 589832 | tf_op jit(solution)/shard_map/ppermute | solution.py:135
  47.4 26.0 %collective-permute-start.19 = (bf16[64,2560]{1,0:T(8,128)(2,1)S(1)}, bf16[64,2560]{1,0:T(8,128)(2,1)S(1)}, u32[]{:S(2)}, u32[]{:S(2)}) collective-permute-start(bf16[64,2560]{1,0:T(8,128)(2,1)S(1)} %fusion.76), channel_id=1, source_target_pairs={{0,4},{2,6},{4,0},{6,2},{8,12},{10,14},{12,8},{14,10},{1,5},{3,7},... | collective-permute-start | bytes 983048 | tf_op jit(solution)/shard_map/ppermute | solution.py:111
  52.0 21.4 %collective-permute-start.21 = (bf16[64,2560]{1,0:T(8,128)(2,1)S(1)}, bf16[64,2560]{1,0:T(8,128)(2,1)S(1)}, u32[]{:S(2)}, u32[]{:S(2)}) collective-permute-start(bf16[64,2560]{1,0:T(8,128)(2,1)S(1)} %add_convert_fusion), channel_id=1, source_target_pairs={{0,8},{2,10},{4,12},{6,14},{8,0},{10,2},{12,4},{14,6},{1,9},{3,11}... | collective-permute-start | bytes 983048 | tf_op jit(solution)/shard_map/ppermute | solution.py:111
  52.9 2.1 %collective-permute-start.15 = (f32[64,256]{1,0:T(8,128)S(1)}, f32[64,256]{1,0:T(8,128)S(1)}, u32[]{:S(2)}, u32[]{:S(2)}) collective-permute-start(f32[64,256]{1,0:T(8,128)S(1)} %fusion.77), channel_id=1, source_target_pairs={{0,1},{1,0},{2,3},{3,2},{4,5},{5,4},{6,7},{7,6},{8,9},{9,8},{10,11... | collective-permute-start | bytes 196616 | tf_op jit(solution)/shard_map/ppermute | solution.py:135
  53.3 23.4 %collective-permute-start.13 = (bf16[128,2560]{1,0:T(8,128)(2,1)S(1)}, bf16[128,2560]{1,0:T(8,128)(2,1)S(1)}, u32[]{:S(2)}, u32[]{:S(2)}) collective-permute-start(bf16[128,2560]{1,0:T(8,128)(2,1)S(1)} %convolution_convert_fusion.1), channel_id=1, source_target_pairs={{0,2},{2,0},{4,6},{6,4},{8,10},{10,8},{12,14},{14,12},{1,3},{3,1},... | collective-permute-start | bytes 1966088 | tf_op jit(solution)/shard_map/ppermute | solution.py:111
  55.6 17.3 %collective-permute-start.17 = (bf16[64,2560]{1,0:T(8,128)(2,1)S(1)}, bf16[64,2560]{1,0:T(8,128)(2,1)S(1)}, u32[]{:S(2)}, u32[]{:S(2)}) collective-permute-start(bf16[64,2560]{1,0:T(8,128)(2,1)S(1)} %fusion.44), channel_id=1, source_target_pairs={{0,4},{2,6},{4,0},{6,2},{8,12},{10,14},{12,8},{14,10},{1,5},{3,7},... | collective-permute-start | bytes 983048 | tf_op jit(solution)/shard_map/ppermute | solution.py:111
  59.5 25.0 %collective-permute-start.16 = (bf16[128,2560]{1,0:T(8,128)(2,1)S(1)}, bf16[128,2560]{1,0:T(8,128)(2,1)S(1)}, u32[]{:S(2)}, u32[]{:S(2)}) collective-permute-start(bf16[128,2560]{1,0:T(8,128)(2,1)S(1)} %convolution_convert_fusion), channel_id=1, source_target_pairs={{0,2},{2,0},{4,6},{6,4},{8,10},{10,8},{12,14},{14,12},{1,3},{3,1},... | collective-permute-start | bytes 1966088 | tf_op jit(solution)/shard_map/ppermute | solution.py:111
  73.0 17.4 %collective-permute-start.18 = (bf16[64,2560]{1,0:T(8,128)(2,1)S(1)}, bf16[64,2560]{1,0:T(8,128)(2,1)S(1)}, u32[]{:S(2)}, u32[]{:S(2)}) collective-permute-start(bf16[64,2560]{1,0:T(8,128)(2,1)S(1)} %add_convert_fusion.1), channel_id=1, source_target_pairs={{0,8},{2,10},{4,12},{6,14},{8,0},{10,2},{12,4},{14,6},{1,9},{3,11}... | collective-permute-start | bytes 983048 | tf_op jit(solution)/shard_map/ppermute | solution.py:111
  73.4 17.1 %collective-permute-start.20 = (bf16[64,2560]{1,0:T(8,128)(2,1)S(1)}, bf16[64,2560]{1,0:T(8,128)(2,1)S(1)}, u32[]{:S(2)}, u32[]{:S(2)}) collective-permute-start(bf16[64,2560]{1,0:T(8,128)(2,1)S(1)} %fusion.79), channel_id=1, source_target_pairs={{0,4},{2,6},{4,0},{6,2},{8,12},{10,14},{12,8},{14,10},{1,5},{3,7},... | collective-permute-start | bytes 983048 | tf_op jit(solution)/shard_map/ppermute | solution.py:111
  (3 other events, 12.6 us)

commit v15 on v14

--- a/solution.py
+++ b/solution.py
@@ -150,7 +150,7 @@
         (move(gating, xor_line(1)), down_matrix, up_matrix)
     )
     near_down, up_last = lax.optimization_barrier((move(down_later, xor_line(1)), up_matrix))
-    near_up = move(up_last, xor_line(1))
+    far_up = lax.ppermute(up_last, ("groups", "adapter"), FAR)
     cot2 = move(cotangent, PARTNER)
     gates = jnp.concatenate([gating, near_gate])
     gates = jnp.concatenate([gates, move(gates, xor_line(2))])
@@ -165,7 +165,8 @@
     taken = lists[:, :, None] == ids[None, None, :]
     scale = jnp.sum(jnp.where(taken, gate_rows[:, :, None], 0.0), axis=1)
 
-    far_up = lax.ppermute(up_later, ("groups", "adapter"), FAR)
+    up_later, scale = lax.optimization_barrier((up_later, scale))
+    near_up = move(up_later, xor_line(1))
     ready, scale = lax.optimization_barrier((far_down, scale))
     cross_down = lax.ppermute(ready, "groups", SWAP)
     tokens2 = jnp.concatenate([tokens, tokens2], axis=0)

time: 91.7 us -> 93.1 us (1.015)
  waiting for transfers between devices: 49.3 us -> 58.7 us
  starting transfers between devices: 23.4 us -> 15.4 us
    ppermute x1, waiting for transfers between devices: 0.01 us -> 8.24 us  [by_pairs(): far_up = lax.ppermute(up_last, ('groups', 'adapter'), FAR)]
    ppermute x14, starting transfers between devices: 14.6 us -> 10.7 us  [move(): return lax.ppermute(value, 'adapter', pairs)]
    ppermute x1, starting transfers between devices: 4.26 us -> 1.63 us  [by_pairs(): cross_down = lax.ppermute(ready, 'groups', SWAP)]
    ppermute x1, waiting for transfers between devices: 0.01 us -> 2.49 us  [by_pairs(): cross_up = lax.ppermute(far_up, 'groups', SWAP)]
    ppermute x1, waiting for transfers between devices: 1.86 us -> 0.01 us  [by_pairs(): cross_down = lax.ppermute(ready, 'groups', SWAP)]
    ppermute x1, starting transfers between devices: 1.64 us -> 0.01 us  [by_pairs(): cross_up = lax.ppermute(far_up, 'groups', SWAP)]
  transfers between devices with their start and end apart: 22 -> 22, of which waited for: 13 -> 11; matrix products, arithmetic and copies ran while one was open for 18% -> 18% of each run, Pallas kernels for 0% -> 0%
where the time goes in v15:
time: 93.1 us; the launch traced here: 92.8 us
  waiting for transfers between devices  58.7 us (63%)
  starting transfers between devices  15.4 us (17%)
  matrix products  11.1 us (12%)
  local copies, waits for them, and re-layouts  4.09 us (4%)
  other arithmetic  2.54 us (3%)
  between operations  0.98 us (1%)
    ppermute x14, waiting for transfers between devices, move(): return lax.ppermute(value, 'adapter', pairs)  44.1 us
    ppermute x14, starting transfers between devices, move(): return lax.ppermute(value, 'adapter', pairs)  10.7 us
    ppermute x1, waiting for transfers between devices, by_pairs(): far_up = lax.ppermute(up_last, ('groups', 'adapter'), FAR)  8.24 us
    dot_general x4, matrix products, contract_first(): lax.dot_general(left_op, right_op, (((0,), (0,)), ((), ())), preferred_el...  5.06 us
    ppermute x4, waiting for transfers between devices, both_cores(): return partial + lax.ppermute(partial, 'tensor', SWAP)  3.84 us
    dot_general x4, matrix products, contract_last(): lax.dot_general(left_op, right_op, (((1,), (1,)), ((), ())), preferred_el...  3.18 us
    dot_general x8, matrix products, partial_sums(): jnp.dot(weight, rows, preferred_element_type=jnp.float32)  2.84 us
    ppermute x1, starting transfers between devices, by_pairs(): far_down = lax.ppermute(down_matrix, ('groups', 'adapter'), FAR)  2.59 us
  transfers between devices with their start and end apart: 22, of which 11 were waited for; matrix products, arithmetic and copies ran while one was open for 18% of the time, Pallas kernels for 0%

profile of v15, /device:TPU:0, one launch (start us, length us, event | category | flops | bytes accessed | tf_op | source)
XLA Modules:
  0.0 92.8 jit_solution(3005113488706736027)
XLA Ops:
  0.7 3.1 %collective-permute-start.2 = (f32[1,256]{1,0:T(1,128)}, f32[1,256]{1,0:T(1,128)S(1)}, u32[]{:S(2)}, u32[]{:S(2)}) collective-permute-start(f32[1,256]{1,0:T(1,128)} %param.11), channel_id=1, source_target_pairs={{0,4},{2,6},{4,0},{6,2},{8,12},{10,14},{12,8},{14,10},{1,5},{3,7},... | collective-permute-start | bytes 3080 | tf_op jit(solution)/shard_map/ppermute | solution.py:111
  3.7 2.6 %collective-permute-start.1 = (bf16[64,2560]{1,0:T(8,128)(2,1)}, bf16[64,2560]{1,0:T(8,128)(2,1)}, u32[]{:S(2)}, u32[]{:S(2)}) collective-permute-start(bf16[64,2560]{1,0:T(8,128)(2,1)} %bitcast.51), channel_id=1, source_target_pairs={{0,8},{2,10},{4,12},{6,14},{8,0},{10,2},{12,4},{14,6},{16,28},{18,... | collective-permute-start | bytes 983048 | tf_op jit(solution)/shard_map/ppermute | solution.py:147
  6.3 1.5 %collective-permute-start.5 = (bf16[128,2560]{1,0:T(8,128)(2,1)}, bf16[128,2560]{1,0:T(8,128)(2,1)}, u32[]{:S(2)}, u32[]{:S(2)}) collective-permute-start(bf16[128,2560]{1,0:T(8,128)(2,1)} %param.6), channel_id=1, source_target_pairs={{0,2},{2,0},{4,6},{6,4},{8,10},{10,8},{12,14},{14,12},{1,3},{3,1},... | collective-permute-start | bytes 1966088 | tf_op jit(solution)/shard_map/ppermute | solution.py:111
  8.4 1.1 %constant_dynamic-update-slice_fusion.1 = bf16[256,2560]{1,0:T(8,128)(2,1)S(1)} fusion(bf16[128,2560]{1,0:T(8,128)(2,1)} %param.6), kind=kLoop, calls=%fused_computation.77 | loop fusion | bytes 1310720
  11.1 10.1 %collective-permute-done.3 = f32[2,256]{1,0:T(2,128)S(1)} collective-permute-done((f32[2,256]{1,0:T(2,128)S(1)}, f32[2,256]{1,0:T(2,128)S(1)}, u32[]{:S(2)}, u32[]{:S(2)}) %collective-permute-start.3) | collective-permute-done | bytes 2080 | tf_op jit(solution)/shard_map/ppermute | solution.py:111
  21.6 1.6 %collective-permute-start.7 = (bf16[64,2560]{1,0:T(8,128)(2,1)}, bf16[64,2560]{1,0:T(8,128)(2,1)S(1)}, u32[]{:S(2)}, u32[]{:S(2)}) collective-permute-start(bf16[64,2560]{1,0:T(8,128)(2,1)} %collective-permute-done.1), channel_id=1, source_target_pairs={{0,16},{16,0},{1,17},{17,1},{2,18},{18,2},{3,19},{19,3},{4,20},{20... | collective-permute-start | bytes 983048 | tf_op jit(solution)/shard_map/ppermute | solution.py:171
  23.2 4.6 %collective-permute-done.4 = bf16[64,2560]{1,0:T(8,128)(2,1)S(1)} collective-permute-done((bf16[64,2560]{1,0:T(8,128)(2,1)}, bf16[64,2560]{1,0:T(8,128)(2,1)S(1)}, u32[]{:S(2)}, u32[]{:S(2)}) %collective-permute-start.4) | collective-permute-done | bytes 327712 | tf_op jit(solution)/shard_map/ppermute | solution.py:111
  27.8 1.1 %constant_dynamic-update-slice_fusion = bf16[256,2560]{1,0:T(8,128)(2,1)S(1)} fusion(bf16[256,2560]{1,0:T(8,128)(2,1)S(1)} %constant_dynamic-update-slice_fusion.1, bf16[128,2560]{1,0:T(8,128)(2,1)} %collective-permute-done.5), kind=kLoop, calls=%fused_computation.76 | loop fusion | bytes 1310720 | tf_op jit(solution)/shard_map/concatenate | solution.py:172
  29.0 1.6 %fusion.2 = f32[192,256]{1,0:T(8,128)S(1)} fusion(bf16[256,2560]{1,0:T(8,128)(2,1)S(1)} %constant_dynamic-update-slice_fusion, bf16[64,2560]{1,0:T(8,128)(2,1)} %collective-permute-done.1, bf16[64,2560]{1,0:T(8,128)(2,1)S(1)} %collective-permute-done.4, bf16[64,2560]{1,0:T(8,128)(2,1)S(1)} %bitcast.53), kind=kOutput, calls=%fused_computation.10 | convolution fusion | flops 254607360 | bytes 2490368 | tf_op jit(solution)/shard_map/dot_general | solution.py:10
  30.8 1.3 %collective-permute-done.6 = f32[192,256]{1,0:T(8,128)S(1)} collective-permute-done((f32[192,256]{1,0:T(8,128)S(1)}, f32[192,256]{1,0:T(8,128)S(1)}, u32[]{:S(2)}, u32[]{:S(2)}) %collective-permute-start.6) | collective-permute-done | bytes 196640 | tf_op jit(solution)/shard_map/ppermute | solution.py:135
  32.9 1.1 %collective-permute-done.8 = f32[64,256]{1,0:T(8,128)S(1)} collective-permute-done((f32[64,256]{1,0:T(8,128)S(1)}, f32[64,256]{1,0:T(8,128)S(1)}, u32[]{:S(2)}, u32[]{:S(2)}) %collective-permute-start.8) | collective-permute-done | bytes 65568 | tf_op jit(solution)/shard_map/ppermute | solution.py:135
  34.0 2.6 %collective-permute-done = bf16[128,2560]{1,0:T(8,128)(2,1)} collective-permute-done((bf16[128,2560]{1,0:T(8,128)(2,1)}, bf16[128,2560]{1,0:T(8,128)(2,1)}, u32[]{:S(2)}, u32[]{:S(2)}) %collective-permute-start) | collective-permute-done | bytes 655392 | tf_op jit(solution)/shard_map/ppermute | solution.py:111
  36.6 1.1 %constant_dynamic-update-slice_fusion.2 = bf16[256,2560]{1,0:T(8,128)(2,1)S(1)} fusion(bf16[256,2560]{1,0:T(8,128)(2,1)S(1)} %constant_dynamic-update-slice_fusion.3, bf16[128,2560]{1,0:T(8,128)(2,1)} %collective-permute-done), kind=kLoop, calls=%fused_computation.78 | loop fusion | bytes 1310720 | tf_op jit(solution)/shard_map/concatenate | solution.py:200
  39.7 8.2 %collective-permute-done.10 = bf16[64,2560]{1,0:T(8,128)(2,1)S(1)} collective-permute-done((bf16[64,2560]{1,0:T(8,128)(2,1)S(1)}, bf16[64,2560]{1,0:T(8,128)(2,1)S(1)}, u32[]{:S(2)}, u32[]{:S(2)}) %collective-permute-start.10) | collective-permute-done | bytes 327712 | tf_op jit(solution)/shard_map/ppermute | solution.py:153
  48.6 1.4 %collective-permute-done.14 = f32[192,256]{1,0:T(8,128)S(1)} collective-permute-done((f32[192,256]{1,0:T(8,128)S(1)}, f32[192,256]{1,0:T(8,128)S(1)}, u32[]{:S(2)}, u32[]{:S(2)}) %collective-permute-start.14) | collective-permute-done | bytes 196640 | tf_op jit(solution)/shard_map/ppermute | solution.py:135
  50.9 4.0 %collective-permute-done.12 = bf16[64,2560]{1,0:T(8,128)(2,1)S(1)} collective-permute-done((bf16[64,2560]{1,0:T(8,128)(2,1)S(1)}, bf16[64,2560]{1,0:T(8,128)(2,1)S(1)}, u32[]{:S(2)}, u32[]{:S(2)}) %collective-permute-start.12) | collective-permute-done | bytes 327712 | tf_op jit(solution)/shard_map/ppermute | solution.py:111
  55.1 2.5 %collective-permute-done.11 = bf16[64,2560]{1,0:T(8,128)(2,1)S(1)} collective-permute-done((bf16[64,2560]{1,0:T(8,128)(2,1)S(1)}, bf16[64,2560]{1,0:T(8,128)(2,1)S(1)}, u32[]{:S(2)}, u32[]{:S(2)}) %collective-permute-start.11) | collective-permute-done | bytes 327712 | tf_op jit(solution)/shard_map/ppermute | solution.py:204
  58.5 1.5 %collective-permute-start.13 = (bf16[128,2560]{1,0:T(8,128)(2,1)S(1)}, bf16[128,2560]{1,0:T(8,128)(2,1)S(1)}, u32[]{:S(2)}, u32[]{:S(2)}) collective-permute-start(bf16[128,2560]{1,0:T(8,128)(2,1)S(1)} %convolution_convert_fusion.1), channel_id=1, source_target_pairs={{0,2},{2,0},{4,6},{6,4},{8,10},{10,8},{12,14},{14,12},{1,3},{3,1},... | collective-permute-start | bytes 1966088 | tf_op jit(solution)/shard_map/ppermute | solution.py:111
  60.9 1.3 %convolution_convert_fusion = bf16[128,2560]{1,0:T(8,128)(2,1)S(1)} fusion(bf16[64,2560]{1,0:T(8,128)(2,1)S(1)} %collective-permute-done.7, bf16[64,2560]{1,0:T(8,128)(2,1)} %collective-permute-done.1, bf16[64,2560]{1,0:T(8,128)(2,1)S(1)} %collective-permute-done.4, bf16[64,2560]{1,0:T(8,128)(2,1)S(1)} %bitcast.54, ...), kind=kOutput, calls=%fused_computation.5 | convolution fusion | flops 173604864 | bytes 2031616 | tf_op jit(solution)/shard_map/dot_general | solution.py:16
  63.1 12.1 %collective-permute-done.17 = bf16[64,2560]{1,0:T(8,128)(2,1)S(1)} collective-permute-done((bf16[64,2560]{1,0:T(8,128)(2,1)S(1)}, bf16[64,2560]{1,0:T(8,128)(2,1)S(1)}, u32[]{:S(2)}, u32[]{:S(2)}) %collective-permute-start.17) | collective-permute-done | bytes 327712 | tf_op jit(solution)/shard_map/ppermute | solution.py:111
  75.4 1.7 %collective-permute-start.20 = (bf16[64,2560]{1,0:T(8,128)(2,1)S(1)}, bf16[64,2560]{1,0:T(8,128)(2,1)S(1)}, u32[]{:S(2)}, u32[]{:S(2)}) collective-permute-start(bf16[64,2560]{1,0:T(8,128)(2,1)S(1)} %fusion.79), channel_id=1, source_target_pairs={{0,4},{2,6},{4,0},{6,2},{8,12},{10,14},{12,8},{14,10},{1,5},{3,7},... | collective-permute-start | bytes 983048 | tf_op jit(solution)/shard_map/ppermute | solution.py:111
  78.0 1.2 %fusion = bf16[128,2560]{1,0:T(8,128)(2,1)} fusion(bf16[128,2560]{1,0:T(8,128)(2,1)S(1)} %collective-permute-done.13, bf16[64,2560]{1,0:T(8,128)(2,1)S(1)} %collective-permute-done.11, bf16[64,2560]{1,0:T(8,128)(2,1)S(1)} %collective-permute-done.10, bf16[64,2560]{1,0:T(8,128)(2,1)S(1)} %collective-permute-done.9, bf16[64,2560]{1,0:T(8,128)(2,1)S(1)} %bitcast.50, ...), kind=kOutput, calls=%fused_computation.3 | convolution fusion | flops 174260224 | bytes 2686976 | tf_op jit(solution)/shard_map/dot_general | solution.py:16
  79.2 10.6 %collective-permute-done.16 = bf16[128,2560]{1,0:T(8,128)(2,1)S(1)} collective-permute-done((bf16[128,2560]{1,0:T(8,128)(2,1)S(1)}, bf16[128,2560]{1,0:T(8,128)(2,1)S(1)}, u32[]{:S(2)}, u32[]{:S(2)}) %collective-permute-start.16) | collective-permute-done | bytes 655392 | tf_op jit(solution)/shard_map/ppermute | solution.py:111
  89.8 2.2 %fusion.1 = bf16[128,2560]{1,0:T(8,128)(2,1)} fusion(bf16[128,2560]{1,0:T(8,128)(2,1)S(1)} %collective-permute-done.16, bf16[64,2560]{1,0:T(8,128)(2,1)S(1)} %collective-permute-done.7, bf16[64,2560]{1,0:T(8,128)(2,1)} %collective-permute-done.1, bf16[64,2560]{1,0:T(8,128)(2,1)S(1)} %collective-permute-done.4, bf16[64,2560]{1,0:T(8,128)(2,1)S(1)} %bitcast.55, ...), kind=kOutput, calls=%fused_computation.4 | convolution fusion | flops 174260224 | bytes 2686976 | tf_op jit(solution)/shard_map/dot_general | solution.py:16
  (80 shorter events, 11.5 us)
Async XLA Ops:
  0.6 9.1 %copy-start = (s32[8,256]{1,0:T(8,128)S(1)}, s32[8,256]{1,0:T(8,128)}, u32[]{:S(2)}) copy-start(s32[8,256]{1,0:T(8,128)} %param.10) | copy-start | bytes 24580
  0.7 9.8 %collective-permute-start.2 = (f32[1,256]{1,0:T(1,128)}, f32[1,256]{1,0:T(1,128)S(1)}, u32[]{:S(2)}, u32[]{:S(2)}) collective-permute-start(f32[1,256]{1,0:T(1,128)} %param.11), channel_id=1, source_target_pairs={{0,4},{2,6},{4,0},{6,2},{8,12},{10,14},{12,8},{14,10},{1,5},{3,7},... | collective-permute-start | bytes 3080 | tf_op jit(solution)/shard_map/ppermute | solution.py:111
  3.7 17.8 %collective-permute-start.1 = (bf16[64,2560]{1,0:T(8,128)(2,1)}, bf16[64,2560]{1,0:T(8,128)(2,1)}, u32[]{:S(2)}, u32[]{:S(2)}) collective-permute-start(bf16[64,2560]{1,0:T(8,128)(2,1)} %bitcast.51), channel_id=1, source_target_pairs={{0,8},{2,10},{4,12},{6,14},{8,0},{10,2},{12,4},{14,6},{16,28},{18,... | collective-permute-start | bytes 983048 | tf_op jit(solution)/shard_map/ppermute | solution.py:147
  6.3 21.5 %collective-permute-start.5 = (bf16[128,2560]{1,0:T(8,128)(2,1)}, bf16[128,2560]{1,0:T(8,128)(2,1)}, u32[]{:S(2)}, u32[]{:S(2)}) collective-permute-start(bf16[128,2560]{1,0:T(8,128)(2,1)} %param.6), channel_id=1, source_target_pairs={{0,2},{2,0},{4,6},{6,4},{8,10},{10,8},{12,14},{14,12},{1,3},{3,1},... | collective-permute-start | bytes 1966088 | tf_op jit(solution)/shard_map/ppermute | solution.py:111
  7.8 28.8 %collective-permute-start = (bf16[128,2560]{1,0:T(8,128)(2,1)}, bf16[128,2560]{1,0:T(8,128)(2,1)}, u32[]{:S(2)}, u32[]{:S(2)}) collective-permute-start(bf16[128,2560]{1,0:T(8,128)(2,1)} %param.7), channel_id=1, source_target_pairs={{0,2},{2,0},{4,6},{6,4},{8,10},{10,8},{12,14},{14,12},{1,3},{3,1},... | collective-permute-start | bytes 1966088 | tf_op jit(solution)/shard_map/ppermute | solution.py:111
  9.6 19.4 %copy-start.4 = (bf16[1,64,2560]{2,1,0:T(8,128)(2,1)S(1)}, bf16[1,64,2560]{2,1,0:T(8,128)(2,1)}, u32[]{:S(2)}) copy-start(bf16[1,64,2560]{2,1,0:T(8,128)(2,1)} %param.8) | copy-start | bytes 983044
  10.4 10.7 %collective-permute-start.3 = (f32[2,256]{1,0:T(2,128)S(1)}, f32[2,256]{1,0:T(2,128)S(1)}, u32[]{:S(2)}, u32[]{:S(2)}) collective-permute-start(f32[2,256]{1,0:T(2,128)S(1)} %pad_maximum_fusion.7), channel_id=1, source_target_pairs={{0,8},{2,10},{4,12},{6,14},{8,0},{10,2},{12,4},{14,6},{1,9},{3,11}... | collective-permute-start | bytes 6152 | tf_op jit(solution)/shard_map/ppermute | solution.py:111
  10.9 17.0 %collective-permute-start.4 = (bf16[64,2560]{1,0:T(8,128)(2,1)}, bf16[64,2560]{1,0:T(8,128)(2,1)S(1)}, u32[]{:S(2)}, u32[]{:S(2)}) collective-permute-start(bf16[64,2560]{1,0:T(8,128)(2,1)} %bitcast.52), channel_id=1, source_target_pairs={{0,4},{2,6},{4,0},{6,2},{8,12},{10,14},{12,8},{14,10},{1,5},{3,7},... | collective-permute-start | bytes 983048 | tf_op jit(solution)/shard_map/ppermute | solution.py:111
  21.5 26.4 %collective-permute-start.9 = (bf16[64,2560]{1,0:T(8,128)(2,1)}, bf16[64,2560]{1,0:T(8,128)(2,1)S(1)}, u32[]{:S(2)}, u32[]{:S(2)}) collective-permute-start(bf16[64,2560]{1,0:T(8,128)(2,1)} %bitcast.46), channel_id=1, source_target_pairs={{0,4},{2,6},{4,0},{6,2},{8,12},{10,14},{12,8},{14,10},{1,5},{3,7},... | collective-permute-start | bytes 983048 | tf_op jit(solution)/shard_map/ppermute | solution.py:111
  21.6 10.5 %collective-permute-start.7 = (bf16[64,2560]{1,0:T(8,128)(2,1)}, bf16[64,2560]{1,0:T(8,128)(2,1)S(1)}, u32[]{:S(2)}, u32[]{:S(2)}) collective-permute-start(bf16[64,2560]{1,0:T(8,128)(2,1)} %collective-permute-done.1), channel_id=1, source_target_pairs={{0,16},{16,0},{1,17},{17,1},{2,18},{18,2},{3,19},{19,3},{4,20},{20... | collective-permute-start | bytes 983048 | tf_op jit(solution)/shard_map/ppermute | solution.py:171
  30.6 1.5 %collective-permute-start.6 = (f32[192,256]{1,0:T(8,128)S(1)}, f32[192,256]{1,0:T(8,128)S(1)}, u32[]{:S(2)}, u32[]{:S(2)}) collective-permute-start(f32[192,256]{1,0:T(8,128)S(1)} %fusion.2), channel_id=1, source_target_pairs={{0,1},{1,0},{2,3},{3,2},{4,5},{5,4},{6,7},{7,6},{8,9},{9,8},{10,11... | collective-permute-start | bytes 589832 | tf_op jit(solution)/shard_map/ppermute | solution.py:135
  30.7 17.3 %collective-permute-start.10 = (bf16[64,2560]{1,0:T(8,128)(2,1)S(1)}, bf16[64,2560]{1,0:T(8,128)(2,1)S(1)}, u32[]{:S(2)}, u32[]{:S(2)}) collective-permute-start(bf16[64,2560]{1,0:T(8,128)(2,1)S(1)} %bitcast.47), channel_id=1, source_target_pairs={{0,8},{2,10},{4,12},{6,14},{8,0},{10,2},{12,4},{14,6},{16,28},{18,... | collective-permute-start | bytes 983048 | tf_op jit(solution)/shard_map/ppermute | solution.py:153
  32.6 1.3 %collective-permute-start.8 = (f32[64,256]{1,0:T(8,128)S(1)}, f32[64,256]{1,0:T(8,128)S(1)}, u32[]{:S(2)}, u32[]{:S(2)}) collective-permute-start(f32[64,256]{1,0:T(8,128)S(1)} %fusion.74), channel_id=1, source_target_pairs={{0,1},{1,0},{2,3},{3,2},{4,5},{5,4},{6,7},{7,6},{8,9},{9,8},{10,11... | collective-permute-start | bytes 196616 | tf_op jit(solution)/shard_map/ppermute | solution.py:135
  39.2 15.8 %collective-permute-start.12 = (bf16[64,2560]{1,0:T(8,128)(2,1)S(1)}, bf16[64,2560]{1,0:T(8,128)(2,1)S(1)}, u32[]{:S(2)}, u32[]{:S(2)}) collective-permute-start(bf16[64,2560]{1,0:T(8,128)(2,1)S(1)} %fusion.48), channel_id=1, source_target_pairs={{0,4},{2,6},{4,0},{6,2},{8,12},{10,14},{12,8},{14,10},{1,5},{3,7},... | collective-permute-start | bytes 983048 | tf_op jit(solution)/shard_map/ppermute | solution.py:111
  47.9 9.6 %collective-permute-start.11 = (bf16[64,2560]{1,0:T(8,128)(2,1)S(1)}, bf16[64,2560]{1,0:T(8,128)(2,1)S(1)}, u32[]{:S(2)}, u32[]{:S(2)}) collective-permute-start(bf16[64,2560]{1,0:T(8,128)(2,1)S(1)} %collective-permute-done.10), channel_id=1, source_target_pairs={{0,16},{16,0},{1,17},{17,1},{2,18},{18,2},{3,19},{19,3},{4,20},{20... | collective-permute-start | bytes 983048 | tf_op jit(solution)/shard_map/ppermute | solution.py:204
  48.5 1.5 %collective-permute-start.14 = (f32[192,256]{1,0:T(8,128)S(1)}, f32[192,256]{1,0:T(8,128)S(1)}, u32[]{:S(2)}, u32[]{:S(2)}) collective-permute-start(f32[192,256]{1,0:T(8,128)S(1)} %fusion.8), channel_id=1, source_target_pairs={{0,1},{1,0},{2,3},{3,2},{4,5},{5,4},{6,7},{7,6},{8,9},{9,8},{10,11... | collective-permute-start | bytes 589832 | tf_op jit(solution)/shard_map/ppermute | solution.py:135
  50.5 25.0 %collective-permute-start.19 = (bf16[64,2560]{1,0:T(8,128)(2,1)S(1)}, bf16[64,2560]{1,0:T(8,128)(2,1)S(1)}, u32[]{:S(2)}, u32[]{:S(2)}) collective-permute-start(bf16[64,2560]{1,0:T(8,128)(2,1)S(1)} %fusion.76), channel_id=1, source_target_pairs={{0,4},{2,6},{4,0},{6,2},{8,12},{10,14},{12,8},{14,10},{1,5},{3,7},... | collective-permute-start | bytes 983048 | tf_op jit(solution)/shard_map/ppermute | solution.py:111
  55.0 20.4 %collective-permute-start.21 = (bf16[64,2560]{1,0:T(8,128)(2,1)S(1)}, bf16[64,2560]{1,0:T(8,128)(2,1)S(1)}, u32[]{:S(2)}, u32[]{:S(2)}) collective-permute-start(bf16[64,2560]{1,0:T(8,128)(2,1)S(1)} %add_convert_fusion), channel_id=1, source_target_pairs={{0,8},{2,10},{4,12},{6,14},{8,0},{10,2},{12,4},{14,6},{1,9},{3,11}... | collective-permute-start | bytes 983048 | tf_op jit(solution)/shard_map/ppermute | solution.py:111
  58.1 2.0 %collective-permute-start.15 = (f32[64,256]{1,0:T(8,128)S(1)}, f32[64,256]{1,0:T(8,128)S(1)}, u32[]{:S(2)}, u32[]{:S(2)}) collective-permute-start(f32[64,256]{1,0:T(8,128)S(1)} %fusion.77), channel_id=1, source_target_pairs={{0,1},{1,0},{2,3},{3,2},{4,5},{5,4},{6,7},{7,6},{8,9},{9,8},{10,11... | collective-permute-start | bytes 196616 | tf_op jit(solution)/shard_map/ppermute | solution.py:135
  58.5 19.4 %collective-permute-start.13 = (bf16[128,2560]{1,0:T(8,128)(2,1)S(1)}, bf16[128,2560]{1,0:T(8,128)(2,1)S(1)}, u32[]{:S(2)}, u32[]{:S(2)}) collective-permute-start(bf16[128,2560]{1,0:T(8,128)(2,1)S(1)} %convolution_convert_fusion.1), channel_id=1, source_target_pairs={{0,2},{2,0},{4,6},{6,4},{8,10},{10,8},{12,14},{14,12},{1,3},{3,1},... | collective-permute-start | bytes 1966088 | tf_op jit(solution)/shard_map/ppermute | solution.py:111
  60.8 14.4 %collective-permute-start.17 = (bf16[64,2560]{1,0:T(8,128)(2,1)S(1)}, bf16[64,2560]{1,0:T(8,128)(2,1)S(1)}, u32[]{:S(2)}, u32[]{:S(2)}) collective-permute-start(bf16[64,2560]{1,0:T(8,128)(2,1)S(1)} %fusion.44), channel_id=1, source_target_pairs={{0,4},{2,6},{4,0},{6,2},{8,12},{10,14},{12,8},{14,10},{1,5},{3,7},... | collective-permute-start | bytes 983048 | tf_op jit(solution)/shard_map/ppermute | solution.py:111
  62.2 27.6 %collective-permute-start.16 = (bf16[128,2560]{1,0:T(8,128)(2,1)S(1)}, bf16[128,2560]{1,0:T(8,128)(2,1)S(1)}, u32[]{:S(2)}, u32[]{:S(2)}) collective-permute-start(bf16[128,2560]{1,0:T(8,128)(2,1)S(1)} %convolution_convert_fusion), channel_id=1, source_target_pairs={{0,2},{2,0},{4,6},{6,4},{8,10},{10,8},{12,14},{14,12},{1,3},{3,1},... | collective-permute-start | bytes 1966088 | tf_op jit(solution)/shard_map/ppermute | solution.py:111
  75.3 16.7 %collective-permute-start.18 = (bf16[64,2560]{1,0:T(8,128)(2,1)S(1)}, bf16[64,2560]{1,0:T(8,128)(2,1)S(1)}, u32[]{:S(2)}, u32[]{:S(2)}) collective-permute-start(bf16[64,2560]{1,0:T(8,128)(2,1)S(1)} %add_convert_fusion.1), channel_id=1, source_target_pairs={{0,8},{2,10},{4,12},{6,14},{8,0},{10,2},{12,4},{14,6},{1,9},{3,11}... | collective-permute-start | bytes 983048 | tf_op jit(solution)/shard_map/ppermute | solution.py:111
  75.4 16.5 %collective-permute-start.20 = (bf16[64,2560]{1,0:T(8,128)(2,1)S(1)}, bf16[64,2560]{1,0:T(8,128)(2,1)S(1)}, u32[]{:S(2)}, u32[]{:S(2)}) collective-permute-start(bf16[64,2560]{1,0:T(8,128)(2,1)S(1)} %fusion.79), channel_id=1, source_target_pairs={{0,4},{2,6},{4,0},{6,2},{8,12},{10,14},{12,8},{14,10},{1,5},{3,7},... | collective-permute-start | bytes 983048 | tf_op jit(solution)/shard_map/ppermute | solution.py:111
  (3 other events, 12.6 us)

commit v16 on v14

--- a/solution.py
+++ b/solution.py
@@ -149,8 +149,7 @@
     near_gate, down_later, up_later = lax.optimization_barrier(
         (move(gating, xor_line(1)), down_matrix, up_matrix)
     )
-    near_down, up_last = lax.optimization_barrier((move(down_later, xor_line(1)), up_matrix))
-    near_up = move(up_last, xor_line(1))
+    near_down = move(down_later, xor_line(1))
     cot2 = move(cotangent, PARTNER)
     gates = jnp.concatenate([gating, near_gate])
     gates = jnp.concatenate([gates, move(gates, xor_line(2))])
@@ -166,6 +165,8 @@
     scale = jnp.sum(jnp.where(taken, gate_rows[:, :, None], 0.0), axis=1)
 
     far_up = lax.ppermute(up_later, ("groups", "adapter"), FAR)
+    up_last, scale = lax.optimization_barrier((up_matrix, scale))
+    near_up = move(up_last, xor_line(1))
     ready, scale = lax.optimization_barrier((far_down, scale))
     cross_down = lax.ppermute(ready, "groups", SWAP)
     tokens2 = jnp.concatenate([tokens, tokens2], axis=0)

time: 91.7 us -> 86.8 us (0.947)
  waiting for transfers between devices: 49.3 us -> 42.9 us
  starting transfers between devices: 23.4 us -> 25 us
    ppermute x14, waiting for transfers between devices: 43.5 us -> 36.7 us  [move(): return lax.ppermute(value, 'adapter', pairs)]
    ppermute x14, starting transfers between devices: 14.6 us -> 19.4 us  [move(): return lax.ppermute(value, 'adapter', pairs)]
    ppermute x1, starting transfers between devices: 4.26 us -> 1.07 us  [by_pairs(): cross_down = lax.ppermute(ready, 'groups', SWAP)]
  transfers between devices with their start and end apart: 22 -> 22, of which waited for: 13 -> 11; matrix products, arithmetic and copies ran while one was open for 18% -> 19% of each run, Pallas kernels for 0% -> 0%
where the time goes in v16:
time: 86.8 us; the launch traced here: 86.4 us
  waiting for transfers between devices  42.9 us (49%)
  starting transfers between devices  25 us (29%)
  matrix products  11 us (13%)
  local copies, waits for them, and re-layouts  4.08 us (5%)
  other arithmetic  2.54 us (3%)
  between operations  0.91 us (1%)
    ppermute x14, waiting for transfers between devices, move(): return lax.ppermute(value, 'adapter', pairs)  36.7 us
    ppermute x14, starting transfers between devices, move(): return lax.ppermute(value, 'adapter', pairs)  19.4 us
    dot_general x4, matrix products, contract_first(): lax.dot_general(left_op, right_op, (((0,), (0,)), ((), ())), preferred_el...  5.06 us
    ppermute x4, waiting for transfers between devices, both_cores(): return partial + lax.ppermute(partial, 'tensor', SWAP)  4.05 us
    dot_general x4, matrix products, contract_last(): lax.dot_general(left_op, right_op, (((1,), (1,)), ((), ())), preferred_el...  3.13 us
    dot_general x8, matrix products, partial_sums(): jnp.dot(weight, rows, preferred_element_type=jnp.float32)  2.83 us
    ppermute x1, starting transfers between devices, by_pairs(): far_down = lax.ppermute(down_matrix, ('groups', 'adapter'), FAR)  2.59 us
    ppermute x1, waiting for transfers between devices, by_pairs(): cross_down = lax.ppermute(ready, 'groups', SWAP)  2.14 us
  transfers between devices with their start and end apart: 22, of which 11 were waited for; matrix products, arithmetic and copies ran while one was open for 19% of the time, Pallas kernels for 0%

profile of v16, /device:TPU:0, one launch (start us, length us, event | category | flops | bytes accessed | tf_op | source)
XLA Modules:
  0.0 86.4 jit_solution(11404959223165984462)
XLA Ops:
  0.7 3.1 %collective-permute-start.2 = (f32[1,256]{1,0:T(1,128)}, f32[1,256]{1,0:T(1,128)S(1)}, u32[]{:S(2)}, u32[]{:S(2)}) collective-permute-start(f32[1,256]{1,0:T(1,128)} %param.11), channel_id=1, source_target_pairs={{0,4},{2,6},{4,0},{6,2},{8,12},{10,14},{12,8},{14,10},{1,5},{3,7},... | collective-permute-start | bytes 3080 | tf_op jit(solution)/shard_map/ppermute | solution.py:111
  3.7 2.6 %collective-permute-start.1 = (bf16[64,2560]{1,0:T(8,128)(2,1)}, bf16[64,2560]{1,0:T(8,128)(2,1)}, u32[]{:S(2)}, u32[]{:S(2)}) collective-permute-start(bf16[64,2560]{1,0:T(8,128)(2,1)} %bitcast.51), channel_id=1, source_target_pairs={{0,8},{2,10},{4,12},{6,14},{8,0},{10,2},{12,4},{14,6},{16,28},{18,... | collective-permute-start | bytes 983048 | tf_op jit(solution)/shard_map/ppermute | solution.py:147
  6.3 1.5 %collective-permute-start.5 = (bf16[128,2560]{1,0:T(8,128)(2,1)}, bf16[128,2560]{1,0:T(8,128)(2,1)}, u32[]{:S(2)}, u32[]{:S(2)}) collective-permute-start(bf16[128,2560]{1,0:T(8,128)(2,1)} %param.6), channel_id=1, source_target_pairs={{0,2},{2,0},{4,6},{6,4},{8,10},{10,8},{12,14},{14,12},{1,3},{3,1},... | collective-permute-start | bytes 1966088 | tf_op jit(solution)/shard_map/ppermute | solution.py:111
  11.1 10.1 %collective-permute-done.3 = f32[2,256]{1,0:T(2,128)S(1)} collective-permute-done((f32[2,256]{1,0:T(2,128)S(1)}, f32[2,256]{1,0:T(2,128)S(1)}, u32[]{:S(2)}, u32[]{:S(2)}) %collective-permute-start.3) | collective-permute-done | bytes 2080 | tf_op jit(solution)/shard_map/ppermute | solution.py:111
  21.5 3.3 %collective-permute-start.9 = (bf16[64,2560]{1,0:T(8,128)(2,1)}, bf16[64,2560]{1,0:T(8,128)(2,1)S(1)}, u32[]{:S(2)}, u32[]{:S(2)}) collective-permute-start(bf16[64,2560]{1,0:T(8,128)(2,1)} %bitcast.47), channel_id=1, source_target_pairs={{0,4},{2,6},{4,0},{6,2},{8,12},{10,14},{12,8},{14,10},{1,5},{3,7},... | collective-permute-start | bytes 983048 | tf_op jit(solution)/shard_map/ppermute | solution.py:111
  27.8 1.5 %fusion.2 = f32[192,256]{1,0:T(8,128)S(1)} fusion(bf16[256,2560]{1,0:T(8,128)(2,1)S(1)} %constant_dynamic-update-slice_fusion, bf16[64,2560]{1,0:T(8,128)(2,1)} %collective-permute-done.1, bf16[64,2560]{1,0:T(8,128)(2,1)S(1)} %collective-permute-done.4, bf16[64,2560]{1,0:T(8,128)(2,1)S(1)} %bitcast.53), kind=kOutput, calls=%fused_computation.10 | convolution fusion | flops 254607360 | bytes 2490368 | tf_op jit(solution)/shard_map/dot_general | solution.py:10
  29.4 1.4 %collective-permute-done.6 = f32[192,256]{1,0:T(8,128)S(1)} collective-permute-done((f32[192,256]{1,0:T(8,128)S(1)}, f32[192,256]{1,0:T(8,128)S(1)}, u32[]{:S(2)}, u32[]{:S(2)}) %collective-permute-start.6) | collective-permute-done | bytes 196640 | tf_op jit(solution)/shard_map/ppermute | solution.py:135
  30.9 2.1 %collective-permute-done.7 = bf16[64,2560]{1,0:T(8,128)(2,1)S(1)} collective-permute-done((bf16[64,2560]{1,0:T(8,128)(2,1)}, bf16[64,2560]{1,0:T(8,128)(2,1)S(1)}, u32[]{:S(2)}, u32[]{:S(2)}) %collective-permute-start.7) | collective-permute-done | bytes 327712 | tf_op jit(solution)/shard_map/ppermute | solution.py:171
  33.6 1.2 %collective-permute-done.8 = f32[64,256]{1,0:T(8,128)S(1)} collective-permute-done((f32[64,256]{1,0:T(8,128)S(1)}, f32[64,256]{1,0:T(8,128)S(1)}, u32[]{:S(2)}, u32[]{:S(2)}) %collective-permute-start.8) | collective-permute-done | bytes 65568 | tf_op jit(solution)/shard_map/ppermute | solution.py:135
  34.8 1.8 %collective-permute-done = bf16[128,2560]{1,0:T(8,128)(2,1)} collective-permute-done((bf16[128,2560]{1,0:T(8,128)(2,1)}, bf16[128,2560]{1,0:T(8,128)(2,1)}, u32[]{:S(2)}, u32[]{:S(2)}) %collective-permute-start) | collective-permute-done | bytes 655392 | tf_op jit(solution)/shard_map/ppermute | solution.py:111
  39.7 1.6 %collective-permute-start.11 = (bf16[64,2560]{1,0:T(8,128)(2,1)S(1)}, bf16[64,2560]{1,0:T(8,128)(2,1)S(1)}, u32[]{:S(2)}, u32[]{:S(2)}) collective-permute-start(bf16[64,2560]{1,0:T(8,128)(2,1)S(1)} %collective-permute-done.10), channel_id=1, source_target_pairs={{0,16},{16,0},{1,17},{17,1},{2,18},{18,2},{3,19},{19,3},{4,20},{20... | collective-permute-start | bytes 983048 | tf_op jit(solution)/shard_map/ppermute | solution.py:204
  42.0 1.4 %collective-permute-done.14 = f32[192,256]{1,0:T(8,128)S(1)} collective-permute-done((f32[192,256]{1,0:T(8,128)S(1)}, f32[192,256]{1,0:T(8,128)S(1)}, u32[]{:S(2)}, u32[]{:S(2)}) %collective-permute-start.14) | collective-permute-done | bytes 196640 | tf_op jit(solution)/shard_map/ppermute | solution.py:135
  43.9 1.4 %collective-permute-start.19 = (bf16[64,2560]{1,0:T(8,128)(2,1)S(1)}, bf16[64,2560]{1,0:T(8,128)(2,1)S(1)}, u32[]{:S(2)}, u32[]{:S(2)}) collective-permute-start(bf16[64,2560]{1,0:T(8,128)(2,1)S(1)} %fusion.76), channel_id=1, source_target_pairs={{0,4},{2,6},{4,0},{6,2},{8,12},{10,14},{12,8},{14,10},{1,5},{3,7},... | collective-permute-start | bytes 983048 | tf_op jit(solution)/shard_map/ppermute | solution.py:111
  45.6 2.2 %collective-permute-done.12 = bf16[64,2560]{1,0:T(8,128)(2,1)S(1)} collective-permute-done((bf16[64,2560]{1,0:T(8,128)(2,1)S(1)}, bf16[64,2560]{1,0:T(8,128)(2,1)S(1)}, u32[]{:S(2)}, u32[]{:S(2)}) %collective-permute-start.12) | collective-permute-done | bytes 327712 | tf_op jit(solution)/shard_map/ppermute | solution.py:111
  50.0 1.7 %collective-permute-start.13 = (bf16[128,2560]{1,0:T(8,128)(2,1)S(1)}, bf16[128,2560]{1,0:T(8,128)(2,1)S(1)}, u32[]{:S(2)}, u32[]{:S(2)}) collective-permute-start(bf16[128,2560]{1,0:T(8,128)(2,1)S(1)} %convolution_convert_fusion.1), channel_id=1, source_target_pairs={{0,2},{2,0},{4,6},{6,4},{8,10},{10,8},{12,14},{14,12},{1,3},{3,1},... | collective-permute-start | bytes 1966088 | tf_op jit(solution)/shard_map/ppermute | solution.py:111
  52.3 2.0 %collective-permute-start.17 = (bf16[64,2560]{1,0:T(8,128)(2,1)S(1)}, bf16[64,2560]{1,0:T(8,128)(2,1)S(1)}, u32[]{:S(2)}, u32[]{:S(2)}) collective-permute-start(bf16[64,2560]{1,0:T(8,128)(2,1)S(1)} %fusion.44), channel_id=1, source_target_pairs={{0,4},{2,6},{4,0},{6,2},{8,12},{10,14},{12,8},{14,10},{1,5},{3,7},... | collective-permute-start | bytes 983048 | tf_op jit(solution)/shard_map/ppermute | solution.py:111
  54.3 1.3 %convolution_convert_fusion = bf16[128,2560]{1,0:T(8,128)(2,1)S(1)} fusion(bf16[64,2560]{1,0:T(8,128)(2,1)S(1)} %collective-permute-done.7, bf16[64,2560]{1,0:T(8,128)(2,1)} %collective-permute-done.1, bf16[64,2560]{1,0:T(8,128)(2,1)S(1)} %collective-permute-done.4, bf16[64,2560]{1,0:T(8,128)(2,1)S(1)} %bitcast.54, ...), kind=kOutput, calls=%fused_computation.5 | convolution fusion | flops 173604864 | bytes 2031616 | tf_op jit(solution)/shard_map/dot_general | solution.py:16
  56.5 11.8 %collective-permute-done.17 = bf16[64,2560]{1,0:T(8,128)(2,1)S(1)} collective-permute-done((bf16[64,2560]{1,0:T(8,128)(2,1)S(1)}, bf16[64,2560]{1,0:T(8,128)(2,1)S(1)}, u32[]{:S(2)}, u32[]{:S(2)}) %collective-permute-start.17) | collective-permute-done | bytes 327712 | tf_op jit(solution)/shard_map/ppermute | solution.py:111
  68.4 1.3 %collective-permute-start.18 = (bf16[64,2560]{1,0:T(8,128)(2,1)S(1)}, bf16[64,2560]{1,0:T(8,128)(2,1)S(1)}, u32[]{:S(2)}, u32[]{:S(2)}) collective-permute-start(bf16[64,2560]{1,0:T(8,128)(2,1)S(1)} %add_convert_fusion.1), channel_id=1, source_target_pairs={{0,8},{2,10},{4,12},{6,14},{8,0},{10,2},{12,4},{14,6},{1,9},{3,11}... | collective-permute-start | bytes 983048 | tf_op jit(solution)/shard_map/ppermute | solution.py:111
  69.7 1.6 %collective-permute-start.20 = (bf16[64,2560]{1,0:T(8,128)(2,1)S(1)}, bf16[64,2560]{1,0:T(8,128)(2,1)S(1)}, u32[]{:S(2)}, u32[]{:S(2)}) collective-permute-start(bf16[64,2560]{1,0:T(8,128)(2,1)S(1)} %fusion.79), channel_id=1, source_target_pairs={{0,4},{2,6},{4,0},{6,2},{8,12},{10,14},{12,8},{14,10},{1,5},{3,7},... | collective-permute-start | bytes 983048 | tf_op jit(solution)/shard_map/ppermute | solution.py:111
  72.1 1.2 %fusion = bf16[128,2560]{1,0:T(8,128)(2,1)} fusion(bf16[128,2560]{1,0:T(8,128)(2,1)S(1)} %collective-permute-done.13, bf16[64,2560]{1,0:T(8,128)(2,1)S(1)} %collective-permute-done.11, bf16[64,2560]{1,0:T(8,128)(2,1)S(1)} %collective-permute-done.10, bf16[64,2560]{1,0:T(8,128)(2,1)S(1)} %collective-permute-done.9, bf16[64,2560]{1,0:T(8,128)(2,1)S(1)} %bitcast.50, ...), kind=kOutput, calls=%fused_computation.3 | convolution fusion | flops 174260224 | bytes 2686976 | tf_op jit(solution)/shard_map/dot_general | solution.py:16
  73.3 7.9 %collective-permute-done.16 = bf16[128,2560]{1,0:T(8,128)(2,1)S(1)} collective-permute-done((bf16[128,2560]{1,0:T(8,128)(2,1)S(1)}, bf16[128,2560]{1,0:T(8,128)(2,1)S(1)}, u32[]{:S(2)}, u32[]{:S(2)}) %collective-permute-start.16) | collective-permute-done | bytes 655392 | tf_op jit(solution)/shard_map/ppermute | solution.py:111
  81.2 2.2 %fusion.1 = bf16[128,2560]{1,0:T(8,128)(2,1)} fusion(bf16[128,2560]{1,0:T(8,128)(2,1)S(1)} %collective-permute-done.16, bf16[64,2560]{1,0:T(8,128)(2,1)S(1)} %collective-permute-done.7, bf16[64,2560]{1,0:T(8,128)(2,1)} %collective-permute-done.1, bf16[64,2560]{1,0:T(8,128)(2,1)S(1)} %collective-permute-done.4, bf16[64,2560]{1,0:T(8,128)(2,1)S(1)} %bitcast.55, ...), kind=kOutput, calls=%fused_computation.4 | convolution fusion | flops 174260224 | bytes 2686976 | tf_op jit(solution)/shard_map/dot_general | solution.py:16
  83.4 2.2 %collective-permute-done.18 = bf16[64,2560]{1,0:T(8,128)(2,1)S(1)} collective-permute-done((bf16[64,2560]{1,0:T(8,128)(2,1)S(1)}, bf16[64,2560]{1,0:T(8,128)(2,1)S(1)}, u32[]{:S(2)}, u32[]{:S(2)}) %collective-permute-start.18) | collective-permute-done | bytes 327712 | tf_op jit(solution)/shard_map/ppermute | solution.py:111
  (80 shorter events, 17.2 us)
Async XLA Ops:
  0.6 9.1 %copy-start = (s32[8,256]{1,0:T(8,128)S(1)}, s32[8,256]{1,0:T(8,128)}, u32[]{:S(2)}) copy-start(s32[8,256]{1,0:T(8,128)} %param.10) | copy-start | bytes 24580
  0.7 9.8 %collective-permute-start.2 = (f32[1,256]{1,0:T(1,128)}, f32[1,256]{1,0:T(1,128)S(1)}, u32[]{:S(2)}, u32[]{:S(2)}) collective-permute-start(f32[1,256]{1,0:T(1,128)} %param.11), channel_id=1, source_target_pairs={{0,4},{2,6},{4,0},{6,2},{8,12},{10,14},{12,8},{14,10},{1,5},{3,7},... | collective-permute-start | bytes 3080 | tf_op jit(solution)/shard_map/ppermute | solution.py:111
  3.7 17.8 %collective-permute-start.1 = (bf16[64,2560]{1,0:T(8,128)(2,1)}, bf16[64,2560]{1,0:T(8,128)(2,1)}, u32[]{:S(2)}, u32[]{:S(2)}) collective-permute-start(bf16[64,2560]{1,0:T(8,128)(2,1)} %bitcast.51), channel_id=1, source_target_pairs={{0,8},{2,10},{4,12},{6,14},{8,0},{10,2},{12,4},{14,6},{16,28},{18,... | collective-permute-start | bytes 983048 | tf_op jit(solution)/shard_map/ppermute | solution.py:147
  6.3 18.5 %collective-permute-start.5 = (bf16[128,2560]{1,0:T(8,128)(2,1)}, bf16[128,2560]{1,0:T(8,128)(2,1)}, u32[]{:S(2)}, u32[]{:S(2)}) collective-permute-start(bf16[128,2560]{1,0:T(8,128)(2,1)} %param.6), channel_id=1, source_target_pairs={{0,2},{2,0},{4,6},{6,4},{8,10},{10,8},{12,14},{14,12},{1,3},{3,1},... | collective-permute-start | bytes 1966088 | tf_op jit(solution)/shard_map/ppermute | solution.py:111
  7.8 28.8 %collective-permute-start = (bf16[128,2560]{1,0:T(8,128)(2,1)}, bf16[128,2560]{1,0:T(8,128)(2,1)}, u32[]{:S(2)}, u32[]{:S(2)}) collective-permute-start(bf16[128,2560]{1,0:T(8,128)(2,1)} %param.7), channel_id=1, source_target_pairs={{0,2},{2,0},{4,6},{6,4},{8,10},{10,8},{12,14},{14,12},{1,3},{3,1},... | collective-permute-start | bytes 1966088 | tf_op jit(solution)/shard_map/ppermute | solution.py:111
  9.6 18.2 %copy-start.4 = (bf16[1,64,2560]{2,1,0:T(8,128)(2,1)S(1)}, bf16[1,64,2560]{2,1,0:T(8,128)(2,1)}, u32[]{:S(2)}) copy-start(bf16[1,64,2560]{2,1,0:T(8,128)(2,1)} %param.8) | copy-start | bytes 983044
  10.4 10.7 %collective-permute-start.3 = (f32[2,256]{1,0:T(2,128)S(1)}, f32[2,256]{1,0:T(2,128)S(1)}, u32[]{:S(2)}, u32[]{:S(2)}) collective-permute-start(f32[2,256]{1,0:T(2,128)S(1)} %pad_maximum_fusion.7), channel_id=1, source_target_pairs={{0,8},{2,10},{4,12},{6,14},{8,0},{10,2},{12,4},{14,6},{1,9},{3,11}... | collective-permute-start | bytes 6152 | tf_op jit(solution)/shard_map/ppermute | solution.py:111
  10.9 16.9 %collective-permute-start.4 = (bf16[64,2560]{1,0:T(8,128)(2,1)}, bf16[64,2560]{1,0:T(8,128)(2,1)S(1)}, u32[]{:S(2)}, u32[]{:S(2)}) collective-permute-start(bf16[64,2560]{1,0:T(8,128)(2,1)} %bitcast.52), channel_id=1, source_target_pairs={{0,4},{2,6},{4,0},{6,2},{8,12},{10,14},{12,8},{14,10},{1,5},{3,7},... | collective-permute-start | bytes 983048 | tf_op jit(solution)/shard_map/ppermute | solution.py:111
  21.1 18.6 %collective-permute-start.10 = (bf16[64,2560]{1,0:T(8,128)(2,1)}, bf16[64,2560]{1,0:T(8,128)(2,1)S(1)}, u32[]{:S(2)}, u32[]{:S(2)}) collective-permute-start(bf16[64,2560]{1,0:T(8,128)(2,1)} %bitcast.46), channel_id=1, source_target_pairs={{0,8},{2,10},{4,12},{6,14},{8,0},{10,2},{12,4},{14,6},{16,28},{18,... | collective-permute-start | bytes 983048 | tf_op jit(solution)/shard_map/ppermute | solution.py:167
  21.5 19.8 %collective-permute-start.9 = (bf16[64,2560]{1,0:T(8,128)(2,1)}, bf16[64,2560]{1,0:T(8,128)(2,1)S(1)}, u32[]{:S(2)}, u32[]{:S(2)}) collective-permute-start(bf16[64,2560]{1,0:T(8,128)(2,1)} %bitcast.47), channel_id=1, source_target_pairs={{0,4},{2,6},{4,0},{6,2},{8,12},{10,14},{12,8},{14,10},{1,5},{3,7},... | collective-permute-start | bytes 983048 | tf_op jit(solution)/shard_map/ppermute | solution.py:111
  24.8 8.2 %collective-permute-start.7 = (bf16[64,2560]{1,0:T(8,128)(2,1)}, bf16[64,2560]{1,0:T(8,128)(2,1)S(1)}, u32[]{:S(2)}, u32[]{:S(2)}) collective-permute-start(bf16[64,2560]{1,0:T(8,128)(2,1)} %collective-permute-done.1), channel_id=1, source_target_pairs={{0,16},{16,0},{1,17},{17,1},{2,18},{18,2},{3,19},{19,3},{4,20},{20... | collective-permute-start | bytes 983048 | tf_op jit(solution)/shard_map/ppermute | solution.py:171
  29.3 1.5 %collective-permute-start.6 = (f32[192,256]{1,0:T(8,128)S(1)}, f32[192,256]{1,0:T(8,128)S(1)}, u32[]{:S(2)}, u32[]{:S(2)}) collective-permute-start(f32[192,256]{1,0:T(8,128)S(1)} %fusion.2), channel_id=1, source_target_pairs={{0,1},{1,0},{2,3},{3,2},{4,5},{5,4},{6,7},{7,6},{8,9},{9,8},{10,11... | collective-permute-start | bytes 589832 | tf_op jit(solution)/shard_map/ppermute | solution.py:135
  33.5 1.3 %collective-permute-start.8 = (f32[64,256]{1,0:T(8,128)S(1)}, f32[64,256]{1,0:T(8,128)S(1)}, u32[]{:S(2)}, u32[]{:S(2)}) collective-permute-start(f32[64,256]{1,0:T(8,128)S(1)} %fusion.74), channel_id=1, source_target_pairs={{0,1},{1,0},{2,3},{3,2},{4,5},{5,4},{6,7},{7,6},{8,9},{9,8},{10,11... | collective-permute-start | bytes 196616 | tf_op jit(solution)/shard_map/ppermute | solution.py:135
  39.2 8.6 %collective-permute-start.12 = (bf16[64,2560]{1,0:T(8,128)(2,1)S(1)}, bf16[64,2560]{1,0:T(8,128)(2,1)S(1)}, u32[]{:S(2)}, u32[]{:S(2)}) collective-permute-start(bf16[64,2560]{1,0:T(8,128)(2,1)S(1)} %fusion.48), channel_id=1, source_target_pairs={{0,4},{2,6},{4,0},{6,2},{8,12},{10,14},{12,8},{14,10},{1,5},{3,7},... | collective-permute-start | bytes 983048 | tf_op jit(solution)/shard_map/ppermute | solution.py:111
  39.7 9.3 %collective-permute-start.11 = (bf16[64,2560]{1,0:T(8,128)(2,1)S(1)}, bf16[64,2560]{1,0:T(8,128)(2,1)S(1)}, u32[]{:S(2)}, u32[]{:S(2)}) collective-permute-start(bf16[64,2560]{1,0:T(8,128)(2,1)S(1)} %collective-permute-done.10), channel_id=1, source_target_pairs={{0,16},{16,0},{1,17},{17,1},{2,18},{18,2},{3,19},{19,3},{4,20},{20... | collective-permute-start | bytes 983048 | tf_op jit(solution)/shard_map/ppermute | solution.py:204
  41.9 1.5 %collective-permute-start.14 = (f32[192,256]{1,0:T(8,128)S(1)}, f32[192,256]{1,0:T(8,128)S(1)}, u32[]{:S(2)}, u32[]{:S(2)}) collective-permute-start(f32[192,256]{1,0:T(8,128)S(1)} %fusion.8), channel_id=1, source_target_pairs={{0,1},{1,0},{2,3},{3,2},{4,5},{5,4},{6,7},{7,6},{8,9},{9,8},{10,11... | collective-permute-start | bytes 589832 | tf_op jit(solution)/shard_map/ppermute | solution.py:135
  43.9 25.8 %collective-permute-start.19 = (bf16[64,2560]{1,0:T(8,128)(2,1)S(1)}, bf16[64,2560]{1,0:T(8,128)(2,1)S(1)}, u32[]{:S(2)}, u32[]{:S(2)}) collective-permute-start(bf16[64,2560]{1,0:T(8,128)(2,1)S(1)} %fusion.76), channel_id=1, source_target_pairs={{0,4},{2,6},{4,0},{6,2},{8,12},{10,14},{12,8},{14,10},{1,5},{3,7},... | collective-permute-start | bytes 983048 | tf_op jit(solution)/shard_map/ppermute | solution.py:111
  47.9 21.8 %collective-permute-start.21 = (bf16[64,2560]{1,0:T(8,128)(2,1)S(1)}, bf16[64,2560]{1,0:T(8,128)(2,1)S(1)}, u32[]{:S(2)}, u32[]{:S(2)}) collective-permute-start(bf16[64,2560]{1,0:T(8,128)(2,1)S(1)} %add_convert_fusion), channel_id=1, source_target_pairs={{0,8},{2,10},{4,12},{6,14},{8,0},{10,2},{12,4},{14,6},{1,9},{3,11}... | collective-permute-start | bytes 983048 | tf_op jit(solution)/shard_map/ppermute | solution.py:111
  49.5 2.1 %collective-permute-start.15 = (f32[64,256]{1,0:T(8,128)S(1)}, f32[64,256]{1,0:T(8,128)S(1)}, u32[]{:S(2)}, u32[]{:S(2)}) collective-permute-start(f32[64,256]{1,0:T(8,128)S(1)} %fusion.77), channel_id=1, source_target_pairs={{0,1},{1,0},{2,3},{3,2},{4,5},{5,4},{6,7},{7,6},{8,9},{9,8},{10,11... | collective-permute-start | bytes 196616 | tf_op jit(solution)/shard_map/ppermute | solution.py:135
  50.0 22.2 %collective-permute-start.13 = (bf16[128,2560]{1,0:T(8,128)(2,1)S(1)}, bf16[128,2560]{1,0:T(8,128)(2,1)S(1)}, u32[]{:S(2)}, u32[]{:S(2)}) collective-permute-start(bf16[128,2560]{1,0:T(8,128)(2,1)S(1)} %convolution_convert_fusion.1), channel_id=1, source_target_pairs={{0,2},{2,0},{4,6},{6,4},{8,10},{10,8},{12,14},{14,12},{1,3},{3,1},... | collective-permute-start | bytes 1966088 | tf_op jit(solution)/shard_map/ppermute | solution.py:111
  52.3 16.0 %collective-permute-start.17 = (bf16[64,2560]{1,0:T(8,128)(2,1)S(1)}, bf16[64,2560]{1,0:T(8,128)(2,1)S(1)}, u32[]{:S(2)}, u32[]{:S(2)}) collective-permute-start(bf16[64,2560]{1,0:T(8,128)(2,1)S(1)} %fusion.44), channel_id=1, source_target_pairs={{0,4},{2,6},{4,0},{6,2},{8,12},{10,14},{12,8},{14,10},{1,5},{3,7},... | collective-permute-start | bytes 983048 | tf_op jit(solution)/shard_map/ppermute | solution.py:111
  55.7 25.5 %collective-permute-start.16 = (bf16[128,2560]{1,0:T(8,128)(2,1)S(1)}, bf16[128,2560]{1,0:T(8,128)(2,1)S(1)}, u32[]{:S(2)}, u32[]{:S(2)}) collective-permute-start(bf16[128,2560]{1,0:T(8,128)(2,1)S(1)} %convolution_convert_fusion), channel_id=1, source_target_pairs={{0,2},{2,0},{4,6},{6,4},{8,10},{10,8},{12,14},{14,12},{1,3},{3,1},... | collective-permute-start | bytes 1966088 | tf_op jit(solution)/shard_map/ppermute | solution.py:111
  68.4 17.2 %collective-permute-start.18 = (bf16[64,2560]{1,0:T(8,128)(2,1)S(1)}, bf16[64,2560]{1,0:T(8,128)(2,1)S(1)}, u32[]{:S(2)}, u32[]{:S(2)}) collective-permute-start(bf16[64,2560]{1,0:T(8,128)(2,1)S(1)} %add_convert_fusion.1), channel_id=1, source_target_pairs={{0,8},{2,10},{4,12},{6,14},{8,0},{10,2},{12,4},{14,6},{1,9},{3,11}... | collective-permute-start | bytes 983048 | tf_op jit(solution)/shard_map/ppermute | solution.py:111
  69.7 15.9 %collective-permute-start.20 = (bf16[64,2560]{1,0:T(8,128)(2,1)S(1)}, bf16[64,2560]{1,0:T(8,128)(2,1)S(1)}, u32[]{:S(2)}, u32[]{:S(2)}) collective-permute-start(bf16[64,2560]{1,0:T(8,128)(2,1)S(1)} %fusion.79), channel_id=1, source_target_pairs={{0,4},{2,6},{4,0},{6,2},{8,12},{10,14},{12,8},{14,10},{1,5},{3,7},... | collective-permute-start | bytes 983048 | tf_op jit(solution)/shard_map/ppermute | solution.py:111
  (3 other events, 13.5 us)

commit v17 on v16

--- a/solution.py
+++ b/solution.py
@@ -198,22 +198,24 @@
     low = low_rank(most, tokens2, cross_down)
     cot2, low = lax.optimization_barrier((cot2, low))
     cot2 = jnp.concatenate([cotangent, cot2], axis=0)
-    (own, first, second, third), up_send = partial_sums(for_line(low), cot2)
-    up_third = move(up_send[2], xor_line(1))
-    far_up = after(far_up, up_send)
+    *others, for_third = for_line(low)
+    up_send_third = narrow(jnp.dot(for_third, cot2, preferred_element_type=jnp.float32))
+    up_third = move(up_send_third, xor_line(1))
+    far_up = after(far_up, up_send_third)
     cross_up = lax.ppermute(far_up, "groups", SWAP)
     most = most_products(cot2, up_matrix, near_up, far_up)
-    most, up_next = lax.optimization_barrier((most, up_send[0]))
-    up_first = move(up_next, xor_line(1))
-
-    cross_up = after(cross_up, up_third)
+    most, rows_later = lax.optimization_barrier((most, cot2))
+    (own, first, second), up_send = partial_sums(others, rows_later)
+    up_first = move(up_send[0], xor_line(1))
+
+    cross_up, up_sum = lax.optimization_barrier((cross_up, narrow(add_up(second, up_third))))
+    up_far = move(up_sum, xor_line(2))
     up_all = jnp.concatenate([up_matrix, near_up, far_up, cross_up], axis=0)
     low_back = low_rank(most, cot2, cross_up)
     (own_b, first_b, second_b, third_b), down_send = partial_sums(for_line(low_back), tokens2)
     down_third = move(down_send[2], xor_line(1))
     branch_back = outward_start(low, up_all)
     input_back = outward_start(low_back, down_all)
-    up_far = move(narrow(add_up(second, up_third)), xor_line(2))
     down_sum = narrow(add_up(second_b, down_third))
     down_far = move(down_sum, xor_line(2))
     down_first = move(after(down_send[0], (up_first, down_sum)), xor_line(1))

time: 86.8 us -> 86.6 us (level)
  starting transfers between devices: 25 us -> 22.7 us
  waiting for transfers between devices: 42.9 us -> 45 us
    ppermute x14, starting transfers between devices: 19.4 us -> 17.1 us  [move(): return lax.ppermute(value, 'adapter', pairs)]
    ppermute x14, waiting for transfers between devices: 36.7 us -> 38.6 us  [move(): return lax.ppermute(value, 'adapter', pairs)]
    dot_general x8 -> x7, matrix products: 2.83 us -> 2.49 us  [partial_sums(): jnp.dot(weight, rows, preferred_element_type=jnp.float32)]
  transfers between devices with their start and end apart: 22 -> 22, of which waited for: 11 -> 13; matrix products, arithmetic and copies ran while one was open for 19% -> 19% of each run, Pallas kernels for 0% -> 0%
where the time goes in v17:
time: 86.6 us; the launch traced here: 86.3 us
  waiting for transfers between devices  45 us (52%)
  starting transfers between devices  22.7 us (26%)
  matrix products  11 us (13%)
  local copies, waits for them, and re-layouts  4.13 us (5%)
  other arithmetic  2.54 us (3%)
  between operations  0.9 us (1%)
    ppermute x14, waiting for transfers between devices, move(): return lax.ppermute(value, 'adapter', pairs)  38.6 us
    ppermute x14, starting transfers between devices, move(): return lax.ppermute(value, 'adapter', pairs)  17.1 us
    dot_general x4, matrix products, contract_first(): lax.dot_general(left_op, right_op, (((0,), (0,)), ((), ())), preferred_el...  5.07 us
    ppermute x4, waiting for transfers between devices, both_cores(): return partial + lax.ppermute(partial, 'tensor', SWAP)  4.03 us
    dot_general x4, matrix products, contract_last(): lax.dot_general(left_op, right_op, (((1,), (1,)), ((), ())), preferred_el...  3.13 us
    ppermute x1, starting transfers between devices, by_pairs(): far_down = lax.ppermute(down_matrix, ('groups', 'adapter'), FAR)  2.59 us
    dot_general x7, matrix products, partial_sums(): jnp.dot(weight, rows, preferred_element_type=jnp.float32)  2.49 us
    ppermute x1, waiting for transfers between devices, by_pairs(): cross_down = lax.ppermute(ready, 'groups', SWAP)  2.13 us
  transfers between devices with their start and end apart: 22, of which 13 were waited for; matrix products, arithmetic and copies ran while one was open for 19% of the time, Pallas kernels for 0%

profile of v17, /device:TPU:0, one launch (start us, length us, event | category | flops | bytes accessed | tf_op | source)
XLA Modules:
  0.0 86.3 jit_solution(13309983477982760508)
XLA Ops:
  0.7 3.1 %collective-permute-start.2 = (f32[1,256]{1,0:T(1,128)}, f32[1,256]{1,0:T(1,128)S(1)}, u32[]{:S(2)}, u32[]{:S(2)}) collective-permute-start(f32[1,256]{1,0:T(1,128)} %param.11), channel_id=1, source_target_pairs={{0,4},{2,6},{4,0},{6,2},{8,12},{10,14},{12,8},{14,10},{1,5},{3,7},... | collective-permute-start | bytes 3080 | tf_op jit(solution)/shard_map/ppermute | solution.py:111
  3.7 2.6 %collective-permute-start.1 = (bf16[64,2560]{1,0:T(8,128)(2,1)}, bf16[64,2560]{1,0:T(8,128)(2,1)}, u32[]{:S(2)}, u32[]{:S(2)}) collective-permute-start(bf16[64,2560]{1,0:T(8,128)(2,1)} %bitcast.51), channel_id=1, source_target_pairs={{0,8},{2,10},{4,12},{6,14},{8,0},{10,2},{12,4},{14,6},{16,28},{18,... | collective-permute-start | bytes 983048 | tf_op jit(solution)/shard_map/ppermute | solution.py:147
  6.3 1.5 %collective-permute-start.5 = (bf16[128,2560]{1,0:T(8,128)(2,1)}, bf16[128,2560]{1,0:T(8,128)(2,1)}, u32[]{:S(2)}, u32[]{:S(2)}) collective-permute-start(bf16[128,2560]{1,0:T(8,128)(2,1)} %param.6), channel_id=1, source_target_pairs={{0,2},{2,0},{4,6},{6,4},{8,10},{10,8},{12,14},{14,12},{1,3},{3,1},... | collective-permute-start | bytes 1966088 | tf_op jit(solution)/shard_map/ppermute | solution.py:111
  11.1 10.1 %collective-permute-done.3 = f32[2,256]{1,0:T(2,128)S(1)} collective-permute-done((f32[2,256]{1,0:T(2,128)S(1)}, f32[2,256]{1,0:T(2,128)S(1)}, u32[]{:S(2)}, u32[]{:S(2)}) %collective-permute-start.3) | collective-permute-done | bytes 2080 | tf_op jit(solution)/shard_map/ppermute | solution.py:111
  21.5 3.3 %collective-permute-start.9 = (bf16[64,2560]{1,0:T(8,128)(2,1)}, bf16[64,2560]{1,0:T(8,128)(2,1)S(1)}, u32[]{:S(2)}, u32[]{:S(2)}) collective-permute-start(bf16[64,2560]{1,0:T(8,128)(2,1)} %bitcast.47), channel_id=1, source_target_pairs={{0,4},{2,6},{4,0},{6,2},{8,12},{10,14},{12,8},{14,10},{1,5},{3,7},... | collective-permute-start | bytes 983048 | tf_op jit(solution)/shard_map/ppermute | solution.py:111
  27.8 1.5 %fusion.2 = f32[192,256]{1,0:T(8,128)S(1)} fusion(bf16[256,2560]{1,0:T(8,128)(2,1)S(1)} %constant_dynamic-update-slice_fusion, bf16[64,2560]{1,0:T(8,128)(2,1)} %collective-permute-done.1, bf16[64,2560]{1,0:T(8,128)(2,1)S(1)} %collective-permute-done.4, bf16[64,2560]{1,0:T(8,128)(2,1)S(1)} %bitcast.53), kind=kOutput, calls=%fused_computation.11 | convolution fusion | flops 254607360 | bytes 2490368 | tf_op jit(solution)/shard_map/dot_general | solution.py:10
  29.4 1.4 %collective-permute-done.6 = f32[192,256]{1,0:T(8,128)S(1)} collective-permute-done((f32[192,256]{1,0:T(8,128)S(1)}, f32[192,256]{1,0:T(8,128)S(1)}, u32[]{:S(2)}, u32[]{:S(2)}) %collective-permute-start.6) | collective-permute-done | bytes 196640 | tf_op jit(solution)/shard_map/ppermute | solution.py:135
  30.9 2.1 %collective-permute-done.7 = bf16[64,2560]{1,0:T(8,128)(2,1)S(1)} collective-permute-done((bf16[64,2560]{1,0:T(8,128)(2,1)}, bf16[64,2560]{1,0:T(8,128)(2,1)S(1)}, u32[]{:S(2)}, u32[]{:S(2)}) %collective-permute-start.7) | collective-permute-done | bytes 327712 | tf_op jit(solution)/shard_map/ppermute | solution.py:171
  33.6 1.2 %collective-permute-done.8 = f32[64,256]{1,0:T(8,128)S(1)} collective-permute-done((f32[64,256]{1,0:T(8,128)S(1)}, f32[64,256]{1,0:T(8,128)S(1)}, u32[]{:S(2)}, u32[]{:S(2)}) %collective-permute-start.8) | collective-permute-done | bytes 65568 | tf_op jit(solution)/shard_map/ppermute | solution.py:135
  34.8 1.8 %collective-permute-done = bf16[128,2560]{1,0:T(8,128)(2,1)} collective-permute-done((bf16[128,2560]{1,0:T(8,128)(2,1)}, bf16[128,2560]{1,0:T(8,128)(2,1)}, u32[]{:S(2)}, u32[]{:S(2)}) %collective-permute-start) | collective-permute-done | bytes 655392 | tf_op jit(solution)/shard_map/ppermute | solution.py:111
  36.6 1.2 %constant_dynamic-update-slice_fusion.2 = bf16[256,2560]{1,0:T(8,128)(2,1)S(1)} fusion(bf16[256,2560]{1,0:T(8,128)(2,1)S(1)} %constant_dynamic-update-slice_fusion.3, bf16[128,2560]{1,0:T(8,128)(2,1)} %collective-permute-done), kind=kLoop, calls=%fused_computation.78 | loop fusion | bytes 1310720 | tf_op jit(solution)/shard_map/concatenate | solution.py:200
  38.7 1.6 %collective-permute-start.11 = (bf16[64,2560]{1,0:T(8,128)(2,1)S(1)}, bf16[64,2560]{1,0:T(8,128)(2,1)S(1)}, u32[]{:S(2)}, u32[]{:S(2)}) collective-permute-start(bf16[64,2560]{1,0:T(8,128)(2,1)S(1)} %collective-permute-done.10), channel_id=1, source_target_pairs={{0,16},{16,0},{1,17},{17,1},{2,18},{18,2},{3,19},{19,3},{4,20},{20... | collective-permute-start | bytes 983048 | tf_op jit(solution)/shard_map/ppermute | solution.py:205
  41.7 1.4 %collective-permute-done.12 = f32[192,256]{1,0:T(8,128)S(1)} collective-permute-done((f32[192,256]{1,0:T(8,128)S(1)}, f32[192,256]{1,0:T(8,128)S(1)}, u32[]{:S(2)}, u32[]{:S(2)}) %collective-permute-start.12) | collective-permute-done | bytes 196640 | tf_op jit(solution)/shard_map/ppermute | solution.py:135
  45.7 1.5 %collective-permute-done.13 = bf16[64,2560]{1,0:T(8,128)(2,1)S(1)} collective-permute-done((bf16[64,2560]{1,0:T(8,128)(2,1)S(1)}, bf16[64,2560]{1,0:T(8,128)(2,1)S(1)}, u32[]{:S(2)}, u32[]{:S(2)}) %collective-permute-start.13) | collective-permute-done | bytes 327712 | tf_op jit(solution)/shard_map/ppermute | solution.py:111
  48.1 1.3 %collective-permute-start.21 = (bf16[64,2560]{1,0:T(8,128)(2,1)S(1)}, bf16[64,2560]{1,0:T(8,128)(2,1)S(1)}, u32[]{:S(2)}, u32[]{:S(2)}) collective-permute-start(bf16[64,2560]{1,0:T(8,128)(2,1)S(1)} %add_convert_fusion.1), channel_id=1, source_target_pairs={{0,8},{2,10},{4,12},{6,14},{8,0},{10,2},{12,4},{14,6},{1,9},{3,11}... | collective-permute-start | bytes 983048 | tf_op jit(solution)/shard_map/ppermute | solution.py:111
  49.8 1.6 %collective-permute-start.14 = (bf16[128,2560]{1,0:T(8,128)(2,1)S(1)}, bf16[128,2560]{1,0:T(8,128)(2,1)S(1)}, u32[]{:S(2)}, u32[]{:S(2)}) collective-permute-start(bf16[128,2560]{1,0:T(8,128)(2,1)S(1)} %convolution_convert_fusion.1), channel_id=1, source_target_pairs={{0,2},{2,0},{4,6},{6,4},{8,10},{10,8},{12,14},{14,12},{1,3},{3,1},... | collective-permute-start | bytes 1966088 | tf_op jit(solution)/shard_map/ppermute | solution.py:111
  52.1 1.6 %collective-permute-start.17 = (bf16[64,2560]{1,0:T(8,128)(2,1)S(1)}, bf16[64,2560]{1,0:T(8,128)(2,1)S(1)}, u32[]{:S(2)}, u32[]{:S(2)}) collective-permute-start(bf16[64,2560]{1,0:T(8,128)(2,1)S(1)} %fusion.44), channel_id=1, source_target_pairs={{0,4},{2,6},{4,0},{6,2},{8,12},{10,14},{12,8},{14,10},{1,5},{3,7},... | collective-permute-start | bytes 983048 | tf_op jit(solution)/shard_map/ppermute | solution.py:111
  53.7 1.3 %convolution_convert_fusion = bf16[128,2560]{1,0:T(8,128)(2,1)S(1)} fusion(bf16[64,2560]{1,0:T(8,128)(2,1)S(1)} %collective-permute-done.7, bf16[64,2560]{1,0:T(8,128)(2,1)} %collective-permute-done.1, bf16[64,2560]{1,0:T(8,128)(2,1)S(1)} %collective-permute-done.4, bf16[64,2560]{1,0:T(8,128)(2,1)S(1)} %bitcast.54, ...), kind=kOutput, calls=%fused_computation.5 | convolution fusion | flops 173604864 | bytes 2031616 | tf_op jit(solution)/shard_map/dot_general | solution.py:16
  55.6 12.9 %collective-permute-done.17 = bf16[64,2560]{1,0:T(8,128)(2,1)S(1)} collective-permute-done((bf16[64,2560]{1,0:T(8,128)(2,1)S(1)}, bf16[64,2560]{1,0:T(8,128)(2,1)S(1)}, u32[]{:S(2)}, u32[]{:S(2)}) %collective-permute-start.17) | collective-permute-done | bytes 327712 | tf_op jit(solution)/shard_map/ppermute | solution.py:111
  69.2 1.2 %collective-permute-start.20 = (bf16[64,2560]{1,0:T(8,128)(2,1)S(1)}, bf16[64,2560]{1,0:T(8,128)(2,1)S(1)}, u32[]{:S(2)}, u32[]{:S(2)}) collective-permute-start(bf16[64,2560]{1,0:T(8,128)(2,1)S(1)} %fusion.78), channel_id=1, source_target_pairs={{0,4},{2,6},{4,0},{6,2},{8,12},{10,14},{12,8},{14,10},{1,5},{3,7},... | collective-permute-start | bytes 983048 | tf_op jit(solution)/shard_map/ppermute | solution.py:111
  71.2 1.2 %fusion = bf16[128,2560]{1,0:T(8,128)(2,1)} fusion(bf16[128,2560]{1,0:T(8,128)(2,1)S(1)} %collective-permute-done.14, bf16[64,2560]{1,0:T(8,128)(2,1)S(1)} %collective-permute-done.11, bf16[64,2560]{1,0:T(8,128)(2,1)S(1)} %collective-permute-done.10, bf16[64,2560]{1,0:T(8,128)(2,1)S(1)} %collective-permute-done.9, bf16[64,2560]{1,0:T(8,128)(2,1)S(1)} %bitcast.50, ...), kind=kOutput, calls=%fused_computation.3 | convolution fusion | flops 174260224 | bytes 2686976 | tf_op jit(solution)/shard_map/dot_general | solution.py:16
  72.4 8.3 %collective-permute-done.16 = bf16[128,2560]{1,0:T(8,128)(2,1)S(1)} collective-permute-done((bf16[128,2560]{1,0:T(8,128)(2,1)S(1)}, bf16[128,2560]{1,0:T(8,128)(2,1)S(1)}, u32[]{:S(2)}, u32[]{:S(2)}) %collective-permute-start.16) | collective-permute-done | bytes 655392 | tf_op jit(solution)/shard_map/ppermute | solution.py:111
  80.7 2.2 %fusion.1 = bf16[128,2560]{1,0:T(8,128)(2,1)} fusion(bf16[128,2560]{1,0:T(8,128)(2,1)S(1)} %collective-permute-done.16, bf16[64,2560]{1,0:T(8,128)(2,1)S(1)} %collective-permute-done.7, bf16[64,2560]{1,0:T(8,128)(2,1)} %collective-permute-done.1, bf16[64,2560]{1,0:T(8,128)(2,1)S(1)} %collective-permute-done.4, bf16[64,2560]{1,0:T(8,128)(2,1)S(1)} %bitcast.55, ...), kind=kOutput, calls=%fused_computation.4 | convolution fusion | flops 174260224 | bytes 2686976 | tf_op jit(solution)/shard_map/dot_general | solution.py:16
  82.9 2.6 %collective-permute-done.18 = bf16[64,2560]{1,0:T(8,128)(2,1)S(1)} collective-permute-done((bf16[64,2560]{1,0:T(8,128)(2,1)S(1)}, bf16[64,2560]{1,0:T(8,128)(2,1)S(1)}, u32[]{:S(2)}, u32[]{:S(2)}) %collective-permute-start.18) | collective-permute-done | bytes 327712 | tf_op jit(solution)/shard_map/ppermute | solution.py:111
  (80 shorter events, 16.9 us)
Async XLA Ops:
  0.6 9.1 %copy-start = (s32[8,256]{1,0:T(8,128)S(1)}, s32[8,256]{1,0:T(8,128)}, u32[]{:S(2)}) copy-start(s32[8,256]{1,0:T(8,128)} %param.10) | copy-start | bytes 24580
  0.7 9.8 %collective-permute-start.2 = (f32[1,256]{1,0:T(1,128)}, f32[1,256]{1,0:T(1,128)S(1)}, u32[]{:S(2)}, u32[]{:S(2)}) collective-permute-start(f32[1,256]{1,0:T(1,128)} %param.11), channel_id=1, source_target_pairs={{0,4},{2,6},{4,0},{6,2},{8,12},{10,14},{12,8},{14,10},{1,5},{3,7},... | collective-permute-start | bytes 3080 | tf_op jit(solution)/shard_map/ppermute | solution.py:111
  3.7 17.8 %collective-permute-start.1 = (bf16[64,2560]{1,0:T(8,128)(2,1)}, bf16[64,2560]{1,0:T(8,128)(2,1)}, u32[]{:S(2)}, u32[]{:S(2)}) collective-permute-start(bf16[64,2560]{1,0:T(8,128)(2,1)} %bitcast.51), channel_id=1, source_target_pairs={{0,8},{2,10},{4,12},{6,14},{8,0},{10,2},{12,4},{14,6},{16,28},{18,... | collective-permute-start | bytes 983048 | tf_op jit(solution)/shard_map/ppermute | solution.py:147
  6.3 18.5 %collective-permute-start.5 = (bf16[128,2560]{1,0:T(8,128)(2,1)}, bf16[128,2560]{1,0:T(8,128)(2,1)}, u32[]{:S(2)}, u32[]{:S(2)}) collective-permute-start(bf16[128,2560]{1,0:T(8,128)(2,1)} %param.6), channel_id=1, source_target_pairs={{0,2},{2,0},{4,6},{6,4},{8,10},{10,8},{12,14},{14,12},{1,3},{3,1},... | collective-permute-start | bytes 1966088 | tf_op jit(solution)/shard_map/ppermute | solution.py:111
  7.8 28.8 %collective-permute-start = (bf16[128,2560]{1,0:T(8,128)(2,1)}, bf16[128,2560]{1,0:T(8,128)(2,1)}, u32[]{:S(2)}, u32[]{:S(2)}) collective-permute-start(bf16[128,2560]{1,0:T(8,128)(2,1)} %param.7), channel_id=1, source_target_pairs={{0,2},{2,0},{4,6},{6,4},{8,10},{10,8},{12,14},{14,12},{1,3},{3,1},... | collective-permute-start | bytes 1966088 | tf_op jit(solution)/shard_map/ppermute | solution.py:111
  9.6 18.2 %copy-start.4 = (bf16[1,64,2560]{2,1,0:T(8,128)(2,1)S(1)}, bf16[1,64,2560]{2,1,0:T(8,128)(2,1)}, u32[]{:S(2)}) copy-start(bf16[1,64,2560]{2,1,0:T(8,128)(2,1)} %param.8) | copy-start | bytes 983044
  10.4 10.7 %collective-permute-start.3 = (f32[2,256]{1,0:T(2,128)S(1)}, f32[2,256]{1,0:T(2,128)S(1)}, u32[]{:S(2)}, u32[]{:S(2)}) collective-permute-start(f32[2,256]{1,0:T(2,128)S(1)} %pad_maximum_fusion.7), channel_id=1, source_target_pairs={{0,8},{2,10},{4,12},{6,14},{8,0},{10,2},{12,4},{14,6},{1,9},{3,11}... | collective-permute-start | bytes 6152 | tf_op jit(solution)/shard_map/ppermute | solution.py:111
  10.9 16.9 %collective-permute-start.4 = (bf16[64,2560]{1,0:T(8,128)(2,1)}, bf16[64,2560]{1,0:T(8,128)(2,1)S(1)}, u32[]{:S(2)}, u32[]{:S(2)}) collective-permute-start(bf16[64,2560]{1,0:T(8,128)(2,1)} %bitcast.52), channel_id=1, source_target_pairs={{0,4},{2,6},{4,0},{6,2},{8,12},{10,14},{12,8},{14,10},{1,5},{3,7},... | collective-permute-start | bytes 983048 | tf_op jit(solution)/shard_map/ppermute | solution.py:111
  21.1 17.5 %collective-permute-start.10 = (bf16[64,2560]{1,0:T(8,128)(2,1)}, bf16[64,2560]{1,0:T(8,128)(2,1)S(1)}, u32[]{:S(2)}, u32[]{:S(2)}) collective-permute-start(bf16[64,2560]{1,0:T(8,128)(2,1)} %bitcast.46), channel_id=1, source_target_pairs={{0,8},{2,10},{4,12},{6,14},{8,0},{10,2},{12,4},{14,6},{16,28},{18,... | collective-permute-start | bytes 983048 | tf_op jit(solution)/shard_map/ppermute | solution.py:167
  21.5 19.5 %collective-permute-start.9 = (bf16[64,2560]{1,0:T(8,128)(2,1)}, bf16[64,2560]{1,0:T(8,128)(2,1)S(1)}, u32[]{:S(2)}, u32[]{:S(2)}) collective-permute-start(bf16[64,2560]{1,0:T(8,128)(2,1)} %bitcast.47), channel_id=1, source_target_pairs={{0,4},{2,6},{4,0},{6,2},{8,12},{10,14},{12,8},{14,10},{1,5},{3,7},... | collective-permute-start | bytes 983048 | tf_op jit(solution)/shard_map/ppermute | solution.py:111
  24.8 8.2 %collective-permute-start.7 = (bf16[64,2560]{1,0:T(8,128)(2,1)}, bf16[64,2560]{1,0:T(8,128)(2,1)S(1)}, u32[]{:S(2)}, u32[]{:S(2)}) collective-permute-start(bf16[64,2560]{1,0:T(8,128)(2,1)} %collective-permute-done.1), channel_id=1, source_target_pairs={{0,16},{16,0},{1,17},{17,1},{2,18},{18,2},{3,19},{19,3},{4,20},{20... | collective-permute-start | bytes 983048 | tf_op jit(solution)/shard_map/ppermute | solution.py:171
  29.3 1.5 %collective-permute-start.6 = (f32[192,256]{1,0:T(8,128)S(1)}, f32[192,256]{1,0:T(8,128)S(1)}, u32[]{:S(2)}, u32[]{:S(2)}) collective-permute-start(f32[192,256]{1,0:T(8,128)S(1)} %fusion.2), channel_id=1, source_target_pairs={{0,1},{1,0},{2,3},{3,2},{4,5},{5,4},{6,7},{7,6},{8,9},{9,8},{10,11... | collective-permute-start | bytes 589832 | tf_op jit(solution)/shard_map/ppermute | solution.py:135
  33.5 1.3 %collective-permute-start.8 = (f32[64,256]{1,0:T(8,128)S(1)}, f32[64,256]{1,0:T(8,128)S(1)}, u32[]{:S(2)}, u32[]{:S(2)}) collective-permute-start(f32[64,256]{1,0:T(8,128)S(1)} %fusion.73), channel_id=1, source_target_pairs={{0,1},{1,0},{2,3},{3,2},{4,5},{5,4},{6,7},{7,6},{8,9},{9,8},{10,11... | collective-permute-start | bytes 196616 | tf_op jit(solution)/shard_map/ppermute | solution.py:135
  38.2 9.0 %collective-permute-start.13 = (bf16[64,2560]{1,0:T(8,128)(2,1)S(1)}, bf16[64,2560]{1,0:T(8,128)(2,1)S(1)}, u32[]{:S(2)}, u32[]{:S(2)}) collective-permute-start(bf16[64,2560]{1,0:T(8,128)(2,1)S(1)} %convolution_convert_fusion.2), channel_id=1, source_target_pairs={{0,4},{2,6},{4,0},{6,2},{8,12},{10,14},{12,8},{14,10},{1,5},{3,7},... | collective-permute-start | bytes 983048 | tf_op jit(solution)/shard_map/ppermute | solution.py:111
  38.7 8.8 %collective-permute-start.11 = (bf16[64,2560]{1,0:T(8,128)(2,1)S(1)}, bf16[64,2560]{1,0:T(8,128)(2,1)S(1)}, u32[]{:S(2)}, u32[]{:S(2)}) collective-permute-start(bf16[64,2560]{1,0:T(8,128)(2,1)S(1)} %collective-permute-done.10), channel_id=1, source_target_pairs={{0,16},{16,0},{1,17},{17,1},{2,18},{18,2},{3,19},{19,3},{4,20},{20... | collective-permute-start | bytes 983048 | tf_op jit(solution)/shard_map/ppermute | solution.py:205
  41.6 1.5 %collective-permute-start.12 = (f32[192,256]{1,0:T(8,128)S(1)}, f32[192,256]{1,0:T(8,128)S(1)}, u32[]{:S(2)}, u32[]{:S(2)}) collective-permute-start(f32[192,256]{1,0:T(8,128)S(1)} %fusion.8), channel_id=1, source_target_pairs={{0,1},{1,0},{2,3},{3,2},{4,5},{5,4},{6,7},{7,6},{8,9},{9,8},{10,11... | collective-permute-start | bytes 589832 | tf_op jit(solution)/shard_map/ppermute | solution.py:135
  44.6 24.6 %collective-permute-start.19 = (bf16[64,2560]{1,0:T(8,128)(2,1)S(1)}, bf16[64,2560]{1,0:T(8,128)(2,1)S(1)}, u32[]{:S(2)}, u32[]{:S(2)}) collective-permute-start(bf16[64,2560]{1,0:T(8,128)(2,1)S(1)} %fusion.75), channel_id=1, source_target_pairs={{0,4},{2,6},{4,0},{6,2},{8,12},{10,14},{12,8},{14,10},{1,5},{3,7},... | collective-permute-start | bytes 983048 | tf_op jit(solution)/shard_map/ppermute | solution.py:111
  48.0 3.4 %collective-permute-start.15 = (f32[64,256]{1,0:T(8,128)S(1)}, f32[64,256]{1,0:T(8,128)S(1)}, u32[]{:S(2)}, u32[]{:S(2)}) collective-permute-start(f32[64,256]{1,0:T(8,128)S(1)} %fusion.76), channel_id=1, source_target_pairs={{0,1},{1,0},{2,3},{3,2},{4,5},{5,4},{6,7},{7,6},{8,9},{9,8},{10,11... | collective-permute-start | bytes 196616 | tf_op jit(solution)/shard_map/ppermute | solution.py:135
  48.1 21.1 %collective-permute-start.21 = (bf16[64,2560]{1,0:T(8,128)(2,1)S(1)}, bf16[64,2560]{1,0:T(8,128)(2,1)S(1)}, u32[]{:S(2)}, u32[]{:S(2)}) collective-permute-start(bf16[64,2560]{1,0:T(8,128)(2,1)S(1)} %add_convert_fusion.1), channel_id=1, source_target_pairs={{0,8},{2,10},{4,12},{6,14},{8,0},{10,2},{12,4},{14,6},{1,9},{3,11}... | collective-permute-start | bytes 983048 | tf_op jit(solution)/shard_map/ppermute | solution.py:111
  49.8 21.4 %collective-permute-start.14 = (bf16[128,2560]{1,0:T(8,128)(2,1)S(1)}, bf16[128,2560]{1,0:T(8,128)(2,1)S(1)}, u32[]{:S(2)}, u32[]{:S(2)}) collective-permute-start(bf16[128,2560]{1,0:T(8,128)(2,1)S(1)} %convolution_convert_fusion.1), channel_id=1, source_target_pairs={{0,2},{2,0},{4,6},{6,4},{8,10},{10,8},{12,14},{14,12},{1,3},{3,1},... | collective-permute-start | bytes 1966088 | tf_op jit(solution)/shard_map/ppermute | solution.py:111
  52.1 16.3 %collective-permute-start.17 = (bf16[64,2560]{1,0:T(8,128)(2,1)S(1)}, bf16[64,2560]{1,0:T(8,128)(2,1)S(1)}, u32[]{:S(2)}, u32[]{:S(2)}) collective-permute-start(bf16[64,2560]{1,0:T(8,128)(2,1)S(1)} %fusion.44), channel_id=1, source_target_pairs={{0,4},{2,6},{4,0},{6,2},{8,12},{10,14},{12,8},{14,10},{1,5},{3,7},... | collective-permute-start | bytes 983048 | tf_op jit(solution)/shard_map/ppermute | solution.py:111
  55.1 25.7 %collective-permute-start.16 = (bf16[128,2560]{1,0:T(8,128)(2,1)S(1)}, bf16[128,2560]{1,0:T(8,128)(2,1)S(1)}, u32[]{:S(2)}, u32[]{:S(2)}) collective-permute-start(bf16[128,2560]{1,0:T(8,128)(2,1)S(1)} %convolution_convert_fusion), channel_id=1, source_target_pairs={{0,2},{2,0},{4,6},{6,4},{8,10},{10,8},{12,14},{14,12},{1,3},{3,1},... | collective-permute-start | bytes 1966088 | tf_op jit(solution)/shard_map/ppermute | solution.py:111
  68.5 16.9 %collective-permute-start.18 = (bf16[64,2560]{1,0:T(8,128)(2,1)S(1)}, bf16[64,2560]{1,0:T(8,128)(2,1)S(1)}, u32[]{:S(2)}, u32[]{:S(2)}) collective-permute-start(bf16[64,2560]{1,0:T(8,128)(2,1)S(1)} %add_convert_fusion), channel_id=1, source_target_pairs={{0,8},{2,10},{4,12},{6,14},{8,0},{10,2},{12,4},{14,6},{1,9},{3,11}... | collective-permute-start | bytes 983048 | tf_op jit(solution)/shard_map/ppermute | solution.py:111
  69.2 16.3 %collective-permute-start.20 = (bf16[64,2560]{1,0:T(8,128)(2,1)S(1)}, bf16[64,2560]{1,0:T(8,128)(2,1)S(1)}, u32[]{:S(2)}, u32[]{:S(2)}) collective-permute-start(bf16[64,2560]{1,0:T(8,128)(2,1)S(1)} %fusion.78), channel_id=1, source_target_pairs={{0,4},{2,6},{4,0},{6,2},{8,12},{10,14},{12,8},{14,10},{1,5},{3,7},... | collective-permute-start | bytes 983048 | tf_op jit(solution)/shard_map/ppermute | solution.py:111
  (3 other events, 15.4 us)

commit v18 on v17

--- a/solution.py
+++ b/solution.py
@@ -196,11 +196,15 @@
     most = most_products(tokens2, down_matrix, near_down, far_down)
     most, tokens2 = lax.optimization_barrier((most, tokens2))
     low = low_rank(most, tokens2, cross_down)
-    cot2, low = lax.optimization_barrier((cot2, low))
-    cot2 = jnp.concatenate([cotangent, cot2], axis=0)
+    low, far_up = lax.optimization_barrier((low, far_up))
     *others, for_third = for_line(low)
-    up_send_third = narrow(jnp.dot(for_third, cot2, preferred_element_type=jnp.float32))
+    part = jnp.dot(for_third[:, :tok_local], cotangent, preferred_element_type=jnp.float32)
+    theirs, for_third, part = lax.optimization_barrier((cot2, for_third[:, tok_local:], part))
+    part = part + jnp.dot(for_third, theirs, preferred_element_type=jnp.float32)
+    up_send_third = narrow(part)
     up_third = move(up_send_third, xor_line(1))
+    theirs = after(theirs, up_send_third)
+    cot2 = jnp.concatenate([cotangent, theirs], axis=0)
     far_up = after(far_up, up_send_third)
     cross_up = lax.ppermute(far_up, "groups", SWAP)
     most = most_products(cot2, up_matrix, near_up, far_up)

time: 86.6 us -> 88.6 us (1.023)
  matrix products: 11 us -> 12.2 us
    ppermute x1, waiting for transfers between devices: 0.01 us -> 3.08 us  [by_pairs(): far_up = lax.ppermute(up_later, ('groups', 'adapter'), FAR)]
    ppermute x14, waiting for transfers between devices: 38.6 us -> 36 us  [move(): return lax.ppermute(value, 'adapter', pairs)]
    ppermute x14, starting transfers between devices: 17.1 us -> 18.5 us  [move(): return lax.ppermute(value, 'adapter', pairs)]
    dot_general x1 -> x2, matrix products: 0.35 us -> 1.55 us  [the longest x1 1.32 us: by_pairs(): part = part + jnp.dot(for_third, theirs, preferred_element_type=jnp.float32)]
    ppermute x1, starting transfers between devices: 1.63 us -> 0.63 us  [by_pairs(): cross_up = lax.ppermute(far_up, 'groups', SWAP)]
  transfers between devices with their start and end apart: 22 -> 22, of which waited for: 13 -> 12; matrix products, arithmetic and copies ran while one was open for 19% -> 20% of each run, Pallas kernels for 0% -> 0%
where the time goes in v18:
time: 88.6 us; the launch traced here: 88.3 us
  waiting for transfers between devices  45.2 us (51%)
  starting transfers between devices  23.1 us (26%)
  matrix products  12.2 us (14%)
  local copies, waits for them, and re-layouts  4.09 us (5%)
  other arithmetic  2.61 us (3%)
  between operations  0.98 us (1%)
    ppermute x14, waiting for transfers between devices, move(): return lax.ppermute(value, 'adapter', pairs)  36 us
    ppermute x14, starting transfers between devices, move(): return lax.ppermute(value, 'adapter', pairs)  18.5 us
    dot_general x4, matrix products, contract_first(): lax.dot_general(left_op, right_op, (((0,), (0,)), ((), ())), preferred_el...  5.06 us
    ppermute x4, waiting for transfers between devices, both_cores(): return partial + lax.ppermute(partial, 'tensor', SWAP)  4.03 us
    dot_general x4, matrix products, contract_last(): lax.dot_general(left_op, right_op, (((1,), (1,)), ((), ())), preferred_el...  3.13 us
    ppermute x1, waiting for transfers between devices, by_pairs(): far_up = lax.ppermute(up_later, ('groups', 'adapter'), FAR)  3.08 us
    ppermute x1, starting transfers between devices, by_pairs(): far_down = lax.ppermute(down_matrix, ('groups', 'adapter'), FAR)  2.59 us
    dot_general x7, matrix products, partial_sums(): jnp.dot(weight, rows, preferred_element_type=jnp.float32)  2.48 us
  transfers between devices with their start and end apart: 22, of which 12 were waited for; matrix products, arithmetic and copies ran while one was open for 20% of the time, Pallas kernels for 0%

profile of v18, /device:TPU:0, one launch (start us, length us, event | category | flops | bytes accessed | tf_op | source)
XLA Modules:
  0.0 88.3 jit_solution(13058121950188191078)
XLA Ops:
  0.7 3.1 %collective-permute-start.1 = (f32[1,256]{1,0:T(1,128)}, f32[1,256]{1,0:T(1,128)S(1)}, u32[]{:S(2)}, u32[]{:S(2)}) collective-permute-start(f32[1,256]{1,0:T(1,128)} %param.11), channel_id=1, source_target_pairs={{0,4},{2,6},{4,0},{6,2},{8,12},{10,14},{12,8},{14,10},{1,5},{3,7},... | collective-permute-start | bytes 3080 | tf_op jit(solution)/shard_map/ppermute | solution.py:111
  3.7 2.6 %collective-permute-start = (bf16[64,2560]{1,0:T(8,128)(2,1)}, bf16[64,2560]{1,0:T(8,128)(2,1)}, u32[]{:S(2)}, u32[]{:S(2)}) collective-permute-start(bf16[64,2560]{1,0:T(8,128)(2,1)} %bitcast.53), channel_id=1, source_target_pairs={{0,8},{2,10},{4,12},{6,14},{8,0},{10,2},{12,4},{14,6},{16,28},{18,... | collective-permute-start | bytes 983048 | tf_op jit(solution)/shard_map/ppermute | solution.py:147
  6.3 1.5 %collective-permute-start.4 = (bf16[128,2560]{1,0:T(8,128)(2,1)}, bf16[128,2560]{1,0:T(8,128)(2,1)}, u32[]{:S(2)}, u32[]{:S(2)}) collective-permute-start(bf16[128,2560]{1,0:T(8,128)(2,1)} %param.6), channel_id=1, source_target_pairs={{0,2},{2,0},{4,6},{6,4},{8,10},{10,8},{12,14},{14,12},{1,3},{3,1},... | collective-permute-start | bytes 1966088 | tf_op jit(solution)/shard_map/ppermute | solution.py:111
  11.1 10.1 %collective-permute-done.2 = f32[2,256]{1,0:T(2,128)S(1)} collective-permute-done((f32[2,256]{1,0:T(2,128)S(1)}, f32[2,256]{1,0:T(2,128)S(1)}, u32[]{:S(2)}, u32[]{:S(2)}) %collective-permute-start.2) | collective-permute-done | bytes 2080 | tf_op jit(solution)/shard_map/ppermute | solution.py:111
  21.5 3.3 %collective-permute-start.9 = (bf16[64,2560]{1,0:T(8,128)(2,1)}, bf16[64,2560]{1,0:T(8,128)(2,1)S(1)}, u32[]{:S(2)}, u32[]{:S(2)}) collective-permute-start(bf16[64,2560]{1,0:T(8,128)(2,1)} %bitcast.49), channel_id=1, source_target_pairs={{0,4},{2,6},{4,0},{6,2},{8,12},{10,14},{12,8},{14,10},{1,5},{3,7},... | collective-permute-start | bytes 983048 | tf_op jit(solution)/shard_map/ppermute | solution.py:111
  27.8 1.5 %fusion.2 = f32[192,256]{1,0:T(8,128)S(1)} fusion(bf16[256,2560]{1,0:T(8,128)(2,1)S(1)} %constant_dynamic-update-slice_fusion, bf16[64,2560]{1,0:T(8,128)(2,1)} %collective-permute-done, bf16[64,2560]{1,0:T(8,128)(2,1)S(1)} %collective-permute-done.3, bf16[64,2560]{1,0:T(8,128)(2,1)S(1)} %bitcast.55), kind=kOutput, calls=%fused_computation.10 | convolution fusion | flops 254607360 | bytes 2490368 | tf_op jit(solution)/shard_map/dot_general | solution.py:10
  29.4 1.4 %collective-permute-done.5 = f32[192,256]{1,0:T(8,128)S(1)} collective-permute-done((f32[192,256]{1,0:T(8,128)S(1)}, f32[192,256]{1,0:T(8,128)S(1)}, u32[]{:S(2)}, u32[]{:S(2)}) %collective-permute-start.5) | collective-permute-done | bytes 196640 | tf_op jit(solution)/shard_map/ppermute | solution.py:135
  30.9 2.1 %collective-permute-done.6 = bf16[64,2560]{1,0:T(8,128)(2,1)S(1)} collective-permute-done((bf16[64,2560]{1,0:T(8,128)(2,1)}, bf16[64,2560]{1,0:T(8,128)(2,1)S(1)}, u32[]{:S(2)}, u32[]{:S(2)}) %collective-permute-start.6) | collective-permute-done | bytes 327712 | tf_op jit(solution)/shard_map/ppermute | solution.py:171
  33.6 1.2 %collective-permute-done.7 = f32[64,256]{1,0:T(8,128)S(1)} collective-permute-done((f32[64,256]{1,0:T(8,128)S(1)}, f32[64,256]{1,0:T(8,128)S(1)}, u32[]{:S(2)}, u32[]{:S(2)}) %collective-permute-start.7) | collective-permute-done | bytes 65568 | tf_op jit(solution)/shard_map/ppermute | solution.py:135
  34.8 3.1 %collective-permute-done.8 = bf16[64,2560]{1,0:T(8,128)(2,1)S(1)} collective-permute-done((bf16[64,2560]{1,0:T(8,128)(2,1)}, bf16[64,2560]{1,0:T(8,128)(2,1)S(1)}, u32[]{:S(2)}, u32[]{:S(2)}) %collective-permute-start.8) | collective-permute-done | bytes 327712 | tf_op jit(solution)/shard_map/ppermute | solution.py:167
  38.2 1.3 %fusion.74 = f32[64,2560]{1,0:T(8,128)S(1)} fusion(bf16[64,128]{1,0:T(8,128)(2,1)S(1)} %slice.128, bf16[128,2560]{1,0:T(8,128)(2,1)} %collective-permute-done.10), kind=kOutput, calls=%fused_computation.111 | convolution fusion | flops 41943040 | bytes 1327104 | tf_op jit(solution)/shard_map/dot_general | solution.py:203
  42.2 1.4 %collective-permute-done.12 = f32[192,256]{1,0:T(8,128)S(1)} collective-permute-done((f32[192,256]{1,0:T(8,128)S(1)}, f32[192,256]{1,0:T(8,128)S(1)}, u32[]{:S(2)}, u32[]{:S(2)}) %collective-permute-start.12) | collective-permute-done | bytes 196640 | tf_op jit(solution)/shard_map/ppermute | solution.py:135
  45.0 1.5 %collective-permute-start.19 = (bf16[64,2560]{1,0:T(8,128)(2,1)S(1)}, bf16[64,2560]{1,0:T(8,128)(2,1)S(1)}, u32[]{:S(2)}, u32[]{:S(2)}) collective-permute-start(bf16[64,2560]{1,0:T(8,128)(2,1)S(1)} %fusion.76), channel_id=1, source_target_pairs={{0,4},{2,6},{4,0},{6,2},{8,12},{10,14},{12,8},{14,10},{1,5},{3,7},... | collective-permute-start | bytes 983048 | tf_op jit(solution)/shard_map/ppermute | solution.py:111
  46.9 3.3 %collective-permute-done.13 = bf16[64,2560]{1,0:T(8,128)(2,1)S(1)} collective-permute-done((bf16[64,2560]{1,0:T(8,128)(2,1)S(1)}, bf16[64,2560]{1,0:T(8,128)(2,1)S(1)}, u32[]{:S(2)}, u32[]{:S(2)}) %collective-permute-start.13) | collective-permute-done | bytes 327712 | tf_op jit(solution)/shard_map/ppermute | solution.py:111
  50.9 1.6 %collective-permute-start.21 = (bf16[64,2560]{1,0:T(8,128)(2,1)S(1)}, bf16[64,2560]{1,0:T(8,128)(2,1)S(1)}, u32[]{:S(2)}, u32[]{:S(2)}) collective-permute-start(bf16[64,2560]{1,0:T(8,128)(2,1)S(1)} %add_convert_fusion.1), channel_id=1, source_target_pairs={{0,8},{2,10},{4,12},{6,14},{8,0},{10,2},{12,4},{14,6},{1,9},{3,11}... | collective-permute-start | bytes 983048 | tf_op jit(solution)/shard_map/ppermute | solution.py:111
  52.8 1.6 %collective-permute-start.14 = (bf16[128,2560]{1,0:T(8,128)(2,1)S(1)}, bf16[128,2560]{1,0:T(8,128)(2,1)S(1)}, u32[]{:S(2)}, u32[]{:S(2)}) collective-permute-start(bf16[128,2560]{1,0:T(8,128)(2,1)S(1)} %convolution_convert_fusion.1), channel_id=1, source_target_pairs={{0,2},{2,0},{4,6},{6,4},{8,10},{10,8},{12,14},{14,12},{1,3},{3,1},... | collective-permute-start | bytes 1966088 | tf_op jit(solution)/shard_map/ppermute | solution.py:111
  55.2 1.3 %collective-permute-start.17 = (bf16[64,2560]{1,0:T(8,128)(2,1)S(1)}, bf16[64,2560]{1,0:T(8,128)(2,1)S(1)}, u32[]{:S(2)}, u32[]{:S(2)}) collective-permute-start(bf16[64,2560]{1,0:T(8,128)(2,1)S(1)} %fusion.44), channel_id=1, source_target_pairs={{0,4},{2,6},{4,0},{6,2},{8,12},{10,14},{12,8},{14,10},{1,5},{3,7},... | collective-permute-start | bytes 983048 | tf_op jit(solution)/shard_map/ppermute | solution.py:111
  56.5 1.3 %convolution_convert_fusion = bf16[128,2560]{1,0:T(8,128)(2,1)S(1)} fusion(bf16[64,2560]{1,0:T(8,128)(2,1)S(1)} %collective-permute-done.6, bf16[64,2560]{1,0:T(8,128)(2,1)} %collective-permute-done, bf16[64,2560]{1,0:T(8,128)(2,1)S(1)} %collective-permute-done.3, bf16[64,2560]{1,0:T(8,128)(2,1)S(1)} %bitcast.56, bf16[64,128]{1,0:T(8,128)(2,1)S(1)} %get-tuple-element.85, ...), kind=kOutput, calls=%fused_computation.5 | convolution fusion | flops 173604864 | bytes 2031616 | tf_op jit(solution)/shard_map/dot_general | solution.py:16
  58.4 11.9 %collective-permute-done.17 = bf16[64,2560]{1,0:T(8,128)(2,1)S(1)} collective-permute-done((bf16[64,2560]{1,0:T(8,128)(2,1)S(1)}, bf16[64,2560]{1,0:T(8,128)(2,1)S(1)}, u32[]{:S(2)}, u32[]{:S(2)}) %collective-permute-start.17) | collective-permute-done | bytes 327712 | tf_op jit(solution)/shard_map/ppermute | solution.py:111
  71.5 1.7 %collective-permute-start.20 = (bf16[64,2560]{1,0:T(8,128)(2,1)S(1)}, bf16[64,2560]{1,0:T(8,128)(2,1)S(1)}, u32[]{:S(2)}, u32[]{:S(2)}) collective-permute-start(bf16[64,2560]{1,0:T(8,128)(2,1)S(1)} %fusion.79), channel_id=1, source_target_pairs={{0,4},{2,6},{4,0},{6,2},{8,12},{10,14},{12,8},{14,10},{1,5},{3,7},... | collective-permute-start | bytes 983048 | tf_op jit(solution)/shard_map/ppermute | solution.py:111
  74.1 1.2 %fusion = bf16[128,2560]{1,0:T(8,128)(2,1)} fusion(bf16[128,2560]{1,0:T(8,128)(2,1)S(1)} %collective-permute-done.14, bf16[64,2560]{1,0:T(8,128)(2,1)S(1)} %collective-permute-done.11, bf16[64,2560]{1,0:T(8,128)(2,1)S(1)} %collective-permute-done.8, bf16[64,2560]{1,0:T(8,128)(2,1)S(1)} %collective-permute-done.9, bf16[64,2560]{1,0:T(8,128)(2,1)S(1)} %bitcast.52, ...), kind=kOutput, calls=%fused_computation.3 | convolution fusion | flops 174260224 | bytes 2686976 | tf_op jit(solution)/shard_map/dot_general | solution.py:16
  75.3 8.5 %collective-permute-done.16 = bf16[128,2560]{1,0:T(8,128)(2,1)S(1)} collective-permute-done((bf16[128,2560]{1,0:T(8,128)(2,1)S(1)}, bf16[128,2560]{1,0:T(8,128)(2,1)S(1)}, u32[]{:S(2)}, u32[]{:S(2)}) %collective-permute-start.16) | collective-permute-done | bytes 655392 | tf_op jit(solution)/shard_map/ppermute | solution.py:111
  83.8 2.2 %fusion.1 = bf16[128,2560]{1,0:T(8,128)(2,1)} fusion(bf16[128,2560]{1,0:T(8,128)(2,1)S(1)} %collective-permute-done.16, bf16[64,2560]{1,0:T(8,128)(2,1)S(1)} %collective-permute-done.6, bf16[64,2560]{1,0:T(8,128)(2,1)} %collective-permute-done, bf16[64,2560]{1,0:T(8,128)(2,1)S(1)} %collective-permute-done.3, bf16[64,2560]{1,0:T(8,128)(2,1)S(1)} %bitcast.57, ...), kind=kOutput, calls=%fused_computation.4 | convolution fusion | flops 174260224 | bytes 2686976 | tf_op jit(solution)/shard_map/dot_general | solution.py:16
  85.9 1.4 %collective-permute-done.18 = bf16[64,2560]{1,0:T(8,128)(2,1)S(1)} collective-permute-done((bf16[64,2560]{1,0:T(8,128)(2,1)S(1)}, bf16[64,2560]{1,0:T(8,128)(2,1)S(1)}, u32[]{:S(2)}, u32[]{:S(2)}) %collective-permute-start.18) | collective-permute-done | bytes 327712 | tf_op jit(solution)/shard_map/ppermute | solution.py:111
  (84 shorter events, 17.1 us)
Async XLA Ops:
  0.6 9.0 %copy-start = (s32[8,256]{1,0:T(8,128)S(1)}, s32[8,256]{1,0:T(8,128)}, u32[]{:S(2)}) copy-start(s32[8,256]{1,0:T(8,128)} %param.10) | copy-start | bytes 24580
  0.7 9.8 %collective-permute-start.1 = (f32[1,256]{1,0:T(1,128)}, f32[1,256]{1,0:T(1,128)S(1)}, u32[]{:S(2)}, u32[]{:S(2)}) collective-permute-start(f32[1,256]{1,0:T(1,128)} %param.11), channel_id=1, source_target_pairs={{0,4},{2,6},{4,0},{6,2},{8,12},{10,14},{12,8},{14,10},{1,5},{3,7},... | collective-permute-start | bytes 3080 | tf_op jit(solution)/shard_map/ppermute | solution.py:111
  3.7 17.8 %collective-permute-start = (bf16[64,2560]{1,0:T(8,128)(2,1)}, bf16[64,2560]{1,0:T(8,128)(2,1)}, u32[]{:S(2)}, u32[]{:S(2)}) collective-permute-start(bf16[64,2560]{1,0:T(8,128)(2,1)} %bitcast.53), channel_id=1, source_target_pairs={{0,8},{2,10},{4,12},{6,14},{8,0},{10,2},{12,4},{14,6},{16,28},{18,... | collective-permute-start | bytes 983048 | tf_op jit(solution)/shard_map/ppermute | solution.py:147
  6.3 18.5 %collective-permute-start.4 = (bf16[128,2560]{1,0:T(8,128)(2,1)}, bf16[128,2560]{1,0:T(8,128)(2,1)}, u32[]{:S(2)}, u32[]{:S(2)}) collective-permute-start(bf16[128,2560]{1,0:T(8,128)(2,1)} %param.6), channel_id=1, source_target_pairs={{0,2},{2,0},{4,6},{6,4},{8,10},{10,8},{12,14},{14,12},{1,3},{3,1},... | collective-permute-start | bytes 1966088 | tf_op jit(solution)/shard_map/ppermute | solution.py:111
  7.8 30.3 %collective-permute-start.10 = (bf16[128,2560]{1,0:T(8,128)(2,1)}, bf16[128,2560]{1,0:T(8,128)(2,1)}, u32[]{:S(2)}, u32[]{:S(2)}) collective-permute-start(bf16[128,2560]{1,0:T(8,128)(2,1)} %param.7), channel_id=1, source_target_pairs={{0,2},{2,0},{4,6},{6,4},{8,10},{10,8},{12,14},{14,12},{1,3},{3,1},... | collective-permute-start | bytes 1966088 | tf_op jit(solution)/shard_map/ppermute | solution.py:111
  10.2 17.5 %copy-start.4 = (bf16[1,64,2560]{2,1,0:T(8,128)(2,1)S(1)}, bf16[1,64,2560]{2,1,0:T(8,128)(2,1)}, u32[]{:S(2)}) copy-start(bf16[1,64,2560]{2,1,0:T(8,128)(2,1)} %param.8) | copy-start | bytes 983044
  10.4 10.7 %collective-permute-start.2 = (f32[2,256]{1,0:T(2,128)S(1)}, f32[2,256]{1,0:T(2,128)S(1)}, u32[]{:S(2)}, u32[]{:S(2)}) collective-permute-start(f32[2,256]{1,0:T(2,128)S(1)} %pad_maximum_fusion.7), channel_id=1, source_target_pairs={{0,8},{2,10},{4,12},{6,14},{8,0},{10,2},{12,4},{14,6},{1,9},{3,11}... | collective-permute-start | bytes 6152 | tf_op jit(solution)/shard_map/ppermute | solution.py:111
  10.9 16.9 %collective-permute-start.3 = (bf16[64,2560]{1,0:T(8,128)(2,1)}, bf16[64,2560]{1,0:T(8,128)(2,1)S(1)}, u32[]{:S(2)}, u32[]{:S(2)}) collective-permute-start(bf16[64,2560]{1,0:T(8,128)(2,1)} %bitcast.54), channel_id=1, source_target_pairs={{0,4},{2,6},{4,0},{6,2},{8,12},{10,14},{12,8},{14,10},{1,5},{3,7},... | collective-permute-start | bytes 983048 | tf_op jit(solution)/shard_map/ppermute | solution.py:111
  21.1 16.8 %collective-permute-start.8 = (bf16[64,2560]{1,0:T(8,128)(2,1)}, bf16[64,2560]{1,0:T(8,128)(2,1)S(1)}, u32[]{:S(2)}, u32[]{:S(2)}) collective-permute-start(bf16[64,2560]{1,0:T(8,128)(2,1)} %bitcast.48), channel_id=1, source_target_pairs={{0,8},{2,10},{4,12},{6,14},{8,0},{10,2},{12,4},{14,6},{16,28},{18,... | collective-permute-start | bytes 983048 | tf_op jit(solution)/shard_map/ppermute | solution.py:167
  21.5 19.9 %collective-permute-start.9 = (bf16[64,2560]{1,0:T(8,128)(2,1)}, bf16[64,2560]{1,0:T(8,128)(2,1)S(1)}, u32[]{:S(2)}, u32[]{:S(2)}) collective-permute-start(bf16[64,2560]{1,0:T(8,128)(2,1)} %bitcast.49), channel_id=1, source_target_pairs={{0,4},{2,6},{4,0},{6,2},{8,12},{10,14},{12,8},{14,10},{1,5},{3,7},... | collective-permute-start | bytes 983048 | tf_op jit(solution)/shard_map/ppermute | solution.py:111
  24.8 8.2 %collective-permute-start.6 = (bf16[64,2560]{1,0:T(8,128)(2,1)}, bf16[64,2560]{1,0:T(8,128)(2,1)S(1)}, u32[]{:S(2)}, u32[]{:S(2)}) collective-permute-start(bf16[64,2560]{1,0:T(8,128)(2,1)} %collective-permute-done), channel_id=1, source_target_pairs={{0,16},{16,0},{1,17},{17,1},{2,18},{18,2},{3,19},{19,3},{4,20},{20... | collective-permute-start | bytes 983048 | tf_op jit(solution)/shard_map/ppermute | solution.py:171
  29.3 1.5 %collective-permute-start.5 = (f32[192,256]{1,0:T(8,128)S(1)}, f32[192,256]{1,0:T(8,128)S(1)}, u32[]{:S(2)}, u32[]{:S(2)}) collective-permute-start(f32[192,256]{1,0:T(8,128)S(1)} %fusion.2), channel_id=1, source_target_pairs={{0,1},{1,0},{2,3},{3,2},{4,5},{5,4},{6,7},{7,6},{8,9},{9,8},{10,11... | collective-permute-start | bytes 589832 | tf_op jit(solution)/shard_map/ppermute | solution.py:135
  33.5 1.3 %collective-permute-start.7 = (f32[64,256]{1,0:T(8,128)S(1)}, f32[64,256]{1,0:T(8,128)S(1)}, u32[]{:S(2)}, u32[]{:S(2)}) collective-permute-start(f32[64,256]{1,0:T(8,128)S(1)} %fusion.73), channel_id=1, source_target_pairs={{0,1},{1,0},{2,3},{3,2},{4,5},{5,4},{6,7},{7,6},{8,9},{9,8},{10,11... | collective-permute-start | bytes 196616 | tf_op jit(solution)/shard_map/ppermute | solution.py:135
  39.6 10.6 %collective-permute-start.13 = (bf16[64,2560]{1,0:T(8,128)(2,1)S(1)}, bf16[64,2560]{1,0:T(8,128)(2,1)S(1)}, u32[]{:S(2)}, u32[]{:S(2)}) collective-permute-start(bf16[64,2560]{1,0:T(8,128)(2,1)S(1)} %add_convert_fusion.2), channel_id=1, source_target_pairs={{0,4},{2,6},{4,0},{6,2},{8,12},{10,14},{12,8},{14,10},{1,5},{3,7},... | collective-permute-start | bytes 983048 | tf_op jit(solution)/shard_map/ppermute | solution.py:111
  39.7 10.6 %collective-permute-start.11 = (bf16[64,2560]{1,0:T(8,128)(2,1)S(1)}, bf16[64,2560]{1,0:T(8,128)(2,1)S(1)}, u32[]{:S(2)}, u32[]{:S(2)}) collective-permute-start(bf16[64,2560]{1,0:T(8,128)(2,1)S(1)} %collective-permute-done.8), channel_id=1, source_target_pairs={{0,16},{16,0},{1,17},{17,1},{2,18},{18,2},{3,19},{19,3},{4,20},{20... | collective-permute-start | bytes 983048 | tf_op jit(solution)/shard_map/ppermute | solution.py:209
  42.1 1.5 %collective-permute-start.12 = (f32[192,256]{1,0:T(8,128)S(1)}, f32[192,256]{1,0:T(8,128)S(1)}, u32[]{:S(2)}, u32[]{:S(2)}) collective-permute-start(f32[192,256]{1,0:T(8,128)S(1)} %fusion.8), channel_id=1, source_target_pairs={{0,1},{1,0},{2,3},{3,2},{4,5},{5,4},{6,7},{7,6},{8,9},{9,8},{10,11... | collective-permute-start | bytes 589832 | tf_op jit(solution)/shard_map/ppermute | solution.py:135
  45.0 26.5 %collective-permute-start.19 = (bf16[64,2560]{1,0:T(8,128)(2,1)S(1)}, bf16[64,2560]{1,0:T(8,128)(2,1)S(1)}, u32[]{:S(2)}, u32[]{:S(2)}) collective-permute-start(bf16[64,2560]{1,0:T(8,128)(2,1)S(1)} %fusion.76), channel_id=1, source_target_pairs={{0,4},{2,6},{4,0},{6,2},{8,12},{10,14},{12,8},{14,10},{1,5},{3,7},... | collective-permute-start | bytes 983048 | tf_op jit(solution)/shard_map/ppermute | solution.py:111
  50.8 3.6 %collective-permute-start.15 = (f32[64,256]{1,0:T(8,128)S(1)}, f32[64,256]{1,0:T(8,128)S(1)}, u32[]{:S(2)}, u32[]{:S(2)}) collective-permute-start(f32[64,256]{1,0:T(8,128)S(1)} %fusion.77), channel_id=1, source_target_pairs={{0,1},{1,0},{2,3},{3,2},{4,5},{5,4},{6,7},{7,6},{8,9},{9,8},{10,11... | collective-permute-start | bytes 196616 | tf_op jit(solution)/shard_map/ppermute | solution.py:135
  50.9 20.6 %collective-permute-start.21 = (bf16[64,2560]{1,0:T(8,128)(2,1)S(1)}, bf16[64,2560]{1,0:T(8,128)(2,1)S(1)}, u32[]{:S(2)}, u32[]{:S(2)}) collective-permute-start(bf16[64,2560]{1,0:T(8,128)(2,1)S(1)} %add_convert_fusion.1), channel_id=1, source_target_pairs={{0,8},{2,10},{4,12},{6,14},{8,0},{10,2},{12,4},{14,6},{1,9},{3,11}... | collective-permute-start | bytes 983048 | tf_op jit(solution)/shard_map/ppermute | solution.py:111
  52.8 21.2 %collective-permute-start.14 = (bf16[128,2560]{1,0:T(8,128)(2,1)S(1)}, bf16[128,2560]{1,0:T(8,128)(2,1)S(1)}, u32[]{:S(2)}, u32[]{:S(2)}) collective-permute-start(bf16[128,2560]{1,0:T(8,128)(2,1)S(1)} %convolution_convert_fusion.1), channel_id=1, source_target_pairs={{0,2},{2,0},{4,6},{6,4},{8,10},{10,8},{12,14},{14,12},{1,3},{3,1},... | collective-permute-start | bytes 1966088 | tf_op jit(solution)/shard_map/ppermute | solution.py:111
  55.2 15.1 %collective-permute-start.17 = (bf16[64,2560]{1,0:T(8,128)(2,1)S(1)}, bf16[64,2560]{1,0:T(8,128)(2,1)S(1)}, u32[]{:S(2)}, u32[]{:S(2)}) collective-permute-start(bf16[64,2560]{1,0:T(8,128)(2,1)S(1)} %fusion.44), channel_id=1, source_target_pairs={{0,4},{2,6},{4,0},{6,2},{8,12},{10,14},{12,8},{14,10},{1,5},{3,7},... | collective-permute-start | bytes 983048 | tf_op jit(solution)/shard_map/ppermute | solution.py:111
  57.9 25.9 %collective-permute-start.16 = (bf16[128,2560]{1,0:T(8,128)(2,1)S(1)}, bf16[128,2560]{1,0:T(8,128)(2,1)S(1)}, u32[]{:S(2)}, u32[]{:S(2)}) collective-permute-start(bf16[128,2560]{1,0:T(8,128)(2,1)S(1)} %convolution_convert_fusion), channel_id=1, source_target_pairs={{0,2},{2,0},{4,6},{6,4},{8,10},{10,8},{12,14},{14,12},{1,3},{3,1},... | collective-permute-start | bytes 1966088 | tf_op jit(solution)/shard_map/ppermute | solution.py:111
  70.4 17.0 %collective-permute-start.18 = (bf16[64,2560]{1,0:T(8,128)(2,1)S(1)}, bf16[64,2560]{1,0:T(8,128)(2,1)S(1)}, u32[]{:S(2)}, u32[]{:S(2)}) collective-permute-start(bf16[64,2560]{1,0:T(8,128)(2,1)S(1)} %add_convert_fusion), channel_id=1, source_target_pairs={{0,8},{2,10},{4,12},{6,14},{8,0},{10,2},{12,4},{14,6},{1,9},{3,11}... | collective-permute-start | bytes 983048 | tf_op jit(solution)/shard_map/ppermute | solution.py:111
  71.5 15.9 %collective-permute-start.20 = (bf16[64,2560]{1,0:T(8,128)(2,1)S(1)}, bf16[64,2560]{1,0:T(8,128)(2,1)S(1)}, u32[]{:S(2)}, u32[]{:S(2)}) collective-permute-start(bf16[64,2560]{1,0:T(8,128)(2,1)S(1)} %fusion.79), channel_id=1, source_target_pairs={{0,4},{2,6},{4,0},{6,2},{8,12},{10,14},{12,8},{14,10},{1,5},{3,7},... | collective-permute-start | bytes 983048 | tf_op jit(solution)/shard_map/ppermute | solution.py:111
  (3 other events, 12.9 us)

commit v19 on v17

--- a/solution.py
+++ b/solution.py
@@ -206,7 +206,6 @@
     most = most_products(cot2, up_matrix, near_up, far_up)
     most, rows_later = lax.optimization_barrier((most, cot2))
     (own, first, second), up_send = partial_sums(others, rows_later)
-    up_first = move(up_send[0], xor_line(1))
 
     cross_up, up_sum = lax.optimization_barrier((cross_up, narrow(add_up(second, up_third))))
     up_far = move(up_sum, xor_line(2))
@@ -214,11 +213,13 @@
     low_back = low_rank(most, cot2, cross_up)
     (own_b, first_b, second_b, third_b), down_send = partial_sums(for_line(low_back), tokens2)
     down_third = move(down_send[2], xor_line(1))
+    up_later, down_send = lax.optimization_barrier((up_send[0], down_send))
+    up_first = move(up_later, xor_line(1))
     branch_back = outward_start(low, up_all)
     input_back = outward_start(low_back, down_all)
     down_sum = narrow(add_up(second_b, down_third))
     down_far = move(down_sum, xor_line(2))
-    down_first = move(after(down_send[0], (up_first, down_sum)), xor_line(1))
+    down_first = move(after(down_send[0], down_sum), xor_line(1))
     branch_out = outward_end(low, up_all, branch_back)
     up_grad = add_up(own, up_first, after(up_far, down_sum))
     input_grad = outward_end(low_back, down_all, input_back)

time: 86.6 us -> 90.8 us (1.048)
  waiting for transfers between devices: 45 us -> 49.1 us
    ppermute x14, waiting for transfers between devices: 38.6 us -> 42.7 us  [move(): return lax.ppermute(value, 'adapter', pairs)]
  transfers between devices with their start and end apart: 22 -> 22, of which waited for: 13 -> 14; matrix products, arithmetic and copies ran while one was open for 19% -> 18% of each run, Pallas kernels for 0% -> 0%
where the time goes in v19:
time: 90.8 us; the launch traced here: 90.5 us
  waiting for transfers between devices  49.1 us (54%)
  starting transfers between devices  22.8 us (25%)
  matrix products  11 us (12%)
  local copies, waits for them, and re-layouts  4.13 us (5%)
  other arithmetic  2.54 us (3%)
  between operations  0.93 us (1%)
    ppermute x14, waiting for transfers between devices, move(): return lax.ppermute(value, 'adapter', pairs)  42.7 us
    ppermute x14, starting transfers between devices, move(): return lax.ppermute(value, 'adapter', pairs)  17.2 us
    dot_general x4, matrix products, contract_first(): lax.dot_general(left_op, right_op, (((0,), (0,)), ((), ())), preferred_el...  5.06 us
    ppermute x4, waiting for transfers between devices, both_cores(): return partial + lax.ppermute(partial, 'tensor', SWAP)  4.03 us
    dot_general x4, matrix products, contract_last(): lax.dot_general(left_op, right_op, (((1,), (1,)), ((), ())), preferred_el...  3.13 us
    ppermute x1, starting transfers between devices, by_pairs(): far_down = lax.ppermute(down_matrix, ('groups', 'adapter'), FAR)  2.59 us
    dot_general x7, matrix products, partial_sums(): jnp.dot(weight, rows, preferred_element_type=jnp.float32)  2.49 us
    ppermute x1, waiting for transfers between devices, by_pairs(): cross_down = lax.ppermute(ready, 'groups', SWAP)  2.13 us
  transfers between devices with their start and end apart: 22, of which 14 were waited for; matrix products, arithmetic and copies ran while one was open for 18% of the time, Pallas kernels for 0%

profile of v19, /device:TPU:0, one launch (start us, length us, event | category | flops | bytes accessed | tf_op | source)
XLA Modules:
  0.0 90.5 jit_solution(14311529808609942097)
XLA Ops:
  0.7 3.1 %collective-permute-start.2 = (f32[1,256]{1,0:T(1,128)}, f32[1,256]{1,0:T(1,128)S(1)}, u32[]{:S(2)}, u32[]{:S(2)}) collective-permute-start(f32[1,256]{1,0:T(1,128)} %param.11), channel_id=1, source_target_pairs={{0,4},{2,6},{4,0},{6,2},{8,12},{10,14},{12,8},{14,10},{1,5},{3,7},... | collective-permute-start | bytes 3080 | tf_op jit(solution)/shard_map/ppermute | solution.py:111
  3.7 2.6 %collective-permute-start.1 = (bf16[64,2560]{1,0:T(8,128)(2,1)}, bf16[64,2560]{1,0:T(8,128)(2,1)}, u32[]{:S(2)}, u32[]{:S(2)}) collective-permute-start(bf16[64,2560]{1,0:T(8,128)(2,1)} %bitcast.51), channel_id=1, source_target_pairs={{0,8},{2,10},{4,12},{6,14},{8,0},{10,2},{12,4},{14,6},{16,28},{18,... | collective-permute-start | bytes 983048 | tf_op jit(solution)/shard_map/ppermute | solution.py:147
  6.3 1.5 %collective-permute-start.5 = (bf16[128,2560]{1,0:T(8,128)(2,1)}, bf16[128,2560]{1,0:T(8,128)(2,1)}, u32[]{:S(2)}, u32[]{:S(2)}) collective-permute-start(bf16[128,2560]{1,0:T(8,128)(2,1)} %param.6), channel_id=1, source_target_pairs={{0,2},{2,0},{4,6},{6,4},{8,10},{10,8},{12,14},{14,12},{1,3},{3,1},... | collective-permute-start | bytes 1966088 | tf_op jit(solution)/shard_map/ppermute | solution.py:111
  11.1 10.1 %collective-permute-done.3 = f32[2,256]{1,0:T(2,128)S(1)} collective-permute-done((f32[2,256]{1,0:T(2,128)S(1)}, f32[2,256]{1,0:T(2,128)S(1)}, u32[]{:S(2)}, u32[]{:S(2)}) %collective-permute-start.3) | collective-permute-done | bytes 2080 | tf_op jit(solution)/shard_map/ppermute | solution.py:111
  21.5 3.3 %collective-permute-start.9 = (bf16[64,2560]{1,0:T(8,128)(2,1)}, bf16[64,2560]{1,0:T(8,128)(2,1)S(1)}, u32[]{:S(2)}, u32[]{:S(2)}) collective-permute-start(bf16[64,2560]{1,0:T(8,128)(2,1)} %bitcast.47), channel_id=1, source_target_pairs={{0,4},{2,6},{4,0},{6,2},{8,12},{10,14},{12,8},{14,10},{1,5},{3,7},... | collective-permute-start | bytes 983048 | tf_op jit(solution)/shard_map/ppermute | solution.py:111
  27.8 1.5 %fusion.2 = f32[192,256]{1,0:T(8,128)S(1)} fusion(bf16[256,2560]{1,0:T(8,128)(2,1)S(1)} %constant_dynamic-update-slice_fusion, bf16[64,2560]{1,0:T(8,128)(2,1)} %collective-permute-done.1, bf16[64,2560]{1,0:T(8,128)(2,1)S(1)} %collective-permute-done.4, bf16[64,2560]{1,0:T(8,128)(2,1)S(1)} %bitcast.53), kind=kOutput, calls=%fused_computation.11 | convolution fusion | flops 254607360 | bytes 2490368 | tf_op jit(solution)/shard_map/dot_general | solution.py:10
  29.4 1.4 %collective-permute-done.6 = f32[192,256]{1,0:T(8,128)S(1)} collective-permute-done((f32[192,256]{1,0:T(8,128)S(1)}, f32[192,256]{1,0:T(8,128)S(1)}, u32[]{:S(2)}, u32[]{:S(2)}) %collective-permute-start.6) | collective-permute-done | bytes 196640 | tf_op jit(solution)/shard_map/ppermute | solution.py:135
  30.9 2.1 %collective-permute-done.7 = bf16[64,2560]{1,0:T(8,128)(2,1)S(1)} collective-permute-done((bf16[64,2560]{1,0:T(8,128)(2,1)}, bf16[64,2560]{1,0:T(8,128)(2,1)S(1)}, u32[]{:S(2)}, u32[]{:S(2)}) %collective-permute-start.7) | collective-permute-done | bytes 327712 | tf_op jit(solution)/shard_map/ppermute | solution.py:171
  33.6 1.2 %collective-permute-done.8 = f32[64,256]{1,0:T(8,128)S(1)} collective-permute-done((f32[64,256]{1,0:T(8,128)S(1)}, f32[64,256]{1,0:T(8,128)S(1)}, u32[]{:S(2)}, u32[]{:S(2)}) %collective-permute-start.8) | collective-permute-done | bytes 65568 | tf_op jit(solution)/shard_map/ppermute | solution.py:135
  34.8 1.8 %collective-permute-done = bf16[128,2560]{1,0:T(8,128)(2,1)} collective-permute-done((bf16[128,2560]{1,0:T(8,128)(2,1)}, bf16[128,2560]{1,0:T(8,128)(2,1)}, u32[]{:S(2)}, u32[]{:S(2)}) %collective-permute-start) | collective-permute-done | bytes 655392 | tf_op jit(solution)/shard_map/ppermute | solution.py:111
  38.7 1.6 %collective-permute-start.11 = (bf16[64,2560]{1,0:T(8,128)(2,1)S(1)}, bf16[64,2560]{1,0:T(8,128)(2,1)S(1)}, u32[]{:S(2)}, u32[]{:S(2)}) collective-permute-start(bf16[64,2560]{1,0:T(8,128)(2,1)S(1)} %collective-permute-done.10), channel_id=1, source_target_pairs={{0,16},{16,0},{1,17},{17,1},{2,18},{18,2},{3,19},{19,3},{4,20},{20... | collective-permute-start | bytes 983048 | tf_op jit(solution)/shard_map/ppermute | solution.py:205
  41.7 1.4 %collective-permute-done.12 = f32[192,256]{1,0:T(8,128)S(1)} collective-permute-done((f32[192,256]{1,0:T(8,128)S(1)}, f32[192,256]{1,0:T(8,128)S(1)}, u32[]{:S(2)}, u32[]{:S(2)}) %collective-permute-start.12) | collective-permute-done | bytes 196640 | tf_op jit(solution)/shard_map/ppermute | solution.py:135
  45.0 2.2 %collective-permute-done.13 = bf16[64,2560]{1,0:T(8,128)(2,1)S(1)} collective-permute-done((bf16[64,2560]{1,0:T(8,128)(2,1)S(1)}, bf16[64,2560]{1,0:T(8,128)(2,1)S(1)}, u32[]{:S(2)}, u32[]{:S(2)}) %collective-permute-start.13) | collective-permute-done | bytes 327712 | tf_op jit(solution)/shard_map/ppermute | solution.py:111
  48.1 1.3 %collective-permute-start.21 = (bf16[64,2560]{1,0:T(8,128)(2,1)S(1)}, bf16[64,2560]{1,0:T(8,128)(2,1)S(1)}, u32[]{:S(2)}, u32[]{:S(2)}) collective-permute-start(bf16[64,2560]{1,0:T(8,128)(2,1)S(1)} %add_convert_fusion.1), channel_id=1, source_target_pairs={{0,8},{2,10},{4,12},{6,14},{8,0},{10,2},{12,4},{14,6},{1,9},{3,11}... | collective-permute-start | bytes 983048 | tf_op jit(solution)/shard_map/ppermute | solution.py:111
  49.8 1.6 %collective-permute-start.14 = (bf16[128,2560]{1,0:T(8,128)(2,1)S(1)}, bf16[128,2560]{1,0:T(8,128)(2,1)S(1)}, u32[]{:S(2)}, u32[]{:S(2)}) collective-permute-start(bf16[128,2560]{1,0:T(8,128)(2,1)S(1)} %convolution_convert_fusion.1), channel_id=1, source_target_pairs={{0,2},{2,0},{4,6},{6,4},{8,10},{10,8},{12,14},{14,12},{1,3},{3,1},... | collective-permute-start | bytes 1966088 | tf_op jit(solution)/shard_map/ppermute | solution.py:111
  52.1 1.6 %collective-permute-start.17 = (bf16[64,2560]{1,0:T(8,128)(2,1)S(1)}, bf16[64,2560]{1,0:T(8,128)(2,1)S(1)}, u32[]{:S(2)}, u32[]{:S(2)}) collective-permute-start(bf16[64,2560]{1,0:T(8,128)(2,1)S(1)} %fusion.44), channel_id=1, source_target_pairs={{0,4},{2,6},{4,0},{6,2},{8,12},{10,14},{12,8},{14,10},{1,5},{3,7},... | collective-permute-start | bytes 983048 | tf_op jit(solution)/shard_map/ppermute | solution.py:111
  54.2 1.3 %convolution_convert_fusion = bf16[128,2560]{1,0:T(8,128)(2,1)S(1)} fusion(bf16[64,2560]{1,0:T(8,128)(2,1)S(1)} %collective-permute-done.7, bf16[64,2560]{1,0:T(8,128)(2,1)} %collective-permute-done.1, bf16[64,2560]{1,0:T(8,128)(2,1)S(1)} %collective-permute-done.4, bf16[64,2560]{1,0:T(8,128)(2,1)S(1)} %bitcast.54, ...), kind=kOutput, calls=%fused_computation.5 | convolution fusion | flops 173604864 | bytes 2031616 | tf_op jit(solution)/shard_map/dot_general | solution.py:16
  56.1 13.6 %collective-permute-done.17 = bf16[64,2560]{1,0:T(8,128)(2,1)S(1)} collective-permute-done((bf16[64,2560]{1,0:T(8,128)(2,1)S(1)}, bf16[64,2560]{1,0:T(8,128)(2,1)S(1)}, u32[]{:S(2)}, u32[]{:S(2)}) %collective-permute-start.17) | collective-permute-done | bytes 327712 | tf_op jit(solution)/shard_map/ppermute | solution.py:111
  69.9 2.1 %collective-permute-start.19 = (bf16[64,2560]{1,0:T(8,128)(2,1)S(1)}, bf16[64,2560]{1,0:T(8,128)(2,1)S(1)}, u32[]{:S(2)}, u32[]{:S(2)}) collective-permute-start(bf16[64,2560]{1,0:T(8,128)(2,1)S(1)} %fusion.78), channel_id=1, source_target_pairs={{0,4},{2,6},{4,0},{6,2},{8,12},{10,14},{12,8},{14,10},{1,5},{3,7},... | collective-permute-start | bytes 983048 | tf_op jit(solution)/shard_map/ppermute | solution.py:111
  71.9 6.7 %collective-permute-done.20 = bf16[64,2560]{1,0:T(8,128)(2,1)S(1)} collective-permute-done((bf16[64,2560]{1,0:T(8,128)(2,1)S(1)}, bf16[64,2560]{1,0:T(8,128)(2,1)S(1)}, u32[]{:S(2)}, u32[]{:S(2)}) %collective-permute-start.20) | collective-permute-done | bytes 327712 | tf_op jit(solution)/shard_map/ppermute | solution.py:111
  79.5 1.2 %fusion = bf16[128,2560]{1,0:T(8,128)(2,1)} fusion(bf16[128,2560]{1,0:T(8,128)(2,1)S(1)} %collective-permute-done.14, bf16[64,2560]{1,0:T(8,128)(2,1)S(1)} %collective-permute-done.11, bf16[64,2560]{1,0:T(8,128)(2,1)S(1)} %collective-permute-done.10, bf16[64,2560]{1,0:T(8,128)(2,1)S(1)} %collective-permute-done.9, bf16[64,2560]{1,0:T(8,128)(2,1)S(1)} %bitcast.50, ...), kind=kOutput, calls=%fused_computation.3 | convolution fusion | flops 174260224 | bytes 2686976 | tf_op jit(solution)/shard_map/dot_general | solution.py:16
  80.7 2.2 %fusion.1 = bf16[128,2560]{1,0:T(8,128)(2,1)} fusion(bf16[128,2560]{1,0:T(8,128)(2,1)S(1)} %collective-permute-done.16, bf16[64,2560]{1,0:T(8,128)(2,1)S(1)} %collective-permute-done.7, bf16[64,2560]{1,0:T(8,128)(2,1)} %collective-permute-done.1, bf16[64,2560]{1,0:T(8,128)(2,1)S(1)} %collective-permute-done.4, bf16[64,2560]{1,0:T(8,128)(2,1)S(1)} %bitcast.55, ...), kind=kOutput, calls=%fused_computation.4 | convolution fusion | flops 174260224 | bytes 2686976 | tf_op jit(solution)/shard_map/dot_general | solution.py:16
  82.9 2.5 %collective-permute-done.18 = bf16[64,2560]{1,0:T(8,128)(2,1)S(1)} collective-permute-done((bf16[64,2560]{1,0:T(8,128)(2,1)S(1)}, bf16[64,2560]{1,0:T(8,128)(2,1)S(1)}, u32[]{:S(2)}, u32[]{:S(2)}) %collective-permute-start.18) | collective-permute-done | bytes 327712 | tf_op jit(solution)/shard_map/ppermute | solution.py:111
  85.4 4.2 %collective-permute-done.19 = bf16[64,2560]{1,0:T(8,128)(2,1)S(1)} collective-permute-done((bf16[64,2560]{1,0:T(8,128)(2,1)S(1)}, bf16[64,2560]{1,0:T(8,128)(2,1)S(1)}, u32[]{:S(2)}, u32[]{:S(2)}) %collective-permute-start.19) | collective-permute-done | bytes 327712 | tf_op jit(solution)/shard_map/ppermute | solution.py:111
  (80 shorter events, 17.3 us)
Async XLA Ops:
  0.6 9.1 %copy-start = (s32[8,256]{1,0:T(8,128)S(1)}, s32[8,256]{1,0:T(8,128)}, u32[]{:S(2)}) copy-start(s32[8,256]{1,0:T(8,128)} %param.10) | copy-start | bytes 24580
  0.7 9.8 %collective-permute-start.2 = (f32[1,256]{1,0:T(1,128)}, f32[1,256]{1,0:T(1,128)S(1)}, u32[]{:S(2)}, u32[]{:S(2)}) collective-permute-start(f32[1,256]{1,0:T(1,128)} %param.11), channel_id=1, source_target_pairs={{0,4},{2,6},{4,0},{6,2},{8,12},{10,14},{12,8},{14,10},{1,5},{3,7},... | collective-permute-start | bytes 3080 | tf_op jit(solution)/shard_map/ppermute | solution.py:111
  3.7 17.8 %collective-permute-start.1 = (bf16[64,2560]{1,0:T(8,128)(2,1)}, bf16[64,2560]{1,0:T(8,128)(2,1)}, u32[]{:S(2)}, u32[]{:S(2)}) collective-permute-start(bf16[64,2560]{1,0:T(8,128)(2,1)} %bitcast.51), channel_id=1, source_target_pairs={{0,8},{2,10},{4,12},{6,14},{8,0},{10,2},{12,4},{14,6},{16,28},{18,... | collective-permute-start | bytes 983048 | tf_op jit(solution)/shard_map/ppermute | solution.py:147
  6.3 18.5 %collective-permute-start.5 = (bf16[128,2560]{1,0:T(8,128)(2,1)}, bf16[128,2560]{1,0:T(8,128)(2,1)}, u32[]{:S(2)}, u32[]{:S(2)}) collective-permute-start(bf16[128,2560]{1,0:T(8,128)(2,1)} %param.6), channel_id=1, source_target_pairs={{0,2},{2,0},{4,6},{6,4},{8,10},{10,8},{12,14},{14,12},{1,3},{3,1},... | collective-permute-start | bytes 1966088 | tf_op jit(solution)/shard_map/ppermute | solution.py:111
  7.8 28.8 %collective-permute-start = (bf16[128,2560]{1,0:T(8,128)(2,1)}, bf16[128,2560]{1,0:T(8,128)(2,1)}, u32[]{:S(2)}, u32[]{:S(2)}) collective-permute-start(bf16[128,2560]{1,0:T(8,128)(2,1)} %param.7), channel_id=1, source_target_pairs={{0,2},{2,0},{4,6},{6,4},{8,10},{10,8},{12,14},{14,12},{1,3},{3,1},... | collective-permute-start | bytes 1966088 | tf_op jit(solution)/shard_map/ppermute | solution.py:111
  9.6 18.2 %copy-start.4 = (bf16[1,64,2560]{2,1,0:T(8,128)(2,1)S(1)}, bf16[1,64,2560]{2,1,0:T(8,128)(2,1)}, u32[]{:S(2)}) copy-start(bf16[1,64,2560]{2,1,0:T(8,128)(2,1)} %param.8) | copy-start | bytes 983044
  10.4 10.7 %collective-permute-start.3 = (f32[2,256]{1,0:T(2,128)S(1)}, f32[2,256]{1,0:T(2,128)S(1)}, u32[]{:S(2)}, u32[]{:S(2)}) collective-permute-start(f32[2,256]{1,0:T(2,128)S(1)} %pad_maximum_fusion.7), channel_id=1, source_target_pairs={{0,8},{2,10},{4,12},{6,14},{8,0},{10,2},{12,4},{14,6},{1,9},{3,11}... | collective-permute-start | bytes 6152 | tf_op jit(solution)/shard_map/ppermute | solution.py:111
  10.9 16.9 %collective-permute-start.4 = (bf16[64,2560]{1,0:T(8,128)(2,1)}, bf16[64,2560]{1,0:T(8,128)(2,1)S(1)}, u32[]{:S(2)}, u32[]{:S(2)}) collective-permute-start(bf16[64,2560]{1,0:T(8,128)(2,1)} %bitcast.52), channel_id=1, source_target_pairs={{0,4},{2,6},{4,0},{6,2},{8,12},{10,14},{12,8},{14,10},{1,5},{3,7},... | collective-permute-start | bytes 983048 | tf_op jit(solution)/shard_map/ppermute | solution.py:111
  21.1 17.5 %collective-permute-start.10 = (bf16[64,2560]{1,0:T(8,128)(2,1)}, bf16[64,2560]{1,0:T(8,128)(2,1)S(1)}, u32[]{:S(2)}, u32[]{:S(2)}) collective-permute-start(bf16[64,2560]{1,0:T(8,128)(2,1)} %bitcast.46), channel_id=1, source_target_pairs={{0,8},{2,10},{4,12},{6,14},{8,0},{10,2},{12,4},{14,6},{16,28},{18,... | collective-permute-start | bytes 983048 | tf_op jit(solution)/shard_map/ppermute | solution.py:167
  21.5 19.5 %collective-permute-start.9 = (bf16[64,2560]{1,0:T(8,128)(2,1)}, bf16[64,2560]{1,0:T(8,128)(2,1)S(1)}, u32[]{:S(2)}, u32[]{:S(2)}) collective-permute-start(bf16[64,2560]{1,0:T(8,128)(2,1)} %bitcast.47), channel_id=1, source_target_pairs={{0,4},{2,6},{4,0},{6,2},{8,12},{10,14},{12,8},{14,10},{1,5},{3,7},... | collective-permute-start | bytes 983048 | tf_op jit(solution)/shard_map/ppermute | solution.py:111
  24.8 8.2 %collective-permute-start.7 = (bf16[64,2560]{1,0:T(8,128)(2,1)}, bf16[64,2560]{1,0:T(8,128)(2,1)S(1)}, u32[]{:S(2)}, u32[]{:S(2)}) collective-permute-start(bf16[64,2560]{1,0:T(8,128)(2,1)} %collective-permute-done.1), channel_id=1, source_target_pairs={{0,16},{16,0},{1,17},{17,1},{2,18},{18,2},{3,19},{19,3},{4,20},{20... | collective-permute-start | bytes 983048 | tf_op jit(solution)/shard_map/ppermute | solution.py:171
  29.3 1.5 %collective-permute-start.6 = (f32[192,256]{1,0:T(8,128)S(1)}, f32[192,256]{1,0:T(8,128)S(1)}, u32[]{:S(2)}, u32[]{:S(2)}) collective-permute-start(f32[192,256]{1,0:T(8,128)S(1)} %fusion.2), channel_id=1, source_target_pairs={{0,1},{1,0},{2,3},{3,2},{4,5},{5,4},{6,7},{7,6},{8,9},{9,8},{10,11... | collective-permute-start | bytes 589832 | tf_op jit(solution)/shard_map/ppermute | solution.py:135
  33.5 1.3 %collective-permute-start.8 = (f32[64,256]{1,0:T(8,128)S(1)}, f32[64,256]{1,0:T(8,128)S(1)}, u32[]{:S(2)}, u32[]{:S(2)}) collective-permute-start(f32[64,256]{1,0:T(8,128)S(1)} %fusion.73), channel_id=1, source_target_pairs={{0,1},{1,0},{2,3},{3,2},{4,5},{5,4},{6,7},{7,6},{8,9},{9,8},{10,11... | collective-permute-start | bytes 196616 | tf_op jit(solution)/shard_map/ppermute | solution.py:135
  38.2 9.0 %collective-permute-start.13 = (bf16[64,2560]{1,0:T(8,128)(2,1)S(1)}, bf16[64,2560]{1,0:T(8,128)(2,1)S(1)}, u32[]{:S(2)}, u32[]{:S(2)}) collective-permute-start(bf16[64,2560]{1,0:T(8,128)(2,1)S(1)} %convolution_convert_fusion.2), channel_id=1, source_target_pairs={{0,4},{2,6},{4,0},{6,2},{8,12},{10,14},{12,8},{14,10},{1,5},{3,7},... | collective-permute-start | bytes 983048 | tf_op jit(solution)/shard_map/ppermute | solution.py:111
  38.7 8.8 %collective-permute-start.11 = (bf16[64,2560]{1,0:T(8,128)(2,1)S(1)}, bf16[64,2560]{1,0:T(8,128)(2,1)S(1)}, u32[]{:S(2)}, u32[]{:S(2)}) collective-permute-start(bf16[64,2560]{1,0:T(8,128)(2,1)S(1)} %collective-permute-done.10), channel_id=1, source_target_pairs={{0,16},{16,0},{1,17},{17,1},{2,18},{18,2},{3,19},{19,3},{4,20},{20... | collective-permute-start | bytes 983048 | tf_op jit(solution)/shard_map/ppermute | solution.py:205
  41.6 1.5 %collective-permute-start.12 = (f32[192,256]{1,0:T(8,128)S(1)}, f32[192,256]{1,0:T(8,128)S(1)}, u32[]{:S(2)}, u32[]{:S(2)}) collective-permute-start(f32[192,256]{1,0:T(8,128)S(1)} %fusion.8), channel_id=1, source_target_pairs={{0,1},{1,0},{2,3},{3,2},{4,5},{5,4},{6,7},{7,6},{8,9},{9,8},{10,11... | collective-permute-start | bytes 589832 | tf_op jit(solution)/shard_map/ppermute | solution.py:135
  48.0 3.4 %collective-permute-start.15 = (f32[64,256]{1,0:T(8,128)S(1)}, f32[64,256]{1,0:T(8,128)S(1)}, u32[]{:S(2)}, u32[]{:S(2)}) collective-permute-start(f32[64,256]{1,0:T(8,128)S(1)} %fusion.76), channel_id=1, source_target_pairs={{0,1},{1,0},{2,3},{3,2},{4,5},{5,4},{6,7},{7,6},{8,9},{9,8},{10,11... | collective-permute-start | bytes 196616 | tf_op jit(solution)/shard_map/ppermute | solution.py:135
  48.1 21.8 %collective-permute-start.21 = (bf16[64,2560]{1,0:T(8,128)(2,1)S(1)}, bf16[64,2560]{1,0:T(8,128)(2,1)S(1)}, u32[]{:S(2)}, u32[]{:S(2)}) collective-permute-start(bf16[64,2560]{1,0:T(8,128)(2,1)S(1)} %add_convert_fusion.1), channel_id=1, source_target_pairs={{0,8},{2,10},{4,12},{6,14},{8,0},{10,2},{12,4},{14,6},{1,9},{3,11}... | collective-permute-start | bytes 983048 | tf_op jit(solution)/shard_map/ppermute | solution.py:111
  49.8 29.7 %collective-permute-start.14 = (bf16[128,2560]{1,0:T(8,128)(2,1)S(1)}, bf16[128,2560]{1,0:T(8,128)(2,1)S(1)}, u32[]{:S(2)}, u32[]{:S(2)}) collective-permute-start(bf16[128,2560]{1,0:T(8,128)(2,1)S(1)} %convolution_convert_fusion.1), channel_id=1, source_target_pairs={{0,2},{2,0},{4,6},{6,4},{8,10},{10,8},{12,14},{14,12},{1,3},{3,1},... | collective-permute-start | bytes 1966088 | tf_op jit(solution)/shard_map/ppermute | solution.py:111
  52.1 17.6 %collective-permute-start.17 = (bf16[64,2560]{1,0:T(8,128)(2,1)S(1)}, bf16[64,2560]{1,0:T(8,128)(2,1)S(1)}, u32[]{:S(2)}, u32[]{:S(2)}) collective-permute-start(bf16[64,2560]{1,0:T(8,128)(2,1)S(1)} %fusion.44), channel_id=1, source_target_pairs={{0,4},{2,6},{4,0},{6,2},{8,12},{10,14},{12,8},{14,10},{1,5},{3,7},... | collective-permute-start | bytes 983048 | tf_op jit(solution)/shard_map/ppermute | solution.py:111
  53.7 25.0 %collective-permute-start.20 = (bf16[64,2560]{1,0:T(8,128)(2,1)S(1)}, bf16[64,2560]{1,0:T(8,128)(2,1)S(1)}, u32[]{:S(2)}, u32[]{:S(2)}) collective-permute-start(bf16[64,2560]{1,0:T(8,128)(2,1)S(1)} %fusion.75), channel_id=1, source_target_pairs={{0,4},{2,6},{4,0},{6,2},{8,12},{10,14},{12,8},{14,10},{1,5},{3,7},... | collective-permute-start | bytes 983048 | tf_op jit(solution)/shard_map/ppermute | solution.py:111
  55.6 25.2 %collective-permute-start.16 = (bf16[128,2560]{1,0:T(8,128)(2,1)S(1)}, bf16[128,2560]{1,0:T(8,128)(2,1)S(1)}, u32[]{:S(2)}, u32[]{:S(2)}) collective-permute-start(bf16[128,2560]{1,0:T(8,128)(2,1)S(1)} %convolution_convert_fusion), channel_id=1, source_target_pairs={{0,2},{2,0},{4,6},{6,4},{8,10},{10,8},{12,14},{14,12},{1,3},{3,1},... | collective-permute-start | bytes 1966088 | tf_op jit(solution)/shard_map/ppermute | solution.py:111
  69.8 15.7 %collective-permute-start.18 = (bf16[64,2560]{1,0:T(8,128)(2,1)S(1)}, bf16[64,2560]{1,0:T(8,128)(2,1)S(1)}, u32[]{:S(2)}, u32[]{:S(2)}) collective-permute-start(bf16[64,2560]{1,0:T(8,128)(2,1)S(1)} %add_convert_fusion), channel_id=1, source_target_pairs={{0,8},{2,10},{4,12},{6,14},{8,0},{10,2},{12,4},{14,6},{1,9},{3,11}... | collective-permute-start | bytes 983048 | tf_op jit(solution)/shard_map/ppermute | solution.py:111
  69.9 19.8 %collective-permute-start.19 = (bf16[64,2560]{1,0:T(8,128)(2,1)S(1)}, bf16[64,2560]{1,0:T(8,128)(2,1)S(1)}, u32[]{:S(2)}, u32[]{:S(2)}) collective-permute-start(bf16[64,2560]{1,0:T(8,128)(2,1)S(1)} %fusion.78), channel_id=1, source_target_pairs={{0,4},{2,6},{4,0},{6,2},{8,12},{10,14},{12,8},{14,10},{1,5},{3,7},... | collective-permute-start | bytes 983048 | tf_op jit(solution)/shard_map/ppermute | solution.py:111
  (3 other events, 15.4 us)

commit v20 on v17

--- a/solution.py
+++ b/solution.py
@@ -144,11 +144,11 @@
     up_matrix = up_adapter[0]
     rank = down_matrix.shape[0]
 
-    far_down = lax.ppermute(down_matrix, ("groups", "adapter"), FAR)
     tokens2 = move(tokens, PARTNER)
     near_gate, down_later, up_later = lax.optimization_barrier(
         (move(gating, xor_line(1)), down_matrix, up_matrix)
     )
+    far_down = lax.ppermute(down_later, ("groups", "adapter"), FAR)
     near_down = move(down_later, xor_line(1))
     cot2 = move(cotangent, PARTNER)
     gates = jnp.concatenate([gating, near_gate])

time: 86.6 us -> 92.8 us (1.072)
  starting transfers between devices: 22.7 us -> 28.1 us
  waiting for transfers between devices: 45 us -> 48.8 us
  matrix products: 11 us -> 8.12 us
    ppermute x1, waiting for transfers between devices: 0.01 us -> 13.8 us  [by_pairs(): far_down = lax.ppermute(down_later, ('groups', 'adapter'), FAR)]
    ppermute x14, waiting for transfers between devices: 38.6 us -> 29.2 us  [move(): return lax.ppermute(value, 'adapter', pairs)]
    ppermute x1, starting transfers between devices: 1.07 us -> 5.69 us  [by_pairs(): cross_down = lax.ppermute(ready, 'groups', SWAP)]
    ppermute x1, starting transfers between devices: 0.01 us -> 2.57 us  [by_pairs(): far_up = lax.ppermute(up_later, ('groups', 'adapter'), FAR)]
    ppermute x1, starting transfers between devices: 2.59 us -> 0.34 us  [by_pairs(): far_down = lax.ppermute(down_later, ('groups', 'adapter'), FAR)]
    dot_general x4, matrix products: 5.07 us -> 3.12 us  [contract_first(): lax.dot_general(left_op, right_op, (((0,), (0,)), ((), ())), preferred_el...]
    dot_general x4, matrix products: 3.13 us -> 2.16 us  [contract_last(): lax.dot_general(left_op, right_op, (((1,), (1,)), ((), ())), preferred_el...]
  transfers between devices with their start and end apart: 22 -> 22, of which waited for: 13 -> 12; matrix products, arithmetic and copies ran while one was open for 19% -> 15% of each run, Pallas kernels for 0% -> 0%
where the time goes in v20:
time: 92.8 us; the launch traced here: 92.6 us
  waiting for transfers between devices  48.8 us (53%)
  starting transfers between devices  28.1 us (30%)
  matrix products  8.12 us (9%)
  local copies, waits for them, and re-layouts  4.13 us (4%)
  other arithmetic  2.54 us (3%)
  between operations  0.93 us (1%)
    ppermute x14, waiting for transfers between devices, move(): return lax.ppermute(value, 'adapter', pairs)  29.2 us
    ppermute x14, starting transfers between devices, move(): return lax.ppermute(value, 'adapter', pairs)  17.5 us
    ppermute x1, waiting for transfers between devices, by_pairs(): far_down = lax.ppermute(down_later, ('groups', 'adapter'), FAR)  13.8 us
    ppermute x1, starting transfers between devices, by_pairs(): cross_down = lax.ppermute(ready, 'groups', SWAP)  5.69 us
    ppermute x4, waiting for transfers between devices, both_cores(): return partial + lax.ppermute(partial, 'tensor', SWAP)  4.03 us
    dot_general x4, matrix products, contract_first(): lax.dot_general(left_op, right_op, (((0,), (0,)), ((), ())), preferred_el...  3.12 us
    ppermute x1, starting transfers between devices, by_pairs(): far_up = lax.ppermute(up_later, ('groups', 'adapter'), FAR)  2.57 us
    dot_general x7, matrix products, partial_sums(): jnp.dot(weight, rows, preferred_element_type=jnp.float32)  2.48 us
  transfers between devices with their start and end apart: 22, of which 12 were waited for; matrix products, arithmetic and copies ran while one was open for 15% of the time, Pallas kernels for 0%

profile of v20, /device:TPU:0, one launch (start us, length us, event | category | flops | bytes accessed | tf_op | source)
XLA Modules:
  0.0 92.6 jit_solution(18130524471192378081)
XLA Ops:
  0.7 3.1 %collective-permute-start.1 = (f32[1,256]{1,0:T(1,128)}, f32[1,256]{1,0:T(1,128)S(1)}, u32[]{:S(2)}, u32[]{:S(2)}) collective-permute-start(f32[1,256]{1,0:T(1,128)} %param.11), channel_id=1, source_target_pairs={{0,4},{2,6},{4,0},{6,2},{8,12},{10,14},{12,8},{14,10},{1,5},{3,7},... | collective-permute-start | bytes 3080 | tf_op jit(solution)/shard_map/ppermute | solution.py:111
  3.7 1.5 %collective-permute-start.5 = (bf16[128,2560]{1,0:T(8,128)(2,1)}, bf16[128,2560]{1,0:T(8,128)(2,1)}, u32[]{:S(2)}, u32[]{:S(2)}) collective-permute-start(bf16[128,2560]{1,0:T(8,128)(2,1)} %param.6), channel_id=1, source_target_pairs={{0,2},{2,0},{4,6},{6,4},{8,10},{10,8},{12,14},{14,12},{1,3},{3,1},... | collective-permute-start | bytes 1966088 | tf_op jit(solution)/shard_map/ppermute | solution.py:111
  5.8 1.1 %constant_dynamic-update-slice_fusion.1 = bf16[256,2560]{1,0:T(8,128)(2,1)S(1)} fusion(bf16[128,2560]{1,0:T(8,128)(2,1)} %param.6), kind=kLoop, calls=%fused_computation.77 | loop fusion | bytes 1310720
  7.9 2.7 %collective-permute-start.3 = (f32[2,256]{1,0:T(2,128)S(1)}, f32[2,256]{1,0:T(2,128)S(1)}, u32[]{:S(2)}, u32[]{:S(2)}) collective-permute-start(f32[2,256]{1,0:T(2,128)S(1)} %pad_maximum_fusion.7), channel_id=1, source_target_pairs={{0,8},{2,10},{4,12},{6,14},{8,0},{10,2},{12,4},{14,6},{1,9},{3,11}... | collective-permute-start | bytes 6152 | tf_op jit(solution)/shard_map/ppermute | solution.py:111
  11.1 1.5 %collective-permute-done.3 = f32[2,256]{1,0:T(2,128)S(1)} collective-permute-done((f32[2,256]{1,0:T(2,128)S(1)}, f32[2,256]{1,0:T(2,128)S(1)}, u32[]{:S(2)}, u32[]{:S(2)}) %collective-permute-start.3) | collective-permute-done | bytes 2080 | tf_op jit(solution)/shard_map/ppermute | solution.py:111
  12.5 2.6 %collective-permute-start.10 = (bf16[64,2560]{1,0:T(8,128)(2,1)}, bf16[64,2560]{1,0:T(8,128)(2,1)S(1)}, u32[]{:S(2)}, u32[]{:S(2)}) collective-permute-start(bf16[64,2560]{1,0:T(8,128)(2,1)} %bitcast.46), channel_id=1, source_target_pairs={{0,8},{2,10},{4,12},{6,14},{8,0},{10,2},{12,4},{14,6},{16,28},{18,... | collective-permute-start | bytes 983048 | tf_op jit(solution)/shard_map/ppermute | solution.py:167
  15.5 13.8 %collective-permute-done.2 = bf16[64,2560]{1,0:T(8,128)(2,1)S(1)} collective-permute-done((bf16[64,2560]{1,0:T(8,128)(2,1)}, bf16[64,2560]{1,0:T(8,128)(2,1)S(1)}, u32[]{:S(2)}, u32[]{:S(2)}) %collective-permute-start.2) | collective-permute-done | bytes 327712 | tf_op jit(solution)/shard_map/ppermute | solution.py:151
  29.3 5.7 %collective-permute-start.7 = (bf16[64,2560]{1,0:T(8,128)(2,1)S(1)}, bf16[64,2560]{1,0:T(8,128)(2,1)S(1)}, u32[]{:S(2)}, u32[]{:S(2)}) collective-permute-start(bf16[64,2560]{1,0:T(8,128)(2,1)S(1)} %collective-permute-done.2), channel_id=1, source_target_pairs={{0,16},{16,0},{1,17},{17,1},{2,18},{18,2},{3,19},{19,3},{4,20},{20... | collective-permute-start | bytes 983048 | tf_op jit(solution)/shard_map/ppermute | solution.py:171
  36.8 1.4 %collective-permute-done.6 = f32[192,256]{1,0:T(8,128)S(1)} collective-permute-done((f32[192,256]{1,0:T(8,128)S(1)}, f32[192,256]{1,0:T(8,128)S(1)}, u32[]{:S(2)}, u32[]{:S(2)}) %collective-permute-start.6) | collective-permute-done | bytes 196640 | tf_op jit(solution)/shard_map/ppermute | solution.py:135
  38.2 1.8 %collective-permute-done.7 = bf16[64,2560]{1,0:T(8,128)(2,1)S(1)} collective-permute-done((bf16[64,2560]{1,0:T(8,128)(2,1)S(1)}, bf16[64,2560]{1,0:T(8,128)(2,1)S(1)}, u32[]{:S(2)}, u32[]{:S(2)}) %collective-permute-start.7) | collective-permute-done | bytes 327712 | tf_op jit(solution)/shard_map/ppermute | solution.py:171
  40.6 1.2 %collective-permute-done.8 = f32[64,256]{1,0:T(8,128)S(1)} collective-permute-done((f32[64,256]{1,0:T(8,128)S(1)}, f32[64,256]{1,0:T(8,128)S(1)}, u32[]{:S(2)}, u32[]{:S(2)}) %collective-permute-start.8) | collective-permute-done | bytes 65568 | tf_op jit(solution)/shard_map/ppermute | solution.py:135
  41.9 1.2 %constant_dynamic-update-slice_fusion.2 = bf16[256,2560]{1,0:T(8,128)(2,1)S(1)} fusion(bf16[256,2560]{1,0:T(8,128)(2,1)S(1)} %constant_dynamic-update-slice_fusion.3, bf16[128,2560]{1,0:T(8,128)(2,1)} %collective-permute-done), kind=kLoop, calls=%fused_computation.78 | loop fusion | bytes 1310720 | tf_op jit(solution)/shard_map/concatenate | solution.py:200
  43.9 1.7 %collective-permute-start.11 = (bf16[64,2560]{1,0:T(8,128)(2,1)S(1)}, bf16[64,2560]{1,0:T(8,128)(2,1)S(1)}, u32[]{:S(2)}, u32[]{:S(2)}) collective-permute-start(bf16[64,2560]{1,0:T(8,128)(2,1)S(1)} %collective-permute-done.10), channel_id=1, source_target_pairs={{0,16},{16,0},{1,17},{17,1},{2,18},{18,2},{3,19},{19,3},{4,20},{20... | collective-permute-start | bytes 983048 | tf_op jit(solution)/shard_map/ppermute | solution.py:205
  46.4 1.4 %collective-permute-done.12 = f32[192,256]{1,0:T(8,128)S(1)} collective-permute-done((f32[192,256]{1,0:T(8,128)S(1)}, f32[192,256]{1,0:T(8,128)S(1)}, u32[]{:S(2)}, u32[]{:S(2)}) %collective-permute-start.12) | collective-permute-done | bytes 196640 | tf_op jit(solution)/shard_map/ppermute | solution.py:135
  49.3 1.9 %collective-permute-start.19 = (bf16[64,2560]{1,0:T(8,128)(2,1)S(1)}, bf16[64,2560]{1,0:T(8,128)(2,1)S(1)}, u32[]{:S(2)}, u32[]{:S(2)}) collective-permute-start(bf16[64,2560]{1,0:T(8,128)(2,1)S(1)} %fusion.75), channel_id=1, source_target_pairs={{0,4},{2,6},{4,0},{6,2},{8,12},{10,14},{12,8},{14,10},{1,5},{3,7},... | collective-permute-start | bytes 983048 | tf_op jit(solution)/shard_map/ppermute | solution.py:111
  51.5 2.5 %collective-permute-done.13 = bf16[64,2560]{1,0:T(8,128)(2,1)S(1)} collective-permute-done((bf16[64,2560]{1,0:T(8,128)(2,1)S(1)}, bf16[64,2560]{1,0:T(8,128)(2,1)S(1)}, u32[]{:S(2)}, u32[]{:S(2)}) %collective-permute-start.13) | collective-permute-done | bytes 327712 | tf_op jit(solution)/shard_map/ppermute | solution.py:111
  54.7 1.9 %collective-permute-start.21 = (bf16[64,2560]{1,0:T(8,128)(2,1)S(1)}, bf16[64,2560]{1,0:T(8,128)(2,1)S(1)}, u32[]{:S(2)}, u32[]{:S(2)}) collective-permute-start(bf16[64,2560]{1,0:T(8,128)(2,1)S(1)} %add_convert_fusion.1), channel_id=1, source_target_pairs={{0,8},{2,10},{4,12},{6,14},{8,0},{10,2},{12,4},{14,6},{1,9},{3,11}... | collective-permute-start | bytes 983048 | tf_op jit(solution)/shard_map/ppermute | solution.py:111
  57.0 1.6 %collective-permute-start.14 = (bf16[128,2560]{1,0:T(8,128)(2,1)S(1)}, bf16[128,2560]{1,0:T(8,128)(2,1)S(1)}, u32[]{:S(2)}, u32[]{:S(2)}) collective-permute-start(bf16[128,2560]{1,0:T(8,128)(2,1)S(1)} %convolution_convert_fusion.1), channel_id=1, source_target_pairs={{0,2},{2,0},{4,6},{6,4},{8,10},{10,8},{12,14},{14,12},{1,3},{3,1},... | collective-permute-start | bytes 1966088 | tf_op jit(solution)/shard_map/ppermute | solution.py:111
  61.2 13.2 %collective-permute-done.17 = bf16[64,2560]{1,0:T(8,128)(2,1)S(1)} collective-permute-done((bf16[64,2560]{1,0:T(8,128)(2,1)S(1)}, bf16[64,2560]{1,0:T(8,128)(2,1)S(1)}, u32[]{:S(2)}, u32[]{:S(2)}) %collective-permute-start.17) | collective-permute-done | bytes 327712 | tf_op jit(solution)/shard_map/ppermute | solution.py:111
  74.4 1.9 %collective-permute-start.18 = (bf16[64,2560]{1,0:T(8,128)(2,1)S(1)}, bf16[64,2560]{1,0:T(8,128)(2,1)S(1)}, u32[]{:S(2)}, u32[]{:S(2)}) collective-permute-start(bf16[64,2560]{1,0:T(8,128)(2,1)S(1)} %add_convert_fusion), channel_id=1, source_target_pairs={{0,8},{2,10},{4,12},{6,14},{8,0},{10,2},{12,4},{14,6},{1,9},{3,11}... | collective-permute-start | bytes 983048 | tf_op jit(solution)/shard_map/ppermute | solution.py:111
  77.4 1.2 %fusion = bf16[128,2560]{1,0:T(8,128)(2,1)} fusion(bf16[128,2560]{1,0:T(8,128)(2,1)S(1)} %collective-permute-done.14, bf16[64,2560]{1,0:T(8,128)(2,1)S(1)} %collective-permute-done.11, bf16[64,2560]{1,0:T(8,128)(2,1)S(1)} %collective-permute-done.10, bf16[64,2560]{1,0:T(8,128)(2,1)S(1)} %collective-permute-done.9, bf16[64,2560]{1,0:T(8,128)(2,1)S(1)} %bitcast.50, ...), kind=kOutput, calls=%fused_computation.3 | convolution fusion | flops 174260224 | bytes 2686976 | tf_op jit(solution)/shard_map/dot_general | solution.py:16
  78.6 9.3 %collective-permute-done.16 = bf16[128,2560]{1,0:T(8,128)(2,1)S(1)} collective-permute-done((bf16[128,2560]{1,0:T(8,128)(2,1)S(1)}, bf16[128,2560]{1,0:T(8,128)(2,1)S(1)}, u32[]{:S(2)}, u32[]{:S(2)}) %collective-permute-start.16) | collective-permute-done | bytes 655392 | tf_op jit(solution)/shard_map/ppermute | solution.py:111
  87.9 1.2 %fusion.1 = bf16[128,2560]{1,0:T(8,128)(2,1)} fusion(bf16[128,2560]{1,0:T(8,128)(2,1)S(1)} %collective-permute-done.16, bf16[64,2560]{1,0:T(8,128)(2,1)S(1)} %collective-permute-done.7, bf16[64,2560]{1,0:T(8,128)(2,1)S(1)} %collective-permute-done.2, bf16[64,2560]{1,0:T(8,128)(2,1)S(1)} %collective-permute-done.4, bf16[64,2560]{1,0:T(8,128)(2,1)S(1)} %bitcast.55, ...), kind=kOutput, calls=%fused_computation.4 | convolution fusion | flops 174260224 | bytes 2686976 | tf_op jit(solution)/shard_map/dot_general | solution.py:16
  89.1 2.3 %collective-permute-done.18 = bf16[64,2560]{1,0:T(8,128)(2,1)S(1)} collective-permute-done((bf16[64,2560]{1,0:T(8,128)(2,1)S(1)}, bf16[64,2560]{1,0:T(8,128)(2,1)S(1)}, u32[]{:S(2)}, u32[]{:S(2)}) %collective-permute-start.18) | collective-permute-done | bytes 327712 | tf_op jit(solution)/shard_map/ppermute | solution.py:111
  (80 shorter events, 14.2 us)
Async XLA Ops:
  0.6 6.5 %copy-start = (s32[8,256]{1,0:T(8,128)S(1)}, s32[8,256]{1,0:T(8,128)}, u32[]{:S(2)}) copy-start(s32[8,256]{1,0:T(8,128)} %param.10) | copy-start | bytes 24580
  0.7 7.2 %collective-permute-start.1 = (f32[1,256]{1,0:T(1,128)}, f32[1,256]{1,0:T(1,128)S(1)}, u32[]{:S(2)}, u32[]{:S(2)}) collective-permute-start(f32[1,256]{1,0:T(1,128)} %param.11), channel_id=1, source_target_pairs={{0,4},{2,6},{4,0},{6,2},{8,12},{10,14},{12,8},{14,10},{1,5},{3,7},... | collective-permute-start | bytes 3080 | tf_op jit(solution)/shard_map/ppermute | solution.py:111
  3.7 25.5 %collective-permute-start.5 = (bf16[128,2560]{1,0:T(8,128)(2,1)}, bf16[128,2560]{1,0:T(8,128)(2,1)}, u32[]{:S(2)}, u32[]{:S(2)}) collective-permute-start(bf16[128,2560]{1,0:T(8,128)(2,1)} %param.6), channel_id=1, source_target_pairs={{0,2},{2,0},{4,6},{6,4},{8,10},{10,8},{12,14},{14,12},{1,3},{3,1},... | collective-permute-start | bytes 1966088 | tf_op jit(solution)/shard_map/ppermute | solution.py:111
  5.2 36.6 %collective-permute-start = (bf16[128,2560]{1,0:T(8,128)(2,1)}, bf16[128,2560]{1,0:T(8,128)(2,1)}, u32[]{:S(2)}, u32[]{:S(2)}) collective-permute-start(bf16[128,2560]{1,0:T(8,128)(2,1)} %param.7), channel_id=1, source_target_pairs={{0,2},{2,0},{4,6},{6,4},{8,10},{10,8},{12,14},{14,12},{1,3},{3,1},... | collective-permute-start | bytes 1966088 | tf_op jit(solution)/shard_map/ppermute | solution.py:111
  7.0 29.1 %copy-start.4 = (bf16[1,64,2560]{2,1,0:T(8,128)(2,1)S(1)}, bf16[1,64,2560]{2,1,0:T(8,128)(2,1)}, u32[]{:S(2)}) copy-start(bf16[1,64,2560]{2,1,0:T(8,128)(2,1)} %param.8) | copy-start | bytes 983044
  7.9 4.7 %collective-permute-start.3 = (f32[2,256]{1,0:T(2,128)S(1)}, f32[2,256]{1,0:T(2,128)S(1)}, u32[]{:S(2)}, u32[]{:S(2)}) collective-permute-start(f32[2,256]{1,0:T(2,128)S(1)} %pad_maximum_fusion.7), channel_id=1, source_target_pairs={{0,8},{2,10},{4,12},{6,14},{8,0},{10,2},{12,4},{14,6},{1,9},{3,11}... | collective-permute-start | bytes 6152 | tf_op jit(solution)/shard_map/ppermute | solution.py:111
  10.5 18.7 %collective-permute-start.2 = (bf16[64,2560]{1,0:T(8,128)(2,1)}, bf16[64,2560]{1,0:T(8,128)(2,1)S(1)}, u32[]{:S(2)}, u32[]{:S(2)}) collective-permute-start(bf16[64,2560]{1,0:T(8,128)(2,1)} %bitcast.51), channel_id=1, source_target_pairs={{0,8},{2,10},{4,12},{6,14},{8,0},{10,2},{12,4},{14,6},{16,28},{18,... | collective-permute-start | bytes 983048 | tf_op jit(solution)/shard_map/ppermute | solution.py:151
  10.9 25.2 %collective-permute-start.4 = (bf16[64,2560]{1,0:T(8,128)(2,1)}, bf16[64,2560]{1,0:T(8,128)(2,1)S(1)}, u32[]{:S(2)}, u32[]{:S(2)}) collective-permute-start(bf16[64,2560]{1,0:T(8,128)(2,1)} %bitcast.52), channel_id=1, source_target_pairs={{0,4},{2,6},{4,0},{6,2},{8,12},{10,14},{12,8},{14,10},{1,5},{3,7},... | collective-permute-start | bytes 983048 | tf_op jit(solution)/shard_map/ppermute | solution.py:111
  12.5 31.4 %collective-permute-start.10 = (bf16[64,2560]{1,0:T(8,128)(2,1)}, bf16[64,2560]{1,0:T(8,128)(2,1)S(1)}, u32[]{:S(2)}, u32[]{:S(2)}) collective-permute-start(bf16[64,2560]{1,0:T(8,128)(2,1)} %bitcast.46), channel_id=1, source_target_pairs={{0,8},{2,10},{4,12},{6,14},{8,0},{10,2},{12,4},{14,6},{16,28},{18,... | collective-permute-start | bytes 983048 | tf_op jit(solution)/shard_map/ppermute | solution.py:167
  29.2 16.5 %collective-permute-start.9 = (bf16[64,2560]{1,0:T(8,128)(2,1)}, bf16[64,2560]{1,0:T(8,128)(2,1)S(1)}, u32[]{:S(2)}, u32[]{:S(2)}) collective-permute-start(bf16[64,2560]{1,0:T(8,128)(2,1)} %bitcast.47), channel_id=1, source_target_pairs={{0,4},{2,6},{4,0},{6,2},{8,12},{10,14},{12,8},{14,10},{1,5},{3,7},... | collective-permute-start | bytes 983048 | tf_op jit(solution)/shard_map/ppermute | solution.py:111
  29.3 10.7 %collective-permute-start.7 = (bf16[64,2560]{1,0:T(8,128)(2,1)S(1)}, bf16[64,2560]{1,0:T(8,128)(2,1)S(1)}, u32[]{:S(2)}, u32[]{:S(2)}) collective-permute-start(bf16[64,2560]{1,0:T(8,128)(2,1)S(1)} %collective-permute-done.2), channel_id=1, source_target_pairs={{0,16},{16,0},{1,17},{17,1},{2,18},{18,2},{3,19},{19,3},{4,20},{20... | collective-permute-start | bytes 983048 | tf_op jit(solution)/shard_map/ppermute | solution.py:171
  36.7 1.5 %collective-permute-start.6 = (f32[192,256]{1,0:T(8,128)S(1)}, f32[192,256]{1,0:T(8,128)S(1)}, u32[]{:S(2)}, u32[]{:S(2)}) collective-permute-start(f32[192,256]{1,0:T(8,128)S(1)} %fusion.2), channel_id=1, source_target_pairs={{0,1},{1,0},{2,3},{3,2},{4,5},{5,4},{6,7},{7,6},{8,9},{9,8},{10,11... | collective-permute-start | bytes 589832 | tf_op jit(solution)/shard_map/ppermute | solution.py:135
  40.5 1.3 %collective-permute-start.8 = (f32[64,256]{1,0:T(8,128)S(1)}, f32[64,256]{1,0:T(8,128)S(1)}, u32[]{:S(2)}, u32[]{:S(2)}) collective-permute-start(f32[64,256]{1,0:T(8,128)S(1)} %fusion.73), channel_id=1, source_target_pairs={{0,1},{1,0},{2,3},{3,2},{4,5},{5,4},{6,7},{7,6},{8,9},{9,8},{10,11... | collective-permute-start | bytes 196616 | tf_op jit(solution)/shard_map/ppermute | solution.py:135
  43.4 10.6 %collective-permute-start.13 = (bf16[64,2560]{1,0:T(8,128)(2,1)S(1)}, bf16[64,2560]{1,0:T(8,128)(2,1)S(1)}, u32[]{:S(2)}, u32[]{:S(2)}) collective-permute-start(bf16[64,2560]{1,0:T(8,128)(2,1)S(1)} %convolution_convert_fusion.2), channel_id=1, source_target_pairs={{0,4},{2,6},{4,0},{6,2},{8,12},{10,14},{12,8},{14,10},{1,5},{3,7},... | collective-permute-start | bytes 983048 | tf_op jit(solution)/shard_map/ppermute | solution.py:111
  43.9 10.2 %collective-permute-start.11 = (bf16[64,2560]{1,0:T(8,128)(2,1)S(1)}, bf16[64,2560]{1,0:T(8,128)(2,1)S(1)}, u32[]{:S(2)}, u32[]{:S(2)}) collective-permute-start(bf16[64,2560]{1,0:T(8,128)(2,1)S(1)} %collective-permute-done.10), channel_id=1, source_target_pairs={{0,16},{16,0},{1,17},{17,1},{2,18},{18,2},{3,19},{19,3},{4,20},{20... | collective-permute-start | bytes 983048 | tf_op jit(solution)/shard_map/ppermute | solution.py:205
  46.3 1.5 %collective-permute-start.12 = (f32[192,256]{1,0:T(8,128)S(1)}, f32[192,256]{1,0:T(8,128)S(1)}, u32[]{:S(2)}, u32[]{:S(2)}) collective-permute-start(f32[192,256]{1,0:T(8,128)S(1)} %fusion.8), channel_id=1, source_target_pairs={{0,1},{1,0},{2,3},{3,2},{4,5},{5,4},{6,7},{7,6},{8,9},{9,8},{10,11... | collective-permute-start | bytes 589832 | tf_op jit(solution)/shard_map/ppermute | solution.py:135
  49.3 27.0 %collective-permute-start.19 = (bf16[64,2560]{1,0:T(8,128)(2,1)S(1)}, bf16[64,2560]{1,0:T(8,128)(2,1)S(1)}, u32[]{:S(2)}, u32[]{:S(2)}) collective-permute-start(bf16[64,2560]{1,0:T(8,128)(2,1)S(1)} %fusion.75), channel_id=1, source_target_pairs={{0,4},{2,6},{4,0},{6,2},{8,12},{10,14},{12,8},{14,10},{1,5},{3,7},... | collective-permute-start | bytes 983048 | tf_op jit(solution)/shard_map/ppermute | solution.py:111
  54.6 3.9 %collective-permute-start.15 = (f32[64,256]{1,0:T(8,128)S(1)}, f32[64,256]{1,0:T(8,128)S(1)}, u32[]{:S(2)}, u32[]{:S(2)}) collective-permute-start(f32[64,256]{1,0:T(8,128)S(1)} %fusion.76), channel_id=1, source_target_pairs={{0,1},{1,0},{2,3},{3,2},{4,5},{5,4},{6,7},{7,6},{8,9},{9,8},{10,11... | collective-permute-start | bytes 196616 | tf_op jit(solution)/shard_map/ppermute | solution.py:135
  54.7 21.6 %collective-permute-start.21 = (bf16[64,2560]{1,0:T(8,128)(2,1)S(1)}, bf16[64,2560]{1,0:T(8,128)(2,1)S(1)}, u32[]{:S(2)}, u32[]{:S(2)}) collective-permute-start(bf16[64,2560]{1,0:T(8,128)(2,1)S(1)} %add_convert_fusion.1), channel_id=1, source_target_pairs={{0,8},{2,10},{4,12},{6,14},{8,0},{10,2},{12,4},{14,6},{1,9},{3,11}... | collective-permute-start | bytes 983048 | tf_op jit(solution)/shard_map/ppermute | solution.py:111
  57.0 20.5 %collective-permute-start.14 = (bf16[128,2560]{1,0:T(8,128)(2,1)S(1)}, bf16[128,2560]{1,0:T(8,128)(2,1)S(1)}, u32[]{:S(2)}, u32[]{:S(2)}) collective-permute-start(bf16[128,2560]{1,0:T(8,128)(2,1)S(1)} %convolution_convert_fusion.1), channel_id=1, source_target_pairs={{0,2},{2,0},{4,6},{6,4},{8,10},{10,8},{12,14},{14,12},{1,3},{3,1},... | collective-permute-start | bytes 1966088 | tf_op jit(solution)/shard_map/ppermute | solution.py:111
  59.2 15.1 %collective-permute-start.17 = (bf16[64,2560]{1,0:T(8,128)(2,1)S(1)}, bf16[64,2560]{1,0:T(8,128)(2,1)S(1)}, u32[]{:S(2)}, u32[]{:S(2)}) collective-permute-start(bf16[64,2560]{1,0:T(8,128)(2,1)S(1)} %fusion.44), channel_id=1, source_target_pairs={{0,4},{2,6},{4,0},{6,2},{8,12},{10,14},{12,8},{14,10},{1,5},{3,7},... | collective-permute-start | bytes 983048 | tf_op jit(solution)/shard_map/ppermute | solution.py:111
  60.6 27.3 %collective-permute-start.16 = (bf16[128,2560]{1,0:T(8,128)(2,1)S(1)}, bf16[128,2560]{1,0:T(8,128)(2,1)S(1)}, u32[]{:S(2)}, u32[]{:S(2)}) collective-permute-start(bf16[128,2560]{1,0:T(8,128)(2,1)S(1)} %convolution_convert_fusion), channel_id=1, source_target_pairs={{0,2},{2,0},{4,6},{6,4},{8,10},{10,8},{12,14},{14,12},{1,3},{3,1},... | collective-permute-start | bytes 1966088 | tf_op jit(solution)/shard_map/ppermute | solution.py:111
  74.4 17.0 %collective-permute-start.18 = (bf16[64,2560]{1,0:T(8,128)(2,1)S(1)}, bf16[64,2560]{1,0:T(8,128)(2,1)S(1)}, u32[]{:S(2)}, u32[]{:S(2)}) collective-permute-start(bf16[64,2560]{1,0:T(8,128)(2,1)S(1)} %add_convert_fusion), channel_id=1, source_target_pairs={{0,8},{2,10},{4,12},{6,14},{8,0},{10,2},{12,4},{14,6},{1,9},{3,11}... | collective-permute-start | bytes 983048 | tf_op jit(solution)/shard_map/ppermute | solution.py:111
  76.3 15.5 %collective-permute-start.20 = (bf16[64,2560]{1,0:T(8,128)(2,1)S(1)}, bf16[64,2560]{1,0:T(8,128)(2,1)S(1)}, u32[]{:S(2)}, u32[]{:S(2)}) collective-permute-start(bf16[64,2560]{1,0:T(8,128)(2,1)S(1)} %fusion.78), channel_id=1, source_target_pairs={{0,4},{2,6},{4,0},{6,2},{8,12},{10,14},{12,8},{14,10},{1,5},{3,7},... | collective-permute-start | bytes 983048 | tf_op jit(solution)/shard_map/ppermute | solution.py:111
  (3 other events, 12.2 us)
